TPU v7x, 256 devices: a whole 4x4x8 slice. The times are simulated.
256 devices in a mesh: tok: 64 (over x, z, core), head: 4 (over y).
Axes of the slice: x: 4, y: 4, z: 8, core: 2. Of those that a mesh axis runs over, the one named last changes fastest.
Arguments:
- tokens: bfloat16 [65536, 1536], P('tok'), may hold values from -96 to 96
- qkv_weight: bfloat16 [1536, 4608], P(None, 'head'), may hold values from -0.15625 to 0.15625
- rate_weight: bfloat16 [1536, 12], P(None, 'head'), may hold values from -0.15625 to 0.15625
- first_fast: bfloat16 [4, 384, 768], P('head'), may hold values from -0.3125 to 0.3125
- gate_fast: bfloat16 [4, 384, 768], P('head'), may hold values from -0.3125 to 0.3125
- second_fast: bfloat16 [4, 768, 384], P('head'), may hold values from -0.21875 to 0.21875
- fast_gain: float32 [1536], P('head'), may hold values from 0.1 to 1.9
- out_weight: bfloat16 [1536, 1536], P('head'), may hold values from -0.15625 to 0.15625
- frame_lengths: int32 [128], replicated, may hold values from 1 to 1024, 65536 in all
Outputs:
- layer_out: bfloat16 [65536, 1536], P('tok', 'head')
Inputs may be any that keep to these rules, and one draw needn't show every extreme that they name: `frame_lengths`: they sum to 65536; one frame has exactly 1024 tokens.
All inputs are finite; a program needn't handle non-finite values.
Results may differ from a plain program's by a relative error of at most 0.02.
The roundings to bfloat16 on the way count: a program that leaves them out, or rounds other values in their place, can miss the bound.
Values may be sent and summed in bfloat16 or wider, within the bound.
No kernel may reach another device: no remote copies, remote signals or barrier semaphores. Data moves between devices by JAX's collectives and lax.ppermute only.
A program may use at most 128 MiB of HBM per device.

v0:
```python
import math

import jax
import jax.numpy as jnp
from jax import lax
from jax.sharding import PartitionSpec as P

FRAME = 1024


def extended(value, sides, width):
    for axis, dim in sides:
        peers, length = (lax.axis_size(axis), value.shape[dim])
        up = [(i, (i + 1) % peers) for i in range(peers - 1)]
        down = [(j, i) for i, j in up]
        last = lax.slice_in_dim(value, length - width, length, axis=dim)
        first = lax.slice_in_dim(value, 0, width, axis=dim)
        before = lax.ppermute(last, axis, up)
        after = lax.ppermute(first, axis, down)
        value = jnp.concatenate([before, value, after], axis=dim)
    return value


def frame_attention(query, padded, key_ids, query_ids, block, frame):
    dim_head = query.shape[1]
    number = query.shape[0] // block

    def attend(index):
        offset = index * block
        q_blk = lax.dynamic_slice_in_dim(query, offset, block, 0)
        window = lax.dynamic_slice_in_dim(padded, offset, block + 2 * frame, 0)
        k_blk = window[:, :dim_head]
        v_blk = window[:, dim_head:]
        q_ids = lax.dynamic_slice_in_dim(query_ids, offset, block, 0)
        k_ids = lax.dynamic_slice_in_dim(key_ids, offset, block + 2 * frame, 0)
        scores = lax.dot_general(
            q_blk, k_blk, (((1,), (1,)), ((), ())), preferred_element_type=jnp.float32
        ) / math.sqrt(dim_head)
        scores = jnp.where(q_ids[:, None] == k_ids[None, :], scores, -1e30)
        highest = jnp.max(scores, axis=1, keepdims=True)
        weights = jnp.exp(scores - highest)
        probs = (weights / jnp.sum(weights, axis=1, keepdims=True)).astype(jnp.bfloat16)
        return jnp.dot(probs, v_blk, preferred_element_type=jnp.float32)

    blocks = lax.map(attend, jnp.arange(number, dtype=jnp.int32))
    return blocks.reshape(query.shape[0], dim_head)


def fast_update(key_part, value_part, rates, first_w, gate_w, second_w):
    first_act = jnp.dot(key_part, first_w, preferred_element_type=jnp.float32)
    gate_act = jnp.dot(key_part, gate_w, preferred_element_type=jnp.float32)
    sigma = jax.nn.sigmoid(first_act)
    silu_act = first_act * sigma
    hidden = (silu_act * gate_act).astype(jnp.bfloat16)
    back = lax.dot_general(
        value_part, second_w, (((1,), (1,)), ((), ())), preferred_element_type=jnp.float32
    )
    err_first = (
        rates[:, 0:1] * back * gate_act * sigma * (1.0 + first_act * (1.0 - sigma))
    ).astype(jnp.bfloat16)
    err_gate = (rates[:, 1:2] * back * silu_act).astype(jnp.bfloat16)
    err_second = (rates[:, 2:3] * value_part.astype(jnp.float32)).astype(jnp.bfloat16)
    contract = (((0,), (0,)), ((), ()))
    upd_first = lax.dot_general(key_part, err_first, contract, preferred_element_type=jnp.float32)
    upd_gate = lax.dot_general(key_part, err_gate, contract, preferred_element_type=jnp.float32)
    upd_second = lax.dot_general(hidden, err_second, contract, preferred_element_type=jnp.float32)
    return (upd_first, upd_gate, upd_second)


def fast_renorm(old, update):
    old_wide = old.astype(jnp.float32)
    fresh = old_wide + update
    old_sq = jnp.sum(old_wide * old_wide, axis=1, keepdims=True)
    fresh_sq = jnp.sum(fresh * fresh, axis=1, keepdims=True)
    return (fresh * jnp.sqrt(old_sq) / jnp.sqrt(fresh_sq + 1e-06)).astype(jnp.bfloat16)


def fast_apply(query, first_new, gate_new, second_new, gain_part):
    first_act = jnp.dot(query, first_new, preferred_element_type=jnp.float32)
    gate_act = jnp.dot(query, gate_new, preferred_element_type=jnp.float32)
    hidden = (jax.nn.silu(first_act) * gate_act).astype(jnp.bfloat16)
    applied = jnp.dot(hidden, second_new, preferred_element_type=jnp.float32)
    scale = lax.rsqrt(jnp.mean(applied * applied, axis=1, keepdims=True) + 1e-06)
    return applied * scale * gain_part[None, :]


def body(
    tokens,
    qkv_weight,
    rate_weight,
    first_fast,
    gate_fast,
    second_fast,
    fast_gain,
    out_weight,
    frame_lengths,
):
    tok_rows = tokens.shape[0]
    dim_head = qkv_weight.shape[1] // 3
    shards = lax.axis_size("tok")
    mine = lax.axis_index("tok")
    total_tokens = tok_rows * shards
    qkv = jnp.dot(tokens, qkv_weight, preferred_element_type=jnp.float32).astype(jnp.bfloat16)
    rates = (
        0.25
        / math.sqrt(total_tokens)
        * jax.nn.softplus(jnp.dot(tokens, rate_weight, preferred_element_type=jnp.float32))
    )
    query = qkv[:, :dim_head]
    key_part = qkv[:, dim_head : 2 * dim_head]
    value_part = qkv[:, 2 * dim_head :]
    padded = extended(qkv[:, dim_head:], (("tok", 0),), FRAME)
    frame_ends = jnp.cumsum(frame_lengths)
    positions = mine * tok_rows - FRAME + jnp.arange(tok_rows + 2 * FRAME, dtype=jnp.int32)
    inside = (positions >= 0) & (positions < total_tokens)
    counted = jnp.sum((frame_ends[None, :] <= positions[:, None]).astype(jnp.int32), axis=1)
    key_ids = jnp.where(inside, counted, -1)
    query_ids = key_ids[FRAME : FRAME + tok_rows]
    upd_first, upd_gate, upd_second = fast_update(
        key_part, value_part, rates, first_fast[0], gate_fast[0], second_fast[0]
    )
    attended = frame_attention(query, padded, key_ids, query_ids, min(512, tok_rows), FRAME)
    upd_first, upd_gate, upd_second = lax.psum((upd_first, upd_gate, upd_second), "tok")
    first_new = fast_renorm(first_fast[0], upd_first)
    gate_new = fast_renorm(gate_fast[0], upd_gate)
    second_new = fast_renorm(second_fast[0], upd_second)
    normed = fast_apply(query, first_new, gate_new, second_new, fast_gain)
    mixed = (attended + normed).astype(jnp.bfloat16)
    partial_out = jnp.dot(mixed, out_weight, preferred_element_type=jnp.float32)
    result = lax.psum_scatter(
        partial_out.astype(jnp.bfloat16), "head", scatter_dimension=1, tiled=True
    )
    return result


def solution(mesh):
    placed = (
        P("tok", None),
        P(None, "head"),
        P(None, "head"),
        P("head", None, None),
        P("head", None, None),
        P("head", None, None),
        P("head"),
        P("head", None),
        P(),
    )
    return jax.shard_map(
        body, mesh=mesh, in_specs=placed, out_specs=P("tok", "head"), check_vma=False
    )
```

profile of v0, /device:TPU:1, one launch (start us, length us, event | category | flops | bytes accessed | tf_op | source)
XLA Modules:
  0.0 307.0 jit_solution(14875757642269746152)
XLA Ops:
  6.5 2.0 copy-done
  8.5 6.1 %convolution_convert_fusion.1 = bf16[1024,1152]{1,0:T(8,128)(2,1)S(1)} fusion(bf16[1024,1536]{1,0:T(8,128)(2,1)} %param.11, bf16[1536,1152]{1,0:T(8,128)(2,1)S(1)} %copy-done), kind=kOutput, calls=%fused_computation.13 | convolution fusion | flops 3625058304 | bytes 9043968 | tf_op jit(solution)/shard_map/dot_general | solution.py:103
  14.7 1.3 slice.40
  15.9 5.1 %collective-permute-start = (bf16[1024,768]{1,0:T(8,128)(2,1)}, bf16[1024,768]{1,0:T(8,128)(2,1)}, u32[]{:S(2)}, u32[]{:S(2)}) collective-permute-start(bf16[1024,768]{1,0:T(8,128)(2,1)} %slice.40), channel_id=1, source_target_pairs={{0,4},{4,8},{8,12},{12,16},{16,20},{20,24},{24,28},{28,32},{32,36}... | collective-permute-start | bytes 4718600 | tf_op jit(solution)/shard_map/ppermute | solution.py:18
  21.0 2.6 collective-permute-start.1
  28.6 2.4 fusion.14
  30.9 2.2 fusion.13
  33.2 2.7 fusion.16
  35.9 2.1 slice.39
  38.7 1.6 reduce-window.8
  41.3 2.1 convert_reduce_fusion
  44.0 4.1 %pad_maximum_fusion = bf16[3072,768]{1,0:T(8,128)(2,1)} fusion(bf16[1024,768]{1,0:T(8,128)(2,1)} %collective-permute-done.1, bf16[1024,768]{1,0:T(8,128)(2,1)} %slice.40, bf16[1024,768]{1,0:T(8,128)(2,1)} %collective-permute-done), kind=kLoop, calls=%fused_computation.11 | loop fusion | flops 14155776 | bytes 9437184 | tf_op jit(solution)/shard_map/concatenate | solution.py:20
  48.5 32.2 %while.10 = (s32[]{:T(128)}, f32[2,512,384]{2,1,0:T(8,128)}, s32[2]{0:T(128)}, s32[1024]{0:T(1024)}, s32[3072]{0:T(1024)S(1)}, /*index=5*/bf16[1024,384]{1,0:T(8...) while((s32[]{:T(128)}, f32[2,512,384]{2,1,0:T(8,128)}, ...), condition=%wide.region_5.6_spmd, body=%wide.region_2.5_spmd.sunk | while | flops 2025061376 | bytes 41861904 | solution.py:45
  48.5 1.2 dynamic_slice.25
  51.8 3.4 %fusion.73 = (f32[512]{0:T(512)S(1)}, f32[512,2560]{1,0:T(8,128)S(1)}) fusion(bf16[3072,768]{1,0:T(8,128)(2,1)} %get-tuple-element.154, s32[]{:T(128)S(6)} %select_n.29, bf16[1024,384]{1,0:T(8,128)(2,1)} %get-tuple-element.153, s32[]{:T(128)S(6)} %select_n.30, s32[2560]{0:T(1024)} %dynamic_slice.26, s32[512]{0:T(512)S(1)} %dynamic_slice.27), kind=kOutput, calls=%fused_computation.83.clone.1 | convolution fusion | flops 1011875328 | bytes 7618568 | tf_op jit(solution)/shard_map/while/body/eval_jaxpr/dot_general | solution.py:36
  55.2 2.3 copy-done.1
  57.5 1.4 fusion.74
  58.9 5.7 %fusion.75 = f32[2,512,384]{2,1,0:T(8,128)} fusion(f32[2,512,384]{2,1,0:T(8,128)} %get-tuple-element.136, s32[]{:T(128)} %get-tuple-element.135, bf16[3072,768]{1,0:T(8,128)(2,1)} %get-tuple-element.154, s32[]{:T(128)S(6)} %select_n.29, s32[]{:T(128)S(6)} %add.175, f32[512,2560]{1,0:T(8,128)} %copy-done.1, f32[512]{0:T(512)} %fusion.74, ...), kind=kOutput, calls=%fused_computation.8.clone.1 | convolution fusion | flops 1010565120 | bytes 8000008 | tf_op jit(solution)/shard_map/while/body/eval_jaxpr/dot_general | solution.py:43
  64.6 1.2 dynamic_slice.25
  67.9 3.4 %fusion.73 = (f32[512]{0:T(512)S(1)}, f32[512,2560]{1,0:T(8,128)S(1)}) fusion(bf16[3072,768]{1,0:T(8,128)(2,1)} %get-tuple-element.154, s32[]{:T(128)S(6)} %select_n.29, bf16[1024,384]{1,0:T(8,128)(2,1)} %get-tuple-element.153, s32[]{:T(128)S(6)} %select_n.30, s32[2560]{0:T(1024)} %dynamic_slice.26, s32[512]{0:T(512)S(1)} %dynamic_slice.27), kind=kOutput, calls=%fused_computation.83.clone.1 | convolution fusion | flops 1011875328 | bytes 7618568 | tf_op jit(solution)/shard_map/while/body/eval_jaxpr/dot_general | solution.py:36
  71.3 2.3 copy-done.1
  73.6 1.4 fusion.74
  75.0 5.7 %fusion.75 = f32[2,512,384]{2,1,0:T(8,128)} fusion(f32[2,512,384]{2,1,0:T(8,128)} %get-tuple-element.136, s32[]{:T(128)} %get-tuple-element.135, bf16[3072,768]{1,0:T(8,128)(2,1)} %get-tuple-element.154, s32[]{:T(128)S(6)} %select_n.29, s32[]{:T(128)S(6)} %add.175, f32[512,2560]{1,0:T(8,128)} %copy-done.1, f32[512]{0:T(512)} %fusion.74, ...), kind=kOutput, calls=%fused_computation.8.clone.1 | convolution fusion | flops 1010565120 | bytes 8000008 | tf_op jit(solution)/shard_map/while/body/eval_jaxpr/dot_general | solution.py:43
  80.7 3.0 copy.18
  83.7 147.5 %all-reduce.3.cloned.1.call-done = (f32[384,768]{1,0:T(8,128)}, f32[384,768]{1,0:T(8,128)}, f32[768,384]{1,0:T(8,128)}) async-done(((f32[384,768]{1,0:T(8,128)}, f32[384,768]{1,0:T(8,128)}, f32[768,384]{1,0:T(8,128)}), (f32[384,768]{1,0:T(8,128)}, f32[384,768]{1,0:T(8,128)}, f32[768,384]{1,0:T(8,128)})) %all-reduce.3.cloned.1.call-update) | async-done | bytes 3538960 | tf_op jit(solution)/shard_map/psum | solution.py:123
  231.2 2.6 fusion.18
  235.5 3.9 %fusion.27 = f32[1024,768]{1,0:T(8,128)} fusion(f32[384,768]{1,0:T(8,128)S(1)} %copy-done.9, bf16[1,384,768]{2,1,0:T(8,128)(2,1)S(1)} %copy-done.5, f32[384]{0:T(512)S(1)} %add_sqrt_fusion.2, f32[384]{0:T(512)S(1)} %sqrt.48, bf16[1024,1152]{1,0:T(8,128)(2,1)} %copy-done.3), kind=kOutput, calls=%fused_computation.50 | convolution fusion | flops 605454336 | bytes 5704704 | tf_op jit(solution)/shard_map/dot_general | solution.py:79
  239.4 6.5 %multiply_reduce_fusion = (f32[1024]{0:T(1024)S(1)}, f32[1024,384]{0,1:T(8,128)}) fusion(f32[768,384]{1,0:T(8,128)} %get-tuple-element.65, bf16[1,768,384]{2,1,0:T(8,128)(2,1)} %param.16, f32[768]{0:T(1024)S(1)} %add_sqrt_fusion, f32[768]{0:T(1024)S(1)} %sqrt.52, f32[1024,768]{1,0:T(8,128)} %fusion.27, f32[384,768]{1,0:T(8,128)} %get-tuple-element.64, ...), kind=kOutput, calls=%fused_computation.23 | convolution fusion | flops 1216412672 | bytes 9058304 | tf_op jit(solution)/shard_map/dot_general | solution.py:82
  245.9 5.9 %convolution_convert_fusion = bf16[1024,1536]{1,0:T(8,128)(2,1)} fusion(bf16[384,1536]{1,0:T(8,128)(2,1)} %param.18, f32[1024,384]{0,1:T(8,128)} %copy.18, f32[1024,384]{0,1:T(8,128)} %get-tuple-element.72, f32[384]{0:T(512)S(1)} %copy-done.12, f32[1024]{0:T(1024)S(1)} %add_rsqrt_fusion), kind=kOutput, calls=%fused_computation.12 | convolution fusion | flops 1211105280 | bytes 7476736 | tf_op jit(solution)/shard_map/dot_general | solution.py:129
  251.8 4.7 %copy.19 = bf16[1024,1536]{0,1:T(8,128)(2,1)} copy(bf16[1024,1536]{1,0:T(8,128)(2,1)} %convolution_convert_fusion) | data formatting | bytes 6291456
  256.5 41.4 %reduce-scatter.4.cloned.1.call-done = bf16[384,1024]{1,0:T(8,128)(2,1)} async-done(((bf16[1536,1024]{1,0:T(8,128)(2,1)}), bf16[384,1024]{1,0:T(8,128)(2,1)}) %reduce-scatter.4.cloned.1.call-update) | async-done | bytes 786448
  297.9 2.3 copy.20
  (57 shorter events, 12.2 us)
Async XLA Ops:
  6.5 2.0 copy-start
  6.5 224.7 %all-reduce.3.cloned.1.call-start = ((), (), s32[]{:S(2)}) async-start(), calls=%async_computation.2 | async-start | bytes 7077888 | tf_op jit(solution)/shard_map/psum | solution.py:123
  14.7 18.5 %copy-start.3 = (bf16[1024,1152]{1,0:T(8,128)(2,1)}, bf16[1024,1152]{1,0:T(8,128)(2,1)S(1)}, u32[]{:S(2)}) copy-start(bf16[1024,1152]{1,0:T(8,128)(2,1)S(1)} %convolution_convert_fusion.1) | copy-start | bytes 7077892
  14.7 9.0 %copy-start.4 = (bf16[1,384,768]{2,1,0:T(8,128)(2,1)S(1)}, bf16[1,384,768]{2,1,0:T(8,128)(2,1)}, u32[]{:S(2)}) copy-start(bf16[1,384,768]{2,1,0:T(8,128)(2,1)} %param.14) | copy-start | bytes 1769476
  15.9 8.7 %copy-start.7 = (bf16[1,768,384]{2,1,0:T(8,128)(2,1)S(1)}, bf16[1,768,384]{2,1,0:T(8,128)(2,1)}, u32[]{:S(2)}) copy-start(bf16[1,768,384]{2,1,0:T(8,128)(2,1)} %param.16) | copy-start | bytes 1769476
  15.9 28.0 %collective-permute-start = (bf16[1024,768]{1,0:T(8,128)(2,1)}, bf16[1024,768]{1,0:T(8,128)(2,1)}, u32[]{:S(2)}, u32[]{:S(2)}) collective-permute-start(bf16[1024,768]{1,0:T(8,128)(2,1)} %slice.40), channel_id=1, source_target_pairs={{0,4},{4,8},{8,12},{12,16},{16,20},{20,24},{24,28},{28,32},{32,36}... | collective-permute-start | bytes 4718600 | tf_op jit(solution)/shard_map/ppermute | solution.py:18
  21.0 23.0 %collective-permute-start.1 = (bf16[1024,768]{1,0:T(8,128)(2,1)}, bf16[1024,768]{1,0:T(8,128)(2,1)}, u32[]{:S(2)}, u32[]{:S(2)}) collective-permute-start(bf16[1024,768]{1,0:T(8,128)(2,1)} %slice.40), channel_id=1, source_target_pairs={{4,0},{8,4},{12,8},{16,12},{20,16},{24,20},{28,24},{32,28},{36,32}... | collective-permute-start | bytes 4718600 | tf_op jit(solution)/shard_map/ppermute | solution.py:19
  24.6 1.1 copy-start.6
  25.7 1.9 copy-start.2
  25.7 1.9 copy-start.11
  35.8 2.2 copy-start.13
  35.9 262.0 %reduce-scatter.4.cloned.1.call-start = ((), (), s32[]{:S(2)}) async-start(), calls=%async_computation.1 | async-start | bytes 3932160
  55.2 2.3 copy-start.1
  71.3 2.3 copy-start.1
  231.2 3.9 %copy-start.8 = (bf16[1,768,384]{2,1,0:T(8,128)(2,1)S(1)}, bf16[1,768,384]{2,1,0:T(8,128)(2,1)}, u32[]{:S(2)}) copy-start(bf16[1,768,384]{2,1,0:T(8,128)(2,1)} %param.16) | copy-start | bytes 1769476
  231.2 3.9 %copy-start.10 = (f32[768,384]{1,0:T(8,128)S(1)}, f32[768,384]{1,0:T(8,128)}, u32[]{:S(2)}) copy-start(f32[768,384]{1,0:T(8,128)} %get-tuple-element.65) | copy-start | bytes 3538948
  231.2 4.3 %copy-start.5 = (bf16[1,384,768]{2,1,0:T(8,128)(2,1)S(1)}, bf16[1,384,768]{2,1,0:T(8,128)(2,1)}, u32[]{:S(2)}) copy-start(bf16[1,384,768]{2,1,0:T(8,128)(2,1)} %param.14) | copy-start | bytes 1769476
  231.2 4.3 %copy-start.9 = (f32[384,768]{1,0:T(8,128)S(1)}, f32[384,768]{1,0:T(8,128)}, u32[]{:S(2)}) copy-start(f32[384,768]{1,0:T(8,128)} %get-tuple-element.63) | copy-start | bytes 3538948
  239.4 6.5 %copy-start.12 = (f32[384]{0:T(512)S(1)}, f32[384]{0:T(512)}, u32[]{:S(2)}) copy-start(f32[384]{0:T(512)} %param.17) | copy-start | bytes 4612
Sparse Core Ops, SparseCore 0:
  36.0 195.1 all-reduce.2
  256.6 41.1 reduce-scatter.3
where the time goes:
time: 308 us; the launch traced here: 307 us
  waiting for transfers between devices  189 us (61%)
  matrix products  51.8 us (17%)
  local copies, waits for them, and re-layouts  28.6 us (9%)
  other arithmetic  15.1 us (5%)
  between operations  13.6 us (4%)
  starting transfers between devices  7.73 us (3%)
    psum x1, waiting for transfers between devices, body(): lax.psum((upd_first, upd_gate, upd_second), 'tok')  148 us
    unnamed x3, waiting for transfers between devices  41.4 us
    dot_general x2, matrix products, attend(): return jnp.dot(probs, v_blk, preferred_element_type=jnp.float32)  11.4 us
    unnamed x28, local copies, waits for them, and re-layouts  9.98 us
    dot_general x2, matrix products, attend(): lax.dot_general(q_blk, k_blk, (((1,), (1,)), ((), ())), preferred_element...  6.8 us
    dot_general x1, matrix products, fast_apply(): applied = jnp.dot(hidden, second_new, preferred_element_type=jnp.float32)  6.46 us
  transfers between devices with their start and end apart: 4, of which 2 were waited for; matrix products, arithmetic and copies ran while one was open for 17% of the time, Pallas kernels for 0%

commit v1 on v0

v1 whole, which is shorter than its diff:
```python
import functools
import math

import jax
import jax.numpy as jnp
from jax import lax
from jax.experimental import pallas as pl
from jax.experimental.pallas import tpu as pltpu
from jax.sharding import PartitionSpec as P

DH = 384
HID = 768
TOK = 1024
XS, ZS, CS, HS = 4, 8, 2, 4
SHARDS = XS * ZS * CS
TOKENS = TOK * SHARDS
XROWS = DH // XS
ZROWS = 16
OWNERS = XROWS // ZROWS
WIDE = HID + DH
KB = 256
QB = 256
BF, F32, I32 = jnp.bfloat16, jnp.float32, jnp.int32
NT = (((1,), (1,)), ((), ()))
VM = 56 * 1024 * 1024

SMEM = pl.BlockSpec(memory_space=pltpu.SMEM)
WHOLE = pl.BlockSpec(memory_space=pltpu.VMEM)
DEP = pl.BlockSpec(memory_space=pl.ANY)


def params():
    return pltpu.CompilerParams(vmem_limit_bytes=VM)


def mm(a, b):
    return jnp.dot(a, b, preferred_element_type=F32)


def sds(shape, dtype):
    return jax.ShapeDtypeStruct(shape, dtype)


def shift_x(d):
    return [(t, (t + d * ZS * CS) % SHARDS) for t in range(SHARDS)]


def shift_z(d, to_owner=False, from_owner=False):
    pairs = []
    for t in range(SHARDS):
        x, z, c = t // (ZS * CS), t // CS % ZS, t % CS
        other = (z + d) % ZS
        if (to_owner and other >= OWNERS) or (from_owner and z >= OWNERS):
            continue
        pairs.append((t, (x * ZS + other) * CS + c))
    return pairs


SWAP_C = [(t, t ^ 1) for t in range(SHARDS)]


def shift_h(d):
    return [(h, (h + d) % HS) for h in range(HS)]


def front_kernel(
    pos_ref, t_ref, wk_ref, wv_ref, wr_ref, w1_ref, w3_ref, w2_ref,
    kv_ref, send_ref, keep_ref, acc1, acc3, acc2,
):
    step = pl.program_id(0)

    @pl.when(step == 0)
    def _():
        acc1[...] = jnp.zeros_like(acc1)
        acc3[...] = jnp.zeros_like(acc3)
        acc2[...] = jnp.zeros_like(acc2)

    t = t_ref[...]
    k = mm(t, wk_ref[...]).astype(BF)
    v = mm(t, wv_ref[...]).astype(BF)
    kv_ref[:, :DH] = k
    kv_ref[:, DH:] = v
    raw = mm(t, wr_ref[...])
    rates = (0.25 / math.sqrt(TOKENS)) * (
        jnp.maximum(raw, 0.0) + jnp.log1p(jnp.exp(-jnp.abs(raw)))
    )
    a = mm(k, w1_ref[0])
    b = mm(k, w3_ref[0])
    back = lax.dot_general(v, w2_ref[0], NT, preferred_element_type=F32)
    sig = jax.nn.sigmoid(a)
    act = a * sig
    z = (act * b).astype(BF)
    e1 = (rates[:, 0:1] * back * b * sig * (1.0 + a * (1.0 - sig))).astype(BF)
    e3 = (rates[:, 1:2] * back * act).astype(BF)
    e2 = (rates[:, 2:3] * v.astype(F32)).astype(BF)
    k_t = k.T
    acc1[...] += mm(k_t, e1)
    acc3[...] += mm(k_t, e3)
    acc2[...] += mm(e2.T, z)

    @pl.when(step == pl.num_programs(0) - 1)
    def _():
        core = pos_ref[2]
        low = acc2[:, :DH].T
        high = acc2[:, DH:].T

        @pl.when(core == 0)
        def _():
            keep_ref[:, :HID] = acc1[...]
            keep_ref[:, HID:] = low
            send_ref[:, :HID] = acc3[...].astype(BF)
            send_ref[:, HID:] = high.astype(BF)

        @pl.when(core == 1)
        def _():
            keep_ref[:, :HID] = acc3[...]
            keep_ref[:, HID:] = high
            send_ref[:, :HID] = acc1[...].astype(BF)
            send_ref[:, HID:] = low.astype(BF)


def front(pos, tokens, qkv_weight, rate_weight, first_fast, gate_fast, second_fast):
    rows, wide = tokens.shape
    block = 256
    fixed3 = lambda i: (0, 0, 0)
    return pl.pallas_call(
        front_kernel,
        grid=(rows // block,),
        in_specs=[
            SMEM,
            pl.BlockSpec((block, wide), lambda i: (i, 0)),
            pl.BlockSpec((wide, DH), lambda i: (0, 1)),
            pl.BlockSpec((wide, DH), lambda i: (0, 2)),
            pl.BlockSpec((wide, 3), lambda i: (0, 0)),
            pl.BlockSpec((1, DH, HID), fixed3),
            pl.BlockSpec((1, DH, HID), fixed3),
            pl.BlockSpec((1, HID, DH), fixed3),
        ],
        out_specs=[
            pl.BlockSpec((block, 2 * DH), lambda i: (i, 0)),
            pl.BlockSpec((DH, WIDE), lambda i: (0, 0)),
            pl.BlockSpec((DH, WIDE), lambda i: (0, 0)),
        ],
        out_shape=[sds((rows, 2 * DH), BF), sds((DH, WIDE), BF), sds((DH, WIDE), F32)],
        scratch_shapes=[pltpu.VMEM((DH, HID), F32)] * 3,
        compiler_params=params(),
        name="front",
    )(pos, tokens, qkv_weight, qkv_weight, rate_weight, first_fast, gate_fast, second_fast)


def rs_x_kernel(pos_ref, keep_ref, got_ref, own_ref, *outs):
    x = pos_ref[0]
    for d, out in enumerate((own_ref, *outs)):
        rows = pl.ds(pl.multiple_of(lax.rem(x + d, XS) * XROWS, XROWS), XROWS)
        out[...] = (keep_ref[rows, :] + got_ref[rows, :].astype(F32)).astype(out.dtype)


def rs_x(pos, keep, got):
    return pl.pallas_call(
        rs_x_kernel,
        in_specs=[SMEM, WHOLE, WHOLE],
        out_specs=[WHOLE] * XS,
        out_shape=[sds((XROWS, WIDE), F32)] + [sds((XROWS, WIDE), BF)] * (XS - 1),
        compiler_params=params(),
        name="rs_x",
    )(pos, keep, got)


def rs_z_kernel(pos_ref, own_ref, g1, g2, g3, *rest):
    outs, total = rest[-ZS - 1 : -1], rest[-1]
    z = pos_ref[1]
    total[...] = (own_ref[...] + g1[...].astype(F32)) + (
        g2[...].astype(F32) + g3[...].astype(F32)
    )
    for d, out in enumerate(outs):
        owner = jnp.minimum(lax.rem(z + d, ZS), OWNERS - 1)
        rows = pl.ds(pl.multiple_of(owner * ZROWS, ZROWS), ZROWS)
        out[...] = total[rows, :].astype(out.dtype)


def rs_z(pos, own, got, deps):
    return pl.pallas_call(
        rs_z_kernel,
        in_specs=[SMEM] + [WHOLE] * XS + [DEP] * len(deps),
        out_specs=[WHOLE] * ZS,
        out_shape=[sds((ZROWS, WIDE), F32)] + [sds((ZROWS, WIDE), BF)] * (ZS - 1),
        scratch_shapes=[pltpu.VMEM((XROWS, WIDE), F32)],
        compiler_params=params(),
        name="rs_z",
    )(pos, own, *got, *deps)


def renorm_kernel(old_ref, own_ref, *rest):
    got, out = rest[: ZS - 1], rest[-1]
    update = own_ref[...]
    for g in got:
        update = update + g[...].astype(F32)
    old = old_ref[...]
    fresh = old + update
    for cols in (slice(0, HID), slice(HID, WIDE)):
        w, f = old[:, cols], fresh[:, cols]
        w_sq = jnp.sum(w * w, axis=1, keepdims=True)
        f_sq = jnp.sum(f * f, axis=1, keepdims=True)
        out[:, cols] = (f * (jnp.sqrt(w_sq) / jnp.sqrt(f_sq + 1e-6))).astype(BF)


def renorm(old, own, got, deps):
    return pl.pallas_call(
        renorm_kernel,
        in_specs=[WHOLE] * (ZS + 1) + [DEP] * len(deps),
        out_specs=WHOLE,
        out_shape=sds((ZROWS, WIDE), BF),
        compiler_params=params(),
        name="renorm",
    )(old, own, *got, *deps)


def ag_z_kernel(pos_ref, *rest):
    blocks, out = rest[:ZS], rest[-1]
    z = pos_ref[1]
    for d, block in enumerate(blocks):
        owner = lax.rem(z - d + ZS, ZS)

        @pl.when(owner < OWNERS)
        def _():
            out[pl.ds(pl.multiple_of(owner * ZROWS, ZROWS), ZROWS), :] = block[...]


def ag_z(pos, blocks, deps):
    return pl.pallas_call(
        ag_z_kernel,
        in_specs=[SMEM] + [WHOLE] * ZS + [DEP] * len(deps),
        out_specs=WHOLE,
        out_shape=sds((XROWS, WIDE), BF),
        compiler_params=params(),
        name="ag_z",
    )(pos, *blocks, *deps)


def ag_x_kernel(pos_ref, *rest):
    blocks, out = rest[:XS], rest[-1]
    x = pos_ref[0]
    for d, block in enumerate(blocks):
        owner = lax.rem(x - d + XS, XS)
        out[pl.ds(pl.multiple_of(owner * XROWS, XROWS), XROWS), :] = block[...]


def ag_x(pos, blocks, deps):
    return pl.pallas_call(
        ag_x_kernel,
        in_specs=[SMEM] + [WHOLE] * XS + [DEP] * len(deps),
        out_specs=WHOLE,
        out_shape=sds((DH, WIDE), BF),
        compiler_params=params(),
        name="ag_x",
    )(pos, *blocks, *deps)


def project_kernel(t_ref, w_ref, dep_ref, q_ref):
    q_ref[...] = mm(t_ref[...], w_ref[...]).astype(BF)


def project(tokens, qkv_weight, dep):
    rows, wide = tokens.shape
    block = 256
    return pl.pallas_call(
        project_kernel,
        grid=(rows // block,),
        in_specs=[
            pl.BlockSpec((block, wide), lambda i: (i, 0)),
            pl.BlockSpec((wide, DH), lambda i: (0, 0)),
            DEP,
        ],
        out_specs=pl.BlockSpec((block, DH), lambda i: (i, 0)),
        out_shape=sds((rows, DH), BF),
        compiler_params=params(),
        name="project",
    )(tokens, qkv_weight, dep)


def attend_kernel(piece, bounds_ref, rows_ref, q_ref, before, mine, after, dep_ref, out_ref, s_ref):
    low, high = bounds_ref[2 * piece], bounds_ref[2 * piece + 1]
    first = lax.div(low, KB)
    last = lax.div(high + KB - 1, KB)
    q = q_ref[...]
    begin, end = rows_ref[:, 0:1], rows_ref[:, 1:2]
    per = TOK // KB
    scale = 1.0 / math.sqrt(DH)

    def segments(step, carry):
        for s, ref in enumerate((before, mine, after)):
            lo = jnp.clip(first, s * per, (s + 1) * per)
            hi = jnp.clip(last, s * per, (s + 1) * per)
            carry = lax.fori_loop(lo, hi, functools.partial(step, s, ref), carry)
        return carry

    def scores(s, ref, kb, top):
        k = ref[pl.ds(pl.multiple_of((kb - s * per) * KB, KB), KB), :DH]
        sc = lax.dot_general(q, k, NT, preferred_element_type=F32) * scale
        col = lax.broadcasted_iota(I32, (QB, KB), 1) + kb * KB
        sc = jnp.where((col >= begin) & (col < end), sc, -1e30)
        s_ref[kb] = sc
        return jnp.maximum(top, jnp.max(sc, axis=1, keepdims=True))

    top = segments(scores, jnp.full((QB, 1), -1e30, F32))

    def weigh(kb, total):
        w = jnp.exp(s_ref[kb] - top)
        s_ref[kb] = w
        return total + jnp.sum(w, axis=1, keepdims=True)

    total = lax.fori_loop(first, last, weigh, jnp.zeros((QB, 1), F32))
    inverse = 1.0 / total
    out_ref[...] = jnp.zeros_like(out_ref)

    def gather(s, ref, kb, carry):
        v = ref[pl.ds(pl.multiple_of((kb - s * per) * KB, KB), KB), DH:]
        probs = (s_ref[kb] * inverse).astype(BF)
        out_ref[...] += mm(probs, v)
        return carry

    segments(gather, 0)


def attend(piece, bounds, row_bounds, query, before, mine, after, dep):
    return pl.pallas_call(
        functools.partial(attend_kernel, piece),
        grid=(1,),
        in_specs=[
            SMEM,
            pl.BlockSpec((QB, 2), lambda i: (piece, 0)),
            pl.BlockSpec((QB, DH), lambda i: (piece, 0)),
            WHOLE,
            WHOLE,
            WHOLE,
            DEP,
        ],
        out_specs=pl.BlockSpec((QB, DH), lambda i: (0, 0)),
        out_shape=sds((QB, DH), F32),
        scratch_shapes=[pltpu.VMEM((3 * TOK // KB, QB, KB), F32)],
        compiler_params=params(),
        name=f"attend_{piece}",
    )(bounds, row_bounds, query, before, mine, after, dep)


def apply_kernel(pos_ref, q_ref, own_ref, other_ref, att_ref, gain_ref, out_ref, *rest):
    core = pos_ref[2]
    q = q_ref[...]
    mine = mm(q, own_ref[:, :HID])
    theirs = mm(q, other_ref[:, :HID])
    even = core == 0
    a = jnp.where(even, mine, theirs)
    b = jnp.where(even, theirs, mine)
    hidden = (a * jax.nn.sigmoid(a) * b).astype(BF)
    h0, h1 = hidden[:, :DH], hidden[:, DH:]
    h_own = jnp.where(even, h0, h1)
    h_other = jnp.where(even, h1, h0)
    applied = mm(h_own, own_ref[:, HID:]) + mm(h_other, other_ref[:, HID:])
    mean = jnp.mean(applied * applied, axis=1, keepdims=True)
    normed = applied * lax.rsqrt(mean + 1e-6) * gain_ref[...]
    out_ref[...] = (att_ref[...] + normed).astype(BF)


def apply(piece, pos, query, own, other, attended, gain):
    return pl.pallas_call(
        apply_kernel,
        grid=(1,),
        in_specs=[
            SMEM,
            pl.BlockSpec((QB, DH), lambda i: (piece, 0)),
            WHOLE,
            WHOLE,
            WHOLE,
            WHOLE,
        ],
        out_specs=pl.BlockSpec((QB, DH), lambda i: (0, 0)),
        out_shape=sds((QB, DH), BF),
        compiler_params=params(),
        name=f"apply_{piece}",
    )(pos, query, own, other, attended, gain)


def output_kernel(*refs):
    parts, weights, out = refs[:HS], refs[HS : 2 * HS], refs[-1]
    total = mm(parts[0][...], weights[0][...])
    for part, weight in zip(parts[1:], weights[1:]):
        total = total + mm(part[...], weight[...])
    out[...] = total.astype(BF)


def output(piece, parts, weights, buffer):
    extra = [] if buffer is None else [buffer]
    return pl.pallas_call(
        output_kernel,
        grid=(1,),
        in_specs=[WHOLE] * (2 * HS) + [DEP] * len(extra),
        out_specs=pl.BlockSpec((QB, DH), lambda i: (piece, 0)),
        out_shape=sds((TOK, DH), BF),
        input_output_aliases={2 * HS: 0} if extra else {},
        compiler_params=params(),
        name=f"output_{piece}",
    )(*parts, *weights, *extra)


def body(
    tokens,
    qkv_weight,
    rate_weight,
    first_fast,
    gate_fast,
    second_fast,
    fast_gain,
    out_weight,
    frame_lengths,
):
    mine = lax.axis_index("tok")
    head = lax.axis_index("head")
    x, z, core = mine // (ZS * CS), mine // CS % ZS, mine % CS
    pos = jnp.stack([x, z, core]).astype(I32)
    send = lambda value, pairs: lax.ppermute(value, "tok", pairs)

    kv, give, keep = front(
        pos, tokens, qkv_weight, rate_weight, first_fast, gate_fast, second_fast
    )
    got = send(give, SWAP_C)
    up = [(i, i + 1) for i in range(SHARDS - 1)]
    before = send(kv, up)
    after = send(kv, [(j, i) for i, j in up])

    order = jnp.arange(frame_lengths.shape[0], dtype=I32)
    ends = jnp.sum(
        jnp.where(order[:, None] <= order[None, :], frame_lengths[:, None], 0), axis=0
    )
    places = mine * TOK + jnp.arange(TOK, dtype=I32)
    passed = ends[None, :] <= places[:, None]
    begin = jnp.max(jnp.where(passed, ends[None, :], 0), axis=1)
    end = jnp.min(jnp.where(passed, TOKENS, ends[None, :]), axis=1)
    shift = (mine - 1) * TOK
    row_bounds = jnp.stack([begin - shift, end - shift], axis=1)
    bounds = jnp.stack(
        [row_bounds[::QB, 0], row_bounds[QB - 1 :: QB, 1]], axis=1
    ).reshape(-1)

    weights = []
    for d in range(HS):
        cols = lax.dynamic_slice_in_dim(out_weight, (head + d) % HS * DH, DH, 1)
        weights.append(lax.ppermute(cols, "head", shift_h(d)) if d else cols)

    row = jnp.minimum(x * XROWS + z * ZROWS, DH - ZROWS)
    pick = lambda w, at: lax.dynamic_slice_in_dim(w[0], at, ZROWS, 0)
    old = jnp.concatenate(
        [
            jnp.where(core == 0, pick(first_fast, row), pick(gate_fast, row)),
            pick(second_fast, core * DH + row),
        ],
        axis=1,
    ).astype(F32)

    own, *gives = rs_x(pos, keep, got)
    got = [send(g, shift_x(d + 1)) for d, g in enumerate(gives)]
    query = project(tokens, qkv_weight, own)
    att = functools.partial(
        lambda p, dep: attend(p, bounds, row_bounds, query, before, kv, after, dep)
    )

    own, *gives = rs_z(pos, own, got, [query])
    got = [send(g, shift_z(d + 1, to_owner=True)) for d, g in enumerate(gives)]
    att0 = att(0, own)

    fresh = renorm(old, own, got, [att0])
    got = [send(fresh, shift_z(d, from_owner=True)) for d in range(1, ZS)]
    att1 = att(1, fresh)

    block = ag_z(pos, [fresh, *got], [att1])
    got = [send(block, shift_x(d)) for d in range(1, XS)]
    att2 = att(2, block)
    att3 = att(3, block)

    half = ag_x(pos, [block, *got], [att2, att3])
    other = send(half, SWAP_C)

    gain = fast_gain[None, :]
    result = None
    mixed = [
        apply(p, pos, query, half, other, a, gain)
        for p, a in enumerate((att0, att1, att2, att3))
    ]
    for p, part in enumerate(mixed):
        parts = [part] + [
            lax.ppermute(part, "head", shift_h(d)) for d in range(1, HS)
        ]
        result = output(p, parts, weights, result)
    return result


def solution(mesh):
    placed = (
        P("tok", None),
        P(None, "head"),
        P(None, "head"),
        P("head", None, None),
        P("head", None, None),
        P("head", None, None),
        P("head"),
        P("head", None),
        P(),
    )
    return jax.shard_map(
        body, mesh=mesh, in_specs=placed, out_specs=P("tok", "head"), check_vma=False
    )
```

time: 308 us -> 212 us (0.69)
  waiting for transfers between devices: 189 us -> 23.9 us
  Pallas kernels: 0 us -> 84.2 us
  starting transfers between devices: 7.73 us -> 83.9 us
  matrix products: 51.8 us -> 0 us
  local copies, waits for them, and re-layouts: 28.6 us -> 14.8 us
  between operations: 13.6 us -> 0.62 us
  other arithmetic: 15.1 us -> 2.66 us
    psum x1 -> x0, waiting for transfers between devices: 148 us -> none  [body(): lax.psum((upd_first, upd_gate, upd_second), 'tok')]
    pallas_call x0 -> x19, Pallas kernels: none -> 84.2 us  [the longest x4 28 us: attend(): pl.pallas_call(functools.partial(attend_kernel, piece), grid=(1,), in_spe...]
    ppermute x2 -> x39, starting transfers between devices: 7.69 us -> 83.9 us  [the longest x24 67.9 us: body(): send = lambda value, pairs: lax.ppermute(value, 'tok', pairs)]
    dot_general x15 -> x0, matrix products: 51.8 us -> none  [the longest x2 11.4 us: attend(): return jnp.dot(probs, v_blk, preferred_element_type=jnp.float32)]
    unnamed x3 -> x0, waiting for transfers between devices: 41.4 us -> none
    ppermute x2 -> x39, waiting for transfers between devices: 0.01 us -> 23.9 us  [the longest x24 13.9 us: body(): send = lambda value, pairs: lax.ppermute(value, 'tok', pairs)]
    reduce_sum x5 -> x1, other arithmetic: 7.88 us -> 0.1 us  [body(): jnp.sum(jnp.where(order[:, None] <= order[None, :], frame_lengths[:, None...]
    while x4 -> x0, local copies, waits for them, and re-layouts: 4.62 us -> none
  transfers between devices with their start and end apart: 4 -> 39, of which waited for: 2 -> 9; matrix products, arithmetic and copies ran while one was open for 17% -> 3% of each run, Pallas kernels for 0% -> 29%
where the time goes in v1:
time: 212 us; the launch traced here: 210 us
  Pallas kernels  84.2 us (40%)
  starting transfers between devices  83.9 us (40%)
  waiting for transfers between devices  23.9 us (11%)
  local copies, waits for them, and re-layouts  14.8 us (7%)
  other arithmetic  2.66 us (1%)
    ppermute x24, starting transfers between devices, body(): send = lambda value, pairs: lax.ppermute(value, 'tok', pairs)  67.9 us
    pallas_call x4, Pallas kernels, attend(): pl.pallas_call(functools.partial(attend_kernel, piece), grid=(1,), in_spe...  28 us
    pallas_call x1, Pallas kernels, front(): pl.pallas_call(front_kernel, grid=(rows // block,), in_specs=[SMEM, pl.Bl...  15.2 us
    ppermute x24, waiting for transfers between devices, body(): send = lambda value, pairs: lax.ppermute(value, 'tok', pairs)  13.9 us
    pallas_call x4, Pallas kernels, apply(): pl.pallas_call(apply_kernel, grid=(1,), in_specs=[SMEM, pl.BlockSpec((QB,...  13.6 us
    pallas_call x4, Pallas kernels, output(): pl.pallas_call(output_kernel, grid=(1,), in_specs=[WHOLE] * (2 * HS) + [D...  11.4 us
    ppermute x12, starting transfers between devices, body(): lax.ppermute(part, 'head', shift_h(d))  11.1 us
    unnamed x89, local copies, waits for them, and re-layouts  10.6 us
  transfers between devices with their start and end apart: 39, of which 9 were waited for; matrix products, arithmetic and copies ran while one was open for 3% of the time, Pallas kernels for 29%

profile of v1, /device:TPU:1, one launch (start us, length us, event | category | flops | bytes accessed | tf_op | source)
XLA Modules:
  0.0 210.1 jit_solution(15067048717713462771)
XLA Ops:
  2.3 15.2 %front.1 = (bf16[1024,768]{1,0:T(8,128)(2,1)}, bf16[384,1152]{1,0:T(8,128)(2,1)}, f32[384,1152]{1,0:T(8,128)}) custom-call(s32[3]{0:T(128)} %pad_add_fusion.2.pos_ref, bf16[1024,1536]{1,0:T(8,128)(2,1)} %t_ref.3, bf16[1536,1152]{1,0:T(8,128)(2,1)} %w_ref.1, bf16[1536,1152]{1,0:T(8,128)(2,1)} %w_ref.1, bf16[1536,3]{1,0:T(8,128)(2,1)} %copy.24.wr_ref, ...), custom_call_target="tpu_custom_call" | custom-call | tf_op jit(solution)/shard_map/front/pallas_call | solution.py:126
  17.5 4.9 %collective-permute-start.11 = (bf16[1024,768]{1,0:T(8,128)(2,1)}, bf16[1024,768]{1,0:T(8,128)(2,1)S(1)}, u32[]{:S(2)}, u32[]{:S(2)}) collective-permute-start(bf16[1024,768]{1,0:T(8,128)(2,1)} %get-tuple-element.34.mine), channel_id=1, source_target_pairs={{0,4},{4,8},{8,12},{12,16},{16,20},{20,24},{24,28},{28,32},{32,36}... | collective-permute-start | bytes 4718600 | tf_op jit(solution)/shard_map/ppermute | solution.py:420
  28.9 2.9 %rs_x.1 = (f32[96,1152]{1,0:T(8,128)}, bf16[96,1152]{1,0:T(8,128)(2,1)}, bf16[96,1152]{1,0:T(8,128)(2,1)}, bf16[96,1152]{1,0:T(8,128)(2,1)}) custom-call(s32[3]{0:T(128)} %pad_add_fusion.2.pos_ref, f32[384,1152]{1,0:T(8,128)} %get-tuple-element.20.keep_ref, bf16[384,1152]{1,0:T(8,128)(2,1)} %collective-permute-done.got_ref), custom_call_target="tpu_custom_call" | custom-call | tf_op jit(solution)/shard_map/rs_x/pallas_call | solution.py:159
  31.8 3.3 %collective-permute-start.1 = (bf16[96,1152]{1,0:T(8,128)(2,1)}, bf16[96,1152]{1,0:T(8,128)(2,1)S(1)}, u32[]{:S(2)}, u32[]{:S(2)}) collective-permute-start(bf16[96,1152]{1,0:T(8,128)(2,1)} %get-tuple-element.23), channel_id=1, source_target_pairs={{0,64},{4,68},{8,72},{12,76},{16,80},{20,84},{24,88},{28,92},{32,9... | collective-permute-start | bytes 663560 | tf_op jit(solution)/shard_map/ppermute | solution.py:420
  35.0 2.7 %collective-permute-start.2 = (bf16[96,1152]{1,0:T(8,128)(2,1)}, bf16[96,1152]{1,0:T(8,128)(2,1)S(1)}, u32[]{:S(2)}, u32[]{:S(2)}) collective-permute-start(bf16[96,1152]{1,0:T(8,128)(2,1)} %get-tuple-element.24), channel_id=1, source_target_pairs={{0,128},{4,132},{8,136},{12,140},{16,144},{20,148},{24,152},{28,15... | collective-permute-start | bytes 663560 | tf_op jit(solution)/shard_map/ppermute | solution.py:420
  38.7 5.2 %project.1.rest_0_.q_ref = bf16[1024,384]{1,0:T(8,128)(2,1)} custom-call(bf16[1024,1536]{1,0:T(8,128)(2,1)} %t_ref.3, bf16[1536,1152]{1,0:T(8,128)(2,1)} %w_ref.1, f32[96,1152]{1,0:T(8,128)} %get-tuple-element.22.dep_ref.own_ref), custom_call_target="tpu_custom_call" | custom-call | tf_op jit(solution)/shard_map/project/pallas_call | solution.py:266
  43.9 4.0 %collective-permute-done.1.g1 = bf16[96,1152]{1,0:T(8,128)(2,1)S(1)} collective-permute-done((bf16[96,1152]{1,0:T(8,128)(2,1)}, bf16[96,1152]{1,0:T(8,128)(2,1)S(1)}, u32[]{:S(2)}, u32[]{:S(2)}) %collective-permute-start.1) | collective-permute-done | bytes 221216 | tf_op jit(solution)/shard_map/ppermute | solution.py:420
  47.9 8.1 %collective-permute-done.2.g2 = bf16[96,1152]{1,0:T(8,128)(2,1)S(1)} collective-permute-done((bf16[96,1152]{1,0:T(8,128)(2,1)}, bf16[96,1152]{1,0:T(8,128)(2,1)S(1)}, u32[]{:S(2)}, u32[]{:S(2)}) %collective-permute-start.2) | collective-permute-done | bytes 221216 | tf_op jit(solution)/shard_map/ppermute | solution.py:420
  60.8 4.0 %collective-permute-start.4 = (bf16[16,1152]{1,0:T(8,128)(2,1)}, bf16[16,1152]{1,0:T(8,128)(2,1)S(1)}, u32[]{:S(2)}, u32[]{:S(2)}) collective-permute-start(bf16[16,1152]{1,0:T(8,128)(2,1)} %get-tuple-element.27), channel_id=1, source_target_pairs={{0,8},{4,12},{8,16},{12,20},{16,24},{20,28},{24,32},{28,36},{32,40... | collective-permute-start | bytes 110600 | tf_op jit(solution)/shard_map/ppermute | solution.py:420
  70.8 6.4 %collective-permute-start.8 = (bf16[16,1152]{1,0:T(8,128)(2,1)}, bf16[16,1152]{1,0:T(8,128)(2,1)S(1)}, u32[]{:S(2)}, u32[]{:S(2)}) collective-permute-start(bf16[16,1152]{1,0:T(8,128)(2,1)} %get-tuple-element.31), channel_id=1, source_target_pairs={{0,40},{4,44},{24,0},{28,4},{32,8},{36,12},{40,16},{44,20},{48,24}... | collective-permute-start | bytes 110600 | tf_op jit(solution)/shard_map/ppermute | solution.py:420
  80.3 6.8 %attend_0.1.rest_7_.att_ref = f32[256,384]{1,0:T(8,128)} custom-call(s32[8]{0:T(128)} %reshape.32.bounds_ref, s32[1024,2]{1,0:T(8,128)} %copy.26.rows_ref, bf16[1024,384]{1,0:T(8,128)(2,1)} %project.1.rest_0_.q_ref, bf16[1024,768]{1,0:T(8,128)(2,1)} %copy-done, bf16[1024,768]{1,0:T(8,128)(2,1)} %get-tuple-element.34.mine, bf16[1024,768]{1,0:T(8,128)(2,1)} %copy-done.1, ...), custom_call_target="tpu_custom_call" | custom-call | tf_op jit(solution)/shard_map/attend_0/pallas_call | solution.py:326
  90.2 5.2 %collective-permute-start.13 = (bf16[16,1152]{1,0:T(8,128)(2,1)}, bf16[16,1152]{1,0:T(8,128)(2,1)S(1)}, u32[]{:S(2)}, u32[]{:S(2)}) collective-permute-start(bf16[16,1152]{1,0:T(8,128)(2,1)} %renorm.1.dep_ref.rest_0_), channel_id=1, source_target_pairs={{0,8},{4,12},{8,16},{12,20},{16,24},{20,28},{24,32},{28,36},{32,40... | collective-permute-start | bytes 110600 | tf_op jit(solution)/shard_map/ppermute | solution.py:420
  97.0 6.6 %collective-permute-start.15 = (bf16[16,1152]{1,0:T(8,128)(2,1)}, bf16[16,1152]{1,0:T(8,128)(2,1)S(1)}, u32[]{:S(2)}, u32[]{:S(2)}) collective-permute-start(bf16[16,1152]{1,0:T(8,128)(2,1)} %renorm.1.dep_ref.rest_0_), channel_id=1, source_target_pairs={{0,24},{4,28},{8,32},{12,36},{16,40},{20,44},{24,48},{28,52},{32,5... | collective-permute-start | bytes 110600 | tf_op jit(solution)/shard_map/ppermute | solution.py:420
  105.5 6.1 %collective-permute-start.17 = (bf16[16,1152]{1,0:T(8,128)(2,1)}, bf16[16,1152]{1,0:T(8,128)(2,1)S(1)}, u32[]{:S(2)}, u32[]{:S(2)}) collective-permute-start(bf16[16,1152]{1,0:T(8,128)(2,1)} %renorm.1.dep_ref.rest_0_), channel_id=1, source_target_pairs={{0,40},{4,44},{8,48},{12,52},{16,56},{20,60},{24,0},{28,4},{32,8},... | collective-permute-start | bytes 110600 | tf_op jit(solution)/shard_map/ppermute | solution.py:420
  115.5 7.0 %attend_1.1.rest_8_.att_ref = f32[256,384]{1,0:T(8,128)} custom-call(s32[8]{0:T(128)} %reshape.32.bounds_ref, s32[1024,2]{1,0:T(8,128)} %copy.26.rows_ref, bf16[1024,384]{1,0:T(8,128)(2,1)} %project.1.rest_0_.q_ref, bf16[1024,768]{1,0:T(8,128)(2,1)} %copy-done, bf16[1024,768]{1,0:T(8,128)(2,1)} %get-tuple-element.34.mine, bf16[1024,768]{1,0:T(8,128)(2,1)} %copy-done.1, ...), custom_call_target="tpu_custom_call" | custom-call | tf_op jit(solution)/shard_map/attend_1/pallas_call | solution.py:326
  125.5 3.3 %collective-permute-start.21 = (bf16[96,1152]{1,0:T(8,128)(2,1)}, bf16[96,1152]{1,0:T(8,128)(2,1)S(1)}, u32[]{:S(2)}, u32[]{:S(2)}) collective-permute-start(bf16[96,1152]{1,0:T(8,128)(2,1)} %ag_z.1.dep_ref.rest_0_), channel_id=1, source_target_pairs={{0,128},{4,132},{8,136},{12,140},{16,144},{20,148},{24,152},{28,15... | collective-permute-start | bytes 663560 | tf_op jit(solution)/shard_map/ppermute | solution.py:420
  130.9 7.5 %attend_3.1.rest_5_.att_ref = f32[256,384]{1,0:T(8,128)} custom-call(s32[8]{0:T(128)} %reshape.32.bounds_ref, s32[1024,2]{1,0:T(8,128)} %copy.26.rows_ref, bf16[1024,384]{1,0:T(8,128)(2,1)} %project.1.rest_0_.q_ref, bf16[1024,768]{1,0:T(8,128)(2,1)} %copy-done, bf16[1024,768]{1,0:T(8,128)(2,1)} %get-tuple-element.34.mine, bf16[1024,768]{1,0:T(8,128)(2,1)} %copy-done.1, ...), custom_call_target="tpu_custom_call" | custom-call | tf_op jit(solution)/shard_map/attend_3/pallas_call | solution.py:326
  138.4 6.8 %attend_2.1.rest_4_.att_ref = f32[256,384]{1,0:T(8,128)} custom-call(s32[8]{0:T(128)} %reshape.32.bounds_ref, s32[1024,2]{1,0:T(8,128)} %copy.26.rows_ref, bf16[1024,384]{1,0:T(8,128)(2,1)} %project.1.rest_0_.q_ref, bf16[1024,768]{1,0:T(8,128)(2,1)} %copy-done, bf16[1024,768]{1,0:T(8,128)(2,1)} %get-tuple-element.34.mine, bf16[1024,768]{1,0:T(8,128)(2,1)} %copy-done.1, ...), custom_call_target="tpu_custom_call" | custom-call | tf_op jit(solution)/shard_map/attend_2/pallas_call | solution.py:326
  146.6 2.3 %ag_x.1.own_ref = bf16[384,1152]{1,0:T(8,128)(2,1)} custom-call(s32[3]{0:T(128)} %pad_add_fusion.2.pos_ref, bf16[96,1152]{1,0:T(8,128)(2,1)} %ag_z.1.dep_ref.rest_0_, bf16[96,1152]{1,0:T(8,128)(2,1)} %copy-done.13, bf16[96,1152]{1,0:T(8,128)(2,1)} %copy-done.14, bf16[96,1152]{1,0:T(8,128)(2,1)} %copy-done.15, f32[256,384]{1,0:T(8,128)} %attend_2.1.rest_4_.att_ref, ...), custom_call_target="tpu_custom_call" | custom-call | tf_op jit(solution)/shard_map/ag_x/pallas_call | solution.py:249
  148.9 4.8 %collective-permute-start.23 = (bf16[384,1152]{1,0:T(8,128)(2,1)}, bf16[384,1152]{1,0:T(8,128)(2,1)S(1)}, u32[]{:S(2)}, u32[]{:S(2)}) collective-permute-start(bf16[384,1152]{1,0:T(8,128)(2,1)} %ag_x.1.own_ref), channel_id=1, source_target_pairs={{0,4},{4,0},{8,12},{12,8},{16,20},{20,16},{24,28},{28,24},{32,36},... | collective-permute-start | bytes 2654216 | tf_op jit(solution)/shard_map/ppermute | solution.py:420
  155.9 2.6 %collective-permute-start.28 = (bf16[384,384]{1,0:T(8,128)(2,1)S(1)}, bf16[384,384]{1,0:T(8,128)(2,1)S(1)}, u32[]{:S(2)}, u32[]{:S(2)}) collective-permute-start(bf16[384,384]{1,0:T(8,128)(2,1)S(1)} %get-tuple-element.40), channel_id=1, source_target_pairs={{0,2},{1,3},{2,0},{3,1},{4,6},{5,7},{6,4},{7,5},{8,10},{9,11},{10,... | collective-permute-start | bytes 884744 | tf_op jit(solution)/shard_map/ppermute | solution.py:447
  161.1 3.4 %apply_0.1.refs_0_ = bf16[256,384]{1,0:T(8,128)(2,1)} custom-call(s32[3]{0:T(128)} %pad_add_fusion.2.pos_ref, bf16[1024,384]{1,0:T(8,128)(2,1)} %project.1.rest_0_.q_ref, bf16[384,1152]{1,0:T(8,128)(2,1)} %ag_x.1.own_ref, bf16[384,1152]{1,0:T(8,128)(2,1)} %copy-done.2, f32[256,384]{1,0:T(8,128)} %attend_0.1.rest_7_.att_ref, f32[1,384]{1,0:T(1,128)} %broadcast_in_dim.46.gain_ref), custom_call_target="tpu_custom_call" | custom-call | tf_op jit(solution)/shard_map/apply_0/pallas_call | solution.py:365
  165.6 3.4 %apply_1.1.refs_0_ = bf16[256,384]{1,0:T(8,128)(2,1)} custom-call(s32[3]{0:T(128)} %pad_add_fusion.2.pos_ref, bf16[1024,384]{1,0:T(8,128)(2,1)} %project.1.rest_0_.q_ref, bf16[384,1152]{1,0:T(8,128)(2,1)} %ag_x.1.own_ref, bf16[384,1152]{1,0:T(8,128)(2,1)} %copy-done.2, f32[256,384]{1,0:T(8,128)} %attend_1.1.rest_8_.att_ref, f32[1,384]{1,0:T(1,128)} %broadcast_in_dim.46.gain_ref), custom_call_target="tpu_custom_call" | custom-call | tf_op jit(solution)/shard_map/apply_1/pallas_call | solution.py:365
  169.0 3.4 %apply_2.1.refs_0_ = bf16[256,384]{1,0:T(8,128)(2,1)} custom-call(s32[3]{0:T(128)} %pad_add_fusion.2.pos_ref, bf16[1024,384]{1,0:T(8,128)(2,1)} %project.1.rest_0_.q_ref, bf16[384,1152]{1,0:T(8,128)(2,1)} %ag_x.1.own_ref, bf16[384,1152]{1,0:T(8,128)(2,1)} %copy-done.2, f32[256,384]{1,0:T(8,128)} %attend_2.1.rest_4_.att_ref, f32[1,384]{1,0:T(1,128)} %broadcast_in_dim.46.gain_ref), custom_call_target="tpu_custom_call" | custom-call | tf_op jit(solution)/shard_map/apply_2/pallas_call | solution.py:365
  180.5 3.4 %apply_3.1.refs_0_ = bf16[256,384]{1,0:T(8,128)(2,1)} custom-call(s32[3]{0:T(128)} %pad_add_fusion.2.pos_ref, bf16[1024,384]{1,0:T(8,128)(2,1)} %project.1.rest_0_.q_ref, bf16[384,1152]{1,0:T(8,128)(2,1)} %ag_x.1.own_ref, bf16[384,1152]{1,0:T(8,128)(2,1)} %copy-done.2, f32[256,384]{1,0:T(8,128)} %attend_3.1.rest_5_.att_ref, f32[1,384]{1,0:T(1,128)} %broadcast_in_dim.46.gain_ref), custom_call_target="tpu_custom_call" | custom-call | tf_op jit(solution)/shard_map/apply_3/pallas_call | solution.py:365
  186.8 2.2 %collective-permute-done.34.refs_2_ = bf16[256,384]{1,0:T(8,128)(2,1)S(1)} collective-permute-done((bf16[256,384]{1,0:T(8,128)(2,1)S(1)}, bf16[256,384]{1,0:T(8,128)(2,1)S(1)}, u32[]{:S(2)}, u32[]{:S(2)}) %collective-permute-start.34) | collective-permute-done | bytes 196640 | tf_op jit(solution)/shard_map/ppermute | solution.py:490
  190.8 2.5 %collective-permute-done.30.refs_1_ = bf16[256,384]{1,0:T(8,128)(2,1)S(1)} collective-permute-done((bf16[256,384]{1,0:T(8,128)(2,1)}, bf16[256,384]{1,0:T(8,128)(2,1)S(1)}, u32[]{:S(2)}, u32[]{:S(2)}) %collective-permute-start.30) | collective-permute-done | bytes 196640 | tf_op jit(solution)/shard_map/ppermute | solution.py:490
  193.4 2.9 %output_0.1.refs_8_ = bf16[1024,384]{1,0:T(8,128)(2,1)} custom-call(bf16[256,384]{1,0:T(8,128)(2,1)} %apply_0.1.refs_0_, bf16[256,384]{1,0:T(8,128)(2,1)} %copy-done.25, bf16[256,384]{1,0:T(8,128)(2,1)} %copy-done.26, bf16[256,384]{1,0:T(8,128)(2,1)} %copy-done.27, bf16[384,384]{1,0:T(8,128)(2,1)} %get-tuple-element.39.refs_4_, bf16[384,384]{1,0:T(8,128)(2,1)} %copy-done.3, ...), custom_call_target="tpu_custom_call" | custom-call | tf_op jit(solution)/shard_map/output_0/pallas_call | solution.py:393
  196.3 2.9 %output_1.1.refs_8_ = bf16[1024,384]{1,0:T(8,128)(2,1)} custom-call(bf16[256,384]{1,0:T(8,128)(2,1)} %apply_1.1.refs_0_, bf16[256,384]{1,0:T(8,128)(2,1)} %copy-done.16, bf16[256,384]{1,0:T(8,128)(2,1)} %copy-done.17, bf16[256,384]{1,0:T(8,128)(2,1)} %copy-done.19, bf16[384,384]{1,0:T(8,128)(2,1)} %get-tuple-element.39.refs_4_, ...), custom_call_target="tpu_custom_call", output_to_operand_aliasing={{}: (8, {})} | custom-call | tf_op jit(solution)/shard_map/output_1/pallas_call | solution.py:393
  200.6 2.9 %output_2.1.refs_8_ = bf16[1024,384]{1,0:T(8,128)(2,1)} custom-call(bf16[256,384]{1,0:T(8,128)(2,1)} %apply_2.1.refs_0_, bf16[256,384]{1,0:T(8,128)(2,1)} %copy-done.18, bf16[256,384]{1,0:T(8,128)(2,1)} %copy-done.21, bf16[256,384]{1,0:T(8,128)(2,1)} %copy-done.23, bf16[384,384]{1,0:T(8,128)(2,1)} %get-tuple-element.39.refs_4_, ...), custom_call_target="tpu_custom_call", output_to_operand_aliasing={{}: (8, {})} | custom-call | tf_op jit(solution)/shard_map/output_2/pallas_call | solution.py:393
  203.4 2.4 %collective-permute-done.25.refs_2_ = bf16[256,384]{1,0:T(8,128)(2,1)S(1)} collective-permute-done((bf16[256,384]{1,0:T(8,128)(2,1)}, bf16[256,384]{1,0:T(8,128)(2,1)S(1)}, u32[]{:S(2)}, u32[]{:S(2)}) %collective-permute-start.25) | collective-permute-done | bytes 196640 | tf_op jit(solution)/shard_map/ppermute | solution.py:490
  207.2 2.9 %output_3.1 = bf16[1024,384]{1,0:T(8,128)(2,1)} custom-call(bf16[256,384]{1,0:T(8,128)(2,1)} %apply_3.1.refs_0_, bf16[256,384]{1,0:T(8,128)(2,1)} %copy-done.20, bf16[256,384]{1,0:T(8,128)(2,1)} %copy-done.22, bf16[256,384]{1,0:T(8,128)(2,1)} %copy-done.24, bf16[384,384]{1,0:T(8,128)(2,1)} %get-tuple-element.39.refs_4_, ...), custom_call_target="tpu_custom_call", output_to_operand_aliasing={{}: (8, {})} | custom-call | tf_op jit(solution)/shard_map/output_3/pallas_call | solution.py:393
  (171 shorter events, 61.7 us)
Async XLA Ops:
  17.5 53.3 %collective-permute-start.11 = (bf16[1024,768]{1,0:T(8,128)(2,1)}, bf16[1024,768]{1,0:T(8,128)(2,1)S(1)}, u32[]{:S(2)}, u32[]{:S(2)}) collective-permute-start(bf16[1024,768]{1,0:T(8,128)(2,1)} %get-tuple-element.34.mine), channel_id=1, source_target_pairs={{0,4},{4,8},{8,12},{12,16},{16,20},{20,24},{24,28},{28,32},{32,36}... | collective-permute-start | bytes 4718600 | tf_op jit(solution)/shard_map/ppermute | solution.py:420
  22.4 54.8 %collective-permute-start.12 = (bf16[1024,768]{1,0:T(8,128)(2,1)}, bf16[1024,768]{1,0:T(8,128)(2,1)S(1)}, u32[]{:S(2)}, u32[]{:S(2)}) collective-permute-start(bf16[1024,768]{1,0:T(8,128)(2,1)} %get-tuple-element.34.mine), channel_id=1, source_target_pairs={{4,0},{8,4},{12,8},{16,12},{20,16},{24,20},{28,24},{32,28},{36,32}... | collective-permute-start | bytes 4718600 | tf_op jit(solution)/shard_map/ppermute | solution.py:420
  31.8 16.1 %collective-permute-start.1 = (bf16[96,1152]{1,0:T(8,128)(2,1)}, bf16[96,1152]{1,0:T(8,128)(2,1)S(1)}, u32[]{:S(2)}, u32[]{:S(2)}) collective-permute-start(bf16[96,1152]{1,0:T(8,128)(2,1)} %get-tuple-element.23), channel_id=1, source_target_pairs={{0,64},{4,68},{8,72},{12,76},{16,80},{20,84},{24,88},{28,92},{32,9... | collective-permute-start | bytes 663560 | tf_op jit(solution)/shard_map/ppermute | solution.py:420
  35.0 20.9 %collective-permute-start.2 = (bf16[96,1152]{1,0:T(8,128)(2,1)}, bf16[96,1152]{1,0:T(8,128)(2,1)S(1)}, u32[]{:S(2)}, u32[]{:S(2)}) collective-permute-start(bf16[96,1152]{1,0:T(8,128)(2,1)} %get-tuple-element.24), channel_id=1, source_target_pairs={{0,128},{4,132},{8,136},{12,140},{16,144},{20,148},{24,152},{28,15... | collective-permute-start | bytes 663560 | tf_op jit(solution)/shard_map/ppermute | solution.py:420
  37.8 18.2 %collective-permute-start.3 = (bf16[96,1152]{1,0:T(8,128)(2,1)}, bf16[96,1152]{1,0:T(8,128)(2,1)S(1)}, u32[]{:S(2)}, u32[]{:S(2)}) collective-permute-start(bf16[96,1152]{1,0:T(8,128)(2,1)} %get-tuple-element.25), channel_id=1, source_target_pairs={{0,192},{4,196},{8,200},{12,204},{16,208},{20,212},{24,216},{28,22... | collective-permute-start | bytes 663560 | tf_op jit(solution)/shard_map/ppermute | solution.py:420
  65.0 22.2 %collective-permute-start.5 = (bf16[16,1152]{1,0:T(8,128)(2,1)}, bf16[16,1152]{1,0:T(8,128)(2,1)S(1)}, u32[]{:S(2)}, u32[]{:S(2)}) collective-permute-start(bf16[16,1152]{1,0:T(8,128)(2,1)} %get-tuple-element.28), channel_id=1, source_target_pairs={{0,16},{4,20},{8,24},{12,28},{16,32},{20,36},{24,40},{28,44},{48,0... | collective-permute-start | bytes 110600 | tf_op jit(solution)/shard_map/ppermute | solution.py:420
  66.9 20.2 %collective-permute-start.6 = (bf16[16,1152]{1,0:T(8,128)(2,1)}, bf16[16,1152]{1,0:T(8,128)(2,1)S(1)}, u32[]{:S(2)}, u32[]{:S(2)}) collective-permute-start(bf16[16,1152]{1,0:T(8,128)(2,1)} %get-tuple-element.29), channel_id=1, source_target_pairs={{0,24},{4,28},{8,32},{12,36},{16,40},{20,44},{40,0},{44,4},{48,8},... | collective-permute-start | bytes 110600 | tf_op jit(solution)/shard_map/ppermute | solution.py:420
  68.9 18.3 %collective-permute-start.7 = (bf16[16,1152]{1,0:T(8,128)(2,1)}, bf16[16,1152]{1,0:T(8,128)(2,1)S(1)}, u32[]{:S(2)}, u32[]{:S(2)}) collective-permute-start(bf16[16,1152]{1,0:T(8,128)(2,1)} %get-tuple-element.30), channel_id=1, source_target_pairs={{0,32},{4,36},{8,40},{12,44},{32,0},{36,4},{40,8},{44,12},{48,16},... | collective-permute-start | bytes 110600 | tf_op jit(solution)/shard_map/ppermute | solution.py:420
  70.8 16.4 %collective-permute-start.8 = (bf16[16,1152]{1,0:T(8,128)(2,1)}, bf16[16,1152]{1,0:T(8,128)(2,1)S(1)}, u32[]{:S(2)}, u32[]{:S(2)}) collective-permute-start(bf16[16,1152]{1,0:T(8,128)(2,1)} %get-tuple-element.31), channel_id=1, source_target_pairs={{0,40},{4,44},{24,0},{28,4},{32,8},{36,12},{40,16},{44,20},{48,24}... | collective-permute-start | bytes 110600 | tf_op jit(solution)/shard_map/ppermute | solution.py:420
  90.2 21.4 %collective-permute-start.13 = (bf16[16,1152]{1,0:T(8,128)(2,1)}, bf16[16,1152]{1,0:T(8,128)(2,1)S(1)}, u32[]{:S(2)}, u32[]{:S(2)}) collective-permute-start(bf16[16,1152]{1,0:T(8,128)(2,1)} %renorm.1.dep_ref.rest_0_), channel_id=1, source_target_pairs={{0,8},{4,12},{8,16},{12,20},{16,24},{20,28},{24,32},{28,36},{32,40... | collective-permute-start | bytes 110600 | tf_op jit(solution)/shard_map/ppermute | solution.py:420
  95.4 18.2 %collective-permute-start.14 = (bf16[16,1152]{1,0:T(8,128)(2,1)}, bf16[16,1152]{1,0:T(8,128)(2,1)S(1)}, u32[]{:S(2)}, u32[]{:S(2)}) collective-permute-start(bf16[16,1152]{1,0:T(8,128)(2,1)} %renorm.1.dep_ref.rest_0_), channel_id=1, source_target_pairs={{0,16},{4,20},{8,24},{12,28},{16,32},{20,36},{24,40},{28,44},{32,4... | collective-permute-start | bytes 110600 | tf_op jit(solution)/shard_map/ppermute | solution.py:420
  97.0 25.5 %collective-permute-start.15 = (bf16[16,1152]{1,0:T(8,128)(2,1)}, bf16[16,1152]{1,0:T(8,128)(2,1)S(1)}, u32[]{:S(2)}, u32[]{:S(2)}) collective-permute-start(bf16[16,1152]{1,0:T(8,128)(2,1)} %renorm.1.dep_ref.rest_0_), channel_id=1, source_target_pairs={{0,24},{4,28},{8,32},{12,36},{16,40},{20,44},{24,48},{28,52},{32,5... | collective-permute-start | bytes 110600 | tf_op jit(solution)/shard_map/ppermute | solution.py:420
  103.6 18.9 %collective-permute-start.16 = (bf16[16,1152]{1,0:T(8,128)(2,1)}, bf16[16,1152]{1,0:T(8,128)(2,1)S(1)}, u32[]{:S(2)}, u32[]{:S(2)}) collective-permute-start(bf16[16,1152]{1,0:T(8,128)(2,1)} %renorm.1.dep_ref.rest_0_), channel_id=1, source_target_pairs={{0,32},{4,36},{8,40},{12,44},{16,48},{20,52},{24,56},{28,60},{32,0... | collective-permute-start | bytes 110600 | tf_op jit(solution)/shard_map/ppermute | solution.py:420
  105.5 17.0 %collective-permute-start.17 = (bf16[16,1152]{1,0:T(8,128)(2,1)}, bf16[16,1152]{1,0:T(8,128)(2,1)S(1)}, u32[]{:S(2)}, u32[]{:S(2)}) collective-permute-start(bf16[16,1152]{1,0:T(8,128)(2,1)} %renorm.1.dep_ref.rest_0_), channel_id=1, source_target_pairs={{0,40},{4,44},{8,48},{12,52},{16,56},{20,60},{24,0},{28,4},{32,8},... | collective-permute-start | bytes 110600 | tf_op jit(solution)/shard_map/ppermute | solution.py:420
  125.5 19.7 %collective-permute-start.20 = (bf16[96,1152]{1,0:T(8,128)(2,1)}, bf16[96,1152]{1,0:T(8,128)(2,1)S(1)}, u32[]{:S(2)}, u32[]{:S(2)}) collective-permute-start(bf16[96,1152]{1,0:T(8,128)(2,1)} %ag_z.1.dep_ref.rest_0_), channel_id=1, source_target_pairs={{0,64},{4,68},{8,72},{12,76},{16,80},{20,84},{24,88},{28,92},{32,9... | collective-permute-start | bytes 663560 | tf_op jit(solution)/shard_map/ppermute | solution.py:420
  125.5 19.7 %collective-permute-start.21 = (bf16[96,1152]{1,0:T(8,128)(2,1)}, bf16[96,1152]{1,0:T(8,128)(2,1)S(1)}, u32[]{:S(2)}, u32[]{:S(2)}) collective-permute-start(bf16[96,1152]{1,0:T(8,128)(2,1)} %ag_z.1.dep_ref.rest_0_), channel_id=1, source_target_pairs={{0,128},{4,132},{8,136},{12,140},{16,144},{20,148},{24,152},{28,15... | collective-permute-start | bytes 663560 | tf_op jit(solution)/shard_map/ppermute | solution.py:420
  128.8 16.4 %collective-permute-start.22 = (bf16[96,1152]{1,0:T(8,128)(2,1)}, bf16[96,1152]{1,0:T(8,128)(2,1)S(1)}, u32[]{:S(2)}, u32[]{:S(2)}) collective-permute-start(bf16[96,1152]{1,0:T(8,128)(2,1)} %ag_z.1.dep_ref.rest_0_), channel_id=1, source_target_pairs={{0,192},{4,196},{8,200},{12,204},{16,208},{20,212},{24,216},{28,22... | collective-permute-start | bytes 663560 | tf_op jit(solution)/shard_map/ppermute | solution.py:420
  148.9 11.2 %collective-permute-start.23 = (bf16[384,1152]{1,0:T(8,128)(2,1)}, bf16[384,1152]{1,0:T(8,128)(2,1)S(1)}, u32[]{:S(2)}, u32[]{:S(2)}) collective-permute-start(bf16[384,1152]{1,0:T(8,128)(2,1)} %ag_x.1.own_ref), channel_id=1, source_target_pairs={{0,4},{4,0},{8,12},{12,8},{16,20},{20,16},{24,28},{28,24},{32,36},... | collective-permute-start | bytes 2654216 | tf_op jit(solution)/shard_map/ppermute | solution.py:420
  154.6 17.9 %collective-permute-start.27 = (bf16[384,384]{1,0:T(8,128)(2,1)S(1)}, bf16[384,384]{1,0:T(8,128)(2,1)S(1)}, u32[]{:S(2)}, u32[]{:S(2)}) collective-permute-start(bf16[384,384]{1,0:T(8,128)(2,1)S(1)} %get-tuple-element.38), channel_id=1, source_target_pairs={{0,1},{1,2},{2,3},{3,0},{4,5},{5,6},{6,7},{7,4},{8,9},{9,10},{10,1... | collective-permute-start | bytes 884744 | tf_op jit(solution)/shard_map/ppermute | solution.py:447
  155.9 18.3 %collective-permute-start.28 = (bf16[384,384]{1,0:T(8,128)(2,1)S(1)}, bf16[384,384]{1,0:T(8,128)(2,1)S(1)}, u32[]{:S(2)}, u32[]{:S(2)}) collective-permute-start(bf16[384,384]{1,0:T(8,128)(2,1)S(1)} %get-tuple-element.40), channel_id=1, source_target_pairs={{0,2},{1,3},{2,0},{3,1},{4,6},{5,7},{6,4},{7,5},{8,10},{9,11},{10,... | collective-permute-start | bytes 884744 | tf_op jit(solution)/shard_map/ppermute | solution.py:447
  158.5 16.2 %collective-permute-start.29 = (bf16[384,384]{1,0:T(8,128)(2,1)S(1)}, bf16[384,384]{1,0:T(8,128)(2,1)S(1)}, u32[]{:S(2)}, u32[]{:S(2)}) collective-permute-start(bf16[384,384]{1,0:T(8,128)(2,1)S(1)} %get-tuple-element.37), channel_id=1, source_target_pairs={{0,3},{1,0},{2,1},{3,2},{4,7},{5,4},{6,5},{7,6},{8,11},{9,8},{10,9... | collective-permute-start | bytes 884744 | tf_op jit(solution)/shard_map/ppermute | solution.py:447
  164.4 12.3 %collective-permute-start.36 = (bf16[256,384]{1,0:T(8,128)(2,1)}, bf16[256,384]{1,0:T(8,128)(2,1)S(1)}, u32[]{:S(2)}, u32[]{:S(2)}) collective-permute-start(bf16[256,384]{1,0:T(8,128)(2,1)} %apply_0.1.refs_0_), channel_id=1, source_target_pairs={{0,1},{1,2},{2,3},{3,0},{4,5},{5,6},{6,7},{7,4},{8,9},{9,10},{10,1... | collective-permute-start | bytes 589832 | tf_op jit(solution)/shard_map/ppermute | solution.py:490
  164.8 15.7 %collective-permute-start.37 = (bf16[256,384]{1,0:T(8,128)(2,1)}, bf16[256,384]{1,0:T(8,128)(2,1)S(1)}, u32[]{:S(2)}, u32[]{:S(2)}) collective-permute-start(bf16[256,384]{1,0:T(8,128)(2,1)} %apply_0.1.refs_0_), channel_id=1, source_target_pairs={{0,2},{1,3},{2,0},{3,1},{4,6},{5,7},{6,4},{7,5},{8,10},{9,11},{10,... | collective-permute-start | bytes 589832 | tf_op jit(solution)/shard_map/ppermute | solution.py:490
  172.4 11.5 %collective-permute-start.38 = (bf16[256,384]{1,0:T(8,128)(2,1)S(1)}, bf16[256,384]{1,0:T(8,128)(2,1)S(1)}, u32[]{:S(2)}, u32[]{:S(2)}) collective-permute-start(bf16[256,384]{1,0:T(8,128)(2,1)S(1)} %copy-done.9), channel_id=1, source_target_pairs={{0,3},{1,0},{2,1},{3,2},{4,7},{5,4},{6,5},{7,6},{8,11},{9,8},{10,9... | collective-permute-start | bytes 589832 | tf_op jit(solution)/shard_map/ppermute | solution.py:490
  174.7 14.2 %collective-permute-start.34 = (bf16[256,384]{1,0:T(8,128)(2,1)S(1)}, bf16[256,384]{1,0:T(8,128)(2,1)S(1)}, u32[]{:S(2)}, u32[]{:S(2)}) collective-permute-start(bf16[256,384]{1,0:T(8,128)(2,1)S(1)} %copy-done.8), channel_id=1, source_target_pairs={{0,2},{1,3},{2,0},{3,1},{4,6},{5,7},{6,4},{7,5},{8,10},{9,11},{10,... | collective-permute-start | bytes 589832 | tf_op jit(solution)/shard_map/ppermute | solution.py:490
  176.7 12.2 %collective-permute-start.35 = (bf16[256,384]{1,0:T(8,128)(2,1)S(1)}, bf16[256,384]{1,0:T(8,128)(2,1)S(1)}, u32[]{:S(2)}, u32[]{:S(2)}) collective-permute-start(bf16[256,384]{1,0:T(8,128)(2,1)S(1)} %copy-done.8), channel_id=1, source_target_pairs={{0,3},{1,0},{2,1},{3,2},{4,7},{5,4},{6,5},{7,6},{8,11},{9,8},{10,9... | collective-permute-start | bytes 589832 | tf_op jit(solution)/shard_map/ppermute | solution.py:490
  180.5 12.9 %collective-permute-start.30 = (bf16[256,384]{1,0:T(8,128)(2,1)}, bf16[256,384]{1,0:T(8,128)(2,1)S(1)}, u32[]{:S(2)}, u32[]{:S(2)}) collective-permute-start(bf16[256,384]{1,0:T(8,128)(2,1)} %apply_2.1.refs_0_), channel_id=1, source_target_pairs={{0,1},{1,2},{2,3},{3,0},{4,5},{5,6},{6,7},{7,4},{8,9},{9,10},{10,1... | collective-permute-start | bytes 589832 | tf_op jit(solution)/shard_map/ppermute | solution.py:490
  184.0 15.2 %collective-permute-start.31 = (bf16[256,384]{1,0:T(8,128)(2,1)S(1)}, bf16[256,384]{1,0:T(8,128)(2,1)S(1)}, u32[]{:S(2)}, u32[]{:S(2)}) collective-permute-start(bf16[256,384]{1,0:T(8,128)(2,1)S(1)} %copy-done.7), channel_id=1, source_target_pairs={{0,2},{1,3},{2,0},{3,1},{4,6},{5,7},{6,4},{7,5},{8,10},{9,11},{10,... | collective-permute-start | bytes 589832 | tf_op jit(solution)/shard_map/ppermute | solution.py:490
  185.2 14.0 %collective-permute-start.32 = (bf16[256,384]{1,0:T(8,128)(2,1)S(1)}, bf16[256,384]{1,0:T(8,128)(2,1)S(1)}, u32[]{:S(2)}, u32[]{:S(2)}) collective-permute-start(bf16[256,384]{1,0:T(8,128)(2,1)S(1)} %copy-done.7), channel_id=1, source_target_pairs={{0,3},{1,0},{2,1},{3,2},{4,7},{5,4},{6,5},{7,6},{8,11},{9,8},{10,9... | collective-permute-start | bytes 589832 | tf_op jit(solution)/shard_map/ppermute | solution.py:490
  188.9 14.5 %collective-permute-start.24 = (bf16[256,384]{1,0:T(8,128)(2,1)}, bf16[256,384]{1,0:T(8,128)(2,1)S(1)}, u32[]{:S(2)}, u32[]{:S(2)}) collective-permute-start(bf16[256,384]{1,0:T(8,128)(2,1)} %apply_3.1.refs_0_), channel_id=1, source_target_pairs={{0,1},{1,2},{2,3},{3,0},{4,5},{5,6},{6,7},{7,4},{8,9},{9,10},{10,1... | collective-permute-start | bytes 589832 | tf_op jit(solution)/shard_map/ppermute | solution.py:490
  189.0 16.9 %collective-permute-start.25 = (bf16[256,384]{1,0:T(8,128)(2,1)}, bf16[256,384]{1,0:T(8,128)(2,1)S(1)}, u32[]{:S(2)}, u32[]{:S(2)}) collective-permute-start(bf16[256,384]{1,0:T(8,128)(2,1)} %apply_3.1.refs_0_), channel_id=1, source_target_pairs={{0,2},{1,3},{2,0},{3,1},{4,6},{5,7},{6,4},{7,5},{8,10},{9,11},{10,... | collective-permute-start | bytes 589832 | tf_op jit(solution)/shard_map/ppermute | solution.py:490
  193.4 12.5 %collective-permute-start.26 = (bf16[256,384]{1,0:T(8,128)(2,1)}, bf16[256,384]{1,0:T(8,128)(2,1)S(1)}, u32[]{:S(2)}, u32[]{:S(2)}) collective-permute-start(bf16[256,384]{1,0:T(8,128)(2,1)} %apply_3.1.refs_0_), channel_id=1, source_target_pairs={{0,3},{1,0},{2,1},{3,2},{4,7},{5,4},{6,5},{7,6},{8,11},{9,8},{10,9... | collective-permute-start | bytes 589832 | tf_op jit(solution)/shard_map/ppermute | solution.py:490
  (51 other events, 301.2 us)

commit v2 on v1

--- a/solution.py
+++ b/solution.py
@@ -14,9 +14,8 @@
 XS, ZS, CS, HS = 4, 8, 2, 4
 SHARDS = XS * ZS * CS
 TOKENS = TOK * SHARDS
-XROWS = DH // XS
+SLOTS = XS * ZS
 ZROWS = 16
-OWNERS = XROWS // ZROWS
 WIDE = HID + DH
 KB = 256
 QB = 256
@@ -41,26 +40,16 @@
     return jax.ShapeDtypeStruct(shape, dtype)
 
 
-def shift_x(d):
-    return [(t, (t + d * ZS * CS) % SHARDS) for t in range(SHARDS)]
-
-
-def shift_z(d, to_owner=False, from_owner=False):
-    pairs = []
-    for t in range(SHARDS):
-        x, z, c = t // (ZS * CS), t // CS % ZS, t % CS
-        other = (z + d) % ZS
-        if (to_owner and other >= OWNERS) or (from_owner and z >= OWNERS):
-            continue
-        pairs.append((t, (x * ZS + other) * CS + c))
-    return pairs
-
-
 SWAP_C = [(t, t ^ 1) for t in range(SHARDS)]
+CHIPS = [[chip * CS + c for chip in range(SHARDS // CS)] for c in range(CS)]
 
 
 def shift_h(d):
     return [(h, (h + d) % HS) for h in range(HS)]
+
+
+def full(shape):
+    return pl.BlockSpec(shape, lambda i: (0,) * len(shape))
 
 
 def front_kernel(
@@ -148,112 +137,66 @@
     )(pos, tokens, qkv_weight, qkv_weight, rate_weight, first_fast, gate_fast, second_fast)
 
 
-def rs_x_kernel(pos_ref, keep_ref, got_ref, own_ref, *outs):
-    x = pos_ref[0]
-    for d, out in enumerate((own_ref, *outs)):
-        rows = pl.ds(pl.multiple_of(lax.rem(x + d, XS) * XROWS, XROWS), XROWS)
-        out[...] = (keep_ref[rows, :] + got_ref[rows, :].astype(F32)).astype(out.dtype)
-
-
-def rs_x(pos, keep, got):
-    return pl.pallas_call(
-        rs_x_kernel,
-        in_specs=[SMEM, WHOLE, WHOLE],
-        out_specs=[WHOLE] * XS,
-        out_shape=[sds((XROWS, WIDE), F32)] + [sds((XROWS, WIDE), BF)] * (XS - 1),
-        compiler_params=params(),
-        name="rs_x",
-    )(pos, keep, got)
-
-
-def rs_z_kernel(pos_ref, own_ref, g1, g2, g3, *rest):
-    outs, total = rest[-ZS - 1 : -1], rest[-1]
-    z = pos_ref[1]
-    total[...] = (own_ref[...] + g1[...].astype(F32)) + (
-        g2[...].astype(F32) + g3[...].astype(F32)
-    )
-    for d, out in enumerate(outs):
-        owner = jnp.minimum(lax.rem(z + d, ZS), OWNERS - 1)
-        rows = pl.ds(pl.multiple_of(owner * ZROWS, ZROWS), ZROWS)
-        out[...] = total[rows, :].astype(out.dtype)
-
-
-def rs_z(pos, own, got, deps):
-    return pl.pallas_call(
-        rs_z_kernel,
-        in_specs=[SMEM] + [WHOLE] * XS + [DEP] * len(deps),
-        out_specs=[WHOLE] * ZS,
-        out_shape=[sds((ZROWS, WIDE), F32)] + [sds((ZROWS, WIDE), BF)] * (ZS - 1),
-        scratch_shapes=[pltpu.VMEM((XROWS, WIDE), F32)],
-        compiler_params=params(),
-        name="rs_z",
-    )(pos, own, *got, *deps)
-
-
-def renorm_kernel(old_ref, own_ref, *rest):
-    got, out = rest[: ZS - 1], rest[-1]
-    update = own_ref[...]
-    for g in got:
-        update = update + g[...].astype(F32)
+def join_kernel(keep_ref, got_ref, out_ref):
+    out_ref[:DH, :] = (keep_ref[...] + got_ref[...].astype(F32)).astype(BF)
+    out_ref[DH:, :] = jnp.zeros((SLOTS * ZROWS - DH, WIDE), BF)
+
+
+def join(keep, got):
+    return pl.pallas_call(
+        join_kernel,
+        grid=(1,),
+        in_specs=[full((DH, WIDE)), full((DH, WIDE))],
+        out_specs=full((SLOTS * ZROWS, WIDE)),
+        out_shape=sds((SLOTS * ZROWS, WIDE), BF),
+        compiler_params=params(),
+        name="join",
+    )(keep, got)
+
+
+def renorm_kernel(old_ref, got_ref, *rest):
+    out = rest[-1]
+    update = got_ref[0].astype(F32)
+    for s in range(1, SLOTS):
+        update = update + got_ref[s].astype(F32)
     old = old_ref[...]
     fresh = old + update
     for cols in (slice(0, HID), slice(HID, WIDE)):
         w, f = old[:, cols], fresh[:, cols]
         w_sq = jnp.sum(w * w, axis=1, keepdims=True)
         f_sq = jnp.sum(f * f, axis=1, keepdims=True)
-        out[:, cols] = (f * (jnp.sqrt(w_sq) / jnp.sqrt(f_sq + 1e-6))).astype(BF)
-
-
-def renorm(old, own, got, deps):
+        new = (f * (jnp.sqrt(w_sq) / jnp.sqrt(f_sq + 1e-6))).astype(BF)
+        for s in range(SLOTS):
+            out[s, :, cols] = new
+
+
+def renorm(old, got, deps):
+    shape = (SLOTS, ZROWS, WIDE)
     return pl.pallas_call(
         renorm_kernel,
-        in_specs=[WHOLE] * (ZS + 1) + [DEP] * len(deps),
-        out_specs=WHOLE,
-        out_shape=sds((ZROWS, WIDE), BF),
+        grid=(1,),
+        in_specs=[full((ZROWS, WIDE)), full(shape)] + [DEP] * len(deps),
+        out_specs=full(shape),
+        out_shape=sds(shape, BF),
         compiler_params=params(),
         name="renorm",
-    )(old, own, *got, *deps)
-
-
-def ag_z_kernel(pos_ref, *rest):
-    blocks, out = rest[:ZS], rest[-1]
-    z = pos_ref[1]
-    for d, block in enumerate(blocks):
-        owner = lax.rem(z - d + ZS, ZS)
-
-        @pl.when(owner < OWNERS)
-        def _():
-            out[pl.ds(pl.multiple_of(owner * ZROWS, ZROWS), ZROWS), :] = block[...]
-
-
-def ag_z(pos, blocks, deps):
-    return pl.pallas_call(
-        ag_z_kernel,
-        in_specs=[SMEM] + [WHOLE] * ZS + [DEP] * len(deps),
-        out_specs=WHOLE,
-        out_shape=sds((XROWS, WIDE), BF),
-        compiler_params=params(),
-        name="ag_z",
-    )(pos, *blocks, *deps)
-
-
-def ag_x_kernel(pos_ref, *rest):
-    blocks, out = rest[:XS], rest[-1]
-    x = pos_ref[0]
-    for d, block in enumerate(blocks):
-        owner = lax.rem(x - d + XS, XS)
-        out[pl.ds(pl.multiple_of(owner * XROWS, XROWS), XROWS), :] = block[...]
-
-
-def ag_x(pos, blocks, deps):
-    return pl.pallas_call(
-        ag_x_kernel,
-        in_specs=[SMEM] + [WHOLE] * XS + [DEP] * len(deps),
-        out_specs=WHOLE,
-        out_shape=sds((DH, WIDE), BF),
-        compiler_params=params(),
-        name="ag_x",
-    )(pos, *blocks, *deps)
+    )(old, got, *deps)
+
+
+def hold_kernel(value_ref, dep_ref, out_ref):
+    pass
+
+
+def hold(value, dep):
+    return pl.pallas_call(
+        hold_kernel,
+        in_specs=[DEP, DEP],
+        out_specs=DEP,
+        out_shape=sds(value.shape, value.dtype),
+        input_output_aliases={0: 0},
+        compiler_params=params(),
+        name="hold",
+    )(value, dep)
 
 
 def project_kernel(t_ref, w_ref, dep_ref, q_ref):
@@ -278,7 +221,8 @@
     )(tokens, qkv_weight, dep)
 
 
-def attend_kernel(piece, bounds_ref, rows_ref, q_ref, before, mine, after, dep_ref, out_ref, s_ref):
+def attend_kernel(start, bounds_ref, rows_ref, q_ref, before, mine, after, dep_ref, out_ref, s_ref):
+    piece = pl.program_id(0) + start
     low, high = bounds_ref[2 * piece], bounds_ref[2 * piece + 1]
     first = lax.div(low, KB)
     last = lax.div(high + KB - 1, KB)
@@ -322,28 +266,29 @@
     segments(gather, 0)
 
 
-def attend(piece, bounds, row_bounds, query, before, mine, after, dep):
-    return pl.pallas_call(
-        functools.partial(attend_kernel, piece),
-        grid=(1,),
+def attend(start, count, bounds, row_bounds, query, before, mine, after, dep):
+    whole = full((TOK, 2 * DH))
+    return pl.pallas_call(
+        functools.partial(attend_kernel, start),
+        grid=(count,),
         in_specs=[
             SMEM,
-            pl.BlockSpec((QB, 2), lambda i: (piece, 0)),
-            pl.BlockSpec((QB, DH), lambda i: (piece, 0)),
-            WHOLE,
-            WHOLE,
-            WHOLE,
+            pl.BlockSpec((QB, 2), lambda i: (i + start, 0)),
+            pl.BlockSpec((QB, DH), lambda i: (i + start, 0)),
+            whole,
+            whole,
+            whole,
             DEP,
         ],
-        out_specs=pl.BlockSpec((QB, DH), lambda i: (0, 0)),
-        out_shape=sds((QB, DH), F32),
+        out_specs=pl.BlockSpec((QB, DH), lambda i: (i, 0)),
+        out_shape=sds((count * QB, DH), F32),
         scratch_shapes=[pltpu.VMEM((3 * TOK // KB, QB, KB), F32)],
         compiler_params=params(),
-        name=f"attend_{piece}",
+        name=f"attend_{start}",
     )(bounds, row_bounds, query, before, mine, after, dep)
 
 
-def apply_kernel(pos_ref, q_ref, own_ref, other_ref, att_ref, gain_ref, out_ref, *rest):
+def apply_kernel(pos_ref, q_ref, own_ref, other_ref, att_ref, gain_ref, dep_ref, out_ref):
     core = pos_ref[2]
     q = q_ref[...]
     mine = mm(q, own_ref[:, :HID])
@@ -361,23 +306,25 @@
     out_ref[...] = (att_ref[...] + normed).astype(BF)
 
 
-def apply(piece, pos, query, own, other, attended, gain):
+def apply(start, count, pos, query, own, other, attended, att_start, gain, dep):
+    weight = full((DH, WIDE))
     return pl.pallas_call(
         apply_kernel,
-        grid=(1,),
+        grid=(count,),
         in_specs=[
             SMEM,
-            pl.BlockSpec((QB, DH), lambda i: (piece, 0)),
-            WHOLE,
-            WHOLE,
-            WHOLE,
-            WHOLE,
-        ],
-        out_specs=pl.BlockSpec((QB, DH), lambda i: (0, 0)),
-        out_shape=sds((QB, DH), BF),
-        compiler_params=params(),
-        name=f"apply_{piece}",
-    )(pos, query, own, other, attended, gain)
+            pl.BlockSpec((QB, DH), lambda i: (i + start, 0)),
+            weight,
+            weight,
+            pl.BlockSpec((QB, DH), lambda i: (i + att_start, 0)),
+            full((1, DH)),
+            DEP,
+        ],
+        out_specs=pl.BlockSpec((QB, DH), lambda i: (i, 0)),
+        out_shape=sds((count * QB, DH), BF),
+        compiler_params=params(),
+        name=f"apply_{start}",
+    )(pos, query, own, other, attended, gain, dep)
 
 
 def output_kernel(*refs):
@@ -388,17 +335,19 @@
     out[...] = total.astype(BF)
 
 
-def output(piece, parts, weights, buffer):
+def output(start, count, parts, weights, buffer):
     extra = [] if buffer is None else [buffer]
     return pl.pallas_call(
         output_kernel,
-        grid=(1,),
-        in_specs=[WHOLE] * (2 * HS) + [DEP] * len(extra),
-        out_specs=pl.BlockSpec((QB, DH), lambda i: (piece, 0)),
+        grid=(count,),
+        in_specs=[pl.BlockSpec((QB, DH), lambda i: (i, 0))] * HS
+        + [full((DH, DH))] * HS
+        + [DEP] * len(extra),
+        out_specs=pl.BlockSpec((QB, DH), lambda i: (i + start, 0)),
         out_shape=sds((TOK, DH), BF),
         input_output_aliases={2 * HS: 0} if extra else {},
         compiler_params=params(),
-        name=f"output_{piece}",
+        name=f"output_{start}",
     )(*parts, *weights, *extra)
 
 
@@ -446,7 +395,7 @@
         cols = lax.dynamic_slice_in_dim(out_weight, (head + d) % HS * DH, DH, 1)
         weights.append(lax.ppermute(cols, "head", shift_h(d)) if d else cols)
 
-    row = jnp.minimum(x * XROWS + z * ZROWS, DH - ZROWS)
+    row = jnp.minimum((mine // CS) * ZROWS, DH - ZROWS)
     pick = lambda w, at: lax.dynamic_slice_in_dim(w[0], at, ZROWS, 0)
     old = jnp.concatenate(
         [
@@ -456,40 +405,31 @@
         axis=1,
     ).astype(F32)
 
-    own, *gives = rs_x(pos, keep, got)
-    got = [send(g, shift_x(d + 1)) for d, g in enumerate(gives)]
-    query = project(tokens, qkv_weight, own)
-    att = functools.partial(
-        lambda p, dep: attend(p, bounds, row_bounds, query, before, kv, after, dep)
-    )
-
-    own, *gives = rs_z(pos, own, got, [query])
-    got = [send(g, shift_z(d + 1, to_owner=True)) for d, g in enumerate(gives)]
-    att0 = att(0, own)
-
-    fresh = renorm(old, own, got, [att0])
-    got = [send(fresh, shift_z(d, from_owner=True)) for d in range(1, ZS)]
-    att1 = att(1, fresh)
-
-    block = ag_z(pos, [fresh, *got], [att1])
-    got = [send(block, shift_x(d)) for d in range(1, XS)]
-    att2 = att(2, block)
-    att3 = att(3, block)
-
-    half = ag_x(pos, [block, *got], [att2, att3])
+    def exchange(blocks):
+        return lax.all_to_all(blocks, "tok", 0, 0, axis_index_groups=CHIPS)
+
+    total = join(keep, got)
+    got = exchange(total.reshape(SLOTS, ZROWS, WIDE))
+    query = project(tokens, qkv_weight, total)
+    att_low = attend(0, 2, bounds, row_bounds, query, before, kv, after, query)
+    fresh = renorm(old, got, [att_low, *weights])
+    got = exchange(fresh)
+    att_high = attend(2, 2, bounds, row_bounds, query, before, kv, after, fresh)
+    half = hold(got, att_high).reshape(SLOTS * ZROWS, WIDE)
     other = send(half, SWAP_C)
 
     gain = fast_gain[None, :]
     result = None
-    mixed = [
-        apply(p, pos, query, half, other, a, gain)
-        for p, a in enumerate((att0, att1, att2, att3))
-    ]
-    for p, part in enumerate(mixed):
+    mixed = []
+    dep = att_high
+    for start, count, attended, at in ((0, 1, att_low, 0), (1, 1, att_low, 1), (2, 2, att_high, 0)):
+        dep = apply(start, count, pos, query, half, other, attended, at, gain, dep)
+        mixed.append((start, count, dep))
+    for start, count, part in mixed:
         parts = [part] + [
             lax.ppermute(part, "head", shift_h(d)) for d in range(1, HS)
         ]
-        result = output(p, parts, weights, result)
+        result = output(start, count, parts, weights, result)
     return result
 
 

time: 212 us -> 197 us (0.929)
  waiting for transfers between devices: 23.9 us -> 63.8 us
  starting transfers between devices: 83.9 us -> 51.4 us
  Pallas kernels: 84.2 us -> 64.8 us
  local copies, waits for them, and re-layouts: 14.8 us -> 12.2 us
    ppermute x24 -> x4, starting transfers between devices: 67.9 us -> 13.8 us  [body(): send = lambda value, pairs: lax.ppermute(value, 'tok', pairs)]
    all_to_all x0 -> x2, starting transfers between devices: none -> 19.9 us  [exchange(): return lax.all_to_all(blocks, 'tok', 0, 0, axis_index_groups=CHIPS)]
    pallas_call x17 -> x11, Pallas kernels: 63.8 us -> 44.4 us  [the longest x2 18.1 us: attend(): pl.pallas_call(functools.partial(attend_kernel, start), grid=(count,), in...]
    all_to_all x0 -> x2, waiting for transfers between devices: none -> 18.3 us  [exchange(): return lax.all_to_all(blocks, 'tok', 0, 0, axis_index_groups=CHIPS)]
    ppermute x24 -> x4, waiting for transfers between devices: 13.9 us -> 26.9 us  [body(): send = lambda value, pairs: lax.ppermute(value, 'tok', pairs)]
    ppermute x12 -> x9, waiting for transfers between devices: 9.99 us -> 18.6 us  [body(): lax.ppermute(part, 'head', shift_h(d))]
    unnamed x89 -> x41, local copies, waits for them, and re-layouts: 10.6 us -> 7.85 us
    ppermute x12 -> x9, starting transfers between devices: 11.1 us -> 12.8 us  [body(): lax.ppermute(part, 'head', shift_h(d))]
  transfers between devices with their start and end apart: 39 -> 18, of which waited for: 9 -> 7; matrix products, arithmetic and copies ran while one was open for 3% -> 3% of each run, Pallas kernels for 29% -> 19%
where the time goes in v2:
time: 197 us; the launch traced here: 195 us
  Pallas kernels  64.8 us (33%)
  waiting for transfers between devices  63.8 us (32%)
  starting transfers between devices  51.4 us (26%)
  local copies, waits for them, and re-layouts  12.2 us (6%)
  other arithmetic  2.73 us (1%)
    ppermute x4, waiting for transfers between devices, body(): send = lambda value, pairs: lax.ppermute(value, 'tok', pairs)  26.9 us
    all_to_all x2, starting transfers between devices, exchange(): return lax.all_to_all(blocks, 'tok', 0, 0, axis_index_groups=CHIPS)  19.9 us
    ppermute x9, waiting for transfers between devices, body(): lax.ppermute(part, 'head', shift_h(d))  18.6 us
    all_to_all x2, waiting for transfers between devices, exchange(): return lax.all_to_all(blocks, 'tok', 0, 0, axis_index_groups=CHIPS)  18.3 us
    pallas_call x2, Pallas kernels, attend(): pl.pallas_call(functools.partial(attend_kernel, start), grid=(count,), in...  18.1 us
    pallas_call x1, Pallas kernels, front(): pl.pallas_call(front_kernel, grid=(rows // block,), in_specs=[SMEM, pl.Bl...  15.2 us
    ppermute x4, starting transfers between devices, body(): send = lambda value, pairs: lax.ppermute(value, 'tok', pairs)  13.8 us
    ppermute x9, starting transfers between devices, body(): lax.ppermute(part, 'head', shift_h(d))  12.8 us
  transfers between devices with their start and end apart: 18, of which 7 were waited for; matrix products, arithmetic and copies ran while one was open for 3% of the time, Pallas kernels for 19%

profile of v2, /device:TPU:1, one launch (start us, length us, event | category | flops | bytes accessed | tf_op | source)
XLA Modules:
  0.0 195.2 jit_solution(16651480160827542152)
XLA Ops:
  0.0 1.7 copy.22.wr_ref
  2.3 15.2 %front.1 = (bf16[1024,768]{1,0:T(8,128)(2,1)}, bf16[384,1152]{1,0:T(8,128)(2,1)}, f32[384,1152]{1,0:T(8,128)}) custom-call(s32[3]{0:T(128)} %pad_add_fusion.2.pos_ref, bf16[1024,1536]{1,0:T(8,128)(2,1)} %t_ref.3, bf16[1536,1152]{1,0:T(8,128)(2,1)} %w_ref.1, bf16[1536,1152]{1,0:T(8,128)(2,1)} %w_ref.1, bf16[1536,3]{1,0:T(8,128)(2,1)} %copy.22.wr_ref, ...), custom_call_target="tpu_custom_call" | custom-call | tf_op jit(solution)/shard_map/front/pallas_call | solution.py:115
  17.5 3.2 %collective-permute-start = (bf16[384,1152]{1,0:T(8,128)(2,1)}, bf16[384,1152]{1,0:T(8,128)(2,1)S(1)}, u32[]{:S(2)}, u32[]{:S(2)}) collective-permute-start(bf16[384,1152]{1,0:T(8,128)(2,1)} %get-tuple-element.9), channel_id=1, source_target_pairs={{0,4},{4,0},{8,12},{12,8},{16,20},{20,16},{24,28},{28,24},{32,36},... | collective-permute-start | bytes 2654216 | tf_op jit(solution)/shard_map/ppermute | solution.py:369
  20.7 2.3 %collective-permute-done.got_ref = bf16[384,1152]{1,0:T(8,128)(2,1)S(1)} collective-permute-done((bf16[384,1152]{1,0:T(8,128)(2,1)}, bf16[384,1152]{1,0:T(8,128)(2,1)S(1)}, u32[]{:S(2)}, u32[]{:S(2)}) %collective-permute-start) | collective-permute-done | bytes 884768 | tf_op jit(solution)/shard_map/ppermute | solution.py:369
  23.9 3.0 %join.1.dep_ref = bf16[512,1152]{1,0:T(8,128)(2,1)} custom-call(f32[384,1152]{1,0:T(8,128)} %get-tuple-element.8.keep_ref, bf16[384,1152]{1,0:T(8,128)(2,1)} %copy-done.8), custom_call_target="tpu_custom_call" | custom-call | tf_op jit(solution)/shard_map/join/pallas_call | solution.py:146
  26.9 9.5 %all-to-all-start = ((bf16[32,16,1152]{2,1,0:T(8,128)(2,1)}), bf16[32,16,1152]{2,1,0:T(8,128)(2,1)}, u32[]{:S(2)}, u32[]{:S(2)}) async-start(bf16[32,16,1152]{2,1,0:T(8,128)(2,1)} %bitcast.15), calls=%async_computation | async-start | bytes 2359296 | tf_op jit(solution)/shard_map/all_to_all | solution.py:409
  36.5 3.9 %collective-permute-start.1 = (bf16[1024,768]{1,0:T(8,128)(2,1)S(1)}, bf16[1024,768]{1,0:T(8,128)(2,1)}, u32[]{:S(2)}, u32[]{:S(2)}) collective-permute-start(bf16[1024,768]{1,0:T(8,128)(2,1)S(1)} %copy-done.2), channel_id=1, source_target_pairs={{0,4},{4,8},{8,12},{12,16},{16,20},{20,24},{24,28},{28,32},{32,36}... | collective-permute-start | bytes 4718600 | tf_op jit(solution)/shard_map/ppermute | solution.py:369
  40.4 1.9 collective-permute-start.2
  43.4 1.3 collective-permute-start.3
  44.7 2.6 %collective-permute-start.4 = (bf16[384,384]{1,0:T(8,128)(2,1)S(1)}, bf16[384,384]{1,0:T(8,128)(2,1)S(1)}, u32[]{:S(2)}, u32[]{:S(2)}) collective-permute-start(bf16[384,384]{1,0:T(8,128)(2,1)S(1)} %get-tuple-element.16), channel_id=1, source_target_pairs={{0,2},{1,3},{2,0},{3,1},{4,6},{5,7},{6,4},{7,5},{8,10},{9,11},{10,... | collective-permute-start | bytes 884744 | tf_op jit(solution)/shard_map/ppermute | solution.py:396
  53.2 5.2 %project.1.q_ref.dep_ref = bf16[1024,384]{1,0:T(8,128)(2,1)} custom-call(bf16[1024,1536]{1,0:T(8,128)(2,1)} %t_ref.3, bf16[1536,1152]{1,0:T(8,128)(2,1)} %w_ref.1, bf16[512,1152]{1,0:T(8,128)(2,1)} %join.1.dep_ref), custom_call_target="tpu_custom_call" | custom-call | tf_op jit(solution)/shard_map/project/pallas_call | solution.py:209
  58.4 20.6 %collective-permute-done.1.before = bf16[1024,768]{1,0:T(8,128)(2,1)} collective-permute-done((bf16[1024,768]{1,0:T(8,128)(2,1)S(1)}, bf16[1024,768]{1,0:T(8,128)(2,1)}, u32[]{:S(2)}, u32[]{:S(2)}) %collective-permute-start.1) | collective-permute-done | bytes 1572896 | tf_op jit(solution)/shard_map/ppermute | solution.py:369
  79.0 1.9 collective-permute-done.2.after
  80.9 9.1 %attend_0.1.rest_0_.att_ref = f32[512,384]{1,0:T(8,128)} custom-call(s32[8]{0:T(128)} %reshape.39.bounds_ref, s32[1024,2]{1,0:T(8,128)} %copy.24.rows_ref, bf16[1024,384]{1,0:T(8,128)(2,1)} %project.1.q_ref.dep_ref, bf16[1024,768]{1,0:T(8,128)(2,1)} %collective-permute-done.1.before, bf16[1024,768]{1,0:T(8,128)(2,1)} %get-tuple-element.10.mine, ...), custom_call_target="tpu_custom_call" | custom-call | tf_op jit(solution)/shard_map/attend_0/pallas_call | solution.py:271
  90.9 2.7 %renorm.1.dep_ref = bf16[32,16,1152]{2,1,0:T(8,128)(2,1)} custom-call(f32[16,1152]{1,0:T(8,128)} %maximum_convert_fusion.old_ref, bf16[32,16,1152]{2,1,0:T(8,128)(2,1)} %all-to-all-done.got_ref, f32[512,384]{1,0:T(8,128)} %attend_0.1.rest_0_.att_ref, bf16[384,384]{1,0:T(8,128)(2,1)} %get-tuple-element.15.rest_1_.refs_4_, bf16[384,384]{1,0:T(8,128)(2,1)} %copy-done.3, ...), custom_call_target="tpu_custom_call" | custom-call | tf_op jit(solution)/shard_map/renorm/pallas_call | solution.py:175
  93.6 10.3 %all-to-all-start.1 = ((bf16[32,16,1152]{2,1,0:T(8,128)(2,1)}), bf16[32,16,1152]{2,1,0:T(8,128)(2,1)S(1)}, u32[]{:S(2)}, u32[]{:S(2)}) async-start(bf16[32,16,1152]{2,1,0:T(8,128)(2,1)} %renorm.1.dep_ref), calls=%async_computation.1 | async-start | bytes 2359296 | tf_op jit(solution)/shard_map/all_to_all | solution.py:409
  104.0 9.1 %attend_2.1.dep_ref.att_ref = f32[512,384]{1,0:T(8,128)} custom-call(s32[8]{0:T(128)} %reshape.39.bounds_ref, s32[1024,2]{1,0:T(8,128)} %copy.24.rows_ref, bf16[1024,384]{1,0:T(8,128)(2,1)} %project.1.q_ref.dep_ref, bf16[1024,768]{1,0:T(8,128)(2,1)} %collective-permute-done.1.before, bf16[1024,768]{1,0:T(8,128)(2,1)} %get-tuple-element.10.mine, ...), custom_call_target="tpu_custom_call" | custom-call | tf_op jit(solution)/shard_map/attend_2/pallas_call | solution.py:271
  113.0 18.3 %all-to-all-done.1.value_ref = bf16[32,16,1152]{2,1,0:T(8,128)(2,1)S(1)} async-done(((bf16[32,16,1152]{2,1,0:T(8,128)(2,1)}), bf16[32,16,1152]{2,1,0:T(8,128)(2,1)S(1)}, u32[]{:S(2)}, u32[]{:S(2)}) %all-to-all-start.1) | async-done | bytes 1179680 | tf_op jit(solution)/shard_map/all_to_all | solution.py:409
  132.3 4.8 %collective-permute-start.6 = (bf16[512,1152]{1,0:T(8,128)(2,1)}, bf16[512,1152]{1,0:T(8,128)(2,1)S(1)}, u32[]{:S(2)}, u32[]{:S(2)}) collective-permute-start(bf16[512,1152]{1,0:T(8,128)(2,1)} %bitcast.11), channel_id=1, source_target_pairs={{0,4},{4,0},{8,12},{12,8},{16,20},{20,16},{24,28},{28,24},{32,36},... | collective-permute-start | bytes 3538952 | tf_op jit(solution)/shard_map/ppermute | solution.py:369
  137.7 2.1 %collective-permute-done.6.other_ref = bf16[512,1152]{1,0:T(8,128)(2,1)S(1)} collective-permute-done((bf16[512,1152]{1,0:T(8,128)(2,1)}, bf16[512,1152]{1,0:T(8,128)(2,1)S(1)}, u32[]{:S(2)}, u32[]{:S(2)}) %collective-permute-start.6) | collective-permute-done | bytes 1179680 | tf_op jit(solution)/shard_map/ppermute | solution.py:369
  140.8 3.4 %apply_0.1.dep_ref.refs_0_ = bf16[256,384]{1,0:T(8,128)(2,1)} custom-call(s32[3]{0:T(128)} %pad_add_fusion.2.pos_ref, bf16[1024,384]{1,0:T(8,128)(2,1)} %project.1.q_ref.dep_ref, bf16[512,1152]{1,0:T(8,128)(2,1)} %bitcast.12, bf16[512,1152]{1,0:T(8,128)(2,1)} %copy-done.1, f32[512,384]{1,0:T(8,128)} %attend_0.1.rest_0_.att_ref, ...), custom_call_target="tpu_custom_call" | custom-call | tf_op jit(solution)/shard_map/apply_0/pallas_call | solution.py:311
  145.5 2.6 %collective-permute-start.14 = (bf16[256,384]{1,0:T(8,128)(2,1)}, bf16[256,384]{1,0:T(8,128)(2,1)S(1)}, u32[]{:S(2)}, u32[]{:S(2)}) collective-permute-start(bf16[256,384]{1,0:T(8,128)(2,1)} %apply_0.1.dep_ref.refs_0_), channel_id=1, source_target_pairs={{0,2},{1,3},{2,0},{3,1},{4,6},{5,7},{6,4},{7,5},{8,10},{9,11},{10,... | collective-permute-start | bytes 589832 | tf_op jit(solution)/shard_map/ppermute | solution.py:430
  149.2 3.4 %apply_1.1.dep_ref.refs_0_ = bf16[256,384]{1,0:T(8,128)(2,1)} custom-call(s32[3]{0:T(128)} %pad_add_fusion.2.pos_ref, bf16[1024,384]{1,0:T(8,128)(2,1)} %project.1.q_ref.dep_ref, bf16[512,1152]{1,0:T(8,128)(2,1)} %bitcast.13, bf16[512,1152]{1,0:T(8,128)(2,1)} %copy-done.1, f32[512,384]{1,0:T(8,128)} %attend_0.1.rest_0_.att_ref, ...), custom_call_target="tpu_custom_call" | custom-call | tf_op jit(solution)/shard_map/apply_1/pallas_call | solution.py:311
  153.0 4.5 %apply_2.1.refs_0_ = bf16[512,384]{1,0:T(8,128)(2,1)} custom-call(s32[3]{0:T(128)} %pad_add_fusion.2.pos_ref, bf16[1024,384]{1,0:T(8,128)(2,1)} %project.1.q_ref.dep_ref, bf16[512,1152]{1,0:T(8,128)(2,1)} %bitcast.14, bf16[512,1152]{1,0:T(8,128)(2,1)} %copy-done.1, f32[512,384]{1,0:T(8,128)} %attend_2.1.dep_ref.att_ref, f32[1,384]{1,0:T(1,128)} %broadcast_in_dim.46.gain_ref, ...), custom_call_target="tpu_custom_call" | custom-call | tf_op jit(solution)/shard_map/apply_2/pallas_call | solution.py:311
  157.5 3.4 %collective-permute-start.8 = (bf16[512,384]{1,0:T(8,128)(2,1)}, bf16[512,384]{1,0:T(8,128)(2,1)S(1)}, u32[]{:S(2)}, u32[]{:S(2)}) collective-permute-start(bf16[512,384]{1,0:T(8,128)(2,1)} %apply_2.1.refs_0_), channel_id=1, source_target_pairs={{0,2},{1,3},{2,0},{3,1},{4,6},{5,7},{6,4},{7,5},{8,10},{9,11},{10,... | collective-permute-start | bytes 1179656 | tf_op jit(solution)/shard_map/ppermute | solution.py:430
  161.0 1.6 collective-permute-start.11
  162.7 2.3 %collective-permute-start.12 = (bf16[256,384]{1,0:T(8,128)(2,1)S(1)}, bf16[256,384]{1,0:T(8,128)(2,1)S(1)}, u32[]{:S(2)}, u32[]{:S(2)}) collective-permute-start(bf16[256,384]{1,0:T(8,128)(2,1)S(1)} %copy-done.6), channel_id=1, source_target_pairs={{0,3},{1,0},{2,1},{3,2},{4,7},{5,4},{6,5},{7,6},{8,11},{9,8},{10,9... | collective-permute-start | bytes 589832 | tf_op jit(solution)/shard_map/ppermute | solution.py:430
  164.9 2.9 %output_0.1.refs_8_ = bf16[1024,384]{1,0:T(8,128)(2,1)} custom-call(bf16[256,384]{1,0:T(8,128)(2,1)} %apply_0.1.dep_ref.refs_0_, bf16[256,384]{1,0:T(8,128)(2,1)} %copy-done.15, bf16[256,384]{1,0:T(8,128)(2,1)} %copy-done.16, bf16[256,384]{1,0:T(8,128)(2,1)} %copy-done.17, bf16[384,384]{1,0:T(8,128)(2,1)} %get-tuple-element.15.rest_1_.refs_4_, ...), custom_call_target="tpu_custom_call" | custom-call | tf_op jit(solution)/shard_map/output_0/pallas_call | solution.py:340
  167.8 13.7 %collective-permute-done.11.refs_2_ = bf16[256,384]{1,0:T(8,128)(2,1)S(1)} collective-permute-done((bf16[256,384]{1,0:T(8,128)(2,1)S(1)}, bf16[256,384]{1,0:T(8,128)(2,1)S(1)}, u32[]{:S(2)}, u32[]{:S(2)}) %collective-permute-start.11) | collective-permute-done | bytes 196640 | tf_op jit(solution)/shard_map/ppermute | solution.py:430
  181.5 4.9 %collective-permute-done.12.refs_3_ = bf16[256,384]{1,0:T(8,128)(2,1)S(1)} collective-permute-done((bf16[256,384]{1,0:T(8,128)(2,1)S(1)}, bf16[256,384]{1,0:T(8,128)(2,1)S(1)}, u32[]{:S(2)}, u32[]{:S(2)}) %collective-permute-start.12) | collective-permute-done | bytes 196640 | tf_op jit(solution)/shard_map/ppermute | solution.py:430
  187.0 2.9 %output_1.1.refs_8_ = bf16[1024,384]{1,0:T(8,128)(2,1)} custom-call(bf16[256,384]{1,0:T(8,128)(2,1)} %apply_1.1.dep_ref.refs_0_, bf16[256,384]{1,0:T(8,128)(2,1)} %copy-done.12, bf16[256,384]{1,0:T(8,128)(2,1)} %copy-done.13, bf16[256,384]{1,0:T(8,128)(2,1)} %copy-done.14, ...), custom_call_target="tpu_custom_call", output_to_operand_aliasing={{}: (8, {})} | custom-call | tf_op jit(solution)/shard_map/output_1/pallas_call | solution.py:340
  191.6 3.6 %output_2.1 = bf16[1024,384]{1,0:T(8,128)(2,1)} custom-call(bf16[512,384]{1,0:T(8,128)(2,1)} %apply_2.1.refs_0_, bf16[512,384]{1,0:T(8,128)(2,1)} %copy-done.9, bf16[512,384]{1,0:T(8,128)(2,1)} %copy-done.10, bf16[512,384]{1,0:T(8,128)(2,1)} %copy-done.11, bf16[384,384]{1,0:T(8,128)(2,1)} %get-tuple-element.15.rest_1_.refs_4_, ...), custom_call_target="tpu_custom_call", output_to_operand_aliasing={{}: (8, {})} | custom-call | tf_op jit(solution)/shard_map/output_2/pallas_call | solution.py:340
  (75 shorter events, 17.1 us)
Async XLA Ops:
  17.5 5.5 %collective-permute-start = (bf16[384,1152]{1,0:T(8,128)(2,1)}, bf16[384,1152]{1,0:T(8,128)(2,1)S(1)}, u32[]{:S(2)}, u32[]{:S(2)}) collective-permute-start(bf16[384,1152]{1,0:T(8,128)(2,1)} %get-tuple-element.9), channel_id=1, source_target_pairs={{0,4},{4,0},{8,12},{12,8},{16,20},{20,16},{24,28},{28,24},{32,36},... | collective-permute-start | bytes 2654216 | tf_op jit(solution)/shard_map/ppermute | solution.py:369
  23.0 0.9 copy-start.8
  23.9 18.5 %copy-start.7 = (bf16[384,1536]{1,0:T(8,128)(2,1)S(1)}, bf16[384,1536]{1,0:T(8,128)(2,1)}, u32[]{:S(2)}) copy-start(bf16[384,1536]{1,0:T(8,128)(2,1)} %param.16) | copy-start | bytes 3538948
  26.9 9.6 %copy-start.2 = (bf16[1024,768]{1,0:T(8,128)(2,1)S(1)}, bf16[1024,768]{1,0:T(8,128)(2,1)}, u32[]{:S(2)}) copy-start(bf16[1024,768]{1,0:T(8,128)(2,1)} %get-tuple-element.10.mine) | copy-start | bytes 4718596
  26.9 63.1 %all-to-all-start = ((bf16[32,16,1152]{2,1,0:T(8,128)(2,1)}), bf16[32,16,1152]{2,1,0:T(8,128)(2,1)}, u32[]{:S(2)}, u32[]{:S(2)}) async-start(bf16[32,16,1152]{2,1,0:T(8,128)(2,1)} %bitcast.15), calls=%async_computation | async-start | bytes 2359296 | tf_op jit(solution)/shard_map/all_to_all | solution.py:409
  36.5 42.5 %collective-permute-start.1 = (bf16[1024,768]{1,0:T(8,128)(2,1)S(1)}, bf16[1024,768]{1,0:T(8,128)(2,1)}, u32[]{:S(2)}, u32[]{:S(2)}) collective-permute-start(bf16[1024,768]{1,0:T(8,128)(2,1)S(1)} %copy-done.2), channel_id=1, source_target_pairs={{0,4},{4,8},{8,12},{12,16},{16,20},{20,24},{24,28},{28,32},{32,36}... | collective-permute-start | bytes 4718600 | tf_op jit(solution)/shard_map/ppermute | solution.py:369
  40.4 40.5 %collective-permute-start.2 = (bf16[1024,768]{1,0:T(8,128)(2,1)S(1)}, bf16[1024,768]{1,0:T(8,128)(2,1)}, u32[]{:S(2)}, u32[]{:S(2)}) collective-permute-start(bf16[1024,768]{1,0:T(8,128)(2,1)S(1)} %copy-done.2), channel_id=1, source_target_pairs={{4,0},{8,4},{12,8},{16,12},{20,16},{24,20},{28,24},{32,28},{36,32}... | collective-permute-start | bytes 4718600 | tf_op jit(solution)/shard_map/ppermute | solution.py:369
  42.4 6.0 %copy-start.19 = (s32[128]{0:T(128)S(1)}, s32[128]{0:T(128)}, u32[]{:S(2)}) copy-start(s32[128]{0:T(128)} %param.17) | copy-start | bytes 1540
  43.4 46.6 %collective-permute-start.3 = (bf16[384,384]{1,0:T(8,128)(2,1)}, bf16[384,384]{1,0:T(8,128)(2,1)S(1)}, u32[]{:S(2)}, u32[]{:S(2)}) collective-permute-start(bf16[384,384]{1,0:T(8,128)(2,1)} %get-tuple-element.14), channel_id=1, source_target_pairs={{0,1},{1,2},{2,3},{3,0},{4,5},{5,6},{6,7},{7,4},{8,9},{9,10},{10,1... | collective-permute-start | bytes 884744 | tf_op jit(solution)/shard_map/ppermute | solution.py:396
  44.7 45.3 %collective-permute-start.4 = (bf16[384,384]{1,0:T(8,128)(2,1)S(1)}, bf16[384,384]{1,0:T(8,128)(2,1)S(1)}, u32[]{:S(2)}, u32[]{:S(2)}) collective-permute-start(bf16[384,384]{1,0:T(8,128)(2,1)S(1)} %get-tuple-element.16), channel_id=1, source_target_pairs={{0,2},{1,3},{2,0},{3,1},{4,6},{5,7},{6,4},{7,5},{8,10},{9,11},{10,... | collective-permute-start | bytes 884744 | tf_op jit(solution)/shard_map/ppermute | solution.py:396
  47.3 42.7 %collective-permute-start.5 = (bf16[384,384]{1,0:T(8,128)(2,1)S(1)}, bf16[384,384]{1,0:T(8,128)(2,1)S(1)}, u32[]{:S(2)}, u32[]{:S(2)}) collective-permute-start(bf16[384,384]{1,0:T(8,128)(2,1)S(1)} %get-tuple-element.13), channel_id=1, source_target_pairs={{0,3},{1,0},{2,1},{3,2},{4,7},{5,4},{6,5},{7,6},{8,11},{9,8},{10,9... | collective-permute-start | bytes 884744 | tf_op jit(solution)/shard_map/ppermute | solution.py:396
  93.6 37.7 %all-to-all-start.1 = ((bf16[32,16,1152]{2,1,0:T(8,128)(2,1)}), bf16[32,16,1152]{2,1,0:T(8,128)(2,1)S(1)}, u32[]{:S(2)}, u32[]{:S(2)}) async-start(bf16[32,16,1152]{2,1,0:T(8,128)(2,1)} %renorm.1.dep_ref), calls=%async_computation.1 | async-start | bytes 2359296 | tf_op jit(solution)/shard_map/all_to_all | solution.py:409
  113.0 24.1 %copy-start.18 = (f32[384]{0:T(512)S(1)}, f32[384]{0:T(512)}, u32[]{:S(2)}) copy-start(f32[384]{0:T(512)} %param.15) | copy-start | bytes 4612
  131.3 1.0 copy-start
  132.3 7.5 %collective-permute-start.6 = (bf16[512,1152]{1,0:T(8,128)(2,1)}, bf16[512,1152]{1,0:T(8,128)(2,1)S(1)}, u32[]{:S(2)}, u32[]{:S(2)}) collective-permute-start(bf16[512,1152]{1,0:T(8,128)(2,1)} %bitcast.11), channel_id=1, source_target_pairs={{0,4},{4,0},{8,12},{12,8},{16,20},{20,16},{24,28},{28,24},{32,36},... | collective-permute-start | bytes 3538952 | tf_op jit(solution)/shard_map/ppermute | solution.py:369
  139.8 1.0 copy-start.1
  144.2 13.3 %collective-permute-start.13 = (bf16[256,384]{1,0:T(8,128)(2,1)}, bf16[256,384]{1,0:T(8,128)(2,1)S(1)}, u32[]{:S(2)}, u32[]{:S(2)}) collective-permute-start(bf16[256,384]{1,0:T(8,128)(2,1)} %apply_0.1.dep_ref.refs_0_), channel_id=1, source_target_pairs={{0,1},{1,2},{2,3},{3,0},{4,5},{5,6},{6,7},{7,4},{8,9},{9,10},{10,1... | collective-permute-start | bytes 589832 | tf_op jit(solution)/shard_map/ppermute | solution.py:430
  145.5 15.5 %collective-permute-start.14 = (bf16[256,384]{1,0:T(8,128)(2,1)}, bf16[256,384]{1,0:T(8,128)(2,1)S(1)}, u32[]{:S(2)}, u32[]{:S(2)}) collective-permute-start(bf16[256,384]{1,0:T(8,128)(2,1)} %apply_0.1.dep_ref.refs_0_), channel_id=1, source_target_pairs={{0,2},{1,3},{2,0},{3,1},{4,6},{5,7},{6,4},{7,5},{8,10},{9,11},{10,... | collective-permute-start | bytes 589832 | tf_op jit(solution)/shard_map/ppermute | solution.py:430
  148.1 12.9 %collective-permute-start.15 = (bf16[256,384]{1,0:T(8,128)(2,1)}, bf16[256,384]{1,0:T(8,128)(2,1)S(1)}, u32[]{:S(2)}, u32[]{:S(2)}) collective-permute-start(bf16[256,384]{1,0:T(8,128)(2,1)} %apply_0.1.dep_ref.refs_0_), channel_id=1, source_target_pairs={{0,3},{1,0},{2,1},{3,2},{4,7},{5,4},{6,5},{7,6},{8,11},{9,8},{10,9... | collective-permute-start | bytes 589832 | tf_op jit(solution)/shard_map/ppermute | solution.py:430
  152.6 8.4 %copy-start.6 = (bf16[256,384]{1,0:T(8,128)(2,1)S(1)}, bf16[256,384]{1,0:T(8,128)(2,1)}, u32[]{:S(2)}) copy-start(bf16[256,384]{1,0:T(8,128)(2,1)} %apply_1.1.dep_ref.refs_0_) | copy-start | bytes 589828
  152.6 10.1 %collective-permute-start.10 = (bf16[256,384]{1,0:T(8,128)(2,1)}, bf16[256,384]{1,0:T(8,128)(2,1)S(1)}, u32[]{:S(2)}, u32[]{:S(2)}) collective-permute-start(bf16[256,384]{1,0:T(8,128)(2,1)} %apply_1.1.dep_ref.refs_0_), channel_id=1, source_target_pairs={{0,1},{1,2},{2,3},{3,0},{4,5},{5,6},{6,7},{7,4},{8,9},{9,10},{10,1... | collective-permute-start | bytes 589832 | tf_op jit(solution)/shard_map/ppermute | solution.py:430
  157.5 32.4 %collective-permute-start.7 = (bf16[512,384]{1,0:T(8,128)(2,1)}, bf16[512,384]{1,0:T(8,128)(2,1)S(1)}, u32[]{:S(2)}, u32[]{:S(2)}) collective-permute-start(bf16[512,384]{1,0:T(8,128)(2,1)} %apply_2.1.refs_0_), channel_id=1, source_target_pairs={{0,1},{1,2},{2,3},{3,0},{4,5},{5,6},{6,7},{7,4},{8,9},{9,10},{10,1... | collective-permute-start | bytes 1179656 | tf_op jit(solution)/shard_map/ppermute | solution.py:430
  157.5 7.4 %copy-start.15 = (bf16[256,384]{1,0:T(8,128)(2,1)}, bf16[256,384]{1,0:T(8,128)(2,1)S(1)}, u32[]{:S(2)}) copy-start(bf16[256,384]{1,0:T(8,128)(2,1)S(1)} %collective-permute-done.13.refs_1_) | copy-start | bytes 589828
  157.5 32.4 %collective-permute-start.8 = (bf16[512,384]{1,0:T(8,128)(2,1)}, bf16[512,384]{1,0:T(8,128)(2,1)S(1)}, u32[]{:S(2)}, u32[]{:S(2)}) collective-permute-start(bf16[512,384]{1,0:T(8,128)(2,1)} %apply_2.1.refs_0_), channel_id=1, source_target_pairs={{0,2},{1,3},{2,0},{3,1},{4,6},{5,7},{6,4},{7,5},{8,10},{9,11},{10,... | collective-permute-start | bytes 1179656 | tf_op jit(solution)/shard_map/ppermute | solution.py:430
  161.0 4.0 %copy-start.16 = (bf16[256,384]{1,0:T(8,128)(2,1)}, bf16[256,384]{1,0:T(8,128)(2,1)S(1)}, u32[]{:S(2)}) copy-start(bf16[256,384]{1,0:T(8,128)(2,1)S(1)} %collective-permute-done.14.refs_2_) | copy-start | bytes 589828
  161.0 28.9 %collective-permute-start.9 = (bf16[512,384]{1,0:T(8,128)(2,1)}, bf16[512,384]{1,0:T(8,128)(2,1)S(1)}, u32[]{:S(2)}, u32[]{:S(2)}) collective-permute-start(bf16[512,384]{1,0:T(8,128)(2,1)} %apply_2.1.refs_0_), channel_id=1, source_target_pairs={{0,3},{1,0},{2,1},{3,2},{4,7},{5,4},{6,5},{7,6},{8,11},{9,8},{10,9... | collective-permute-start | bytes 1179656 | tf_op jit(solution)/shard_map/ppermute | solution.py:430
  161.0 3.9 %copy-start.17 = (bf16[256,384]{1,0:T(8,128)(2,1)}, bf16[256,384]{1,0:T(8,128)(2,1)S(1)}, u32[]{:S(2)}) copy-start(bf16[256,384]{1,0:T(8,128)(2,1)S(1)} %collective-permute-done.15.refs_3_) | copy-start | bytes 589828
  161.0 20.5 %collective-permute-start.11 = (bf16[256,384]{1,0:T(8,128)(2,1)S(1)}, bf16[256,384]{1,0:T(8,128)(2,1)S(1)}, u32[]{:S(2)}, u32[]{:S(2)}) collective-permute-start(bf16[256,384]{1,0:T(8,128)(2,1)S(1)} %copy-done.6), channel_id=1, source_target_pairs={{0,2},{1,3},{2,0},{3,1},{4,6},{5,7},{6,4},{7,5},{8,10},{9,11},{10,... | collective-permute-start | bytes 589832 | tf_op jit(solution)/shard_map/ppermute | solution.py:430
  162.7 5.1 %copy-start.12 = (bf16[256,384]{1,0:T(8,128)(2,1)}, bf16[256,384]{1,0:T(8,128)(2,1)S(1)}, u32[]{:S(2)}) copy-start(bf16[256,384]{1,0:T(8,128)(2,1)S(1)} %collective-permute-done.10.refs_1_) | copy-start | bytes 589828
  162.7 23.7 %collective-permute-start.12 = (bf16[256,384]{1,0:T(8,128)(2,1)S(1)}, bf16[256,384]{1,0:T(8,128)(2,1)S(1)}, u32[]{:S(2)}, u32[]{:S(2)}) collective-permute-start(bf16[256,384]{1,0:T(8,128)(2,1)S(1)} %copy-done.6), channel_id=1, source_target_pairs={{0,3},{1,0},{2,1},{3,2},{4,7},{5,4},{6,5},{7,6},{8,11},{9,8},{10,9... | collective-permute-start | bytes 589832 | tf_op jit(solution)/shard_map/ppermute | solution.py:430
  181.5 4.9 %copy-start.13 = (bf16[256,384]{1,0:T(8,128)(2,1)}, bf16[256,384]{1,0:T(8,128)(2,1)S(1)}, u32[]{:S(2)}) copy-start(bf16[256,384]{1,0:T(8,128)(2,1)S(1)} %collective-permute-done.11.refs_2_) | copy-start | bytes 589828
  189.9 0.9 copy-start.10
  (6 other events, 4.5 us)

commit v3 on v2

--- a/solution.py
+++ b/solution.py
@@ -15,7 +15,7 @@
 SHARDS = XS * ZS * CS
 TOKENS = TOK * SHARDS
 SLOTS = XS * ZS
-ZROWS = 16
+PACK = 2 * HID + DH
 WIDE = HID + DH
 KB = 256
 QB = 256
@@ -52,151 +52,177 @@
     return pl.BlockSpec(shape, lambda i: (0,) * len(shape))
 
 
-def front_kernel(
-    pos_ref, t_ref, wk_ref, wv_ref, wr_ref, w1_ref, w3_ref, w2_ref,
-    kv_ref, send_ref, keep_ref, acc1, acc3, acc2,
-):
-    step = pl.program_id(0)
-
-    @pl.when(step == 0)
-    def _():
-        acc1[...] = jnp.zeros_like(acc1)
-        acc3[...] = jnp.zeros_like(acc3)
-        acc2[...] = jnp.zeros_like(acc2)
-
+def keys_kernel(t_ref, wk_ref, wv_ref, wr_ref, kv_ref, rates_ref):
     t = t_ref[...]
-    k = mm(t, wk_ref[...]).astype(BF)
-    v = mm(t, wv_ref[...]).astype(BF)
-    kv_ref[:, :DH] = k
-    kv_ref[:, DH:] = v
-    raw = mm(t, wr_ref[...])
-    rates = (0.25 / math.sqrt(TOKENS)) * (
+    kv_ref[:, :DH] = mm(t, wk_ref[...]).astype(BF)
+    kv_ref[:, DH:] = mm(t, wv_ref[...]).astype(BF)
+    raw = lax.dot_general(t, wr_ref[...], NT, preferred_element_type=F32)
+    rates_ref[...] = (0.25 / math.sqrt(TOKENS)) * (
         jnp.maximum(raw, 0.0) + jnp.log1p(jnp.exp(-jnp.abs(raw)))
     )
-    a = mm(k, w1_ref[0])
-    b = mm(k, w3_ref[0])
-    back = lax.dot_general(v, w2_ref[0], NT, preferred_element_type=F32)
-    sig = jax.nn.sigmoid(a)
-    act = a * sig
-    z = (act * b).astype(BF)
-    e1 = (rates[:, 0:1] * back * b * sig * (1.0 + a * (1.0 - sig))).astype(BF)
-    e3 = (rates[:, 1:2] * back * act).astype(BF)
-    e2 = (rates[:, 2:3] * v.astype(F32)).astype(BF)
-    k_t = k.T
-    acc1[...] += mm(k_t, e1)
-    acc3[...] += mm(k_t, e3)
-    acc2[...] += mm(e2.T, z)
-
-    @pl.when(step == pl.num_programs(0) - 1)
-    def _():
-        core = pos_ref[2]
-        low = acc2[:, :DH].T
-        high = acc2[:, DH:].T
-
-        @pl.when(core == 0)
-        def _():
-            keep_ref[:, :HID] = acc1[...]
-            keep_ref[:, HID:] = low
-            send_ref[:, :HID] = acc3[...].astype(BF)
-            send_ref[:, HID:] = high.astype(BF)
-
-        @pl.when(core == 1)
-        def _():
-            keep_ref[:, :HID] = acc3[...]
-            keep_ref[:, HID:] = high
-            send_ref[:, :HID] = acc1[...].astype(BF)
-            send_ref[:, HID:] = low.astype(BF)
-
-
-def front(pos, tokens, qkv_weight, rate_weight, first_fast, gate_fast, second_fast):
+
+
+def keys(tokens, qkv_weight, rate_weight):
     rows, wide = tokens.shape
     block = 256
-    fixed3 = lambda i: (0, 0, 0)
-    return pl.pallas_call(
-        front_kernel,
+    return pl.pallas_call(
+        keys_kernel,
         grid=(rows // block,),
         in_specs=[
-            SMEM,
             pl.BlockSpec((block, wide), lambda i: (i, 0)),
             pl.BlockSpec((wide, DH), lambda i: (0, 1)),
             pl.BlockSpec((wide, DH), lambda i: (0, 2)),
-            pl.BlockSpec((wide, 3), lambda i: (0, 0)),
-            pl.BlockSpec((1, DH, HID), fixed3),
-            pl.BlockSpec((1, DH, HID), fixed3),
-            pl.BlockSpec((1, HID, DH), fixed3),
+            full((3, wide)),
         ],
         out_specs=[
             pl.BlockSpec((block, 2 * DH), lambda i: (i, 0)),
-            pl.BlockSpec((DH, WIDE), lambda i: (0, 0)),
-            pl.BlockSpec((DH, WIDE), lambda i: (0, 0)),
-        ],
-        out_shape=[sds((rows, 2 * DH), BF), sds((DH, WIDE), BF), sds((DH, WIDE), F32)],
-        scratch_shapes=[pltpu.VMEM((DH, HID), F32)] * 3,
-        compiler_params=params(),
-        name="front",
-    )(pos, tokens, qkv_weight, qkv_weight, rate_weight, first_fast, gate_fast, second_fast)
-
-
-def join_kernel(keep_ref, got_ref, out_ref):
-    out_ref[:DH, :] = (keep_ref[...] + got_ref[...].astype(F32)).astype(BF)
-    out_ref[DH:, :] = jnp.zeros((SLOTS * ZROWS - DH, WIDE), BF)
-
-
-def join(keep, got):
+            pl.BlockSpec((block, 3), lambda i: (i, 0)),
+        ],
+        out_shape=[sds((rows, 2 * DH), BF), sds((rows, 3), F32)],
+        compiler_params=params(),
+        name="keys",
+    )(tokens, qkv_weight, qkv_weight, rate_weight.T)
+
+
+def update_kernel(pos_ref, kv_ref, r_ref, w1_ref, w3_ref, w2_ref, send_ref, keep_ref, second):
+    even = pos_ref[0] == 0
+    k, v = kv_ref[:, :DH], kv_ref[:, DH:]
+    r = r_ref[...]
+    r1, r3 = r[:, 0:1], r[:, 1:2]
+    k_t = k.T
+    e2_t = (r[:, 2:3] * v.astype(F32)).astype(BF).T
+    chunk = 256
+    for j in range(HID // chunk):
+        cols = slice(j * chunk, (j + 1) * chunk)
+        a = mm(k, w1_ref[0, :, cols])
+        b = mm(k, w3_ref[0, :, cols])
+        back = lax.dot_general(v, w2_ref[0, cols, :], NT, preferred_element_type=F32)
+        sig = jax.nn.sigmoid(a)
+        act = a * sig
+        z = (act * b).astype(BF)
+        e1 = (r1 * back * b * (sig * (1.0 + a * (1.0 - sig)))).astype(BF)
+        e3 = (r3 * back * act).astype(BF)
+        first = mm(k_t, e1)
+        gate = mm(k_t, e3)
+        second[cols, :] = mm(e2_t, z).T
+        keep_ref[:, cols] = jnp.where(even, first, gate)
+        send_ref[:, cols] = jnp.where(even, gate, first).astype(BF)
+    low, high = second[:DH, :], second[DH:, :]
+    keep_ref[:, HID:] = jnp.where(even, low, high)
+    send_ref[:, HID:] = jnp.where(even, high, low).astype(BF)
+
+
+def update(pos, kv, rates, first_fast, gate_fast, second_fast):
+    return pl.pallas_call(
+        update_kernel,
+        grid=(1,),
+        in_specs=[
+            SMEM,
+            full(kv.shape),
+            full(rates.shape),
+            full((1, DH, HID)),
+            full((1, DH, HID)),
+            full((1, HID, DH)),
+        ],
+        out_specs=[full((DH, WIDE)), full((DH, WIDE))],
+        out_shape=[sds((DH, WIDE), BF), sds((DH, WIDE), F32)],
+        scratch_shapes=[pltpu.VMEM((HID, DH), F32)],
+        compiler_params=params(),
+        name="update",
+    )(pos, kv, rates, first_fast, gate_fast, second_fast)
+
+
+def places():
+    for pair in range(SLOTS // 2):
+        top, mid, low = (slice(24 * pair + 8 * i, 24 * pair + 8 * i + 8) for i in range(3))
+        yield 2 * pair, slice(0, HID), top, slice(0, HID)
+        yield 2 * pair, slice(HID, 2 * HID), mid, slice(0, HID)
+        yield 2 * pair, slice(2 * HID, PACK), top, slice(HID, WIDE)
+        yield 2 * pair + 1, slice(0, HID), low, slice(0, HID)
+        yield 2 * pair + 1, slice(HID, WIDE), mid, slice(HID, WIDE)
+        yield 2 * pair + 1, slice(WIDE, 2 * HID), low, slice(HID, WIDE)
+
+
+def join_kernel(keep_ref, got_ref, before_ref, after_ref, out_ref, total):
+    total[...] = keep_ref[...] + got_ref[...].astype(F32)
+    for slot, to, rows, cols in places():
+        out_ref[slot, :, to] = total[rows, cols].astype(BF)
+    for slot in range(1, SLOTS, 2):
+        out_ref[slot, :, 2 * HID :] = jnp.zeros((8, DH), BF)
+
+
+def join(keep, got, before, after):
     return pl.pallas_call(
         join_kernel,
         grid=(1,),
-        in_specs=[full((DH, WIDE)), full((DH, WIDE))],
-        out_specs=full((SLOTS * ZROWS, WIDE)),
-        out_shape=sds((SLOTS * ZROWS, WIDE), BF),
+        in_specs=[full((DH, WIDE)), full((DH, WIDE)), DEP, DEP],
+        out_specs=full((SLOTS, 8, PACK)),
+        out_shape=sds((SLOTS, 8, PACK), BF),
+        scratch_shapes=[pltpu.VMEM((DH, WIDE), F32)],
         compiler_params=params(),
         name="join",
-    )(keep, got)
-
-
-def renorm_kernel(old_ref, got_ref, *rest):
+    )(keep, got, before, after)
+
+
+def renorm_kernel(pos_ref, old_ref, got_ref, *rest):
     out = rest[-1]
+    odd = pos_ref[1] == 1
     update = got_ref[0].astype(F32)
     for s in range(1, SLOTS):
         update = update + got_ref[s].astype(F32)
     old = old_ref[...]
     fresh = old + update
-    for cols in (slice(0, HID), slice(HID, WIDE)):
-        w, f = old[:, cols], fresh[:, cols]
-        w_sq = jnp.sum(w * w, axis=1, keepdims=True)
-        f_sq = jnp.sum(f * f, axis=1, keepdims=True)
-        new = (f * (jnp.sqrt(w_sq) / jnp.sqrt(f_sq + 1e-6))).astype(BF)
+
+    def squares(value):
+        u = [
+            jnp.sum(jnp.square(value[:, i * DH : (i + 1) * DH]), axis=1, keepdims=True)
+            for i in range(PACK // DH)
+        ]
+        wide = u[2] + u[3]
+        return (
+            (0, HID, u[0] + u[1]),
+            (HID, WIDE, jnp.where(odd, u[2], wide)),
+            (WIDE, 2 * HID, jnp.where(odd, u[3], wide)),
+            (2 * HID, PACK, u[4]),
+        )
+
+    for (lo, hi, w_sq), (_, _, f_sq) in zip(squares(old), squares(fresh)):
+        new = (fresh[:, lo:hi] * (jnp.sqrt(w_sq) / jnp.sqrt(f_sq + 1e-6))).astype(BF)
         for s in range(SLOTS):
-            out[s, :, cols] = new
-
-
-def renorm(old, got, deps):
-    shape = (SLOTS, ZROWS, WIDE)
+            out[s, :, lo:hi] = new
+
+
+def renorm(pos, old, got, deps):
+    shape = (SLOTS, 8, PACK)
     return pl.pallas_call(
         renorm_kernel,
         grid=(1,),
-        in_specs=[full((ZROWS, WIDE)), full(shape)] + [DEP] * len(deps),
+        in_specs=[SMEM, full((8, PACK)), full(shape)] + [DEP] * len(deps),
         out_specs=full(shape),
         out_shape=sds(shape, BF),
         compiler_params=params(),
         name="renorm",
-    )(old, got, *deps)
-
-
-def hold_kernel(value_ref, dep_ref, out_ref):
-    pass
-
-
-def hold(value, dep):
-    return pl.pallas_call(
-        hold_kernel,
-        in_specs=[DEP, DEP],
-        out_specs=DEP,
-        out_shape=sds(value.shape, value.dtype),
-        input_output_aliases={0: 0},
-        compiler_params=params(),
-        name="hold",
-    )(value, dep)
+    )(pos, old, got, *deps)
+
+
+def unpack_kernel(got_ref, *rest):
+    out, total = rest[-2:]
+    for slot, to, rows, cols in places():
+        total[rows, cols] = got_ref[slot, :, to].astype(F32)
+    out[...] = total[...].astype(BF)
+
+
+def unpack(got, deps):
+    return pl.pallas_call(
+        unpack_kernel,
+        grid=(1,),
+        in_specs=[full((SLOTS, 8, PACK))] + [DEP] * len(deps),
+        out_specs=full((DH, WIDE)),
+        out_shape=sds((DH, WIDE), BF),
+        scratch_shapes=[pltpu.VMEM((DH, WIDE), F32)],
+        compiler_params=params(),
+        name="unpack",
+    )(got, *deps)
 
 
 def project_kernel(t_ref, w_ref, dep_ref, q_ref):
@@ -289,7 +315,7 @@
 
 
 def apply_kernel(pos_ref, q_ref, own_ref, other_ref, att_ref, gain_ref, dep_ref, out_ref):
-    core = pos_ref[2]
+    core = pos_ref[0]
     q = q_ref[...]
     mine = mm(q, own_ref[:, :HID])
     theirs = mm(q, other_ref[:, :HID])
@@ -364,17 +390,17 @@
 ):
     mine = lax.axis_index("tok")
     head = lax.axis_index("head")
-    x, z, core = mine // (ZS * CS), mine // CS % ZS, mine % CS
-    pos = jnp.stack([x, z, core]).astype(I32)
+    chip, core = mine // CS, mine % CS
+    odd = chip % 2
     send = lambda value, pairs: lax.ppermute(value, "tok", pairs)
 
-    kv, give, keep = front(
-        pos, tokens, qkv_weight, rate_weight, first_fast, gate_fast, second_fast
-    )
-    got = send(give, SWAP_C)
+    kv, rates = keys(tokens, qkv_weight, rate_weight)
     up = [(i, i + 1) for i in range(SHARDS - 1)]
     before = send(kv, up)
     after = send(kv, [(j, i) for i, j in up])
+    pos = jnp.stack([core, odd]).astype(I32)
+    give, keep = update(pos, kv, rates, first_fast, gate_fast, second_fast)
+    got = send(give, SWAP_C)
 
     order = jnp.arange(frame_lengths.shape[0], dtype=I32)
     ends = jnp.sum(
@@ -395,41 +421,44 @@
         cols = lax.dynamic_slice_in_dim(out_weight, (head + d) % HS * DH, DH, 1)
         weights.append(lax.ppermute(cols, "head", shift_h(d)) if d else cols)
 
-    row = jnp.minimum((mine // CS) * ZROWS, DH - ZROWS)
-    pick = lambda w, at: lax.dynamic_slice_in_dim(w[0], at, ZROWS, 0)
-    old = jnp.concatenate(
-        [
-            jnp.where(core == 0, pick(first_fast, row), pick(gate_fast, row)),
-            pick(second_fast, core * DH + row),
-        ],
-        axis=1,
-    ).astype(F32)
+    base = chip // 2 * 24
+    wide = lambda at: jnp.where(
+        core == 0,
+        lax.dynamic_slice_in_dim(first_fast[0], at, 8, 0),
+        lax.dynamic_slice_in_dim(gate_fast[0], at, 8, 0),
+    )
+    narrow = lambda at: lax.dynamic_slice_in_dim(second_fast[0], core * DH + at, 8, 0)
+    middle = jnp.where(
+        odd == 1,
+        jnp.concatenate([narrow(base + 8), narrow(base + 16)], axis=1),
+        wide(base + 8),
+    )
+    old = jnp.concatenate([wide(base + 16 * odd), middle, narrow(base)], axis=1).astype(F32)
 
     def exchange(blocks):
         return lax.all_to_all(blocks, "tok", 0, 0, axis_index_groups=CHIPS)
 
-    total = join(keep, got)
-    got = exchange(total.reshape(SLOTS, ZROWS, WIDE))
+    total = join(keep, got, before, after)
+    got = exchange(total)
     query = project(tokens, qkv_weight, total)
     att_low = attend(0, 2, bounds, row_bounds, query, before, kv, after, query)
-    fresh = renorm(old, got, [att_low, *weights])
+    fresh = renorm(pos, old, got, [att_low])
     got = exchange(fresh)
     att_high = attend(2, 2, bounds, row_bounds, query, before, kv, after, fresh)
-    half = hold(got, att_high).reshape(SLOTS * ZROWS, WIDE)
+    half = unpack(got, [att_high, *weights])
     other = send(half, SWAP_C)
 
     gain = fast_gain[None, :]
-    result = None
-    mixed = []
+    result, mixed = None, []
     dep = att_high
-    for start, count, attended, at in ((0, 1, att_low, 0), (1, 1, att_low, 1), (2, 2, att_high, 0)):
-        dep = apply(start, count, pos, query, half, other, attended, at, gain, dep)
-        mixed.append((start, count, dep))
-    for start, count, part in mixed:
+    for start, attended in ((0, att_low), (2, att_high)):
+        dep = apply(start, 2, pos, query, half, other, attended, 0, gain, dep)
+        mixed.append((start, dep))
+    for start, part in mixed:
         parts = [part] + [
             lax.ppermute(part, "head", shift_h(d)) for d in range(1, HS)
         ]
-        result = output(start, count, parts, weights, result)
+        result = output(start, 2, parts, weights, result)
     return result
 
 

time: 197 us -> 169 us (0.86)
  waiting for transfers between devices: 63.8 us -> 43.7 us
  starting transfers between devices: 51.4 us -> 42.4 us
  Pallas kernels: 64.8 us -> 67.2 us
    ppermute x4, waiting for transfers between devices: 26.9 us -> 11.3 us  [body(): send = lambda value, pairs: lax.ppermute(value, 'tok', pairs)]
    all_to_all x2, waiting for transfers between devices: 18.3 us -> 10.3 us  [exchange(): return lax.all_to_all(blocks, 'tok', 0, 0, axis_index_groups=CHIPS)]
    ppermute x9 -> x6, starting transfers between devices: 12.8 us -> 7.59 us  [body(): lax.ppermute(part, 'head', shift_h(d))]
    pallas_call x3 -> x4, Pallas kernels: 17.9 us -> 22.1 us  [the longest x1 9.69 us: update(): pl.pallas_call(update_kernel, grid=(1,), in_specs=[SMEM, full(kv.shape),...]
    pallas_call x2, Pallas kernels: 18.1 us -> 20.8 us  [attend(): pl.pallas_call(functools.partial(attend_kernel, start), grid=(count,), in...]
    ppermute x9 -> x6, waiting for transfers between devices: 18.6 us -> 21 us  [body(): lax.ppermute(part, 'head', shift_h(d))]
    ppermute x4, starting transfers between devices: 13.8 us -> 11.6 us  [body(): send = lambda value, pairs: lax.ppermute(value, 'tok', pairs)]
    pallas_call x3 -> x2, Pallas kernels: 11.3 us -> 9.09 us  [apply(): pl.pallas_call(apply_kernel, grid=(count,), in_specs=[SMEM, pl.BlockSpec(...]
  transfers between devices with their start and end apart: 18 -> 15, of which waited for: 7 -> 11; matrix products, arithmetic and copies ran while one was open for 3% -> 4% of each run, Pallas kernels for 19% -> 26%
where the time goes in v3:
time: 169 us; the launch traced here: 168 us
  Pallas kernels  67.2 us (40%)
  waiting for transfers between devices  43.7 us (26%)
  starting transfers between devices  42.4 us (25%)
  local copies, waits for them, and re-layouts  11.2 us (7%)
  other arithmetic  3.37 us (2%)
    ppermute x6, waiting for transfers between devices, body(): lax.ppermute(part, 'head', shift_h(d))  21 us
    pallas_call x2, Pallas kernels, attend(): pl.pallas_call(functools.partial(attend_kernel, start), grid=(count,), in...  20.8 us
    all_to_all x2, starting transfers between devices, exchange(): return lax.all_to_all(blocks, 'tok', 0, 0, axis_index_groups=CHIPS)  18.3 us
    ppermute x4, starting transfers between devices, body(): send = lambda value, pairs: lax.ppermute(value, 'tok', pairs)  11.6 us
    ppermute x4, waiting for transfers between devices, body(): send = lambda value, pairs: lax.ppermute(value, 'tok', pairs)  11.3 us
    all_to_all x2, waiting for transfers between devices, exchange(): return lax.all_to_all(blocks, 'tok', 0, 0, axis_index_groups=CHIPS)  10.3 us
    pallas_call x1, Pallas kernels, update(): pl.pallas_call(update_kernel, grid=(1,), in_specs=[SMEM, full(kv.shape),...  9.69 us
    pallas_call x2, Pallas kernels, apply(): pl.pallas_call(apply_kernel, grid=(count,), in_specs=[SMEM, pl.BlockSpec(...  9.09 us
  transfers between devices with their start and end apart: 15, of which 11 were waited for; matrix products, arithmetic and copies ran while one was open for 4% of the time, Pallas kernels for 26%

profile of v3, /device:TPU:1, one launch (start us, length us, event | category | flops | bytes accessed | tf_op | source)
XLA Modules:
  0.0 168.2 jit_solution(968088493132234552)
XLA Ops:
  0.0 7.6 %keys.1 = (bf16[1024,768]{1,0:T(8,128)(2,1)}, f32[1024,3]{1,0:T(8,128)}) custom-call(bf16[1024,1536]{1,0:T(8,128)(2,1)} %t_ref.3, bf16[1536,1152]{1,0:T(8,128)(2,1)} %w_ref.1, bf16[1536,1152]{1,0:T(8,128)(2,1)} %w_ref.1, bf16[3,1536]{1,0:T(4,128)(2,1)} %bitcast.19), custom_call_target="tpu_custom_call" | custom-call | tf_op jit(solution)/shard_map/keys/pallas_call | solution.py:68
  7.6 4.9 %collective-permute-start.1 = (bf16[1024,768]{1,0:T(8,128)(2,1)}, bf16[1024,768]{1,0:T(8,128)(2,1)S(1)}, u32[]{:S(2)}, u32[]{:S(2)}) collective-permute-start(bf16[1024,768]{1,0:T(8,128)(2,1)} %get-tuple-element.9.kv_ref.mine), channel_id=1, source_target_pairs={{0,4},{4,8},{8,12},{12,16},{16,20},{20,24},{24,28},{28,32},{32,36}... | collective-permute-start | bytes 4718600 | tf_op jit(solution)/shard_map/ppermute | solution.py:395
  12.6 1.9 %collective-permute-start.2 = (bf16[1024,768]{1,0:T(8,128)(2,1)}, bf16[1024,768]{1,0:T(8,128)(2,1)S(1)}, u32[]{:S(2)}, u32[]{:S(2)}) collective-permute-start(bf16[1024,768]{1,0:T(8,128)(2,1)} %get-tuple-element.9.kv_ref.mine), channel_id=1, source_target_pairs={{4,0},{8,4},{12,8},{16,12},{20,16},{24,20},{28,24},{32,28},{36,32}... | collective-permute-start | bytes 4718600 | tf_op jit(solution)/shard_map/ppermute | solution.py:395
  15.2 9.7 %update.1 = (bf16[384,1152]{1,0:T(8,128)(2,1)}, f32[384,1152]{1,0:T(8,128)}) custom-call(s32[2]{0:T(128)} %pad_add_fusion.2.pos_ref, bf16[1024,768]{1,0:T(8,128)(2,1)} %get-tuple-element.9.kv_ref.mine, f32[1024,3]{1,0:T(8,128)} %get-tuple-element.10.r_ref, bf16[1,384,768]{2,1,0:T(8,128)(2,1)} %w1_ref.1, bf16[1,384,768]{2,1,0:T(8,128)(2,1)} %w3_ref.1, ...), custom_call_target="tpu_custom_call" | custom-call | tf_op jit(solution)/shard_map/update/pallas_call | solution.py:116
  24.9 2.6 %collective-permute-done.got_ref = bf16[384,1152]{1,0:T(8,128)(2,1)S(1)} collective-permute-done((bf16[384,1152]{1,0:T(8,128)(2,1)}, bf16[384,1152]{1,0:T(8,128)(2,1)S(1)}, u32[]{:S(2)}, u32[]{:S(2)}) %collective-permute-start) | collective-permute-done | bytes 884768 | tf_op jit(solution)/shard_map/ppermute | solution.py:395
  27.5 2.7 %collective-permute-done.1.before_ref.before = bf16[1024,768]{1,0:T(8,128)(2,1)S(1)} collective-permute-done((bf16[1024,768]{1,0:T(8,128)(2,1)}, bf16[1024,768]{1,0:T(8,128)(2,1)S(1)}, u32[]{:S(2)}, u32[]{:S(2)}) %collective-permute-start.1) | collective-permute-done | bytes 1572896 | tf_op jit(solution)/shard_map/ppermute | solution.py:395
  30.2 4.3 %collective-permute-done.2.after_ref.after = bf16[1024,768]{1,0:T(8,128)(2,1)S(1)} collective-permute-done((bf16[1024,768]{1,0:T(8,128)(2,1)}, bf16[1024,768]{1,0:T(8,128)(2,1)S(1)}, u32[]{:S(2)}, u32[]{:S(2)}) %collective-permute-start.2) | collective-permute-done | bytes 1572896 | tf_op jit(solution)/shard_map/ppermute | solution.py:395
  34.5 1.2 copy-done.1
  35.7 2.8 %join.1.dep_ref = bf16[32,8,1920]{2,1,0:T(8,128)(2,1)} custom-call(f32[384,1152]{1,0:T(8,128)} %get-tuple-element.11.keep_ref, bf16[384,1152]{1,0:T(8,128)(2,1)} %copy-done.9, bf16[1024,768]{1,0:T(8,128)(2,1)} %copy-done, bf16[1024,768]{1,0:T(8,128)(2,1)} %copy-done.1), custom_call_target="tpu_custom_call" | custom-call | tf_op jit(solution)/shard_map/join/pallas_call | solution.py:155
  38.5 11.0 %all-to-all-start = ((bf16[32,8,1920]{2,1,0:T(8,128)(2,1)}), bf16[32,8,1920]{2,1,0:T(8,128)(2,1)S(1)}, u32[]{:S(2)}, u32[]{:S(2)}) async-start(bf16[32,8,1920]{2,1,0:T(8,128)(2,1)} %join.1.dep_ref), calls=%async_computation | async-start | bytes 1966080 | tf_op jit(solution)/shard_map/all_to_all | solution.py:439
  55.0 5.2 %project.1.q_ref.dep_ref = bf16[1024,384]{1,0:T(8,128)(2,1)} custom-call(bf16[1024,1536]{1,0:T(8,128)(2,1)} %t_ref.3, bf16[1536,1152]{1,0:T(8,128)(2,1)} %w_ref.1, bf16[32,8,1920]{2,1,0:T(8,128)(2,1)} %join.1.dep_ref), custom_call_target="tpu_custom_call" | custom-call | tf_op jit(solution)/shard_map/project/pallas_call | solution.py:235
  60.2 10.4 %attend_0.1.rest_0_.att_ref = f32[512,384]{1,0:T(8,128)} custom-call(s32[8]{0:T(128)} %reshape.38.bounds_ref, s32[1024,2]{1,0:T(8,128)} %copy.18.rows_ref, bf16[1024,384]{1,0:T(8,128)(2,1)} %project.1.q_ref.dep_ref, bf16[1024,768]{1,0:T(8,128)(2,1)} %copy-done, bf16[1024,768]{1,0:T(8,128)(2,1)} %get-tuple-element.9.kv_ref.mine, bf16[1024,768]{1,0:T(8,128)(2,1)} %copy-done.1, ...), custom_call_target="tpu_custom_call" | custom-call | tf_op jit(solution)/shard_map/attend_0/pallas_call | solution.py:297
  70.7 4.1 %all-to-all-done.got_ref = bf16[32,8,1920]{2,1,0:T(8,128)(2,1)S(1)} async-done(((bf16[32,8,1920]{2,1,0:T(8,128)(2,1)}), bf16[32,8,1920]{2,1,0:T(8,128)(2,1)S(1)}, u32[]{:S(2)}, u32[]{:S(2)}) %all-to-all-start) | async-done | bytes 983072 | tf_op jit(solution)/shard_map/all_to_all | solution.py:439
  75.7 2.5 %renorm.1.dep_ref = bf16[32,8,1920]{2,1,0:T(8,128)(2,1)} custom-call(s32[2]{0:T(128)} %pad_add_fusion.2.pos_ref, f32[8,1920]{1,0:T(8,128)} %maximum_convert_fusion.old_ref, bf16[32,8,1920]{2,1,0:T(8,128)(2,1)} %copy-done.2, f32[512,384]{1,0:T(8,128)} %attend_0.1.rest_0_.att_ref), custom_call_target="tpu_custom_call" | custom-call | tf_op jit(solution)/shard_map/renorm/pallas_call | solution.py:197
  78.3 7.3 %all-to-all-start.1 = ((bf16[32,8,1920]{2,1,0:T(8,128)(2,1)}), bf16[32,8,1920]{2,1,0:T(8,128)(2,1)S(1)}, u32[]{:S(2)}, u32[]{:S(2)}) async-start(bf16[32,8,1920]{2,1,0:T(8,128)(2,1)} %renorm.1.dep_ref), calls=%async_computation.1 | async-start | bytes 1966080 | tf_op jit(solution)/shard_map/all_to_all | solution.py:439
  86.5 1.3 collective-permute-start.3
  87.8 2.6 %collective-permute-start.4 = (bf16[384,384]{1,0:T(8,128)(2,1)S(1)}, bf16[384,384]{1,0:T(8,128)(2,1)S(1)}, u32[]{:S(2)}, u32[]{:S(2)}) collective-permute-start(bf16[384,384]{1,0:T(8,128)(2,1)S(1)} %get-tuple-element.18), channel_id=1, source_target_pairs={{0,2},{1,3},{2,0},{3,1},{4,6},{5,7},{6,4},{7,5},{8,10},{9,11},{10,... | collective-permute-start | bytes 884744 | tf_op jit(solution)/shard_map/ppermute | solution.py:422
  91.4 10.4 %attend_2.1.rest_0_.dep_ref.att_ref = f32[512,384]{1,0:T(8,128)} custom-call(s32[8]{0:T(128)} %reshape.38.bounds_ref, s32[1024,2]{1,0:T(8,128)} %copy.18.rows_ref, bf16[1024,384]{1,0:T(8,128)(2,1)} %project.1.q_ref.dep_ref, bf16[1024,768]{1,0:T(8,128)(2,1)} %copy-done, bf16[1024,768]{1,0:T(8,128)(2,1)} %get-tuple-element.9.kv_ref.mine, ...), custom_call_target="tpu_custom_call" | custom-call | tf_op jit(solution)/shard_map/attend_2/pallas_call | solution.py:297
  102.9 6.2 %all-to-all-done.1.got_ref = bf16[32,8,1920]{2,1,0:T(8,128)(2,1)S(1)} async-done(((bf16[32,8,1920]{2,1,0:T(8,128)(2,1)}), bf16[32,8,1920]{2,1,0:T(8,128)(2,1)S(1)}, u32[]{:S(2)}, u32[]{:S(2)}) %all-to-all-start.1) | async-done | bytes 983072 | tf_op jit(solution)/shard_map/all_to_all | solution.py:439
  110.1 2.2 %unpack.1.own_ref = bf16[384,1152]{1,0:T(8,128)(2,1)} custom-call(bf16[32,8,1920]{2,1,0:T(8,128)(2,1)} %copy-done.3, f32[512,384]{1,0:T(8,128)} %attend_2.1.rest_0_.dep_ref.att_ref, bf16[384,384]{1,0:T(8,128)(2,1)} %get-tuple-element.17.rest_1_.refs_4_, bf16[384,384]{1,0:T(8,128)(2,1)} %copy-done.5, bf16[384,384]{1,0:T(8,128)(2,1)} %copy-done.6, ...), custom_call_target="tpu_custom_call" | custom-call | tf_op jit(solution)/shard_map/unpack/pallas_call | solution.py:216
  112.3 4.7 %collective-permute-start.6 = (bf16[384,1152]{1,0:T(8,128)(2,1)}, bf16[384,1152]{1,0:T(8,128)(2,1)S(1)}, u32[]{:S(2)}, u32[]{:S(2)}) collective-permute-start(bf16[384,1152]{1,0:T(8,128)(2,1)} %unpack.1.own_ref), channel_id=1, source_target_pairs={{0,4},{4,0},{8,12},{12,8},{16,20},{20,16},{24,28},{28,24},{32,36},... | collective-permute-start | bytes 2654216 | tf_op jit(solution)/shard_map/ppermute | solution.py:395
  117.6 1.7 %collective-permute-done.6.other_ref = bf16[384,1152]{1,0:T(8,128)(2,1)S(1)} collective-permute-done((bf16[384,1152]{1,0:T(8,128)(2,1)}, bf16[384,1152]{1,0:T(8,128)(2,1)S(1)}, u32[]{:S(2)}, u32[]{:S(2)}) %collective-permute-start.6) | collective-permute-done | bytes 884768 | tf_op jit(solution)/shard_map/ppermute | solution.py:395
  120.2 4.6 %apply_0.1.dep_ref.refs_0_ = bf16[512,384]{1,0:T(8,128)(2,1)} custom-call(s32[2]{0:T(128)} %pad_add_fusion.2.pos_ref, bf16[1024,384]{1,0:T(8,128)(2,1)} %project.1.q_ref.dep_ref, bf16[384,1152]{1,0:T(8,128)(2,1)} %unpack.1.own_ref, bf16[384,1152]{1,0:T(8,128)(2,1)} %copy-done.4, f32[512,384]{1,0:T(8,128)} %attend_0.1.rest_0_.att_ref, ...), custom_call_target="tpu_custom_call" | custom-call | tf_op jit(solution)/shard_map/apply_0/pallas_call | solution.py:337
  124.8 1.3 collective-permute-start.10
  126.0 2.6 %collective-permute-start.11 = (bf16[512,384]{1,0:T(8,128)(2,1)}, bf16[512,384]{1,0:T(8,128)(2,1)S(1)}, u32[]{:S(2)}, u32[]{:S(2)}) collective-permute-start(bf16[512,384]{1,0:T(8,128)(2,1)} %apply_0.1.dep_ref.refs_0_), channel_id=1, source_target_pairs={{0,2},{1,3},{2,0},{3,1},{4,6},{5,7},{6,4},{7,5},{8,10},{9,11},{10,... | collective-permute-start | bytes 1179656 | tf_op jit(solution)/shard_map/ppermute | solution.py:459
  129.7 4.5 %apply_2.1.refs_0_ = bf16[512,384]{1,0:T(8,128)(2,1)} custom-call(s32[2]{0:T(128)} %pad_add_fusion.2.pos_ref, bf16[1024,384]{1,0:T(8,128)(2,1)} %project.1.q_ref.dep_ref, bf16[384,1152]{1,0:T(8,128)(2,1)} %unpack.1.own_ref, bf16[384,1152]{1,0:T(8,128)(2,1)} %copy-done.4, f32[512,384]{1,0:T(8,128)} %attend_2.1.rest_0_.dep_ref.att_ref, ...), custom_call_target="tpu_custom_call" | custom-call | tf_op jit(solution)/shard_map/apply_2/pallas_call | solution.py:337
  136.6 1.4 collective-permute-start.9
  138.0 8.2 %collective-permute-done.11.refs_2_ = bf16[512,384]{1,0:T(8,128)(2,1)S(1)} collective-permute-done((bf16[512,384]{1,0:T(8,128)(2,1)}, bf16[512,384]{1,0:T(8,128)(2,1)S(1)}, u32[]{:S(2)}, u32[]{:S(2)}) %collective-permute-start.11) | collective-permute-done | bytes 393248 | tf_op jit(solution)/shard_map/ppermute | solution.py:459
  147.7 3.6 %output_0.1.refs_8_ = bf16[1024,384]{1,0:T(8,128)(2,1)} custom-call(bf16[512,384]{1,0:T(8,128)(2,1)} %apply_0.1.dep_ref.refs_0_, bf16[512,384]{1,0:T(8,128)(2,1)} %copy-done.10, bf16[512,384]{1,0:T(8,128)(2,1)} %copy-done.12, bf16[512,384]{1,0:T(8,128)(2,1)} %copy-done.14, bf16[384,384]{1,0:T(8,128)(2,1)} %get-tuple-element.17.rest_1_.refs_4_, ...), custom_call_target="tpu_custom_call" | custom-call | tf_op jit(solution)/shard_map/output_0/pallas_call | solution.py:366
  151.4 2.9 %collective-permute-done.7.refs_1_ = bf16[512,384]{1,0:T(8,128)(2,1)S(1)} collective-permute-done((bf16[512,384]{1,0:T(8,128)(2,1)}, bf16[512,384]{1,0:T(8,128)(2,1)S(1)}, u32[]{:S(2)}, u32[]{:S(2)}) %collective-permute-start.7) | collective-permute-done | bytes 393248 | tf_op jit(solution)/shard_map/ppermute | solution.py:459
  154.3 8.8 %collective-permute-done.8.refs_2_ = bf16[512,384]{1,0:T(8,128)(2,1)S(1)} collective-permute-done((bf16[512,384]{1,0:T(8,128)(2,1)}, bf16[512,384]{1,0:T(8,128)(2,1)S(1)}, u32[]{:S(2)}, u32[]{:S(2)}) %collective-permute-start.8) | collective-permute-done | bytes 393248 | tf_op jit(solution)/shard_map/ppermute | solution.py:459
  164.6 3.6 %output_2.1 = bf16[1024,384]{1,0:T(8,128)(2,1)} custom-call(bf16[512,384]{1,0:T(8,128)(2,1)} %apply_2.1.refs_0_, bf16[512,384]{1,0:T(8,128)(2,1)} %copy-done.11, bf16[512,384]{1,0:T(8,128)(2,1)} %copy-done.13, bf16[512,384]{1,0:T(8,128)(2,1)} %copy-done.15, bf16[384,384]{1,0:T(8,128)(2,1)} %get-tuple-element.17.rest_1_.refs_4_, ...), custom_call_target="tpu_custom_call", output_to_operand_aliasing={{}: (8, {})} | custom-call | tf_op jit(solution)/shard_map/output_2/pallas_call | solution.py:366
  (64 shorter events, 18.9 us)
Async XLA Ops:
  7.6 22.6 %collective-permute-start.1 = (bf16[1024,768]{1,0:T(8,128)(2,1)}, bf16[1024,768]{1,0:T(8,128)(2,1)S(1)}, u32[]{:S(2)}, u32[]{:S(2)}) collective-permute-start(bf16[1024,768]{1,0:T(8,128)(2,1)} %get-tuple-element.9.kv_ref.mine), channel_id=1, source_target_pairs={{0,4},{4,8},{8,12},{12,16},{16,20},{20,24},{24,28},{28,32},{32,36}... | collective-permute-start | bytes 4718600 | tf_op jit(solution)/shard_map/ppermute | solution.py:395
  12.6 21.9 %collective-permute-start.2 = (bf16[1024,768]{1,0:T(8,128)(2,1)}, bf16[1024,768]{1,0:T(8,128)(2,1)S(1)}, u32[]{:S(2)}, u32[]{:S(2)}) collective-permute-start(bf16[1024,768]{1,0:T(8,128)(2,1)} %get-tuple-element.9.kv_ref.mine), channel_id=1, source_target_pairs={{4,0},{8,4},{12,8},{16,12},{20,16},{24,20},{28,24},{32,28},{36,32}... | collective-permute-start | bytes 4718600 | tf_op jit(solution)/shard_map/ppermute | solution.py:395
  24.9 2.6 %collective-permute-start = (bf16[384,1152]{1,0:T(8,128)(2,1)}, bf16[384,1152]{1,0:T(8,128)(2,1)S(1)}, u32[]{:S(2)}, u32[]{:S(2)}) collective-permute-start(bf16[384,1152]{1,0:T(8,128)(2,1)} %get-tuple-element.12), channel_id=1, source_target_pairs={{0,4},{4,0},{8,12},{12,8},{16,20},{20,16},{24,28},{28,24},{32,36},... | collective-permute-start | bytes 2654216 | tf_op jit(solution)/shard_map/ppermute | solution.py:395
  27.5 7.0 %copy-start.9 = (bf16[384,1152]{1,0:T(8,128)(2,1)}, bf16[384,1152]{1,0:T(8,128)(2,1)S(1)}, u32[]{:S(2)}) copy-start(bf16[384,1152]{1,0:T(8,128)(2,1)S(1)} %collective-permute-done.got_ref) | copy-start | bytes 2654212
  30.2 4.3 %copy-start = (bf16[1024,768]{1,0:T(8,128)(2,1)}, bf16[1024,768]{1,0:T(8,128)(2,1)S(1)}, u32[]{:S(2)}) copy-start(bf16[1024,768]{1,0:T(8,128)(2,1)S(1)} %collective-permute-done.1.before_ref.before) | copy-start | bytes 4718596
  34.5 1.2 copy-start.1
  38.5 11.1 %copy-start.17 = (s32[128]{0:T(128)S(1)}, s32[128]{0:T(128)}, u32[]{:S(2)}) copy-start(s32[128]{0:T(128)} %param.17) | copy-start | bytes 1540
  38.5 36.3 %all-to-all-start = ((bf16[32,8,1920]{2,1,0:T(8,128)(2,1)}), bf16[32,8,1920]{2,1,0:T(8,128)(2,1)S(1)}, u32[]{:S(2)}, u32[]{:S(2)}) async-start(bf16[32,8,1920]{2,1,0:T(8,128)(2,1)} %join.1.dep_ref), calls=%async_computation | async-start | bytes 1966080 | tf_op jit(solution)/shard_map/all_to_all | solution.py:439
  74.8 0.9 copy-start.2
  78.3 7.3 %copy-start.8 = (bf16[384,1536]{1,0:T(8,128)(2,1)S(1)}, bf16[384,1536]{1,0:T(8,128)(2,1)}, u32[]{:S(2)}) copy-start(bf16[384,1536]{1,0:T(8,128)(2,1)} %param.16) | copy-start | bytes 3538948
  78.3 30.8 %all-to-all-start.1 = ((bf16[32,8,1920]{2,1,0:T(8,128)(2,1)}), bf16[32,8,1920]{2,1,0:T(8,128)(2,1)S(1)}, u32[]{:S(2)}, u32[]{:S(2)}) async-start(bf16[32,8,1920]{2,1,0:T(8,128)(2,1)} %renorm.1.dep_ref), calls=%async_computation.1 | async-start | bytes 1966080 | tf_op jit(solution)/shard_map/all_to_all | solution.py:439
  86.5 15.4 %collective-permute-start.3 = (bf16[384,384]{1,0:T(8,128)(2,1)S(1)}, bf16[384,384]{1,0:T(8,128)(2,1)S(1)}, u32[]{:S(2)}, u32[]{:S(2)}) collective-permute-start(bf16[384,384]{1,0:T(8,128)(2,1)S(1)} %get-tuple-element.16), channel_id=1, source_target_pairs={{0,1},{1,2},{2,3},{3,0},{4,5},{5,6},{6,7},{7,4},{8,9},{9,10},{10,1... | collective-permute-start | bytes 884744 | tf_op jit(solution)/shard_map/ppermute | solution.py:422
  87.8 15.1 %collective-permute-start.4 = (bf16[384,384]{1,0:T(8,128)(2,1)S(1)}, bf16[384,384]{1,0:T(8,128)(2,1)S(1)}, u32[]{:S(2)}, u32[]{:S(2)}) collective-permute-start(bf16[384,384]{1,0:T(8,128)(2,1)S(1)} %get-tuple-element.18), channel_id=1, source_target_pairs={{0,2},{1,3},{2,0},{3,1},{4,6},{5,7},{6,4},{7,5},{8,10},{9,11},{10,... | collective-permute-start | bytes 884744 | tf_op jit(solution)/shard_map/ppermute | solution.py:422
  90.4 12.5 %collective-permute-start.5 = (bf16[384,384]{1,0:T(8,128)(2,1)S(1)}, bf16[384,384]{1,0:T(8,128)(2,1)S(1)}, u32[]{:S(2)}, u32[]{:S(2)}) collective-permute-start(bf16[384,384]{1,0:T(8,128)(2,1)S(1)} %get-tuple-element.15), channel_id=1, source_target_pairs={{0,3},{1,0},{2,1},{3,2},{4,7},{5,4},{6,5},{7,6},{8,11},{9,8},{10,9... | collective-permute-start | bytes 884744 | tf_op jit(solution)/shard_map/ppermute | solution.py:422
  101.8 7.2 %copy-start.5 = (bf16[384,384]{1,0:T(8,128)(2,1)}, bf16[384,384]{1,0:T(8,128)(2,1)S(1)}, u32[]{:S(2)}) copy-start(bf16[384,384]{1,0:T(8,128)(2,1)S(1)} %collective-permute-done.3.rest_2_.refs_5_) | copy-start | bytes 884740
  102.9 6.2 %copy-start.6 = (bf16[384,384]{1,0:T(8,128)(2,1)}, bf16[384,384]{1,0:T(8,128)(2,1)S(1)}, u32[]{:S(2)}) copy-start(bf16[384,384]{1,0:T(8,128)(2,1)S(1)} %collective-permute-done.4.rest_3_.refs_6_) | copy-start | bytes 884740
  102.9 6.2 %copy-start.7 = (bf16[384,384]{1,0:T(8,128)(2,1)}, bf16[384,384]{1,0:T(8,128)(2,1)S(1)}, u32[]{:S(2)}) copy-start(bf16[384,384]{1,0:T(8,128)(2,1)S(1)} %collective-permute-done.5.rest_4_.refs_7_) | copy-start | bytes 884740
  109.1 1.0 copy-start.3
  110.1 6.9 %copy-start.16 = (f32[384]{0:T(512)S(1)}, f32[384]{0:T(512)}, u32[]{:S(2)}) copy-start(f32[384]{0:T(512)} %param.15) | copy-start | bytes 4612
  112.3 7.0 %collective-permute-start.6 = (bf16[384,1152]{1,0:T(8,128)(2,1)}, bf16[384,1152]{1,0:T(8,128)(2,1)S(1)}, u32[]{:S(2)}, u32[]{:S(2)}) collective-permute-start(bf16[384,1152]{1,0:T(8,128)(2,1)} %unpack.1.own_ref), channel_id=1, source_target_pairs={{0,4},{4,0},{8,12},{12,8},{16,20},{20,16},{24,28},{28,24},{32,36},... | collective-permute-start | bytes 2654216 | tf_op jit(solution)/shard_map/ppermute | solution.py:395
  119.3 0.9 copy-start.4
  124.8 11.9 %collective-permute-start.10 = (bf16[512,384]{1,0:T(8,128)(2,1)}, bf16[512,384]{1,0:T(8,128)(2,1)S(1)}, u32[]{:S(2)}, u32[]{:S(2)}) collective-permute-start(bf16[512,384]{1,0:T(8,128)(2,1)} %apply_0.1.dep_ref.refs_0_), channel_id=1, source_target_pairs={{0,1},{1,2},{2,3},{3,0},{4,5},{5,6},{6,7},{7,4},{8,9},{9,10},{10,1... | collective-permute-start | bytes 1179656 | tf_op jit(solution)/shard_map/ppermute | solution.py:459
  126.0 20.2 %collective-permute-start.11 = (bf16[512,384]{1,0:T(8,128)(2,1)}, bf16[512,384]{1,0:T(8,128)(2,1)S(1)}, u32[]{:S(2)}, u32[]{:S(2)}) collective-permute-start(bf16[512,384]{1,0:T(8,128)(2,1)} %apply_0.1.dep_ref.refs_0_), channel_id=1, source_target_pairs={{0,2},{1,3},{2,0},{3,1},{4,6},{5,7},{6,4},{7,5},{8,10},{9,11},{10,... | collective-permute-start | bytes 1179656 | tf_op jit(solution)/shard_map/ppermute | solution.py:459
  128.7 17.6 %collective-permute-start.12 = (bf16[512,384]{1,0:T(8,128)(2,1)}, bf16[512,384]{1,0:T(8,128)(2,1)S(1)}, u32[]{:S(2)}, u32[]{:S(2)}) collective-permute-start(bf16[512,384]{1,0:T(8,128)(2,1)} %apply_0.1.dep_ref.refs_0_), channel_id=1, source_target_pairs={{0,3},{1,0},{2,1},{3,2},{4,7},{5,4},{6,5},{7,6},{8,11},{9,8},{10,9... | collective-permute-start | bytes 1179656 | tf_op jit(solution)/shard_map/ppermute | solution.py:459
  134.3 20.0 %collective-permute-start.7 = (bf16[512,384]{1,0:T(8,128)(2,1)}, bf16[512,384]{1,0:T(8,128)(2,1)S(1)}, u32[]{:S(2)}, u32[]{:S(2)}) collective-permute-start(bf16[512,384]{1,0:T(8,128)(2,1)} %apply_2.1.refs_0_), channel_id=1, source_target_pairs={{0,1},{1,2},{2,3},{3,0},{4,5},{5,6},{6,7},{7,4},{8,9},{9,10},{10,1... | collective-permute-start | bytes 1179656 | tf_op jit(solution)/shard_map/ppermute | solution.py:459
  134.7 28.4 %collective-permute-start.8 = (bf16[512,384]{1,0:T(8,128)(2,1)}, bf16[512,384]{1,0:T(8,128)(2,1)S(1)}, u32[]{:S(2)}, u32[]{:S(2)}) collective-permute-start(bf16[512,384]{1,0:T(8,128)(2,1)} %apply_2.1.refs_0_), channel_id=1, source_target_pairs={{0,2},{1,3},{2,0},{3,1},{4,6},{5,7},{6,4},{7,5},{8,10},{9,11},{10,... | collective-permute-start | bytes 1179656 | tf_op jit(solution)/shard_map/ppermute | solution.py:459
  136.6 9.6 %copy-start.10 = (bf16[512,384]{1,0:T(8,128)(2,1)}, bf16[512,384]{1,0:T(8,128)(2,1)S(1)}, u32[]{:S(2)}) copy-start(bf16[512,384]{1,0:T(8,128)(2,1)S(1)} %collective-permute-done.10.refs_1_) | copy-start | bytes 1179652
  136.6 26.4 %collective-permute-start.9 = (bf16[512,384]{1,0:T(8,128)(2,1)}, bf16[512,384]{1,0:T(8,128)(2,1)S(1)}, u32[]{:S(2)}, u32[]{:S(2)}) collective-permute-start(bf16[512,384]{1,0:T(8,128)(2,1)} %apply_2.1.refs_0_), channel_id=1, source_target_pairs={{0,3},{1,0},{2,1},{3,2},{4,7},{5,4},{6,5},{7,6},{8,11},{9,8},{10,9... | collective-permute-start | bytes 1179656 | tf_op jit(solution)/shard_map/ppermute | solution.py:459
  146.2 0.8 copy-start.12
  147.0 0.8 copy-start.14
  154.3 8.8 %copy-start.11 = (bf16[512,384]{1,0:T(8,128)(2,1)}, bf16[512,384]{1,0:T(8,128)(2,1)S(1)}, u32[]{:S(2)}) copy-start(bf16[512,384]{1,0:T(8,128)(2,1)S(1)} %collective-permute-done.7.refs_1_) | copy-start | bytes 1179652
  163.1 0.8 copy-start.13
  (1 other events, 0.8 us)

commit v4 on v3

--- a/solution.py
+++ b/solution.py
@@ -64,7 +64,7 @@
 
 def keys(tokens, qkv_weight, rate_weight):
     rows, wide = tokens.shape
-    block = 256
+    block = 512
     return pl.pallas_call(
         keys_kernel,
         grid=(rows // block,),
@@ -247,13 +247,18 @@
     )(tokens, qkv_weight, dep)
 
 
-def attend_kernel(start, bounds_ref, rows_ref, q_ref, before, mine, after, dep_ref, out_ref, s_ref):
-    piece = pl.program_id(0) + start
-    low, high = bounds_ref[2 * piece], bounds_ref[2 * piece + 1]
-    first = lax.div(low, KB)
-    last = lax.div(high + KB - 1, KB)
+def attend_kernel(start, pos_ref, ends_ref, q_ref, before, mine, after, *rest):
+    out_ref, s_ref = rest[-2:]
+    shard = pos_ref[3]
+    row = lax.broadcasted_iota(I32, (QB, 1), 0)
+    place = row + (shard * TOK + (pl.program_id(0) + start) * QB)
+    ends = ends_ref[...]
+    shift = (shard - 1) * TOK
+    begin = jnp.max(jnp.where(ends <= place, ends, 0), axis=1, keepdims=True) - shift
+    end = jnp.min(jnp.where(ends <= place, TOKENS, ends), axis=1, keepdims=True) - shift
+    first = lax.div(jnp.min(begin), KB)
+    last = lax.div(jnp.max(end) + KB - 1, KB)
     q = q_ref[...]
-    begin, end = rows_ref[:, 0:1], rows_ref[:, 1:2]
     per = TOK // KB
     scale = 1.0 / math.sqrt(DH)
 
@@ -292,29 +297,32 @@
     segments(gather, 0)
 
 
-def attend(start, count, bounds, row_bounds, query, before, mine, after, dep):
+def attend(start, count, pos, ends, query, before, mine, after, dep, buffer):
     whole = full((TOK, 2 * DH))
+    extra = [] if buffer is None else [buffer]
     return pl.pallas_call(
         functools.partial(attend_kernel, start),
         grid=(count,),
         in_specs=[
             SMEM,
-            pl.BlockSpec((QB, 2), lambda i: (i + start, 0)),
+            full(ends.shape),
             pl.BlockSpec((QB, DH), lambda i: (i + start, 0)),
             whole,
             whole,
             whole,
             DEP,
-        ],
-        out_specs=pl.BlockSpec((QB, DH), lambda i: (i, 0)),
-        out_shape=sds((count * QB, DH), F32),
+        ]
+        + [DEP] * len(extra),
+        out_specs=pl.BlockSpec((QB, DH), lambda i: (i + start, 0)),
+        out_shape=sds((TOK, DH), F32),
+        input_output_aliases={7: 0} if extra else {},
         scratch_shapes=[pltpu.VMEM((3 * TOK // KB, QB, KB), F32)],
         compiler_params=params(),
         name=f"attend_{start}",
-    )(bounds, row_bounds, query, before, mine, after, dep)
-
-
-def apply_kernel(pos_ref, q_ref, own_ref, other_ref, att_ref, gain_ref, dep_ref, out_ref):
+    )(pos, ends, query, before, mine, after, dep, *extra)
+
+
+def apply_kernel(pos_ref, q_ref, own_ref, other_ref, att_ref, gain_ref, *outs):
     core = pos_ref[0]
     q = q_ref[...]
     mine = mm(q, own_ref[:, :HID])
@@ -329,52 +337,72 @@
     applied = mm(h_own, own_ref[:, HID:]) + mm(h_other, other_ref[:, HID:])
     mean = jnp.mean(applied * applied, axis=1, keepdims=True)
     normed = applied * lax.rsqrt(mean + 1e-6) * gain_ref[...]
-    out_ref[...] = (att_ref[...] + normed).astype(BF)
-
-
-def apply(start, count, pos, query, own, other, attended, att_start, gain, dep):
-    weight = full((DH, WIDE))
+    mixed = (att_ref[...] + normed).astype(BF)
+    for step in range(HS):
+
+        @pl.when(pl.program_id(0) == step)
+        def _():
+            outs[step][...] = mixed
+
+
+def apply(pos, query, own, other, attended, gain):
+    weight = pl.BlockSpec((DH, WIDE), lambda i, pos: (0, 0))
+    rows = pl.BlockSpec((QB, DH), lambda i, pos: (lax.rem(pos[2] + i + 1, HS), 0))
     return pl.pallas_call(
         apply_kernel,
-        grid=(count,),
-        in_specs=[
-            SMEM,
-            pl.BlockSpec((QB, DH), lambda i: (i + start, 0)),
-            weight,
-            weight,
-            pl.BlockSpec((QB, DH), lambda i: (i + att_start, 0)),
-            full((1, DH)),
-            DEP,
-        ],
-        out_specs=pl.BlockSpec((QB, DH), lambda i: (i, 0)),
-        out_shape=sds((count * QB, DH), BF),
-        compiler_params=params(),
-        name=f"apply_{start}",
-    )(pos, query, own, other, attended, gain, dep)
-
-
-def output_kernel(*refs):
-    parts, weights, out = refs[:HS], refs[HS : 2 * HS], refs[-1]
-    total = mm(parts[0][...], weights[0][...])
-    for part, weight in zip(parts[1:], weights[1:]):
-        total = total + mm(part[...], weight[...])
-    out[...] = total.astype(BF)
-
-
-def output(start, count, parts, weights, buffer):
-    extra = [] if buffer is None else [buffer]
+        grid_spec=pltpu.PrefetchScalarGridSpec(
+            num_scalar_prefetch=1,
+            grid=(HS,),
+            in_specs=[rows, weight, weight, rows, pl.BlockSpec((1, DH), lambda i, pos: (0, 0))],
+            out_specs=[pl.BlockSpec((QB, DH), lambda i, pos: (0, 0))] * HS,
+        ),
+        out_shape=[sds((QB, DH), BF)] * HS,
+        compiler_params=params(),
+        name="apply",
+    )(pos, query, own, other, attended, gain)
+
+
+def output_kernel(pos_ref, *refs):
+    parts, weights, outs = refs[:HS], refs[HS : 2 * HS], refs[2 * HS :]
+    head = pos_ref[2]
+    for e, out in enumerate(outs):
+        cols = pl.ds(pl.multiple_of(lax.rem(head + e + 1, HS) * DH, DH), DH)
+        total = mm(parts[0][...], weights[0][:, cols])
+        for part, weight in zip(parts[1:], weights[1:]):
+            total = total + mm(part[...], weight[:, cols])
+        out[...] = total.astype(BF)
+
+
+def output(pos, parts, weights):
     return pl.pallas_call(
         output_kernel,
-        grid=(count,),
-        in_specs=[pl.BlockSpec((QB, DH), lambda i: (i, 0))] * HS
-        + [full((DH, DH))] * HS
-        + [DEP] * len(extra),
-        out_specs=pl.BlockSpec((QB, DH), lambda i: (i + start, 0)),
+        grid=(1,),
+        in_specs=[SMEM] + [full((QB, DH))] * HS + [full((DH, HS * DH))] * HS,
+        out_specs=[full((QB, DH))] * HS,
+        out_shape=[sds((QB, DH), BF)] * HS,
+        compiler_params=params(),
+        name="output",
+    )(pos, *parts, *weights)
+
+
+def arrange_kernel(pos_ref, *refs):
+    parts, out = refs[:-1], refs[-1]
+    head = pos_ref[2]
+    for d, part in enumerate(parts):
+        rows = pl.ds(pl.multiple_of(lax.rem(head - d + HS, HS) * QB, QB), QB)
+        out[rows, :] = part[...]
+
+
+def arrange(pos, parts):
+    return pl.pallas_call(
+        arrange_kernel,
+        grid=(1,),
+        in_specs=[SMEM] + [full((QB, DH))] * HS,
+        out_specs=full((TOK, DH)),
         out_shape=sds((TOK, DH), BF),
-        input_output_aliases={2 * HS: 0} if extra else {},
-        compiler_params=params(),
-        name=f"output_{start}",
-    )(*parts, *weights, *extra)
+        compiler_params=params(),
+        name="arrange",
+    )(pos, *parts)
 
 
 def body(
@@ -398,28 +426,21 @@
     up = [(i, i + 1) for i in range(SHARDS - 1)]
     before = send(kv, up)
     after = send(kv, [(j, i) for i, j in up])
-    pos = jnp.stack([core, odd]).astype(I32)
+    pos = jnp.stack([core, odd, head, mine]).astype(I32)
     give, keep = update(pos, kv, rates, first_fast, gate_fast, second_fast)
     got = send(give, SWAP_C)
 
     order = jnp.arange(frame_lengths.shape[0], dtype=I32)
     ends = jnp.sum(
-        jnp.where(order[:, None] <= order[None, :], frame_lengths[:, None], 0), axis=0
-    )
-    places = mine * TOK + jnp.arange(TOK, dtype=I32)
-    passed = ends[None, :] <= places[:, None]
-    begin = jnp.max(jnp.where(passed, ends[None, :], 0), axis=1)
-    end = jnp.min(jnp.where(passed, TOKENS, ends[None, :]), axis=1)
-    shift = (mine - 1) * TOK
-    row_bounds = jnp.stack([begin - shift, end - shift], axis=1)
-    bounds = jnp.stack(
-        [row_bounds[::QB, 0], row_bounds[QB - 1 :: QB, 1]], axis=1
-    ).reshape(-1)
-
-    weights = []
-    for d in range(HS):
-        cols = lax.dynamic_slice_in_dim(out_weight, (head + d) % HS * DH, DH, 1)
-        weights.append(lax.ppermute(cols, "head", shift_h(d)) if d else cols)
+        jnp.where(order[:, None] <= order[None, :], frame_lengths[:, None], 0),
+        axis=0,
+        keepdims=True,
+    )
+
+    def spread(parts):
+        return [lax.ppermute(p, "head", shift_h(d)) if d else p for d, p in enumerate(parts)]
+
+    weights = spread([out_weight] * HS)
 
     base = chip // 2 * 24
     wide = lambda at: jnp.where(
@@ -441,24 +462,18 @@
     total = join(keep, got, before, after)
     got = exchange(total)
     query = project(tokens, qkv_weight, total)
-    att_low = attend(0, 2, bounds, row_bounds, query, before, kv, after, query)
-    fresh = renorm(pos, old, got, [att_low])
+    att = functools.partial(attend, pos=pos, ends=ends, query=query, before=before, mine=kv, after=after)
+    att_low = att(0, 2, dep=query, buffer=None)
+    fresh = renorm(pos, old, got, [att_low, weights[1], weights[3]])
     got = exchange(fresh)
-    att_high = attend(2, 2, bounds, row_bounds, query, before, kv, after, fresh)
-    half = unpack(got, [att_high, *weights])
+    attended = att(2, 2, dep=fresh, buffer=att_low)
+    half = unpack(got, [attended, weights[2]])
     other = send(half, SWAP_C)
 
-    gain = fast_gain[None, :]
-    result, mixed = None, []
-    dep = att_high
-    for start, attended in ((0, att_low), (2, att_high)):
-        dep = apply(start, 2, pos, query, half, other, attended, 0, gain, dep)
-        mixed.append((start, dep))
-    for start, part in mixed:
-        parts = [part] + [
-            lax.ppermute(part, "head", shift_h(d)) for d in range(1, HS)
-        ]
-        result = output(start, 2, parts, weights, result)
+    ahead = apply(pos, query, half, other, attended, fast_gain[None, :])
+    parts = spread([ahead[-1], *ahead[:-1]])
+    ahead = output(pos, parts, weights)
+    result = arrange(pos, spread([ahead[-1], *ahead[:-1]]))
     return result
 
 

time: 169 us -> 173 us (1.024)
  waiting for transfers between devices: 43.7 us -> 52.1 us
  local copies, waits for them, and re-layouts: 11.2 us -> 9.24 us
    ppermute x9, waiting for transfers between devices: 22.1 us -> 40.7 us  [spread(): lax.ppermute(p, 'head', shift_h(d))]
    all_to_all x2, waiting for transfers between devices: 10.3 us -> 0.01 us  [exchange(): return lax.all_to_all(blocks, 'tok', 0, 0, axis_index_groups=CHIPS)]
    ppermute x4, starting transfers between devices: 11.6 us -> 9.13 us  [body(): send = lambda value, pairs: lax.ppermute(value, 'tok', pairs)]
    pallas_call x4 -> x3, Pallas kernels: 16.4 us -> 15.4 us  [the longest x1 7.77 us: apply(): pl.pallas_call(apply_kernel, grid_spec=pltpu.PrefetchScalarGridSpec(num_s...]
    unnamed x36 -> x34, local copies, waits for them, and re-layouts: 7.11 us -> 7.94 us
  transfers between devices with their start and end apart: 15 -> 15, of which waited for: 11 -> 10; matrix products, arithmetic and copies ran while one was open for 4% -> 3% of each run, Pallas kernels for 26% -> 20%
where the time goes in v4:
time: 173 us; the launch traced here: 172 us
  Pallas kernels  65.6 us (38%)
  waiting for transfers between devices  52.1 us (30%)
  starting transfers between devices  41.9 us (24%)
  local copies, waits for them, and re-layouts  9.24 us (5%)
  other arithmetic  3.44 us (2%)
    ppermute x9, waiting for transfers between devices, spread(): lax.ppermute(p, 'head', shift_h(d))  40.7 us
    pallas_call x2, Pallas kernels, attend(): pl.pallas_call(functools.partial(attend_kernel, start), grid=(count,), in...  20.3 us
    all_to_all x2, starting transfers between devices, exchange(): return lax.all_to_all(blocks, 'tok', 0, 0, axis_index_groups=CHIPS)  19.9 us
    ppermute x9, starting transfers between devices, spread(): lax.ppermute(p, 'head', shift_h(d))  12.9 us
    ppermute x4, waiting for transfers between devices, body(): send = lambda value, pairs: lax.ppermute(value, 'tok', pairs)  11.3 us
    pallas_call x1, Pallas kernels, update(): pl.pallas_call(update_kernel, grid=(1,), in_specs=[SMEM, full(kv.shape),...  9.66 us
    ppermute x4, starting transfers between devices, body(): send = lambda value, pairs: lax.ppermute(value, 'tok', pairs)  9.13 us
    unnamed x34, local copies, waits for them, and re-layouts  7.94 us
  transfers between devices with their start and end apart: 15, of which 10 were waited for; matrix products, arithmetic and copies ran while one was open for 3% of the time, Pallas kernels for 20%

profile of v4, /device:TPU:1, one launch (start us, length us, event | category | flops | bytes accessed | tf_op | source)
XLA Modules:
  0.0 172.4 jit_solution(13126187388255307833)
XLA Ops:
  0.0 7.5 %keys.1 = (bf16[1024,768]{1,0:T(8,128)(2,1)}, f32[1024,3]{1,0:T(8,128)}) custom-call(bf16[1024,1536]{1,0:T(8,128)(2,1)} %t_ref.3, bf16[1536,1152]{1,0:T(8,128)(2,1)} %w_ref.1, bf16[1536,1152]{1,0:T(8,128)(2,1)} %w_ref.1, bf16[3,1536]{1,0:T(4,128)(2,1)} %bitcast.16), custom_call_target="tpu_custom_call" | custom-call | tf_op jit(solution)/shard_map/keys/pallas_call | solution.py:68
  7.5 4.9 %collective-permute-start.1 = (bf16[1024,768]{1,0:T(8,128)(2,1)}, bf16[1024,768]{1,0:T(8,128)(2,1)S(1)}, u32[]{:S(2)}, u32[]{:S(2)}) collective-permute-start(bf16[1024,768]{1,0:T(8,128)(2,1)} %get-tuple-element.17.kv_ref.mine), channel_id=1, source_target_pairs={{0,4},{4,8},{8,12},{12,16},{16,20},{20,24},{24,28},{28,32},{32,36}... | collective-permute-start | bytes 4718600 | tf_op jit(solution)/shard_map/ppermute | solution.py:423
  12.5 1.9 %collective-permute-start.2 = (bf16[1024,768]{1,0:T(8,128)(2,1)}, bf16[1024,768]{1,0:T(8,128)(2,1)S(1)}, u32[]{:S(2)}, u32[]{:S(2)}) collective-permute-start(bf16[1024,768]{1,0:T(8,128)(2,1)} %get-tuple-element.17.kv_ref.mine), channel_id=1, source_target_pairs={{4,0},{8,4},{12,8},{16,12},{20,16},{24,20},{28,24},{32,28},{36,32}... | collective-permute-start | bytes 4718600 | tf_op jit(solution)/shard_map/ppermute | solution.py:423
  15.1 9.7 %update.1 = (bf16[384,1152]{1,0:T(8,128)(2,1)}, f32[384,1152]{1,0:T(8,128)}) custom-call(s32[4]{0:T(128)} %pad_add_fusion.pos_ref, bf16[1024,768]{1,0:T(8,128)(2,1)} %get-tuple-element.17.kv_ref.mine, f32[1024,3]{1,0:T(8,128)} %get-tuple-element.18.r_ref, bf16[1,384,768]{2,1,0:T(8,128)(2,1)} %w1_ref.1, bf16[1,384,768]{2,1,0:T(8,128)(2,1)} %w3_ref.1, ...), custom_call_target="tpu_custom_call" | custom-call | tf_op jit(solution)/shard_map/update/pallas_call | solution.py:116
  24.8 2.6 %collective-permute-done.got_ref = bf16[384,1152]{1,0:T(8,128)(2,1)S(1)} collective-permute-done((bf16[384,1152]{1,0:T(8,128)(2,1)}, bf16[384,1152]{1,0:T(8,128)(2,1)S(1)}, u32[]{:S(2)}, u32[]{:S(2)}) %collective-permute-start) | collective-permute-done | bytes 884768 | tf_op jit(solution)/shard_map/ppermute | solution.py:423
  27.4 2.7 %collective-permute-done.1.before_ref.before = bf16[1024,768]{1,0:T(8,128)(2,1)S(1)} collective-permute-done((bf16[1024,768]{1,0:T(8,128)(2,1)}, bf16[1024,768]{1,0:T(8,128)(2,1)S(1)}, u32[]{:S(2)}, u32[]{:S(2)}) %collective-permute-start.1) | collective-permute-done | bytes 1572896 | tf_op jit(solution)/shard_map/ppermute | solution.py:423
  30.1 4.3 %collective-permute-done.2.after_ref.after = bf16[1024,768]{1,0:T(8,128)(2,1)S(1)} collective-permute-done((bf16[1024,768]{1,0:T(8,128)(2,1)}, bf16[1024,768]{1,0:T(8,128)(2,1)S(1)}, u32[]{:S(2)}, u32[]{:S(2)}) %collective-permute-start.2) | collective-permute-done | bytes 1572896 | tf_op jit(solution)/shard_map/ppermute | solution.py:423
  35.6 2.8 %join.1.dep_ref = bf16[32,8,1920]{2,1,0:T(8,128)(2,1)} custom-call(f32[384,1152]{1,0:T(8,128)} %get-tuple-element.19.keep_ref, bf16[384,1152]{1,0:T(8,128)(2,1)} %copy-done.7, bf16[1024,768]{1,0:T(8,128)(2,1)} %copy-done, bf16[1024,768]{1,0:T(8,128)(2,1)} %copy-done.1), custom_call_target="tpu_custom_call" | custom-call | tf_op jit(solution)/shard_map/join/pallas_call | solution.py:155
  38.5 11.0 %all-to-all-start = ((bf16[32,8,1920]{2,1,0:T(8,128)(2,1)}), bf16[32,8,1920]{2,1,0:T(8,128)(2,1)S(1)}, u32[]{:S(2)}, u32[]{:S(2)}) async-start(bf16[32,8,1920]{2,1,0:T(8,128)(2,1)} %join.1.dep_ref), calls=%async_computation | async-start | bytes 1966080 | tf_op jit(solution)/shard_map/all_to_all | solution.py:460
  49.5 1.4 collective-permute-start.3
  50.9 1.7 collective-permute-start.4
  56.1 5.2 %project.1.q_ref.rest_0_ = bf16[1024,384]{1,0:T(8,128)(2,1)} custom-call(bf16[1024,1536]{1,0:T(8,128)(2,1)} %t_ref.3, bf16[1536,1152]{1,0:T(8,128)(2,1)} %w_ref.1, bf16[32,8,1920]{2,1,0:T(8,128)(2,1)} %join.1.dep_ref), custom_call_target="tpu_custom_call" | custom-call | tf_op jit(solution)/shard_map/project/pallas_call | solution.py:235
  61.3 11.5 %attend_0.1.rest_0_.rest_1_ = f32[1024,384]{1,0:T(8,128)} custom-call(s32[4]{0:T(128)} %pad_add_fusion.pos_ref, s32[1,128]{1,0:T(1,128)} %bitcast.17, bf16[1024,384]{1,0:T(8,128)(2,1)} %project.1.q_ref.rest_0_, bf16[1024,768]{1,0:T(8,128)(2,1)} %copy-done, bf16[1024,768]{1,0:T(8,128)(2,1)} %get-tuple-element.17.kv_ref.mine, bf16[1024,768]{1,0:T(8,128)(2,1)} %copy-done.1, ...), custom_call_target="tpu_custom_call" | custom-call | tf_op jit(solution)/shard_map/attend_0/pallas_call | solution.py:303
  72.8 5.9 %collective-permute-done.3.rest_1_.refs_5_ = bf16[384,1536]{1,0:T(8,128)(2,1)S(1)} collective-permute-done((bf16[384,1536]{1,0:T(8,128)(2,1)}, bf16[384,1536]{1,0:T(8,128)(2,1)S(1)}, u32[]{:S(2)}, u32[]{:S(2)}) %collective-permute-start.3) | collective-permute-done | bytes 1179680 | tf_op jit(solution)/shard_map/ppermute | solution.py:441
  81.0 2.5 %renorm.1.rest_0_ = bf16[32,8,1920]{2,1,0:T(8,128)(2,1)} custom-call(s32[4]{0:T(128)} %pad_add_fusion.pos_ref, f32[8,1920]{1,0:T(8,128)} %maximum_convert_fusion.old_ref, bf16[32,8,1920]{2,1,0:T(8,128)(2,1)} %copy-done.5, f32[1024,384]{1,0:T(8,128)} %attend_0.1.rest_0_.rest_1_, bf16[384,1536]{1,0:T(8,128)(2,1)} %copy-done.3, bf16[384,1536]{1,0:T(8,128)(2,1)} %copy-done.4), custom_call_target="tpu_custom_call" | custom-call | tf_op jit(solution)/shard_map/renorm/pallas_call | solution.py:197
  83.5 8.9 %all-to-all-start.1 = ((bf16[32,8,1920]{2,1,0:T(8,128)(2,1)}), bf16[32,8,1920]{2,1,0:T(8,128)(2,1)S(1)}, u32[]{:S(2)}, u32[]{:S(2)}) async-start(bf16[32,8,1920]{2,1,0:T(8,128)(2,1)} %renorm.1.rest_0_), calls=%async_computation.1 | async-start | bytes 1966080 | tf_op jit(solution)/shard_map/all_to_all | solution.py:460
  92.4 1.9 %collective-permute-start.5 = (bf16[384,1536]{1,0:T(8,128)(2,1)}, bf16[384,1536]{1,0:T(8,128)(2,1)S(1)}, u32[]{:S(2)}, u32[]{:S(2)}) collective-permute-start(bf16[384,1536]{1,0:T(8,128)(2,1)} %refs_4_.1), channel_id=1, source_target_pairs={{0,2},{1,3},{2,0},{3,1},{4,6},{5,7},{6,4},{7,5},{8,10},{9,11},{10,... | collective-permute-start | bytes 3538952 | tf_op jit(solution)/shard_map/ppermute | solution.py:441
  94.4 8.8 %attend_2.1.rest_0_.att_ref = f32[1024,384]{1,0:T(8,128)} custom-call(s32[4]{0:T(128)} %pad_add_fusion.pos_ref, s32[1,128]{1,0:T(1,128)} %bitcast.18, bf16[1024,384]{1,0:T(8,128)(2,1)} %project.1.q_ref.rest_0_, bf16[1024,768]{1,0:T(8,128)(2,1)} %copy-done, bf16[1024,768]{1,0:T(8,128)(2,1)} %get-tuple-element.17.kv_ref.mine, ...), custom_call_target="tpu_custom_call", output_to_operand_aliasing={{}: (7, {})} | custom-call | tf_op jit(solution)/shard_map/attend_2/pallas_call | solution.py:303
  103.1 17.2 %collective-permute-done.5.rest_1_.refs_6_ = bf16[384,1536]{1,0:T(8,128)(2,1)S(1)} collective-permute-done((bf16[384,1536]{1,0:T(8,128)(2,1)}, bf16[384,1536]{1,0:T(8,128)(2,1)S(1)}, u32[]{:S(2)}, u32[]{:S(2)}) %collective-permute-start.5) | collective-permute-done | bytes 1179680 | tf_op jit(solution)/shard_map/ppermute | solution.py:441
  122.3 2.2 %unpack.1.own_ref = bf16[384,1152]{1,0:T(8,128)(2,1)} custom-call(bf16[32,8,1920]{2,1,0:T(8,128)(2,1)} %copy-done.6, f32[1024,384]{1,0:T(8,128)} %attend_2.1.rest_0_.att_ref, bf16[384,1536]{1,0:T(8,128)(2,1)} %copy-done.2), custom_call_target="tpu_custom_call" | custom-call | tf_op jit(solution)/shard_map/unpack/pallas_call | solution.py:216
  124.5 2.3 %collective-permute-start.6 = (bf16[384,1152]{1,0:T(8,128)(2,1)}, bf16[384,1152]{1,0:T(8,128)(2,1)S(1)}, u32[]{:S(2)}, u32[]{:S(2)}) collective-permute-start(bf16[384,1152]{1,0:T(8,128)(2,1)} %unpack.1.own_ref), channel_id=1, source_target_pairs={{0,4},{4,0},{8,12},{12,8},{16,20},{20,16},{24,28},{28,24},{32,36},... | collective-permute-start | bytes 2654216 | tf_op jit(solution)/shard_map/ppermute | solution.py:423
  127.4 1.7 collective-permute-done.6.other_ref
  130.0 7.8 %apply.1 = (bf16[256,384]{1,0:T(8,128)(2,1)}, bf16[256,384]{1,0:T(8,128)(2,1)}, bf16[256,384]{1,0:T(8,128)(2,1)}, bf16[256,384]{1,0:T(8,128)(2,1)}) custom-call(s32[4]{0:T(128)} %pad_add_fusion.pos_ref, bf16[1024,384]{1,0:T(8,128)(2,1)} %project.1.q_ref.rest_0_, bf16[384,1152]{1,0:T(8,128)(2,1)} %unpack.1.own_ref, bf16[384,1152]{1,0:T(8,128)(2,1)} %copy-done.8, ...), custom_call_target="tpu_custom_call" | custom-call | tf_op jit(solution)/shard_map/apply/pallas_call | solution.py:351
  138.3 3.1 %collective-permute-start.8 = (bf16[256,384]{1,0:T(8,128)(2,1)}, bf16[256,384]{1,0:T(8,128)(2,1)S(1)}, u32[]{:S(2)}, u32[]{:S(2)}) collective-permute-start(bf16[256,384]{1,0:T(8,128)(2,1)} %get-tuple-element.23), channel_id=1, source_target_pairs={{0,2},{1,3},{2,0},{3,1},{4,6},{5,7},{6,4},{7,5},{8,10},{9,11},{10,... | collective-permute-start | bytes 589832 | tf_op jit(solution)/shard_map/ppermute | solution.py:441
  141.7 3.6 %collective-permute-done.7.refs_1_ = bf16[256,384]{1,0:T(8,128)(2,1)S(1)} collective-permute-done((bf16[256,384]{1,0:T(8,128)(2,1)}, bf16[256,384]{1,0:T(8,128)(2,1)S(1)}, u32[]{:S(2)}, u32[]{:S(2)}) %collective-permute-start.7) | collective-permute-done | bytes 196640 | tf_op jit(solution)/shard_map/ppermute | solution.py:441
  145.3 5.2 %collective-permute-done.8.refs_2_ = bf16[256,384]{1,0:T(8,128)(2,1)S(1)} collective-permute-done((bf16[256,384]{1,0:T(8,128)(2,1)}, bf16[256,384]{1,0:T(8,128)(2,1)S(1)}, u32[]{:S(2)}, u32[]{:S(2)}) %collective-permute-start.8) | collective-permute-done | bytes 196640 | tf_op jit(solution)/shard_map/ppermute | solution.py:441
  151.2 5.5 %output.1 = (bf16[256,384]{1,0:T(8,128)(2,1)}, bf16[256,384]{1,0:T(8,128)(2,1)}, bf16[256,384]{1,0:T(8,128)(2,1)}, bf16[256,384]{1,0:T(8,128)(2,1)}) custom-call(s32[4]{0:T(128)} %pad_add_fusion.pos_ref, bf16[256,384]{1,0:T(8,128)(2,1)} %get-tuple-element.21.refs_0_, bf16[256,384]{1,0:T(8,128)(2,1)} %copy-done.9, bf16[256,384]{1,0:T(8,128)(2,1)} %copy-done.10, ...), custom_call_target="tpu_custom_call" | custom-call | tf_op jit(solution)/shard_map/output/pallas_call | solution.py:377
  156.7 1.5 collective-permute-start.10
  158.2 2.3 %collective-permute-start.11 = (bf16[256,384]{1,0:T(8,128)(2,1)}, bf16[256,384]{1,0:T(8,128)(2,1)S(1)}, u32[]{:S(2)}, u32[]{:S(2)}) collective-permute-start(bf16[256,384]{1,0:T(8,128)(2,1)} %get-tuple-element.27), channel_id=1, source_target_pairs={{0,2},{1,3},{2,0},{3,1},{4,6},{5,7},{6,4},{7,5},{8,10},{9,11},{10,... | collective-permute-start | bytes 589832 | tf_op jit(solution)/shard_map/ppermute | solution.py:441
  160.6 2.7 %collective-permute-done.10.refs_1_ = bf16[256,384]{1,0:T(8,128)(2,1)S(1)} collective-permute-done((bf16[256,384]{1,0:T(8,128)(2,1)}, bf16[256,384]{1,0:T(8,128)(2,1)S(1)}, u32[]{:S(2)}, u32[]{:S(2)}) %collective-permute-start.10) | collective-permute-done | bytes 196640 | tf_op jit(solution)/shard_map/ppermute | solution.py:441
  163.3 6.1 %collective-permute-done.11.refs_2_ = bf16[256,384]{1,0:T(8,128)(2,1)S(1)} collective-permute-done((bf16[256,384]{1,0:T(8,128)(2,1)}, bf16[256,384]{1,0:T(8,128)(2,1)S(1)}, u32[]{:S(2)}, u32[]{:S(2)}) %collective-permute-start.11) | collective-permute-done | bytes 196640 | tf_op jit(solution)/shard_map/ppermute | solution.py:441
  170.2 2.2 %arrange.1 = bf16[1024,384]{1,0:T(8,128)(2,1)} custom-call(s32[4]{0:T(128)} %pad_add_fusion.pos_ref, bf16[256,384]{1,0:T(8,128)(2,1)} %get-tuple-element.25.refs_0_, bf16[256,384]{1,0:T(8,128)(2,1)} %copy-done.12, bf16[256,384]{1,0:T(8,128)(2,1)} %copy-done.13, bf16[256,384]{1,0:T(8,128)(2,1)} %copy-done.14), custom_call_target="tpu_custom_call" | custom-call | tf_op jit(solution)/shard_map/arrange/pallas_call | solution.py:397
  (50 shorter events, 13.6 us)
Async XLA Ops:
  7.5 22.6 %collective-permute-start.1 = (bf16[1024,768]{1,0:T(8,128)(2,1)}, bf16[1024,768]{1,0:T(8,128)(2,1)S(1)}, u32[]{:S(2)}, u32[]{:S(2)}) collective-permute-start(bf16[1024,768]{1,0:T(8,128)(2,1)} %get-tuple-element.17.kv_ref.mine), channel_id=1, source_target_pairs={{0,4},{4,8},{8,12},{12,16},{16,20},{20,24},{24,28},{28,32},{32,36}... | collective-permute-start | bytes 4718600 | tf_op jit(solution)/shard_map/ppermute | solution.py:423
  12.5 21.9 %collective-permute-start.2 = (bf16[1024,768]{1,0:T(8,128)(2,1)}, bf16[1024,768]{1,0:T(8,128)(2,1)S(1)}, u32[]{:S(2)}, u32[]{:S(2)}) collective-permute-start(bf16[1024,768]{1,0:T(8,128)(2,1)} %get-tuple-element.17.kv_ref.mine), channel_id=1, source_target_pairs={{4,0},{8,4},{12,8},{16,12},{20,16},{24,20},{28,24},{32,28},{36,32}... | collective-permute-start | bytes 4718600 | tf_op jit(solution)/shard_map/ppermute | solution.py:423
  24.7 2.6 %collective-permute-start = (bf16[384,1152]{1,0:T(8,128)(2,1)}, bf16[384,1152]{1,0:T(8,128)(2,1)S(1)}, u32[]{:S(2)}, u32[]{:S(2)}) collective-permute-start(bf16[384,1152]{1,0:T(8,128)(2,1)} %get-tuple-element.20), channel_id=1, source_target_pairs={{0,4},{4,0},{8,12},{12,8},{16,20},{20,16},{24,28},{28,24},{32,36},... | collective-permute-start | bytes 2654216 | tf_op jit(solution)/shard_map/ppermute | solution.py:423
  27.4 7.0 %copy-start.7 = (bf16[384,1152]{1,0:T(8,128)(2,1)}, bf16[384,1152]{1,0:T(8,128)(2,1)S(1)}, u32[]{:S(2)}) copy-start(bf16[384,1152]{1,0:T(8,128)(2,1)S(1)} %collective-permute-done.got_ref) | copy-start | bytes 2654212
  30.1 4.3 %copy-start = (bf16[1024,768]{1,0:T(8,128)(2,1)}, bf16[1024,768]{1,0:T(8,128)(2,1)S(1)}, u32[]{:S(2)}) copy-start(bf16[1024,768]{1,0:T(8,128)(2,1)S(1)} %collective-permute-done.1.before_ref.before) | copy-start | bytes 4718596
  34.4 1.2 copy-start.1
  38.5 16.3 %copy-start.16 = (s32[128]{0:T(128)S(1)}, s32[128]{0:T(128)}, u32[]{:S(2)}) copy-start(s32[128]{0:T(128)} %param.17) | copy-start | bytes 1540
  38.5 40.2 %all-to-all-start = ((bf16[32,8,1920]{2,1,0:T(8,128)(2,1)}), bf16[32,8,1920]{2,1,0:T(8,128)(2,1)S(1)}, u32[]{:S(2)}, u32[]{:S(2)}) async-start(bf16[32,8,1920]{2,1,0:T(8,128)(2,1)} %join.1.dep_ref), calls=%async_computation | async-start | bytes 1966080 | tf_op jit(solution)/shard_map/all_to_all | solution.py:460
  49.5 29.2 %collective-permute-start.3 = (bf16[384,1536]{1,0:T(8,128)(2,1)}, bf16[384,1536]{1,0:T(8,128)(2,1)S(1)}, u32[]{:S(2)}, u32[]{:S(2)}) collective-permute-start(bf16[384,1536]{1,0:T(8,128)(2,1)} %refs_4_.1), channel_id=1, source_target_pairs={{0,1},{1,2},{2,3},{3,0},{4,5},{5,6},{6,7},{7,4},{8,9},{9,10},{10,1... | collective-permute-start | bytes 3538952 | tf_op jit(solution)/shard_map/ppermute | solution.py:441
  50.9 27.8 %collective-permute-start.4 = (bf16[384,1536]{1,0:T(8,128)(2,1)}, bf16[384,1536]{1,0:T(8,128)(2,1)S(1)}, u32[]{:S(2)}, u32[]{:S(2)}) collective-permute-start(bf16[384,1536]{1,0:T(8,128)(2,1)} %refs_4_.1), channel_id=1, source_target_pairs={{0,3},{1,0},{2,1},{3,2},{4,7},{5,4},{6,5},{7,6},{8,11},{9,8},{10,9... | collective-permute-start | bytes 3538952 | tf_op jit(solution)/shard_map/ppermute | solution.py:441
  78.7 1.0 copy-start.3
  78.7 1.4 copy-start.4
  80.1 0.9 copy-start.5
  83.5 36.8 %all-to-all-start.1 = ((bf16[32,8,1920]{2,1,0:T(8,128)(2,1)}), bf16[32,8,1920]{2,1,0:T(8,128)(2,1)S(1)}, u32[]{:S(2)}, u32[]{:S(2)}) async-start(bf16[32,8,1920]{2,1,0:T(8,128)(2,1)} %renorm.1.rest_0_), calls=%async_computation.1 | async-start | bytes 1966080 | tf_op jit(solution)/shard_map/all_to_all | solution.py:460
  92.4 27.9 %collective-permute-start.5 = (bf16[384,1536]{1,0:T(8,128)(2,1)}, bf16[384,1536]{1,0:T(8,128)(2,1)S(1)}, u32[]{:S(2)}, u32[]{:S(2)}) collective-permute-start(bf16[384,1536]{1,0:T(8,128)(2,1)} %refs_4_.1), channel_id=1, source_target_pairs={{0,2},{1,3},{2,0},{3,1},{4,6},{5,7},{6,4},{7,5},{8,10},{9,11},{10,... | collective-permute-start | bytes 3538952 | tf_op jit(solution)/shard_map/ppermute | solution.py:441
  103.1 23.7 %copy-start.15 = (f32[384]{0:T(512)S(1)}, f32[384]{0:T(512)}, u32[]{:S(2)}) copy-start(f32[384]{0:T(512)} %param.15) | copy-start | bytes 4612
  120.3 1.0 copy-start.2
  121.4 0.9 copy-start.6
  124.5 4.6 %collective-permute-start.6 = (bf16[384,1152]{1,0:T(8,128)(2,1)}, bf16[384,1152]{1,0:T(8,128)(2,1)S(1)}, u32[]{:S(2)}, u32[]{:S(2)}) collective-permute-start(bf16[384,1152]{1,0:T(8,128)(2,1)} %unpack.1.own_ref), channel_id=1, source_target_pairs={{0,4},{4,0},{8,12},{12,8},{16,20},{20,16},{24,28},{28,24},{32,36},... | collective-permute-start | bytes 2654216 | tf_op jit(solution)/shard_map/ppermute | solution.py:423
  129.1 0.9 copy-start.8
  137.7 7.5 %collective-permute-start.7 = (bf16[256,384]{1,0:T(8,128)(2,1)}, bf16[256,384]{1,0:T(8,128)(2,1)S(1)}, u32[]{:S(2)}, u32[]{:S(2)}) collective-permute-start(bf16[256,384]{1,0:T(8,128)(2,1)} %get-tuple-element.22), channel_id=1, source_target_pairs={{0,1},{1,2},{2,3},{3,0},{4,5},{5,6},{6,7},{7,4},{8,9},{9,10},{10,1... | collective-permute-start | bytes 589832 | tf_op jit(solution)/shard_map/ppermute | solution.py:441
  138.3 12.2 %collective-permute-start.8 = (bf16[256,384]{1,0:T(8,128)(2,1)}, bf16[256,384]{1,0:T(8,128)(2,1)S(1)}, u32[]{:S(2)}, u32[]{:S(2)}) collective-permute-start(bf16[256,384]{1,0:T(8,128)(2,1)} %get-tuple-element.23), channel_id=1, source_target_pairs={{0,2},{1,3},{2,0},{3,1},{4,6},{5,7},{6,4},{7,5},{8,10},{9,11},{10,... | collective-permute-start | bytes 589832 | tf_op jit(solution)/shard_map/ppermute | solution.py:441
  141.4 9.1 %collective-permute-start.9 = (bf16[256,384]{1,0:T(8,128)(2,1)}, bf16[256,384]{1,0:T(8,128)(2,1)S(1)}, u32[]{:S(2)}, u32[]{:S(2)}) collective-permute-start(bf16[256,384]{1,0:T(8,128)(2,1)} %get-tuple-element.24), channel_id=1, source_target_pairs={{0,3},{1,0},{2,1},{3,2},{4,7},{5,4},{6,5},{7,6},{8,11},{9,8},{10,9... | collective-permute-start | bytes 589832 | tf_op jit(solution)/shard_map/ppermute | solution.py:441
  145.3 5.2 %copy-start.9 = (bf16[256,384]{1,0:T(8,128)(2,1)}, bf16[256,384]{1,0:T(8,128)(2,1)S(1)}, u32[]{:S(2)}) copy-start(bf16[256,384]{1,0:T(8,128)(2,1)S(1)} %collective-permute-done.7.refs_1_) | copy-start | bytes 589828
  150.5 0.7 copy-start.10
  150.5 0.7 copy-start.11
  156.7 6.6 %collective-permute-start.10 = (bf16[256,384]{1,0:T(8,128)(2,1)}, bf16[256,384]{1,0:T(8,128)(2,1)S(1)}, u32[]{:S(2)}, u32[]{:S(2)}) collective-permute-start(bf16[256,384]{1,0:T(8,128)(2,1)} %get-tuple-element.26), channel_id=1, source_target_pairs={{0,1},{1,2},{2,3},{3,0},{4,5},{5,6},{6,7},{7,4},{8,9},{9,10},{10,1... | collective-permute-start | bytes 589832 | tf_op jit(solution)/shard_map/ppermute | solution.py:441
  158.2 11.3 %collective-permute-start.11 = (bf16[256,384]{1,0:T(8,128)(2,1)}, bf16[256,384]{1,0:T(8,128)(2,1)S(1)}, u32[]{:S(2)}, u32[]{:S(2)}) collective-permute-start(bf16[256,384]{1,0:T(8,128)(2,1)} %get-tuple-element.27), channel_id=1, source_target_pairs={{0,2},{1,3},{2,0},{3,1},{4,6},{5,7},{6,4},{7,5},{8,10},{9,11},{10,... | collective-permute-start | bytes 589832 | tf_op jit(solution)/shard_map/ppermute | solution.py:441
  160.5 8.9 %collective-permute-start.12 = (bf16[256,384]{1,0:T(8,128)(2,1)}, bf16[256,384]{1,0:T(8,128)(2,1)S(1)}, u32[]{:S(2)}, u32[]{:S(2)}) collective-permute-start(bf16[256,384]{1,0:T(8,128)(2,1)} %get-tuple-element.28), channel_id=1, source_target_pairs={{0,3},{1,0},{2,1},{3,2},{4,7},{5,4},{6,5},{7,6},{8,11},{9,8},{10,9... | collective-permute-start | bytes 589832 | tf_op jit(solution)/shard_map/ppermute | solution.py:441
  163.3 6.2 %copy-start.12 = (bf16[256,384]{1,0:T(8,128)(2,1)}, bf16[256,384]{1,0:T(8,128)(2,1)S(1)}, u32[]{:S(2)}) copy-start(bf16[256,384]{1,0:T(8,128)(2,1)S(1)} %collective-permute-done.10.refs_1_) | copy-start | bytes 589828
  169.4 0.7 copy-start.13
  169.5 0.7 copy-start.14

commit v5 on v4

--- a/solution.py
+++ b/solution.py
@@ -14,8 +14,9 @@
 XS, ZS, CS, HS = 4, 8, 2, 4
 SHARDS = XS * ZS * CS
 TOKENS = TOK * SHARDS
-SLOTS = XS * ZS
-PACK = 2 * HID + DH
+XROWS = DH // XS
+ROWS = 16
+OWNERS = XROWS // ROWS
 WIDE = HID + DH
 KB = 256
 QB = 256
@@ -41,7 +42,13 @@
 
 
 SWAP_C = [(t, t ^ 1) for t in range(SHARDS)]
-CHIPS = [[chip * CS + c for chip in range(SHARDS // CS)] for c in range(CS)]
+ALONG_Z = [
+    [(x * ZS + z) * CS + c for z in range(ZS)] for x in range(XS) for c in range(CS)
+]
+
+
+def shift_x(d):
+    return [(t, (t + d * ZS * CS) % SHARDS) for t in range(SHARDS)]
 
 
 def shift_h(d):
@@ -132,97 +139,115 @@
     )(pos, kv, rates, first_fast, gate_fast, second_fast)
 
 
-def places():
-    for pair in range(SLOTS // 2):
-        top, mid, low = (slice(24 * pair + 8 * i, 24 * pair + 8 * i + 8) for i in range(3))
-        yield 2 * pair, slice(0, HID), top, slice(0, HID)
-        yield 2 * pair, slice(HID, 2 * HID), mid, slice(0, HID)
-        yield 2 * pair, slice(2 * HID, PACK), top, slice(HID, WIDE)
-        yield 2 * pair + 1, slice(0, HID), low, slice(0, HID)
-        yield 2 * pair + 1, slice(HID, WIDE), mid, slice(HID, WIDE)
-        yield 2 * pair + 1, slice(WIDE, 2 * HID), low, slice(HID, WIDE)
-
-
-def join_kernel(keep_ref, got_ref, before_ref, after_ref, out_ref, total):
-    total[...] = keep_ref[...] + got_ref[...].astype(F32)
-    for slot, to, rows, cols in places():
-        out_ref[slot, :, to] = total[rows, cols].astype(BF)
-    for slot in range(1, SLOTS, 2):
-        out_ref[slot, :, 2 * HID :] = jnp.zeros((8, DH), BF)
-
-
-def join(keep, got, before, after):
-    return pl.pallas_call(
-        join_kernel,
+def rs_x_kernel(pos_ref, keep_ref, got_ref, *rest):
+    outs = rest[-XS:]
+    x = pos_ref[1]
+    for d, out in enumerate(outs):
+        rows = pl.ds(pl.multiple_of(lax.rem(x + d, XS) * XROWS, XROWS), XROWS)
+        out[...] = (keep_ref[rows, :] + got_ref[rows, :].astype(F32)).astype(out.dtype)
+
+
+def rs_x(pos, keep, got, deps):
+    return pl.pallas_call(
+        rs_x_kernel,
         grid=(1,),
-        in_specs=[full((DH, WIDE)), full((DH, WIDE)), DEP, DEP],
-        out_specs=full((SLOTS, 8, PACK)),
-        out_shape=sds((SLOTS, 8, PACK), BF),
-        scratch_shapes=[pltpu.VMEM((DH, WIDE), F32)],
-        compiler_params=params(),
-        name="join",
-    )(keep, got, before, after)
-
-
-def renorm_kernel(pos_ref, old_ref, got_ref, *rest):
+        in_specs=[SMEM, full((DH, WIDE)), full((DH, WIDE))] + [DEP] * len(deps),
+        out_specs=[full((XROWS, WIDE))] * XS,
+        out_shape=[sds((XROWS, WIDE), F32)] + [sds((XROWS, WIDE), BF)] * (XS - 1),
+        compiler_params=params(),
+        name="rs_x",
+    )(pos, keep, got, *deps)
+
+
+def rs_z_kernel(own_ref, g1, g2, g3, *rest):
     out = rest[-1]
-    odd = pos_ref[1] == 1
+    for o in range(OWNERS):
+        rows = slice(o * ROWS, (o + 1) * ROWS)
+        total = (own_ref[rows, :] + g1[rows, :].astype(F32)) + (
+            g2[rows, :].astype(F32) + g3[rows, :].astype(F32)
+        )
+        out[o] = total.astype(BF)
+    out[OWNERS:] = jnp.zeros((ZS - OWNERS, ROWS, WIDE), BF)
+
+
+def rs_z(own, got, deps):
+    return pl.pallas_call(
+        rs_z_kernel,
+        grid=(1,),
+        in_specs=[full((XROWS, WIDE))] * XS + [DEP] * len(deps),
+        out_specs=full((ZS, ROWS, WIDE)),
+        out_shape=sds((ZS, ROWS, WIDE), BF),
+        compiler_params=params(),
+        name="rs_z",
+    )(own, *got, *deps)
+
+
+def renorm_kernel(old_ref, got_ref, *rest):
+    out = rest[-1]
     update = got_ref[0].astype(F32)
-    for s in range(1, SLOTS):
+    for s in range(1, ZS):
         update = update + got_ref[s].astype(F32)
     old = old_ref[...]
     fresh = old + update
-
-    def squares(value):
-        u = [
-            jnp.sum(jnp.square(value[:, i * DH : (i + 1) * DH]), axis=1, keepdims=True)
-            for i in range(PACK // DH)
-        ]
-        wide = u[2] + u[3]
-        return (
-            (0, HID, u[0] + u[1]),
-            (HID, WIDE, jnp.where(odd, u[2], wide)),
-            (WIDE, 2 * HID, jnp.where(odd, u[3], wide)),
-            (2 * HID, PACK, u[4]),
-        )
-
-    for (lo, hi, w_sq), (_, _, f_sq) in zip(squares(old), squares(fresh)):
-        new = (fresh[:, lo:hi] * (jnp.sqrt(w_sq) / jnp.sqrt(f_sq + 1e-6))).astype(BF)
-        for s in range(SLOTS):
-            out[s, :, lo:hi] = new
-
-
-def renorm(pos, old, got, deps):
-    shape = (SLOTS, 8, PACK)
+    for cols in (slice(0, HID), slice(HID, WIDE)):
+        w, f = old[:, cols], fresh[:, cols]
+        w_sq = jnp.sum(w * w, axis=1, keepdims=True)
+        f_sq = jnp.sum(f * f, axis=1, keepdims=True)
+        new = (f * (jnp.sqrt(w_sq) / jnp.sqrt(f_sq + 1e-6))).astype(BF)
+        for s in range(ZS):
+            out[s, :, cols] = new
+
+
+def renorm(old, got, deps):
+    shape = (ZS, ROWS, WIDE)
     return pl.pallas_call(
         renorm_kernel,
         grid=(1,),
-        in_specs=[SMEM, full((8, PACK)), full(shape)] + [DEP] * len(deps),
+        in_specs=[full((ROWS, WIDE)), full(shape)] + [DEP] * len(deps),
         out_specs=full(shape),
         out_shape=sds(shape, BF),
         compiler_params=params(),
         name="renorm",
-    )(pos, old, got, *deps)
-
-
-def unpack_kernel(got_ref, *rest):
-    out, total = rest[-2:]
-    for slot, to, rows, cols in places():
-        total[rows, cols] = got_ref[slot, :, to].astype(F32)
-    out[...] = total[...].astype(BF)
-
-
-def unpack(got, deps):
-    return pl.pallas_call(
-        unpack_kernel,
+    )(old, got, *deps)
+
+
+def owned_kernel(got_ref, *rest):
+    out, sem = rest[-2:]
+    copy = pltpu.make_async_copy(got_ref.at[pl.ds(0, OWNERS)], out, sem)
+    copy.start()
+    copy.wait()
+
+
+def owned(got, deps):
+    return pl.pallas_call(
+        owned_kernel,
+        in_specs=[DEP] * (1 + len(deps)),
+        out_specs=DEP,
+        out_shape=sds((OWNERS, ROWS, WIDE), BF),
+        scratch_shapes=[pltpu.SemaphoreType.DMA],
+        compiler_params=params(),
+        name="owned",
+    )(got, *deps)
+
+
+def ag_x_kernel(pos_ref, *rest):
+    blocks, out = rest[:XS], rest[-1]
+    x = pos_ref[1]
+    for d, block in enumerate(blocks):
+        owner = lax.rem(x - d + XS, XS)
+        out[pl.ds(pl.multiple_of(owner * XROWS, XROWS), XROWS), :] = block[...]
+
+
+def ag_x(pos, blocks):
+    return pl.pallas_call(
+        ag_x_kernel,
         grid=(1,),
-        in_specs=[full((SLOTS, 8, PACK))] + [DEP] * len(deps),
+        in_specs=[SMEM] + [full((XROWS, WIDE))] * XS,
         out_specs=full((DH, WIDE)),
         out_shape=sds((DH, WIDE), BF),
-        scratch_shapes=[pltpu.VMEM((DH, WIDE), F32)],
-        compiler_params=params(),
-        name="unpack",
-    )(got, *deps)
+        compiler_params=params(),
+        name="ag_x",
+    )(pos, *blocks)
 
 
 def project_kernel(t_ref, w_ref, dep_ref, q_ref):
@@ -275,17 +300,22 @@
         col = lax.broadcasted_iota(I32, (QB, KB), 1) + kb * KB
         sc = jnp.where((col >= begin) & (col < end), sc, -1e30)
         s_ref[kb] = sc
-        return jnp.maximum(top, jnp.max(sc, axis=1, keepdims=True))
-
-    top = segments(scores, jnp.full((QB, 1), -1e30, F32))
+        for lane in range(0, KB, 128):
+            top = jnp.maximum(top, sc[:, lane : lane + 128])
+        return top
+
+    top = segments(scores, jnp.full((QB, 128), -1e30, F32))
+    top = jnp.max(top, axis=1, keepdims=True)
 
     def weigh(kb, total):
         w = jnp.exp(s_ref[kb] - top)
         s_ref[kb] = w
-        return total + jnp.sum(w, axis=1, keepdims=True)
-
-    total = lax.fori_loop(first, last, weigh, jnp.zeros((QB, 1), F32))
-    inverse = 1.0 / total
+        for lane in range(0, KB, 128):
+            total = total + w[:, lane : lane + 128]
+        return total
+
+    total = lax.fori_loop(first, last, weigh, jnp.zeros((QB, 128), F32))
+    inverse = 1.0 / jnp.sum(total, axis=1, keepdims=True)
     out_ref[...] = jnp.zeros_like(out_ref)
 
     def gather(s, ref, kb, carry):
@@ -364,42 +394,60 @@
 
 def output_kernel(pos_ref, *refs):
     parts, weights, outs = refs[:HS], refs[HS : 2 * HS], refs[2 * HS :]
+    total = mm(parts[0][...], weights[0][...])
+    for part, weight in zip(parts[1:], weights[1:]):
+        total = total + mm(part[...], weight[...])
+    total = total.astype(BF)
+    for step in range(HS):
+
+        @pl.when(pl.program_id(0) == step)
+        def _():
+            outs[step][...] = total
+
+
+def output(pos, parts, weight):
+    rows = pl.BlockSpec((QB, DH), lambda i, pos: (0, 0))
+    cols = [
+        pl.BlockSpec(
+            (DH, DH),
+            lambda i, pos, d=d: (lax.rem(pos[2] - d + HS, HS), lax.rem(pos[2] + i + 1, HS)),
+        )
+        for d in range(HS)
+    ]
+    return pl.pallas_call(
+        output_kernel,
+        grid_spec=pltpu.PrefetchScalarGridSpec(
+            num_scalar_prefetch=1,
+            grid=(HS,),
+            in_specs=[rows] * HS + cols,
+            out_specs=[rows] * HS,
+        ),
+        out_shape=[sds((QB, DH), BF)] * HS,
+        compiler_params=params(),
+        name="output",
+    )(pos, *parts, *[weight] * HS)
+
+
+def arrange_kernel(pos_ref, *refs):
+    parts, out, sems = refs[:HS], refs[HS], refs[HS + 1]
     head = pos_ref[2]
-    for e, out in enumerate(outs):
-        cols = pl.ds(pl.multiple_of(lax.rem(head + e + 1, HS) * DH, DH), DH)
-        total = mm(parts[0][...], weights[0][:, cols])
-        for part, weight in zip(parts[1:], weights[1:]):
-            total = total + mm(part[...], weight[:, cols])
-        out[...] = total.astype(BF)
-
-
-def output(pos, parts, weights):
-    return pl.pallas_call(
-        output_kernel,
-        grid=(1,),
-        in_specs=[SMEM] + [full((QB, DH))] * HS + [full((DH, HS * DH))] * HS,
-        out_specs=[full((QB, DH))] * HS,
-        out_shape=[sds((QB, DH), BF)] * HS,
-        compiler_params=params(),
-        name="output",
-    )(pos, *parts, *weights)
-
-
-def arrange_kernel(pos_ref, *refs):
-    parts, out = refs[:-1], refs[-1]
-    head = pos_ref[2]
+    copies = []
     for d, part in enumerate(parts):
         rows = pl.ds(pl.multiple_of(lax.rem(head - d + HS, HS) * QB, QB), QB)
-        out[rows, :] = part[...]
+        copies.append(pltpu.make_async_copy(part, out.at[rows, :], sems.at[d]))
+    for copy in copies:
+        copy.start()
+    for copy in copies:
+        copy.wait()
 
 
 def arrange(pos, parts):
     return pl.pallas_call(
         arrange_kernel,
-        grid=(1,),
-        in_specs=[SMEM] + [full((QB, DH))] * HS,
-        out_specs=full((TOK, DH)),
+        in_specs=[SMEM] + [DEP] * HS,
+        out_specs=DEP,
         out_shape=sds((TOK, DH), BF),
+        scratch_shapes=[pltpu.SemaphoreType.DMA((HS,))],
         compiler_params=params(),
         name="arrange",
     )(pos, *parts)
@@ -418,15 +466,14 @@
 ):
     mine = lax.axis_index("tok")
     head = lax.axis_index("head")
-    chip, core = mine // CS, mine % CS
-    odd = chip % 2
+    x, z, core = mine // (ZS * CS), mine // CS % ZS, mine % CS
     send = lambda value, pairs: lax.ppermute(value, "tok", pairs)
 
     kv, rates = keys(tokens, qkv_weight, rate_weight)
     up = [(i, i + 1) for i in range(SHARDS - 1)]
     before = send(kv, up)
     after = send(kv, [(j, i) for i, j in up])
-    pos = jnp.stack([core, odd, head, mine]).astype(I32)
+    pos = jnp.stack([core, x, head, mine]).astype(I32)
     give, keep = update(pos, kv, rates, first_fast, gate_fast, second_fast)
     got = send(give, SWAP_C)
 
@@ -440,39 +487,38 @@
     def spread(parts):
         return [lax.ppermute(p, "head", shift_h(d)) if d else p for d, p in enumerate(parts)]
 
-    weights = spread([out_weight] * HS)
-
-    base = chip // 2 * 24
-    wide = lambda at: jnp.where(
-        core == 0,
-        lax.dynamic_slice_in_dim(first_fast[0], at, 8, 0),
-        lax.dynamic_slice_in_dim(gate_fast[0], at, 8, 0),
-    )
-    narrow = lambda at: lax.dynamic_slice_in_dim(second_fast[0], core * DH + at, 8, 0)
-    middle = jnp.where(
-        odd == 1,
-        jnp.concatenate([narrow(base + 8), narrow(base + 16)], axis=1),
-        wide(base + 8),
-    )
-    old = jnp.concatenate([wide(base + 16 * odd), middle, narrow(base)], axis=1).astype(F32)
+    weight = lax.all_gather(out_weight, "head", axis=0, tiled=True)
+
+    row = jnp.minimum(x * XROWS + z * ROWS, DH - ROWS)
+    pick = lambda w, at: lax.dynamic_slice_in_dim(w[0], at, ROWS, 0)
+    old = jnp.concatenate(
+        [
+            jnp.where(core == 0, pick(first_fast, row), pick(gate_fast, row)),
+            pick(second_fast, core * DH + row),
+        ],
+        axis=1,
+    ).astype(F32)
 
     def exchange(blocks):
-        return lax.all_to_all(blocks, "tok", 0, 0, axis_index_groups=CHIPS)
-
-    total = join(keep, got, before, after)
+        return lax.all_to_all(blocks, "tok", 0, 0, axis_index_groups=ALONG_Z)
+
+    own, *gives = rs_x(pos, keep, got, [before, after])
+    got = [send(g, shift_x(d + 1)) for d, g in enumerate(gives)]
+    query = project(tokens, qkv_weight, own)
+    att = functools.partial(attend, pos=pos, ends=ends, query=query, before=before, mine=kv, after=after)
+    total = rs_z(own, got, [query])
     got = exchange(total)
-    query = project(tokens, qkv_weight, total)
-    att = functools.partial(attend, pos=pos, ends=ends, query=query, before=before, mine=kv, after=after)
-    att_low = att(0, 2, dep=query, buffer=None)
-    fresh = renorm(pos, old, got, [att_low, weights[1], weights[3]])
+    att_low = att(0, 2, dep=total, buffer=None)
+    fresh = renorm(old, got, [att_low])
     got = exchange(fresh)
     attended = att(2, 2, dep=fresh, buffer=att_low)
-    half = unpack(got, [attended, weights[2]])
+    block = owned(got, [attended, weight]).reshape(XROWS, WIDE)
+    half = ag_x(pos, [block] + [send(block, shift_x(d)) for d in range(1, XS)])
     other = send(half, SWAP_C)
 
     ahead = apply(pos, query, half, other, attended, fast_gain[None, :])
     parts = spread([ahead[-1], *ahead[:-1]])
-    ahead = output(pos, parts, weights)
+    ahead = output(pos, parts, weight)
     result = arrange(pos, spread([ahead[-1], *ahead[:-1]]))
     return result
 

time: 173 us -> 209 us (1.21)
  Pallas kernels: 65.6 us -> 96.8 us
  between operations: 0.12 us -> 13.5 us
  waiting for transfers between devices: 52.1 us -> 39 us
  starting transfers between devices: 41.9 us -> 46.8 us
    pallas_call x5 -> x7, Pallas kernels: 15.2 us -> 49.2 us  [the longest x1 25.6 us: arrange(): pl.pallas_call(arrange_kernel, in_specs=[SMEM] + [DEP] * HS, out_specs=DE...]
    ppermute x9 -> x6, waiting for transfers between devices: 40.7 us -> 16.8 us  [spread(): lax.ppermute(p, 'head', shift_h(d))]
    ppermute x4 -> x10, starting transfers between devices: 9.13 us -> 20.1 us  [body(): send = lambda value, pairs: lax.ppermute(value, 'tok', pairs)]
    ppermute x4 -> x10, waiting for transfers between devices: 11.3 us -> 20.3 us  [body(): send = lambda value, pairs: lax.ppermute(value, 'tok', pairs)]
    ppermute x9 -> x6, starting transfers between devices: 12.9 us -> 8.85 us  [spread(): lax.ppermute(p, 'head', shift_h(d))]
    pallas_call x2, Pallas kernels: 20.3 us -> 17.3 us  [attend(): pl.pallas_call(functools.partial(attend_kernel, start), grid=(count,), in...]
    all_to_all x2, starting transfers between devices: 19.9 us -> 17.8 us  [exchange(): return lax.all_to_all(blocks, 'tok', 0, 0, axis_index_groups=ALONG_Z)]
    unnamed x34 -> x40, local copies, waits for them, and re-layouts: 7.94 us -> 7.21 us
  transfers between devices with their start and end apart: 15 -> 19, of which waited for: 10 -> 14; matrix products, arithmetic and copies ran while one was open for 3% -> 2% of each run, Pallas kernels for 20% -> 23%
where the time goes in v5:
time: 209 us; the launch traced here: 207 us
  Pallas kernels  96.8 us (46%)
  starting transfers between devices  46.8 us (22%)
  waiting for transfers between devices  39 us (19%)
  between operations  13.5 us (6%)
  local copies, waits for them, and re-layouts  8.53 us (4%)
  other arithmetic  2.78 us (1%)
    pallas_call x1, Pallas kernels, arrange(): pl.pallas_call(arrange_kernel, in_specs=[SMEM] + [DEP] * HS, out_specs=DE...  25.6 us
    ppermute x10, waiting for transfers between devices, body(): send = lambda value, pairs: lax.ppermute(value, 'tok', pairs)  20.3 us
    ppermute x10, starting transfers between devices, body(): send = lambda value, pairs: lax.ppermute(value, 'tok', pairs)  20.1 us
    all_to_all x2, starting transfers between devices, exchange(): return lax.all_to_all(blocks, 'tok', 0, 0, axis_index_groups=ALONG_Z)  17.8 us
    pallas_call x2, Pallas kernels, attend(): pl.pallas_call(functools.partial(attend_kernel, start), grid=(count,), in...  17.3 us
    ppermute x6, waiting for transfers between devices, spread(): lax.ppermute(p, 'head', shift_h(d))  16.8 us
    pallas_call x1, Pallas kernels, update(): pl.pallas_call(update_kernel, grid=(1,), in_specs=[SMEM, full(kv.shape),...  9.74 us
    ppermute x6, starting transfers between devices, spread(): lax.ppermute(p, 'head', shift_h(d))  8.85 us
  transfers between devices with their start and end apart: 19, of which 14 were waited for; matrix products, arithmetic and copies ran while one was open for 2% of the time, Pallas kernels for 23%

profile of v5, /device:TPU:1, one launch (start us, length us, event | category | flops | bytes accessed | tf_op | source)
XLA Modules:
  0.0 207.5 jit_solution(13999887986070781336)
XLA Ops:
  7.3 7.6 %keys.1 = (bf16[1024,768]{1,0:T(8,128)(2,1)}, f32[1024,3]{1,0:T(8,128)}) custom-call(bf16[1024,1536]{1,0:T(8,128)(2,1)} %t_ref.3, bf16[1536,1152]{1,0:T(8,128)(2,1)} %w_ref.1, bf16[1536,1152]{1,0:T(8,128)(2,1)} %w_ref.1, bf16[3,1536]{1,0:T(4,128)(2,1)} %bitcast.15), custom_call_target="tpu_custom_call" | custom-call | tf_op jit(solution)/shard_map/keys/pallas_call | solution.py:75
  14.8 4.9 %collective-permute-start.1 = (bf16[1024,768]{1,0:T(8,128)(2,1)}, bf16[1024,768]{1,0:T(8,128)(2,1)S(1)}, u32[]{:S(2)}, u32[]{:S(2)}) collective-permute-start(bf16[1024,768]{1,0:T(8,128)(2,1)} %get-tuple-element.21.kv_ref.mine), channel_id=1, source_target_pairs={{0,4},{4,8},{8,12},{12,16},{16,20},{20,24},{24,28},{28,32},{32,36}... | collective-permute-start | bytes 4718600 | tf_op jit(solution)/shard_map/ppermute | solution.py:470
  19.8 1.9 collective-permute-start.2
  22.4 9.7 %update.1 = (bf16[384,1152]{1,0:T(8,128)(2,1)}, f32[384,1152]{1,0:T(8,128)}) custom-call(s32[4]{0:T(128)} %pad_add_fusion.pos_ref, bf16[1024,768]{1,0:T(8,128)(2,1)} %get-tuple-element.21.kv_ref.mine, f32[1024,3]{1,0:T(8,128)} %get-tuple-element.22.r_ref, bf16[1,384,768]{2,1,0:T(8,128)(2,1)} %w1_ref.1, bf16[1,384,768]{2,1,0:T(8,128)(2,1)} %w3_ref.1, ...), custom_call_target="tpu_custom_call" | custom-call | tf_op jit(solution)/shard_map/update/pallas_call | solution.py:123
  32.1 2.6 %collective-permute-done.got_ref = bf16[384,1152]{1,0:T(8,128)(2,1)S(1)} collective-permute-done((bf16[384,1152]{1,0:T(8,128)(2,1)}, bf16[384,1152]{1,0:T(8,128)(2,1)S(1)}, u32[]{:S(2)}, u32[]{:S(2)}) %collective-permute-start) | collective-permute-done | bytes 884768 | tf_op jit(solution)/shard_map/ppermute | solution.py:470
  34.7 2.7 %collective-permute-done.1.rest_0_.before = bf16[1024,768]{1,0:T(8,128)(2,1)S(1)} collective-permute-done((bf16[1024,768]{1,0:T(8,128)(2,1)}, bf16[1024,768]{1,0:T(8,128)(2,1)S(1)}, u32[]{:S(2)}, u32[]{:S(2)}) %collective-permute-start.1) | collective-permute-done | bytes 1572896 | tf_op jit(solution)/shard_map/ppermute | solution.py:470
  37.4 4.7 %collective-permute-done.2.rest_1_.after = bf16[1024,768]{1,0:T(8,128)(2,1)S(1)} collective-permute-done((bf16[1024,768]{1,0:T(8,128)(2,1)}, bf16[1024,768]{1,0:T(8,128)(2,1)S(1)}, u32[]{:S(2)}, u32[]{:S(2)}) %collective-permute-start.2) | collective-permute-done | bytes 1572896 | tf_op jit(solution)/shard_map/ppermute | solution.py:470
  43.3 3.0 %rs_x.1 = (f32[96,1152]{1,0:T(8,128)}, bf16[96,1152]{1,0:T(8,128)(2,1)}, bf16[96,1152]{1,0:T(8,128)(2,1)}, bf16[96,1152]{1,0:T(8,128)(2,1)}) custom-call(s32[4]{0:T(128)} %pad_add_fusion.pos_ref, f32[384,1152]{1,0:T(8,128)} %get-tuple-element.23.keep_ref, bf16[384,1152]{1,0:T(8,128)(2,1)} %copy-done.5, bf16[1024,768]{1,0:T(8,128)(2,1)} %copy-done, ...), custom_call_target="tpu_custom_call" | custom-call | tf_op jit(solution)/shard_map/rs_x/pallas_call | solution.py:151
  47.5 2.4 %collective-permute-start.4 = (bf16[96,1152]{1,0:T(8,128)(2,1)}, bf16[96,1152]{1,0:T(8,128)(2,1)S(1)}, u32[]{:S(2)}, u32[]{:S(2)}) collective-permute-start(bf16[96,1152]{1,0:T(8,128)(2,1)} %get-tuple-element.27), channel_id=1, source_target_pairs={{0,128},{4,132},{8,136},{12,140},{16,144},{20,148},{24,152},{28,15... | collective-permute-start | bytes 663560 | tf_op jit(solution)/shard_map/ppermute | solution.py:470
  51.1 5.2 %project.1.rest_0_.q_ref = bf16[1024,384]{1,0:T(8,128)(2,1)} custom-call(bf16[1024,1536]{1,0:T(8,128)(2,1)} %t_ref.3, bf16[1536,1152]{1,0:T(8,128)(2,1)} %w_ref.1, f32[96,1152]{1,0:T(8,128)} %get-tuple-element.25.dep_ref.own_ref), custom_call_target="tpu_custom_call" | custom-call | tf_op jit(solution)/shard_map/project/pallas_call | solution.py:260
  56.3 2.2 %collective-permute-done.4.g2 = bf16[96,1152]{1,0:T(8,128)(2,1)S(1)} collective-permute-done((bf16[96,1152]{1,0:T(8,128)(2,1)}, bf16[96,1152]{1,0:T(8,128)(2,1)S(1)}, u32[]{:S(2)}, u32[]{:S(2)}) %collective-permute-start.4) | collective-permute-done | bytes 221216 | tf_op jit(solution)/shard_map/ppermute | solution.py:470
  59.9 2.1 rs_z.1.rest_0_
  61.9 9.1 %all-to-all-start = ((bf16[8,16,1152]{2,1,0:T(8,128)(2,1)}), bf16[8,16,1152]{2,1,0:T(8,128)(2,1)S(1)}, u32[]{:S(2)}, u32[]{:S(2)}) async-start(bf16[8,16,1152]{2,1,0:T(8,128)(2,1)} %rs_z.1.rest_0_), calls=%async_computation | async-start | bytes 589824 | tf_op jit(solution)/shard_map/all_to_all | solution.py:503
  73.9 7.0 %attend_0.1.rest_0_.rest_1_ = f32[1024,384]{1,0:T(8,128)} custom-call(s32[4]{0:T(128)} %pad_add_fusion.pos_ref, s32[1,128]{1,0:T(1,128)} %bitcast.16, bf16[1024,384]{1,0:T(8,128)(2,1)} %project.1.rest_0_.q_ref, bf16[1024,768]{1,0:T(8,128)(2,1)} %copy-done, bf16[1024,768]{1,0:T(8,128)(2,1)} %get-tuple-element.21.kv_ref.mine, bf16[1024,768]{1,0:T(8,128)(2,1)} %copy-done.1, ...), custom_call_target="tpu_custom_call" | custom-call | tf_op jit(solution)/shard_map/attend_0/pallas_call | solution.py:333
  82.4 1.9 renorm.1.rest_0_
  84.3 8.7 %all-to-all-start.1 = ((bf16[8,16,1152]{2,1,0:T(8,128)(2,1)}), bf16[8,16,1152]{2,1,0:T(8,128)(2,1)S(1)}, u32[]{:S(2)}, u32[]{:S(2)}) async-start(bf16[8,16,1152]{2,1,0:T(8,128)(2,1)} %renorm.1.rest_0_), calls=%async_computation.1 | async-start | bytes 589824 | tf_op jit(solution)/shard_map/all_to_all | solution.py:503
  93.0 10.3 %attend_2.1.rest_0_.att_ref = f32[1024,384]{1,0:T(8,128)} custom-call(s32[4]{0:T(128)} %pad_add_fusion.pos_ref, s32[1,128]{1,0:T(1,128)} %bitcast.17, bf16[1024,384]{1,0:T(8,128)(2,1)} %project.1.rest_0_.q_ref, bf16[1024,768]{1,0:T(8,128)(2,1)} %copy-done, bf16[1024,768]{1,0:T(8,128)(2,1)} %get-tuple-element.21.kv_ref.mine, ...), custom_call_target="tpu_custom_call", output_to_operand_aliasing={{}: (7, {})} | custom-call | tf_op jit(solution)/shard_map/attend_2/pallas_call | solution.py:333
  104.3 7.8 %owned.1 = bf16[6,16,1152]{2,1,0:T(8,128)(2,1)} custom-call(bf16[8,16,1152]{2,1,0:T(8,128)(2,1)} %copy-done.3, f32[1024,384]{1,0:T(8,128)} %attend_2.1.rest_0_.att_ref, bf16[1536,1536]{1,0:T(8,128)(2,1)} %all-gather.2.cloned.1.call-done.rest_1_.refs_4_.refs_5_.refs_6_.refs_7_), custom_call_target="tpu_custom_call" | custom-call | tf_op jit(solution)/shard_map/owned/pallas_call | solution.py:222
  116.3 3.9 %collective-permute-done.6.rest_1_ = bf16[96,1152]{1,0:T(8,128)(2,1)S(1)} collective-permute-done((bf16[96,1152]{1,0:T(8,128)(2,1)}, bf16[96,1152]{1,0:T(8,128)(2,1)S(1)}, u32[]{:S(2)}, u32[]{:S(2)}) %collective-permute-start.6) | collective-permute-done | bytes 221216 | tf_op jit(solution)/shard_map/ppermute | solution.py:470
  120.2 1.7 collective-permute-done.7.rest_2_
  123.4 2.3 %ag_x.1.own_ref = bf16[384,1152]{1,0:T(8,128)(2,1)} custom-call(s32[4]{0:T(128)} %pad_add_fusion.pos_ref, bf16[96,1152]{1,0:T(8,128)(2,1)} %bitcast.14, bf16[96,1152]{1,0:T(8,128)(2,1)} %copy-done.9, bf16[96,1152]{1,0:T(8,128)(2,1)} %copy-done.10, bf16[96,1152]{1,0:T(8,128)(2,1)} %copy-done.11), custom_call_target="tpu_custom_call" | custom-call | tf_op jit(solution)/shard_map/ag_x/pallas_call | solution.py:242
  125.7 4.3 %collective-permute-start.9 = (bf16[384,1152]{1,0:T(8,128)(2,1)}, bf16[384,1152]{1,0:T(8,128)(2,1)S(1)}, u32[]{:S(2)}, u32[]{:S(2)}) collective-permute-start(bf16[384,1152]{1,0:T(8,128)(2,1)} %ag_x.1.own_ref), channel_id=1, source_target_pairs={{0,4},{4,0},{8,12},{12,8},{16,20},{20,16},{24,28},{28,24},{32,36},... | collective-permute-start | bytes 2654216 | tf_op jit(solution)/shard_map/ppermute | solution.py:470
  130.6 1.7 collective-permute-done.9.other_ref
  133.3 7.8 %apply.1 = (bf16[256,384]{1,0:T(8,128)(2,1)}, bf16[256,384]{1,0:T(8,128)(2,1)}, bf16[256,384]{1,0:T(8,128)(2,1)}, bf16[256,384]{1,0:T(8,128)(2,1)}) custom-call(s32[4]{0:T(128)} %pad_add_fusion.pos_ref, bf16[1024,384]{1,0:T(8,128)(2,1)} %project.1.rest_0_.q_ref, bf16[384,1152]{1,0:T(8,128)(2,1)} %ag_x.1.own_ref, bf16[384,1152]{1,0:T(8,128)(2,1)} %copy-done.4, ...), custom_call_target="tpu_custom_call" | custom-call | tf_op jit(solution)/shard_map/apply/pallas_call | solution.py:381
  142.5 2.7 %collective-permute-start.11 = (bf16[256,384]{1,0:T(8,128)(2,1)}, bf16[256,384]{1,0:T(8,128)(2,1)S(1)}, u32[]{:S(2)}, u32[]{:S(2)}) collective-permute-start(bf16[256,384]{1,0:T(8,128)(2,1)} %get-tuple-element.31), channel_id=1, source_target_pairs={{0,2},{1,3},{2,0},{3,1},{4,6},{5,7},{6,4},{7,5},{8,10},{9,11},{10,... | collective-permute-start | bytes 589832 | tf_op jit(solution)/shard_map/ppermute | solution.py:488
  146.1 2.9 %collective-permute-done.10.refs_1_ = bf16[256,384]{1,0:T(8,128)(2,1)S(1)} collective-permute-done((bf16[256,384]{1,0:T(8,128)(2,1)}, bf16[256,384]{1,0:T(8,128)(2,1)S(1)}, u32[]{:S(2)}, u32[]{:S(2)}) %collective-permute-start.10) | collective-permute-done | bytes 196640 | tf_op jit(solution)/shard_map/ppermute | solution.py:488
  149.1 5.2 %collective-permute-done.11.refs_2_ = bf16[256,384]{1,0:T(8,128)(2,1)S(1)} collective-permute-done((bf16[256,384]{1,0:T(8,128)(2,1)}, bf16[256,384]{1,0:T(8,128)(2,1)S(1)}, u32[]{:S(2)}, u32[]{:S(2)}) %collective-permute-start.11) | collective-permute-done | bytes 196640 | tf_op jit(solution)/shard_map/ppermute | solution.py:488
  155.0 6.6 %output.1 = (bf16[256,384]{1,0:T(8,128)(2,1)}, bf16[256,384]{1,0:T(8,128)(2,1)}, bf16[256,384]{1,0:T(8,128)(2,1)}, bf16[256,384]{1,0:T(8,128)(2,1)}) custom-call(s32[4]{0:T(128)} %pad_add_fusion.pos_ref, bf16[256,384]{1,0:T(8,128)(2,1)} %get-tuple-element.29.refs_0_, bf16[256,384]{1,0:T(8,128)(2,1)} %copy-done.12, bf16[256,384]{1,0:T(8,128)(2,1)} %copy-done.13, ...), custom_call_target="tpu_custom_call" | custom-call | tf_op jit(solution)/shard_map/output/pallas_call | solution.py:417
  162.6 2.7 %collective-permute-start.14 = (bf16[256,384]{1,0:T(8,128)(2,1)}, bf16[256,384]{1,0:T(8,128)(2,1)S(1)}, u32[]{:S(2)}, u32[]{:S(2)}) collective-permute-start(bf16[256,384]{1,0:T(8,128)(2,1)} %get-tuple-element.35), channel_id=1, source_target_pairs={{0,2},{1,3},{2,0},{3,1},{4,6},{5,7},{6,4},{7,5},{8,10},{9,11},{10,... | collective-permute-start | bytes 589832 | tf_op jit(solution)/shard_map/ppermute | solution.py:488
  165.5 2.7 %collective-permute-done.13.refs_1_ = bf16[256,384]{1,0:T(8,128)(2,1)S(1)} collective-permute-done((bf16[256,384]{1,0:T(8,128)(2,1)}, bf16[256,384]{1,0:T(8,128)(2,1)S(1)}, u32[]{:S(2)}, u32[]{:S(2)}) %collective-permute-start.13) | collective-permute-done | bytes 196640 | tf_op jit(solution)/shard_map/ppermute | solution.py:488
  168.2 6.0 %collective-permute-done.14.refs_2_ = bf16[256,384]{1,0:T(8,128)(2,1)S(1)} collective-permute-done((bf16[256,384]{1,0:T(8,128)(2,1)}, bf16[256,384]{1,0:T(8,128)(2,1)S(1)}, u32[]{:S(2)}, u32[]{:S(2)}) %collective-permute-start.14) | collective-permute-done | bytes 196640 | tf_op jit(solution)/shard_map/ppermute | solution.py:488
  175.0 25.6 %arrange.1 = bf16[1024,384]{1,0:T(8,128)(2,1)} custom-call(s32[4]{0:T(128)} %pad_add_fusion.pos_ref, bf16[256,384]{1,0:T(8,128)(2,1)} %get-tuple-element.33.refs_0_, bf16[256,384]{1,0:T(8,128)(2,1)} %copy-done.15, bf16[256,384]{1,0:T(8,128)(2,1)} %copy-done.16, bf16[256,384]{1,0:T(8,128)(2,1)} %copy-done.17), custom_call_target="tpu_custom_call" | custom-call | tf_op jit(solution)/shard_map/arrange/pallas_call | solution.py:445
  (66 shorter events, 23.9 us)
Async XLA Ops:
  6.5 97.1 %all-gather.2.cloned.1.call-start = ((), (), s32[]{:S(2)}) async-start(), calls=%async_computation.2 | async-start | bytes 5898240 | tf_op jit(solution)/shard_map/all_gather | solution.py:490
  14.8 22.6 %collective-permute-start.1 = (bf16[1024,768]{1,0:T(8,128)(2,1)}, bf16[1024,768]{1,0:T(8,128)(2,1)S(1)}, u32[]{:S(2)}, u32[]{:S(2)}) collective-permute-start(bf16[1024,768]{1,0:T(8,128)(2,1)} %get-tuple-element.21.kv_ref.mine), channel_id=1, source_target_pairs={{0,4},{4,8},{8,12},{12,16},{16,20},{20,24},{24,28},{28,32},{32,36}... | collective-permute-start | bytes 4718600 | tf_op jit(solution)/shard_map/ppermute | solution.py:470
  19.8 22.3 %collective-permute-start.2 = (bf16[1024,768]{1,0:T(8,128)(2,1)}, bf16[1024,768]{1,0:T(8,128)(2,1)S(1)}, u32[]{:S(2)}, u32[]{:S(2)}) collective-permute-start(bf16[1024,768]{1,0:T(8,128)(2,1)} %get-tuple-element.21.kv_ref.mine), channel_id=1, source_target_pairs={{4,0},{8,4},{12,8},{16,12},{20,16},{24,20},{28,24},{32,28},{36,32}... | collective-permute-start | bytes 4718600 | tf_op jit(solution)/shard_map/ppermute | solution.py:470
  32.1 2.6 %collective-permute-start = (bf16[384,1152]{1,0:T(8,128)(2,1)}, bf16[384,1152]{1,0:T(8,128)(2,1)S(1)}, u32[]{:S(2)}, u32[]{:S(2)}) collective-permute-start(bf16[384,1152]{1,0:T(8,128)(2,1)} %get-tuple-element.24), channel_id=1, source_target_pairs={{0,4},{4,0},{8,12},{12,8},{16,20},{20,16},{24,28},{28,24},{32,36},... | collective-permute-start | bytes 2654216 | tf_op jit(solution)/shard_map/ppermute | solution.py:470
  34.7 7.4 %copy-start.5 = (bf16[384,1152]{1,0:T(8,128)(2,1)}, bf16[384,1152]{1,0:T(8,128)(2,1)S(1)}, u32[]{:S(2)}) copy-start(bf16[384,1152]{1,0:T(8,128)(2,1)S(1)} %collective-permute-done.got_ref) | copy-start | bytes 2654212
  37.4 4.7 %copy-start = (bf16[1024,768]{1,0:T(8,128)(2,1)}, bf16[1024,768]{1,0:T(8,128)(2,1)S(1)}, u32[]{:S(2)}) copy-start(bf16[1024,768]{1,0:T(8,128)(2,1)S(1)} %collective-permute-done.1.rest_0_.before) | copy-start | bytes 4718596
  42.1 1.2 copy-start.1
  46.2 10.0 %collective-permute-start.3 = (bf16[96,1152]{1,0:T(8,128)(2,1)}, bf16[96,1152]{1,0:T(8,128)(2,1)S(1)}, u32[]{:S(2)}, u32[]{:S(2)}) collective-permute-start(bf16[96,1152]{1,0:T(8,128)(2,1)} %get-tuple-element.26), channel_id=1, source_target_pairs={{0,64},{4,68},{8,72},{12,76},{16,80},{20,84},{24,88},{28,92},{32,9... | collective-permute-start | bytes 663560 | tf_op jit(solution)/shard_map/ppermute | solution.py:470
  47.5 11.0 %collective-permute-start.4 = (bf16[96,1152]{1,0:T(8,128)(2,1)}, bf16[96,1152]{1,0:T(8,128)(2,1)S(1)}, u32[]{:S(2)}, u32[]{:S(2)}) collective-permute-start(bf16[96,1152]{1,0:T(8,128)(2,1)} %get-tuple-element.27), channel_id=1, source_target_pairs={{0,128},{4,132},{8,136},{12,140},{16,144},{20,148},{24,152},{28,15... | collective-permute-start | bytes 663560 | tf_op jit(solution)/shard_map/ppermute | solution.py:470
  49.9 8.6 %collective-permute-start.5 = (bf16[96,1152]{1,0:T(8,128)(2,1)}, bf16[96,1152]{1,0:T(8,128)(2,1)S(1)}, u32[]{:S(2)}, u32[]{:S(2)}) collective-permute-start(bf16[96,1152]{1,0:T(8,128)(2,1)} %get-tuple-element.28), channel_id=1, source_target_pairs={{0,192},{4,196},{8,200},{12,204},{16,208},{20,212},{24,216},{28,22... | collective-permute-start | bytes 663560 | tf_op jit(solution)/shard_map/ppermute | solution.py:470
  56.3 16.3 %copy-start.19 = (s32[128]{0:T(128)S(1)}, s32[128]{0:T(128)}, u32[]{:S(2)}) copy-start(s32[128]{0:T(128)} %param.17) | copy-start | bytes 1540
  56.3 2.3 %copy-start.6 = (bf16[96,1152]{1,0:T(8,128)(2,1)}, bf16[96,1152]{1,0:T(8,128)(2,1)S(1)}, u32[]{:S(2)}) copy-start(bf16[96,1152]{1,0:T(8,128)(2,1)S(1)} %collective-permute-done.3.g1) | copy-start | bytes 663556
  61.9 19.7 %all-to-all-start = ((bf16[8,16,1152]{2,1,0:T(8,128)(2,1)}), bf16[8,16,1152]{2,1,0:T(8,128)(2,1)S(1)}, u32[]{:S(2)}, u32[]{:S(2)}) async-start(bf16[8,16,1152]{2,1,0:T(8,128)(2,1)} %rs_z.1.rest_0_), calls=%async_computation | async-start | bytes 589824 | tf_op jit(solution)/shard_map/all_to_all | solution.py:503
  84.3 19.4 %all-to-all-start.1 = ((bf16[8,16,1152]{2,1,0:T(8,128)(2,1)}), bf16[8,16,1152]{2,1,0:T(8,128)(2,1)S(1)}, u32[]{:S(2)}, u32[]{:S(2)}) async-start(bf16[8,16,1152]{2,1,0:T(8,128)(2,1)} %renorm.1.rest_0_), calls=%async_computation.1 | async-start | bytes 589824 | tf_op jit(solution)/shard_map/all_to_all | solution.py:503
  112.2 17.9 %copy-start.18 = (f32[384]{0:T(512)S(1)}, f32[384]{0:T(512)}, u32[]{:S(2)}) copy-start(f32[384]{0:T(512)} %param.15) | copy-start | bytes 4612
  112.2 8.0 %collective-permute-start.6 = (bf16[96,1152]{1,0:T(8,128)(2,1)}, bf16[96,1152]{1,0:T(8,128)(2,1)S(1)}, u32[]{:S(2)}, u32[]{:S(2)}) collective-permute-start(bf16[96,1152]{1,0:T(8,128)(2,1)} %bitcast.11), channel_id=1, source_target_pairs={{0,64},{4,68},{8,72},{12,76},{16,80},{20,84},{24,88},{28,92},{32,9... | collective-permute-start | bytes 663560 | tf_op jit(solution)/shard_map/ppermute | solution.py:470
  113.8 8.1 %collective-permute-start.7 = (bf16[96,1152]{1,0:T(8,128)(2,1)}, bf16[96,1152]{1,0:T(8,128)(2,1)S(1)}, u32[]{:S(2)}, u32[]{:S(2)}) collective-permute-start(bf16[96,1152]{1,0:T(8,128)(2,1)} %bitcast.12), channel_id=1, source_target_pairs={{0,128},{4,132},{8,136},{12,140},{16,144},{20,148},{24,152},{28,15... | collective-permute-start | bytes 663560 | tf_op jit(solution)/shard_map/ppermute | solution.py:470
  114.7 8.1 %collective-permute-start.8 = (bf16[96,1152]{1,0:T(8,128)(2,1)}, bf16[96,1152]{1,0:T(8,128)(2,1)S(1)}, u32[]{:S(2)}, u32[]{:S(2)}) collective-permute-start(bf16[96,1152]{1,0:T(8,128)(2,1)} %bitcast.13), channel_id=1, source_target_pairs={{0,192},{4,196},{8,200},{12,204},{16,208},{20,212},{24,216},{28,22... | collective-permute-start | bytes 663560 | tf_op jit(solution)/shard_map/ppermute | solution.py:470
  120.2 2.5 %copy-start.9 = (bf16[96,1152]{1,0:T(8,128)(2,1)}, bf16[96,1152]{1,0:T(8,128)(2,1)S(1)}, u32[]{:S(2)}) copy-start(bf16[96,1152]{1,0:T(8,128)(2,1)S(1)} %collective-permute-done.6.rest_1_) | copy-start | bytes 663556
  121.9 0.8 copy-start.10
  125.7 6.6 %collective-permute-start.9 = (bf16[384,1152]{1,0:T(8,128)(2,1)}, bf16[384,1152]{1,0:T(8,128)(2,1)S(1)}, u32[]{:S(2)}, u32[]{:S(2)}) collective-permute-start(bf16[384,1152]{1,0:T(8,128)(2,1)} %ag_x.1.own_ref), channel_id=1, source_target_pairs={{0,4},{4,0},{8,12},{12,8},{16,20},{20,16},{24,28},{28,24},{32,36},... | collective-permute-start | bytes 2654216 | tf_op jit(solution)/shard_map/ppermute | solution.py:470
  132.3 1.0 copy-start.4
  141.2 7.9 %collective-permute-start.10 = (bf16[256,384]{1,0:T(8,128)(2,1)}, bf16[256,384]{1,0:T(8,128)(2,1)S(1)}, u32[]{:S(2)}, u32[]{:S(2)}) collective-permute-start(bf16[256,384]{1,0:T(8,128)(2,1)} %get-tuple-element.30), channel_id=1, source_target_pairs={{0,1},{1,2},{2,3},{3,0},{4,5},{5,6},{6,7},{7,4},{8,9},{9,10},{10,1... | collective-permute-start | bytes 589832 | tf_op jit(solution)/shard_map/ppermute | solution.py:488
  142.5 11.8 %collective-permute-start.11 = (bf16[256,384]{1,0:T(8,128)(2,1)}, bf16[256,384]{1,0:T(8,128)(2,1)S(1)}, u32[]{:S(2)}, u32[]{:S(2)}) collective-permute-start(bf16[256,384]{1,0:T(8,128)(2,1)} %get-tuple-element.31), channel_id=1, source_target_pairs={{0,2},{1,3},{2,0},{3,1},{4,6},{5,7},{6,4},{7,5},{8,10},{9,11},{10,... | collective-permute-start | bytes 589832 | tf_op jit(solution)/shard_map/ppermute | solution.py:488
  145.2 9.1 %collective-permute-start.12 = (bf16[256,384]{1,0:T(8,128)(2,1)}, bf16[256,384]{1,0:T(8,128)(2,1)S(1)}, u32[]{:S(2)}, u32[]{:S(2)}) collective-permute-start(bf16[256,384]{1,0:T(8,128)(2,1)} %get-tuple-element.32), channel_id=1, source_target_pairs={{0,3},{1,0},{2,1},{3,2},{4,7},{5,4},{6,5},{7,6},{8,11},{9,8},{10,9... | collective-permute-start | bytes 589832 | tf_op jit(solution)/shard_map/ppermute | solution.py:488
  149.1 5.2 %copy-start.12 = (bf16[256,384]{1,0:T(8,128)(2,1)}, bf16[256,384]{1,0:T(8,128)(2,1)S(1)}, u32[]{:S(2)}) copy-start(bf16[256,384]{1,0:T(8,128)(2,1)S(1)} %collective-permute-done.10.refs_1_) | copy-start | bytes 589828
  154.3 0.8 copy-start.14
  161.6 6.6 %collective-permute-start.13 = (bf16[256,384]{1,0:T(8,128)(2,1)}, bf16[256,384]{1,0:T(8,128)(2,1)S(1)}, u32[]{:S(2)}, u32[]{:S(2)}) collective-permute-start(bf16[256,384]{1,0:T(8,128)(2,1)} %get-tuple-element.34), channel_id=1, source_target_pairs={{0,1},{1,2},{2,3},{3,0},{4,5},{5,6},{6,7},{7,4},{8,9},{9,10},{10,1... | collective-permute-start | bytes 589832 | tf_op jit(solution)/shard_map/ppermute | solution.py:488
  162.6 11.7 %collective-permute-start.14 = (bf16[256,384]{1,0:T(8,128)(2,1)}, bf16[256,384]{1,0:T(8,128)(2,1)S(1)}, u32[]{:S(2)}, u32[]{:S(2)}) collective-permute-start(bf16[256,384]{1,0:T(8,128)(2,1)} %get-tuple-element.35), channel_id=1, source_target_pairs={{0,2},{1,3},{2,0},{3,1},{4,6},{5,7},{6,4},{7,5},{8,10},{9,11},{10,... | collective-permute-start | bytes 589832 | tf_op jit(solution)/shard_map/ppermute | solution.py:488
  165.3 8.9 %collective-permute-start.15 = (bf16[256,384]{1,0:T(8,128)(2,1)}, bf16[256,384]{1,0:T(8,128)(2,1)S(1)}, u32[]{:S(2)}, u32[]{:S(2)}) collective-permute-start(bf16[256,384]{1,0:T(8,128)(2,1)} %get-tuple-element.36), channel_id=1, source_target_pairs={{0,3},{1,0},{2,1},{3,2},{4,7},{5,4},{6,5},{7,6},{8,11},{9,8},{10,9... | collective-permute-start | bytes 589832 | tf_op jit(solution)/shard_map/ppermute | solution.py:488
  168.2 6.0 %copy-start.15 = (bf16[256,384]{1,0:T(8,128)(2,1)}, bf16[256,384]{1,0:T(8,128)(2,1)S(1)}, u32[]{:S(2)}) copy-start(bf16[256,384]{1,0:T(8,128)(2,1)S(1)} %collective-permute-done.13.refs_1_) | copy-start | bytes 589828
  174.2 0.7 copy-start.17
  (7 other events, 4.9 us)
Sparse Core Ops, SparseCore 0:
  9.2 58.9 all-gather.1

commit v6 on v5

--- a/solution.py
+++ b/solution.py
@@ -212,19 +212,18 @@
 
 
 def owned_kernel(got_ref, *rest):
-    out, sem = rest[-2:]
-    copy = pltpu.make_async_copy(got_ref.at[pl.ds(0, OWNERS)], out, sem)
-    copy.start()
-    copy.wait()
+    out = rest[-1]
+    for o in range(OWNERS):
+        out[o * ROWS : (o + 1) * ROWS, :] = got_ref[o]
 
 
 def owned(got, deps):
     return pl.pallas_call(
         owned_kernel,
-        in_specs=[DEP] * (1 + len(deps)),
-        out_specs=DEP,
-        out_shape=sds((OWNERS, ROWS, WIDE), BF),
-        scratch_shapes=[pltpu.SemaphoreType.DMA],
+        grid=(1,),
+        in_specs=[full((ZS, ROWS, WIDE))] + [DEP] * len(deps),
+        out_specs=full((XROWS, WIDE)),
+        out_shape=sds((XROWS, WIDE), BF),
         compiler_params=params(),
         name="owned",
     )(got, *deps)
@@ -238,23 +237,24 @@
         out[pl.ds(pl.multiple_of(owner * XROWS, XROWS), XROWS), :] = block[...]
 
 
-def ag_x(pos, blocks):
+def ag_x(pos, blocks, deps):
     return pl.pallas_call(
         ag_x_kernel,
         grid=(1,),
-        in_specs=[SMEM] + [full((XROWS, WIDE))] * XS,
+        in_specs=[SMEM] + [full((XROWS, WIDE))] * XS + [DEP] * len(deps),
         out_specs=full((DH, WIDE)),
         out_shape=sds((DH, WIDE), BF),
         compiler_params=params(),
         name="ag_x",
-    )(pos, *blocks)
-
-
-def project_kernel(t_ref, w_ref, dep_ref, q_ref):
+    )(pos, *blocks, *deps)
+
+
+def project_kernel(t_ref, w_ref, *rest):
+    q_ref = rest[-1]
     q_ref[...] = mm(t_ref[...], w_ref[...]).astype(BF)
 
 
-def project(tokens, qkv_weight, dep):
+def project(tokens, qkv_weight, deps):
     rows, wide = tokens.shape
     block = 256
     return pl.pallas_call(
@@ -263,27 +263,27 @@
         in_specs=[
             pl.BlockSpec((block, wide), lambda i: (i, 0)),
             pl.BlockSpec((wide, DH), lambda i: (0, 0)),
-            DEP,
-        ],
+        ]
+        + [DEP] * len(deps),
         out_specs=pl.BlockSpec((block, DH), lambda i: (i, 0)),
         out_shape=sds((rows, DH), BF),
         compiler_params=params(),
         name="project",
-    )(tokens, qkv_weight, dep)
-
-
-def attend_kernel(start, pos_ref, ends_ref, q_ref, before, mine, after, *rest):
-    out_ref, s_ref = rest[-2:]
+    )(tokens, qkv_weight, *deps)
+
+
+def attend_kernel(ahead, pos_ref, ends_ref, q_ref, before, mine, after, dep_ref, out_ref, s_ref):
     shard = pos_ref[3]
+    piece = lax.rem(pos_ref[2] + ahead, HS)
     row = lax.broadcasted_iota(I32, (QB, 1), 0)
-    place = row + (shard * TOK + (pl.program_id(0) + start) * QB)
+    place = row + (shard * TOK + piece * QB)
     ends = ends_ref[...]
     shift = (shard - 1) * TOK
     begin = jnp.max(jnp.where(ends <= place, ends, 0), axis=1, keepdims=True) - shift
     end = jnp.min(jnp.where(ends <= place, TOKENS, ends), axis=1, keepdims=True) - shift
     first = lax.div(jnp.min(begin), KB)
     last = lax.div(jnp.max(end) + KB - 1, KB)
-    q = q_ref[...]
+    q = q_ref[pl.ds(pl.multiple_of(piece * QB, QB), QB), :]
     per = TOK // KB
     scale = 1.0 / math.sqrt(DH)
 
@@ -327,127 +327,94 @@
     segments(gather, 0)
 
 
-def attend(start, count, pos, ends, query, before, mine, after, dep, buffer):
+def attend(ahead, pos, ends, query, before, mine, after, dep):
     whole = full((TOK, 2 * DH))
-    extra = [] if buffer is None else [buffer]
-    return pl.pallas_call(
-        functools.partial(attend_kernel, start),
-        grid=(count,),
-        in_specs=[
-            SMEM,
-            full(ends.shape),
-            pl.BlockSpec((QB, DH), lambda i: (i + start, 0)),
-            whole,
-            whole,
-            whole,
-            DEP,
-        ]
-        + [DEP] * len(extra),
-        out_specs=pl.BlockSpec((QB, DH), lambda i: (i + start, 0)),
-        out_shape=sds((TOK, DH), F32),
-        input_output_aliases={7: 0} if extra else {},
+    return pl.pallas_call(
+        functools.partial(attend_kernel, ahead),
+        grid=(1,),
+        in_specs=[SMEM, full(ends.shape), full((TOK, DH)), whole, whole, whole, DEP],
+        out_specs=full((QB, DH)),
+        out_shape=sds((QB, DH), F32),
         scratch_shapes=[pltpu.VMEM((3 * TOK // KB, QB, KB), F32)],
         compiler_params=params(),
-        name=f"attend_{start}",
-    )(pos, ends, query, before, mine, after, dep, *extra)
-
-
-def apply_kernel(pos_ref, q_ref, own_ref, other_ref, att_ref, gain_ref, *outs):
-    core = pos_ref[0]
-    q = q_ref[...]
-    mine = mm(q, own_ref[:, :HID])
-    theirs = mm(q, other_ref[:, :HID])
-    even = core == 0
-    a = jnp.where(even, mine, theirs)
-    b = jnp.where(even, theirs, mine)
-    hidden = (a * jax.nn.sigmoid(a) * b).astype(BF)
-    h0, h1 = hidden[:, :DH], hidden[:, DH:]
-    h_own = jnp.where(even, h0, h1)
-    h_other = jnp.where(even, h1, h0)
-    applied = mm(h_own, own_ref[:, HID:]) + mm(h_other, other_ref[:, HID:])
-    mean = jnp.mean(applied * applied, axis=1, keepdims=True)
-    normed = applied * lax.rsqrt(mean + 1e-6) * gain_ref[...]
-    mixed = (att_ref[...] + normed).astype(BF)
-    for step in range(HS):
-
-        @pl.when(pl.program_id(0) == step)
-        def _():
-            outs[step][...] = mixed
-
-
-def apply(pos, query, own, other, attended, gain):
-    weight = pl.BlockSpec((DH, WIDE), lambda i, pos: (0, 0))
-    rows = pl.BlockSpec((QB, DH), lambda i, pos: (lax.rem(pos[2] + i + 1, HS), 0))
-    return pl.pallas_call(
-        apply_kernel,
-        grid_spec=pltpu.PrefetchScalarGridSpec(
-            num_scalar_prefetch=1,
-            grid=(HS,),
-            in_specs=[rows, weight, weight, rows, pl.BlockSpec((1, DH), lambda i, pos: (0, 0))],
-            out_specs=[pl.BlockSpec((QB, DH), lambda i, pos: (0, 0))] * HS,
-        ),
-        out_shape=[sds((QB, DH), BF)] * HS,
-        compiler_params=params(),
-        name="apply",
-    )(pos, query, own, other, attended, gain)
+        name=f"attend_{ahead}",
+    )(pos, ends, query, before, mine, after, dep)
+
+
+def apply_kernel(aheads, pos_ref, q_ref, own_ref, other_ref, gain_ref, *rest):
+    count = len(aheads)
+    attended, outs = rest[:count], rest[-count:]
+    even = pos_ref[0] == 0
+    for ahead, att_ref, out in zip(aheads, attended, outs):
+        piece = lax.rem(pos_ref[2] + ahead, HS)
+        q = q_ref[pl.ds(pl.multiple_of(piece * QB, QB), QB), :]
+        mine = mm(q, own_ref[:, :HID])
+        theirs = mm(q, other_ref[:, :HID])
+        a = jnp.where(even, mine, theirs)
+        b = jnp.where(even, theirs, mine)
+        hidden = (a * jax.nn.sigmoid(a) * b).astype(BF)
+        h0, h1 = hidden[:, :DH], hidden[:, DH:]
+        h_own = jnp.where(even, h0, h1)
+        h_other = jnp.where(even, h1, h0)
+        applied = mm(h_own, own_ref[:, HID:]) + mm(h_other, other_ref[:, HID:])
+        mean = jnp.mean(applied * applied, axis=1, keepdims=True)
+        normed = applied * lax.rsqrt(mean + 1e-6) * gain_ref[...]
+        out[...] = (att_ref[...] + normed).astype(BF)
+
+
+def apply(aheads, pos, query, own, other, gain, attended, deps):
+    count = len(aheads)
+    return pl.pallas_call(
+        functools.partial(apply_kernel, aheads),
+        grid=(1,),
+        in_specs=[SMEM, full((TOK, DH)), full((DH, WIDE)), full((DH, WIDE)), full((1, DH))]
+        + [full((QB, DH))] * count
+        + [DEP] * len(deps),
+        out_specs=[full((QB, DH))] * count,
+        out_shape=[sds((QB, DH), BF)] * count,
+        compiler_params=params(),
+        name=f"apply_{count}",
+    )(pos, query, own, other, gain, *attended, *deps)
 
 
 def output_kernel(pos_ref, *refs):
     parts, weights, outs = refs[:HS], refs[HS : 2 * HS], refs[2 * HS :]
-    total = mm(parts[0][...], weights[0][...])
-    for part, weight in zip(parts[1:], weights[1:]):
-        total = total + mm(part[...], weight[...])
-    total = total.astype(BF)
-    for step in range(HS):
-
-        @pl.when(pl.program_id(0) == step)
-        def _():
-            outs[step][...] = total
-
-
-def output(pos, parts, weight):
-    rows = pl.BlockSpec((QB, DH), lambda i, pos: (0, 0))
-    cols = [
-        pl.BlockSpec(
-            (DH, DH),
-            lambda i, pos, d=d: (lax.rem(pos[2] - d + HS, HS), lax.rem(pos[2] + i + 1, HS)),
-        )
-        for d in range(HS)
-    ]
+    head = pos_ref[2]
+    for e, out in enumerate(outs):
+        cols = pl.ds(pl.multiple_of(lax.rem(head + e + 1, HS) * DH, DH), DH)
+        total = mm(parts[0][...], weights[0][:, cols])
+        for part, weight in zip(parts[1:], weights[1:]):
+            total = total + mm(part[...], weight[:, cols])
+        out[...] = total.astype(BF)
+
+
+def output(pos, parts, weights):
     return pl.pallas_call(
         output_kernel,
-        grid_spec=pltpu.PrefetchScalarGridSpec(
-            num_scalar_prefetch=1,
-            grid=(HS,),
-            in_specs=[rows] * HS + cols,
-            out_specs=[rows] * HS,
-        ),
+        grid=(1,),
+        in_specs=[SMEM] + [full((QB, DH))] * HS + [full((DH, HS * DH))] * HS,
+        out_specs=[full((QB, DH))] * HS,
         out_shape=[sds((QB, DH), BF)] * HS,
         compiler_params=params(),
         name="output",
-    )(pos, *parts, *[weight] * HS)
+    )(pos, *parts, *weights)
 
 
 def arrange_kernel(pos_ref, *refs):
-    parts, out, sems = refs[:HS], refs[HS], refs[HS + 1]
+    parts, out = refs[:-1], refs[-1]
     head = pos_ref[2]
-    copies = []
     for d, part in enumerate(parts):
         rows = pl.ds(pl.multiple_of(lax.rem(head - d + HS, HS) * QB, QB), QB)
-        copies.append(pltpu.make_async_copy(part, out.at[rows, :], sems.at[d]))
-    for copy in copies:
-        copy.start()
-    for copy in copies:
-        copy.wait()
+        out[rows, :] = part[...]
 
 
 def arrange(pos, parts):
     return pl.pallas_call(
         arrange_kernel,
-        in_specs=[SMEM] + [DEP] * HS,
-        out_specs=DEP,
+        grid=(1,),
+        in_specs=[SMEM] + [full((QB, DH))] * HS,
+        out_specs=full((TOK, DH)),
         out_shape=sds((TOK, DH), BF),
-        scratch_shapes=[pltpu.SemaphoreType.DMA((HS,))],
         compiler_params=params(),
         name="arrange",
     )(pos, *parts)
@@ -487,7 +454,7 @@
     def spread(parts):
         return [lax.ppermute(p, "head", shift_h(d)) if d else p for d, p in enumerate(parts)]
 
-    weight = lax.all_gather(out_weight, "head", axis=0, tiled=True)
+    weights = spread([out_weight] * HS)
 
     row = jnp.minimum(x * XROWS + z * ROWS, DH - ROWS)
     pick = lambda w, at: lax.dynamic_slice_in_dim(w[0], at, ROWS, 0)
@@ -504,21 +471,27 @@
 
     own, *gives = rs_x(pos, keep, got, [before, after])
     got = [send(g, shift_x(d + 1)) for d, g in enumerate(gives)]
-    query = project(tokens, qkv_weight, own)
+    query = project(tokens, qkv_weight, [own, ends, old])
     att = functools.partial(attend, pos=pos, ends=ends, query=query, before=before, mine=kv, after=after)
     total = rs_z(own, got, [query])
     got = exchange(total)
-    att_low = att(0, 2, dep=total, buffer=None)
-    fresh = renorm(old, got, [att_low])
+    att1 = att(1, dep=total)
+    fresh = renorm(old, got, [att1, weights[1], weights[3]])
     got = exchange(fresh)
-    attended = att(2, 2, dep=fresh, buffer=att_low)
-    block = owned(got, [attended, weight]).reshape(XROWS, WIDE)
-    half = ag_x(pos, [block] + [send(block, shift_x(d)) for d in range(1, XS)])
+    att2 = att(2, dep=fresh)
+    block = owned(got, [att2])
+    att3 = att(3, dep=block)
+    half = ag_x(pos, [block] + [send(block, shift_x(d)) for d in range(1, XS)], [att3, weights[2]])
     other = send(half, SWAP_C)
 
-    ahead = apply(pos, query, half, other, attended, fast_gain[None, :])
-    parts = spread([ahead[-1], *ahead[:-1]])
-    ahead = output(pos, parts, weight)
+    mix = functools.partial(
+        apply, pos=pos, query=query, own=half, other=other, gain=fast_gain[None, :]
+    )
+    away = mix((1, 2, 3), attended=[att1, att2, att3], deps=[])
+    att0 = att(0, dep=away[0])
+    [home] = mix((0,), attended=[att0], deps=[away[0]])
+    parts = spread([home, *away])
+    ahead = output(pos, parts, weights)
     result = arrange(pos, spread([ahead[-1], *ahead[:-1]]))
     return result
 

time: 209 us -> 159 us (0.76)
  Pallas kernels: 96.8 us -> 74.9 us
  waiting for transfers between devices: 39 us -> 24 us
  between operations: 13.5 us -> 0.15 us
    pallas_call x6 -> x9, Pallas kernels: 65.2 us -> 43.4 us  [the longest x4 25.3 us: attend(): pl.pallas_call(functools.partial(attend_kernel, ahead), grid=(1,), in_spe...]
    ppermute x10, waiting for transfers between devices: 20.3 us -> 10.3 us  [body(): send = lambda value, pairs: lax.ppermute(value, 'tok', pairs)]
    ppermute x6 -> x9, waiting for transfers between devices: 16.8 us -> 9.1 us  [spread(): lax.ppermute(p, 'head', shift_h(d))]
    all_to_all x2, waiting for transfers between devices: 1.16 us -> 4.69 us  [exchange(): return lax.all_to_all(blocks, 'tok', 0, 0, axis_index_groups=ALONG_Z)]
    all_to_all x2, starting transfers between devices: 17.8 us -> 15.1 us  [exchange(): return lax.all_to_all(blocks, 'tok', 0, 0, axis_index_groups=ALONG_Z)]
    ppermute x6 -> x9, starting transfers between devices: 8.85 us -> 10.9 us  [spread(): lax.ppermute(p, 'head', shift_h(d))]
  transfers between devices with their start and end apart: 19 -> 21, of which waited for: 14 -> 11; matrix products, arithmetic and copies ran while one was open for 2% -> 3% of each run, Pallas kernels for 23% -> 33%
where the time goes in v6:
time: 159 us; the launch traced here: 158 us
  Pallas kernels  74.9 us (47%)
  starting transfers between devices  47.9 us (30%)
  waiting for transfers between devices  24 us (15%)
  local copies, waits for them, and re-layouts  8.37 us (5%)
  other arithmetic  2.72 us (2%)
    pallas_call x4, Pallas kernels, attend(): pl.pallas_call(functools.partial(attend_kernel, ahead), grid=(1,), in_spe...  25.3 us
    ppermute x10, starting transfers between devices, body(): send = lambda value, pairs: lax.ppermute(value, 'tok', pairs)  21.9 us
    all_to_all x2, starting transfers between devices, exchange(): return lax.all_to_all(blocks, 'tok', 0, 0, axis_index_groups=ALONG_Z)  15.1 us
    ppermute x9, starting transfers between devices, spread(): lax.ppermute(p, 'head', shift_h(d))  10.9 us
    ppermute x10, waiting for transfers between devices, body(): send = lambda value, pairs: lax.ppermute(value, 'tok', pairs)  10.3 us
    pallas_call x1, Pallas kernels, update(): pl.pallas_call(update_kernel, grid=(1,), in_specs=[SMEM, full(kv.shape),...  9.68 us
    ppermute x9, waiting for transfers between devices, spread(): lax.ppermute(p, 'head', shift_h(d))  9.1 us
    pallas_call x2, Pallas kernels, apply(): pl.pallas_call(functools.partial(apply_kernel, aheads), grid=(1,), in_spe...  8.82 us
  transfers between devices with their start and end apart: 21, of which 11 were waited for; matrix products, arithmetic and copies ran while one was open for 3% of the time, Pallas kernels for 33%

profile of v6, /device:TPU:1, one launch (start us, length us, event | category | flops | bytes accessed | tf_op | source)
XLA Modules:
  0.0 158.1 jit_solution(12325773046998946630)
XLA Ops:
  0.0 7.5 %keys.1 = (bf16[1024,768]{1,0:T(8,128)(2,1)}, f32[1024,3]{1,0:T(8,128)}) custom-call(bf16[1024,1536]{1,0:T(8,128)(2,1)} %t_ref.3, bf16[1536,1152]{1,0:T(8,128)(2,1)} %w_ref.1, bf16[1536,1152]{1,0:T(8,128)(2,1)} %w_ref.1, bf16[3,1536]{1,0:T(4,128)(2,1)} %bitcast.15), custom_call_target="tpu_custom_call" | custom-call | tf_op jit(solution)/shard_map/keys/pallas_call | solution.py:75
  7.5 5.1 %collective-permute-start.2 = (bf16[1024,768]{1,0:T(8,128)(2,1)}, bf16[1024,768]{1,0:T(8,128)(2,1)S(1)}, u32[]{:S(2)}, u32[]{:S(2)}) collective-permute-start(bf16[1024,768]{1,0:T(8,128)(2,1)} %get-tuple-element.20.kv_ref.mine), channel_id=1, source_target_pairs={{4,0},{8,4},{12,8},{16,12},{20,16},{24,20},{28,24},{32,28},{36,32}... | collective-permute-start | bytes 4718600 | tf_op jit(solution)/shard_map/ppermute | solution.py:437
  12.7 1.9 %collective-permute-start.1 = (bf16[1024,768]{1,0:T(8,128)(2,1)}, bf16[1024,768]{1,0:T(8,128)(2,1)S(1)}, u32[]{:S(2)}, u32[]{:S(2)}) collective-permute-start(bf16[1024,768]{1,0:T(8,128)(2,1)} %get-tuple-element.20.kv_ref.mine), channel_id=1, source_target_pairs={{0,4},{4,8},{8,12},{12,16},{16,20},{20,24},{24,28},{28,32},{32,36}... | collective-permute-start | bytes 4718600 | tf_op jit(solution)/shard_map/ppermute | solution.py:437
  15.3 9.7 %update.1 = (bf16[384,1152]{1,0:T(8,128)(2,1)}, f32[384,1152]{1,0:T(8,128)}) custom-call(s32[4]{0:T(128)} %pad_add_fusion.pos_ref, bf16[1024,768]{1,0:T(8,128)(2,1)} %get-tuple-element.20.kv_ref.mine, f32[1024,3]{1,0:T(8,128)} %get-tuple-element.21.r_ref, bf16[1,384,768]{2,1,0:T(8,128)(2,1)} %w1_ref.1, bf16[1,384,768]{2,1,0:T(8,128)(2,1)} %w3_ref.1, ...), custom_call_target="tpu_custom_call" | custom-call | tf_op jit(solution)/shard_map/update/pallas_call | solution.py:123
  25.6 1.9 %collective-permute-start.7 = (bf16[384,1536]{1,0:T(8,128)(2,1)}, bf16[384,1536]{1,0:T(8,128)(2,1)}, u32[]{:S(2)}, u32[]{:S(2)}) collective-permute-start(bf16[384,1536]{1,0:T(8,128)(2,1)} %refs_4_.1), channel_id=1, source_target_pairs={{0,3},{1,0},{2,1},{3,2},{4,7},{5,4},{6,5},{7,6},{8,11},{9,8},{10,9... | collective-permute-start | bytes 3538952 | tf_op jit(solution)/shard_map/ppermute | solution.py:455
  33.4 2.8 %rs_x.1 = (f32[96,1152]{1,0:T(8,128)}, bf16[96,1152]{1,0:T(8,128)(2,1)}, bf16[96,1152]{1,0:T(8,128)(2,1)}, bf16[96,1152]{1,0:T(8,128)(2,1)}) custom-call(s32[4]{0:T(128)} %pad_add_fusion.pos_ref, f32[384,1152]{1,0:T(8,128)} %get-tuple-element.22.keep_ref, bf16[384,1152]{1,0:T(8,128)(2,1)} %collective-permute-done.got_ref, bf16[1024,768]{1,0:T(8,128)(2,1)} %copy-done.1, ...), custom_call_target="tpu_custom_call" | custom-call | tf_op jit(solution)/shard_map/rs_x/pallas_call | solution.py:151
  36.3 2.9 %collective-permute-start.3 = (bf16[96,1152]{1,0:T(8,128)(2,1)}, bf16[96,1152]{1,0:T(8,128)(2,1)S(1)}, u32[]{:S(2)}, u32[]{:S(2)}) collective-permute-start(bf16[96,1152]{1,0:T(8,128)(2,1)} %get-tuple-element.25), channel_id=1, source_target_pairs={{0,64},{4,68},{8,72},{12,76},{16,80},{20,84},{24,88},{28,92},{32,9... | collective-permute-start | bytes 663560 | tf_op jit(solution)/shard_map/ppermute | solution.py:437
  39.2 2.7 %collective-permute-start.4 = (bf16[96,1152]{1,0:T(8,128)(2,1)}, bf16[96,1152]{1,0:T(8,128)(2,1)S(1)}, u32[]{:S(2)}, u32[]{:S(2)}) collective-permute-start(bf16[96,1152]{1,0:T(8,128)(2,1)} %get-tuple-element.26), channel_id=1, source_target_pairs={{0,128},{4,132},{8,136},{12,140},{16,144},{20,148},{24,152},{28,15... | collective-permute-start | bytes 663560 | tf_op jit(solution)/shard_map/ppermute | solution.py:437
  43.4 5.2 %project.1.rest_0_.q_ref = bf16[1024,384]{1,0:T(8,128)(2,1)} custom-call(bf16[1024,1536]{1,0:T(8,128)(2,1)} %t_ref.3, bf16[1536,1152]{1,0:T(8,128)(2,1)} %w_ref.1, f32[96,1152]{1,0:T(8,128)} %get-tuple-element.24.rest_0_.own_ref, s32[1,128]{1,0:T(1,128)} %bitcast.10, f32[16,1152]{1,0:T(8,128)} %maximum_convert_fusion.rest_2_.old_ref), custom_call_target="tpu_custom_call" | custom-call | tf_op jit(solution)/shard_map/project/pallas_call | solution.py:260
  50.1 2.1 %rs_z.1.dep_ref = bf16[8,16,1152]{2,1,0:T(8,128)(2,1)} custom-call(f32[96,1152]{1,0:T(8,128)} %get-tuple-element.24.rest_0_.own_ref, bf16[96,1152]{1,0:T(8,128)(2,1)} %copy-done.6, bf16[96,1152]{1,0:T(8,128)(2,1)} %copy-done.7, bf16[96,1152]{1,0:T(8,128)(2,1)} %copy-done.9, bf16[1024,384]{1,0:T(8,128)(2,1)} %project.1.rest_0_.q_ref), custom_call_target="tpu_custom_call" | custom-call | tf_op jit(solution)/shard_map/rs_z/pallas_call | solution.py:174
  52.1 9.2 %all-to-all-start = ((bf16[8,16,1152]{2,1,0:T(8,128)(2,1)}), bf16[8,16,1152]{2,1,0:T(8,128)(2,1)S(1)}, u32[]{:S(2)}, u32[]{:S(2)}) async-start(bf16[8,16,1152]{2,1,0:T(8,128)(2,1)} %rs_z.1.dep_ref), calls=%async_computation | async-start | bytes 589824 | tf_op jit(solution)/shard_map/all_to_all | solution.py:470
  61.3 2.9 %collective-permute-start.11 = (bf16[384,1536]{1,0:T(8,128)(2,1)}, bf16[384,1536]{1,0:T(8,128)(2,1)S(1)}, u32[]{:S(2)}, u32[]{:S(2)}) collective-permute-start(bf16[384,1536]{1,0:T(8,128)(2,1)} %refs_4_.1), channel_id=1, source_target_pairs={{0,2},{1,3},{2,0},{3,1},{4,6},{5,7},{6,4},{7,5},{8,10},{9,11},{10,... | collective-permute-start | bytes 3538952 | tf_op jit(solution)/shard_map/ppermute | solution.py:455
  64.3 6.1 %attend_1.1.rest_0_ = f32[256,384]{1,0:T(8,128)} custom-call(s32[4]{0:T(128)} %pad_add_fusion.pos_ref, s32[1,128]{1,0:T(1,128)} %bitcast.11, bf16[1024,384]{1,0:T(8,128)(2,1)} %project.1.rest_0_.q_ref, bf16[1024,768]{1,0:T(8,128)(2,1)} %copy-done.1, bf16[1024,768]{1,0:T(8,128)(2,1)} %get-tuple-element.20.kv_ref.mine, bf16[1024,768]{1,0:T(8,128)(2,1)} %copy-done, ...), custom_call_target="tpu_custom_call" | custom-call | tf_op jit(solution)/shard_map/attend_1/pallas_call | solution.py:332
  70.3 1.7 %all-to-all-done.got_ref = bf16[8,16,1152]{2,1,0:T(8,128)(2,1)S(1)} async-done(((bf16[8,16,1152]{2,1,0:T(8,128)(2,1)}), bf16[8,16,1152]{2,1,0:T(8,128)(2,1)S(1)}, u32[]{:S(2)}, u32[]{:S(2)}) %all-to-all-start) | async-done | bytes 294944 | tf_op jit(solution)/shard_map/all_to_all | solution.py:470
  72.8 1.9 %renorm.1.dep_ref = bf16[8,16,1152]{2,1,0:T(8,128)(2,1)} custom-call(f32[16,1152]{1,0:T(8,128)} %maximum_convert_fusion.rest_2_.old_ref, bf16[8,16,1152]{2,1,0:T(8,128)(2,1)} %copy-done.5, f32[256,384]{1,0:T(8,128)} %attend_1.1.rest_0_, bf16[384,1536]{1,0:T(8,128)(2,1)} %collective-permute-done.6.rest_1_.refs_5_, ...), custom_call_target="tpu_custom_call" | custom-call | tf_op jit(solution)/shard_map/renorm/pallas_call | solution.py:203
  74.6 5.9 %all-to-all-start.1 = ((bf16[8,16,1152]{2,1,0:T(8,128)(2,1)}), bf16[8,16,1152]{2,1,0:T(8,128)(2,1)S(1)}, u32[]{:S(2)}, u32[]{:S(2)}) async-start(bf16[8,16,1152]{2,1,0:T(8,128)(2,1)} %renorm.1.dep_ref), calls=%async_computation.1 | async-start | bytes 589824 | tf_op jit(solution)/shard_map/all_to_all | solution.py:470
  80.5 6.6 %attend_2.1.rest_0_.rest_1_ = f32[256,384]{1,0:T(8,128)} custom-call(s32[4]{0:T(128)} %pad_add_fusion.pos_ref, s32[1,128]{1,0:T(1,128)} %bitcast.12, bf16[1024,384]{1,0:T(8,128)(2,1)} %project.1.rest_0_.q_ref, bf16[1024,768]{1,0:T(8,128)(2,1)} %copy-done.1, bf16[1024,768]{1,0:T(8,128)(2,1)} %get-tuple-element.20.kv_ref.mine, bf16[1024,768]{1,0:T(8,128)(2,1)} %copy-done, ...), custom_call_target="tpu_custom_call" | custom-call | tf_op jit(solution)/shard_map/attend_2/pallas_call | solution.py:332
  87.1 3.0 %all-to-all-done.1.got_ref = bf16[8,16,1152]{2,1,0:T(8,128)(2,1)S(1)} async-done(((bf16[8,16,1152]{2,1,0:T(8,128)(2,1)}), bf16[8,16,1152]{2,1,0:T(8,128)(2,1)S(1)}, u32[]{:S(2)}, u32[]{:S(2)}) %all-to-all-start.1) | async-done | bytes 294944 | tf_op jit(solution)/shard_map/all_to_all | solution.py:470
  92.5 6.3 %collective-permute-start.10 = (bf16[96,1152]{1,0:T(8,128)(2,1)}, bf16[96,1152]{1,0:T(8,128)(2,1)S(1)}, u32[]{:S(2)}, u32[]{:S(2)}) collective-permute-start(bf16[96,1152]{1,0:T(8,128)(2,1)} %owned.1.dep_ref.rest_0_), channel_id=1, source_target_pairs={{0,192},{4,196},{8,200},{12,204},{16,208},{20,212},{24,216},{28,22... | collective-permute-start | bytes 663560 | tf_op jit(solution)/shard_map/ppermute | solution.py:437
  99.4 6.6 %attend_3.1.rest_4_.rest_2_ = f32[256,384]{1,0:T(8,128)} custom-call(s32[4]{0:T(128)} %pad_add_fusion.pos_ref, s32[1,128]{1,0:T(1,128)} %bitcast.13, bf16[1024,384]{1,0:T(8,128)(2,1)} %project.1.rest_0_.q_ref, bf16[1024,768]{1,0:T(8,128)(2,1)} %copy-done.1, bf16[1024,768]{1,0:T(8,128)(2,1)} %get-tuple-element.20.kv_ref.mine, bf16[1024,768]{1,0:T(8,128)(2,1)} %copy-done, ...), custom_call_target="tpu_custom_call" | custom-call | tf_op jit(solution)/shard_map/attend_3/pallas_call | solution.py:332
  106.0 2.5 %collective-permute-done.10.rest_3_ = bf16[96,1152]{1,0:T(8,128)(2,1)S(1)} collective-permute-done((bf16[96,1152]{1,0:T(8,128)(2,1)}, bf16[96,1152]{1,0:T(8,128)(2,1)S(1)}, u32[]{:S(2)}, u32[]{:S(2)}) %collective-permute-start.10) | collective-permute-done | bytes 221216 | tf_op jit(solution)/shard_map/ppermute | solution.py:437
  108.5 3.5 %collective-permute-done.8.rest_1_ = bf16[96,1152]{1,0:T(8,128)(2,1)S(1)} collective-permute-done((bf16[96,1152]{1,0:T(8,128)(2,1)}, bf16[96,1152]{1,0:T(8,128)(2,1)S(1)}, u32[]{:S(2)}, u32[]{:S(2)}) %collective-permute-start.8) | collective-permute-done | bytes 221216 | tf_op jit(solution)/shard_map/ppermute | solution.py:437
  112.7 2.3 %ag_x.1.own_ref = bf16[384,1152]{1,0:T(8,128)(2,1)} custom-call(s32[4]{0:T(128)} %pad_add_fusion.pos_ref, bf16[96,1152]{1,0:T(8,128)(2,1)} %owned.1.dep_ref.rest_0_, bf16[96,1152]{1,0:T(8,128)(2,1)} %copy-done.11, bf16[96,1152]{1,0:T(8,128)(2,1)} %copy-done.10, bf16[96,1152]{1,0:T(8,128)(2,1)} %copy-done.8, f32[256,384]{1,0:T(8,128)} %attend_3.1.rest_4_.rest_2_, ...), custom_call_target="tpu_custom_call" | custom-call | tf_op jit(solution)/shard_map/ag_x/pallas_call | solution.py:241
  119.0 5.3 %apply_3.1 = (bf16[256,384]{1,0:T(8,128)(2,1)}, bf16[256,384]{1,0:T(8,128)(2,1)}, bf16[256,384]{1,0:T(8,128)(2,1)}) custom-call(s32[4]{0:T(128)} %pad_add_fusion.pos_ref, bf16[1024,384]{1,0:T(8,128)(2,1)} %project.1.rest_0_.q_ref, bf16[384,1152]{1,0:T(8,128)(2,1)} %ag_x.1.own_ref, bf16[384,1152]{1,0:T(8,128)(2,1)} %copy-done.3, ...), custom_call_target="tpu_custom_call" | custom-call | tf_op jit(solution)/shard_map/apply_3/pallas_call | solution.py:367
  125.8 6.1 %attend_0.1.rest_0_ = f32[256,384]{1,0:T(8,128)} custom-call(s32[4]{0:T(128)} %pad_add_fusion.pos_ref, s32[1,128]{1,0:T(1,128)} %bitcast.14, bf16[1024,384]{1,0:T(8,128)(2,1)} %project.1.rest_0_.q_ref, bf16[1024,768]{1,0:T(8,128)(2,1)} %copy-done.1, bf16[1024,768]{1,0:T(8,128)(2,1)} %get-tuple-element.20.kv_ref.mine, bf16[1024,768]{1,0:T(8,128)(2,1)} %copy-done, ...), custom_call_target="tpu_custom_call" | custom-call | tf_op jit(solution)/shard_map/attend_0/pallas_call | solution.py:332
  131.8 3.5 %apply_1.1.refs_0_ = bf16[256,384]{1,0:T(8,128)(2,1)} custom-call(s32[4]{0:T(128)} %pad_add_fusion.pos_ref, bf16[1024,384]{1,0:T(8,128)(2,1)} %project.1.rest_0_.q_ref, bf16[384,1152]{1,0:T(8,128)(2,1)} %ag_x.1.own_ref, bf16[384,1152]{1,0:T(8,128)(2,1)} %copy-done.3, f32[1,384]{1,0:T(1,128)} %broadcast_in_dim.24.gain_ref, f32[256,384]{1,0:T(8,128)} %attend_0.1.rest_0_, ...), custom_call_target="tpu_custom_call" | custom-call | tf_op jit(solution)/shard_map/apply_1/pallas_call | solution.py:367
  137.7 5.5 %output.1 = (bf16[256,384]{1,0:T(8,128)(2,1)}, bf16[256,384]{1,0:T(8,128)(2,1)}, bf16[256,384]{1,0:T(8,128)(2,1)}, bf16[256,384]{1,0:T(8,128)(2,1)}) custom-call(s32[4]{0:T(128)} %pad_add_fusion.pos_ref, bf16[256,384]{1,0:T(8,128)(2,1)} %apply_1.1.refs_0_, bf16[256,384]{1,0:T(8,128)(2,1)} %copy-done.14, bf16[256,384]{1,0:T(8,128)(2,1)} %copy-done.12, ...), custom_call_target="tpu_custom_call" | custom-call | tf_op jit(solution)/shard_map/output/pallas_call | solution.py:392
  143.4 2.4 %collective-permute-start.17 = (bf16[256,384]{1,0:T(8,128)(2,1)}, bf16[256,384]{1,0:T(8,128)(2,1)S(1)}, u32[]{:S(2)}, u32[]{:S(2)}) collective-permute-start(bf16[256,384]{1,0:T(8,128)(2,1)} %get-tuple-element.33), channel_id=1, source_target_pairs={{0,2},{1,3},{2,0},{3,1},{4,6},{5,7},{6,4},{7,5},{8,10},{9,11},{10,... | collective-permute-start | bytes 589832 | tf_op jit(solution)/shard_map/ppermute | solution.py:455
  145.8 2.0 %collective-permute-start.18 = (bf16[256,384]{1,0:T(8,128)(2,1)}, bf16[256,384]{1,0:T(8,128)(2,1)S(1)}, u32[]{:S(2)}, u32[]{:S(2)}) collective-permute-start(bf16[256,384]{1,0:T(8,128)(2,1)} %get-tuple-element.34), channel_id=1, source_target_pairs={{0,3},{1,0},{2,1},{3,2},{4,7},{5,4},{6,5},{7,6},{8,11},{9,8},{10,9... | collective-permute-start | bytes 589832 | tf_op jit(solution)/shard_map/ppermute | solution.py:455
  147.8 3.4 %collective-permute-done.16.refs_1_ = bf16[256,384]{1,0:T(8,128)(2,1)S(1)} collective-permute-done((bf16[256,384]{1,0:T(8,128)(2,1)}, bf16[256,384]{1,0:T(8,128)(2,1)S(1)}, u32[]{:S(2)}, u32[]{:S(2)}) %collective-permute-start.16) | collective-permute-done | bytes 196640 | tf_op jit(solution)/shard_map/ppermute | solution.py:455
  151.2 3.0 %collective-permute-done.17.refs_2_ = bf16[256,384]{1,0:T(8,128)(2,1)S(1)} collective-permute-done((bf16[256,384]{1,0:T(8,128)(2,1)}, bf16[256,384]{1,0:T(8,128)(2,1)S(1)}, u32[]{:S(2)}, u32[]{:S(2)}) %collective-permute-start.17) | collective-permute-done | bytes 196640 | tf_op jit(solution)/shard_map/ppermute | solution.py:455
  155.9 2.2 %arrange.1 = bf16[1024,384]{1,0:T(8,128)(2,1)} custom-call(s32[4]{0:T(128)} %pad_add_fusion.pos_ref, bf16[256,384]{1,0:T(8,128)(2,1)} %get-tuple-element.31.refs_0_, bf16[256,384]{1,0:T(8,128)(2,1)} %copy-done.15, bf16[256,384]{1,0:T(8,128)(2,1)} %copy-done.16, bf16[256,384]{1,0:T(8,128)(2,1)} %copy-done.17), custom_call_target="tpu_custom_call" | custom-call | tf_op jit(solution)/shard_map/arrange/pallas_call | solution.py:412
  (72 shorter events, 24.2 us)
Async XLA Ops:
  7.5 23.6 %collective-permute-start.2 = (bf16[1024,768]{1,0:T(8,128)(2,1)}, bf16[1024,768]{1,0:T(8,128)(2,1)S(1)}, u32[]{:S(2)}, u32[]{:S(2)}) collective-permute-start(bf16[1024,768]{1,0:T(8,128)(2,1)} %get-tuple-element.20.kv_ref.mine), channel_id=1, source_target_pairs={{4,0},{8,4},{12,8},{16,12},{20,16},{24,20},{28,24},{32,28},{36,32}... | collective-permute-start | bytes 4718600 | tf_op jit(solution)/shard_map/ppermute | solution.py:437
  12.7 19.6 %collective-permute-start.1 = (bf16[1024,768]{1,0:T(8,128)(2,1)}, bf16[1024,768]{1,0:T(8,128)(2,1)S(1)}, u32[]{:S(2)}, u32[]{:S(2)}) collective-permute-start(bf16[1024,768]{1,0:T(8,128)(2,1)} %get-tuple-element.20.kv_ref.mine), channel_id=1, source_target_pairs={{0,4},{4,8},{8,12},{12,16},{16,20},{20,24},{24,28},{28,32},{32,36}... | collective-permute-start | bytes 4718600 | tf_op jit(solution)/shard_map/ppermute | solution.py:437
  15.3 13.8 %copy-start.19 = (s32[128]{0:T(128)S(1)}, s32[128]{0:T(128)}, u32[]{:S(2)}) copy-start(s32[128]{0:T(128)} %param.17) | copy-start | bytes 1540
  25.0 4.7 %collective-permute-start = (bf16[384,1152]{1,0:T(8,128)(2,1)}, bf16[384,1152]{1,0:T(8,128)(2,1)}, u32[]{:S(2)}, u32[]{:S(2)}) collective-permute-start(bf16[384,1152]{1,0:T(8,128)(2,1)} %get-tuple-element.23), channel_id=1, source_target_pairs={{0,4},{4,0},{8,12},{12,8},{16,20},{20,16},{24,28},{28,24},{32,36},... | collective-permute-start | bytes 2654216 | tf_op jit(solution)/shard_map/ppermute | solution.py:437
  25.6 44.8 %collective-permute-start.7 = (bf16[384,1536]{1,0:T(8,128)(2,1)}, bf16[384,1536]{1,0:T(8,128)(2,1)}, u32[]{:S(2)}, u32[]{:S(2)}) collective-permute-start(bf16[384,1536]{1,0:T(8,128)(2,1)} %refs_4_.1), channel_id=1, source_target_pairs={{0,3},{1,0},{2,1},{3,2},{4,7},{5,4},{6,5},{7,6},{8,11},{9,8},{10,9... | collective-permute-start | bytes 3538952 | tf_op jit(solution)/shard_map/ppermute | solution.py:455
  27.5 42.8 %collective-permute-start.6 = (bf16[384,1536]{1,0:T(8,128)(2,1)}, bf16[384,1536]{1,0:T(8,128)(2,1)}, u32[]{:S(2)}, u32[]{:S(2)}) collective-permute-start(bf16[384,1536]{1,0:T(8,128)(2,1)} %refs_4_.1), channel_id=1, source_target_pairs={{0,1},{1,2},{2,3},{3,0},{4,5},{5,6},{6,7},{7,4},{8,9},{9,10},{10,1... | collective-permute-start | bytes 3538952 | tf_op jit(solution)/shard_map/ppermute | solution.py:455
  31.2 1.2 copy-start
  32.3 1.2 copy-start.1
  36.3 12.3 %collective-permute-start.3 = (bf16[96,1152]{1,0:T(8,128)(2,1)}, bf16[96,1152]{1,0:T(8,128)(2,1)S(1)}, u32[]{:S(2)}, u32[]{:S(2)}) collective-permute-start(bf16[96,1152]{1,0:T(8,128)(2,1)} %get-tuple-element.25), channel_id=1, source_target_pairs={{0,64},{4,68},{8,72},{12,76},{16,80},{20,84},{24,88},{28,92},{32,9... | collective-permute-start | bytes 663560 | tf_op jit(solution)/shard_map/ppermute | solution.py:437
  39.2 9.4 %collective-permute-start.4 = (bf16[96,1152]{1,0:T(8,128)(2,1)}, bf16[96,1152]{1,0:T(8,128)(2,1)S(1)}, u32[]{:S(2)}, u32[]{:S(2)}) collective-permute-start(bf16[96,1152]{1,0:T(8,128)(2,1)} %get-tuple-element.26), channel_id=1, source_target_pairs={{0,128},{4,132},{8,136},{12,140},{16,144},{20,148},{24,152},{28,15... | collective-permute-start | bytes 663560 | tf_op jit(solution)/shard_map/ppermute | solution.py:437
  41.9 6.7 %collective-permute-start.5 = (bf16[96,1152]{1,0:T(8,128)(2,1)}, bf16[96,1152]{1,0:T(8,128)(2,1)S(1)}, u32[]{:S(2)}, u32[]{:S(2)}) collective-permute-start(bf16[96,1152]{1,0:T(8,128)(2,1)} %get-tuple-element.27), channel_id=1, source_target_pairs={{0,192},{4,196},{8,200},{12,204},{16,208},{20,212},{24,216},{28,22... | collective-permute-start | bytes 663560 | tf_op jit(solution)/shard_map/ppermute | solution.py:437
  52.1 19.9 %all-to-all-start = ((bf16[8,16,1152]{2,1,0:T(8,128)(2,1)}), bf16[8,16,1152]{2,1,0:T(8,128)(2,1)S(1)}, u32[]{:S(2)}, u32[]{:S(2)}) async-start(bf16[8,16,1152]{2,1,0:T(8,128)(2,1)} %rs_z.1.dep_ref), calls=%async_computation | async-start | bytes 589824 | tf_op jit(solution)/shard_map/all_to_all | solution.py:470
  61.3 44.6 %collective-permute-start.11 = (bf16[384,1536]{1,0:T(8,128)(2,1)}, bf16[384,1536]{1,0:T(8,128)(2,1)S(1)}, u32[]{:S(2)}, u32[]{:S(2)}) collective-permute-start(bf16[384,1536]{1,0:T(8,128)(2,1)} %refs_4_.1), channel_id=1, source_target_pairs={{0,2},{1,3},{2,0},{3,1},{4,6},{5,7},{6,4},{7,5},{8,10},{9,11},{10,... | collective-permute-start | bytes 3538952 | tf_op jit(solution)/shard_map/ppermute | solution.py:455
  74.6 15.4 %all-to-all-start.1 = ((bf16[8,16,1152]{2,1,0:T(8,128)(2,1)}), bf16[8,16,1152]{2,1,0:T(8,128)(2,1)S(1)}, u32[]{:S(2)}, u32[]{:S(2)}) async-start(bf16[8,16,1152]{2,1,0:T(8,128)(2,1)} %renorm.1.dep_ref), calls=%async_computation.1 | async-start | bytes 589824 | tf_op jit(solution)/shard_map/all_to_all | solution.py:470
  92.5 16.0 %collective-permute-start.10 = (bf16[96,1152]{1,0:T(8,128)(2,1)}, bf16[96,1152]{1,0:T(8,128)(2,1)S(1)}, u32[]{:S(2)}, u32[]{:S(2)}) collective-permute-start(bf16[96,1152]{1,0:T(8,128)(2,1)} %owned.1.dep_ref.rest_0_), channel_id=1, source_target_pairs={{0,192},{4,196},{8,200},{12,204},{16,208},{20,212},{24,216},{28,22... | collective-permute-start | bytes 663560 | tf_op jit(solution)/shard_map/ppermute | solution.py:437
  98.8 9.7 %collective-permute-start.9 = (bf16[96,1152]{1,0:T(8,128)(2,1)}, bf16[96,1152]{1,0:T(8,128)(2,1)S(1)}, u32[]{:S(2)}, u32[]{:S(2)}) collective-permute-start(bf16[96,1152]{1,0:T(8,128)(2,1)} %owned.1.dep_ref.rest_0_), channel_id=1, source_target_pairs={{0,128},{4,132},{8,136},{12,140},{16,144},{20,148},{24,152},{28,15... | collective-permute-start | bytes 663560 | tf_op jit(solution)/shard_map/ppermute | solution.py:437
  98.8 13.2 %collective-permute-start.8 = (bf16[96,1152]{1,0:T(8,128)(2,1)}, bf16[96,1152]{1,0:T(8,128)(2,1)S(1)}, u32[]{:S(2)}, u32[]{:S(2)}) collective-permute-start(bf16[96,1152]{1,0:T(8,128)(2,1)} %owned.1.dep_ref.rest_0_), channel_id=1, source_target_pairs={{0,64},{4,68},{8,72},{12,76},{16,80},{20,84},{24,88},{28,92},{32,9... | collective-permute-start | bytes 663560 | tf_op jit(solution)/shard_map/ppermute | solution.py:437
  106.0 9.8 %copy-start.18 = (f32[384]{0:T(512)S(1)}, f32[384]{0:T(512)}, u32[]{:S(2)}) copy-start(f32[384]{0:T(512)} %param.15) | copy-start | bytes 4612
  106.0 6.0 %copy-start.2 = (bf16[384,1536]{1,0:T(8,128)(2,1)}, bf16[384,1536]{1,0:T(8,128)(2,1)S(1)}, u32[]{:S(2)}) copy-start(bf16[384,1536]{1,0:T(8,128)(2,1)S(1)} %collective-permute-done.11.rest_5_.refs_6_) | copy-start | bytes 3538948
  108.5 3.5 %copy-start.8 = (bf16[96,1152]{1,0:T(8,128)(2,1)}, bf16[96,1152]{1,0:T(8,128)(2,1)S(1)}, u32[]{:S(2)}) copy-start(bf16[96,1152]{1,0:T(8,128)(2,1)S(1)} %collective-permute-done.10.rest_3_) | copy-start | bytes 663556
  108.5 3.5 %copy-start.10 = (bf16[96,1152]{1,0:T(8,128)(2,1)}, bf16[96,1152]{1,0:T(8,128)(2,1)S(1)}, u32[]{:S(2)}) copy-start(bf16[96,1152]{1,0:T(8,128)(2,1)S(1)} %collective-permute-done.9.rest_2_) | copy-start | bytes 663556
  115.0 3.1 %collective-permute-start.12 = (bf16[384,1152]{1,0:T(8,128)(2,1)}, bf16[384,1152]{1,0:T(8,128)(2,1)S(1)}, u32[]{:S(2)}, u32[]{:S(2)}) collective-permute-start(bf16[384,1152]{1,0:T(8,128)(2,1)} %ag_x.1.own_ref), channel_id=1, source_target_pairs={{0,4},{4,0},{8,12},{12,8},{16,20},{20,16},{24,28},{28,24},{32,36},... | collective-permute-start | bytes 2654216 | tf_op jit(solution)/shard_map/ppermute | solution.py:437
  124.3 11.0 %collective-permute-start.14 = (bf16[256,384]{1,0:T(8,128)(2,1)}, bf16[256,384]{1,0:T(8,128)(2,1)S(1)}, u32[]{:S(2)}, u32[]{:S(2)}) collective-permute-start(bf16[256,384]{1,0:T(8,128)(2,1)} %get-tuple-element.29), channel_id=1, source_target_pairs={{0,2},{1,3},{2,0},{3,1},{4,6},{5,7},{6,4},{7,5},{8,10},{9,11},{10,... | collective-permute-start | bytes 589832 | tf_op jit(solution)/shard_map/ppermute | solution.py:455
  124.3 11.1 %collective-permute-start.15 = (bf16[256,384]{1,0:T(8,128)(2,1)}, bf16[256,384]{1,0:T(8,128)(2,1)S(1)}, u32[]{:S(2)}, u32[]{:S(2)}) collective-permute-start(bf16[256,384]{1,0:T(8,128)(2,1)} %get-tuple-element.30), channel_id=1, source_target_pairs={{0,3},{1,0},{2,1},{3,2},{4,7},{5,4},{6,5},{7,6},{8,11},{9,8},{10,9... | collective-permute-start | bytes 589832 | tf_op jit(solution)/shard_map/ppermute | solution.py:455
  124.3 12.7 %collective-permute-start.13 = (bf16[256,384]{1,0:T(8,128)(2,1)}, bf16[256,384]{1,0:T(8,128)(2,1)S(1)}, u32[]{:S(2)}, u32[]{:S(2)}) collective-permute-start(bf16[256,384]{1,0:T(8,128)(2,1)} %get-tuple-element.28.dep_ref.rest_1_), channel_id=1, source_target_pairs={{0,1},{1,2},{2,3},{3,0},{4,5},{5,6},{6,7},{7,4},{8,9},{9,10},{10,1... | collective-permute-start | bytes 589832 | tf_op jit(solution)/shard_map/ppermute | solution.py:455
  135.3 1.7 %copy-start.12 = (bf16[256,384]{1,0:T(8,128)(2,1)}, bf16[256,384]{1,0:T(8,128)(2,1)S(1)}, u32[]{:S(2)}) copy-start(bf16[256,384]{1,0:T(8,128)(2,1)S(1)} %collective-permute-done.14.refs_2_) | copy-start | bytes 589828
  135.3 1.7 %copy-start.13 = (bf16[256,384]{1,0:T(8,128)(2,1)}, bf16[256,384]{1,0:T(8,128)(2,1)S(1)}, u32[]{:S(2)}) copy-start(bf16[256,384]{1,0:T(8,128)(2,1)S(1)} %collective-permute-done.15.refs_3_) | copy-start | bytes 589828
  143.2 8.0 %collective-permute-start.16 = (bf16[256,384]{1,0:T(8,128)(2,1)}, bf16[256,384]{1,0:T(8,128)(2,1)S(1)}, u32[]{:S(2)}, u32[]{:S(2)}) collective-permute-start(bf16[256,384]{1,0:T(8,128)(2,1)} %get-tuple-element.32), channel_id=1, source_target_pairs={{0,1},{1,2},{2,3},{3,0},{4,5},{5,6},{6,7},{7,4},{8,9},{9,10},{10,1... | collective-permute-start | bytes 589832 | tf_op jit(solution)/shard_map/ppermute | solution.py:455
  143.4 10.8 %collective-permute-start.17 = (bf16[256,384]{1,0:T(8,128)(2,1)}, bf16[256,384]{1,0:T(8,128)(2,1)S(1)}, u32[]{:S(2)}, u32[]{:S(2)}) collective-permute-start(bf16[256,384]{1,0:T(8,128)(2,1)} %get-tuple-element.33), channel_id=1, source_target_pairs={{0,2},{1,3},{2,0},{3,1},{4,6},{5,7},{6,4},{7,5},{8,10},{9,11},{10,... | collective-permute-start | bytes 589832 | tf_op jit(solution)/shard_map/ppermute | solution.py:455
  145.8 9.4 %collective-permute-start.18 = (bf16[256,384]{1,0:T(8,128)(2,1)}, bf16[256,384]{1,0:T(8,128)(2,1)S(1)}, u32[]{:S(2)}, u32[]{:S(2)}) collective-permute-start(bf16[256,384]{1,0:T(8,128)(2,1)} %get-tuple-element.34), channel_id=1, source_target_pairs={{0,3},{1,0},{2,1},{3,2},{4,7},{5,4},{6,5},{7,6},{8,11},{9,8},{10,9... | collective-permute-start | bytes 589832 | tf_op jit(solution)/shard_map/ppermute | solution.py:455
  151.2 4.0 %copy-start.15 = (bf16[256,384]{1,0:T(8,128)(2,1)}, bf16[256,384]{1,0:T(8,128)(2,1)S(1)}, u32[]{:S(2)}) copy-start(bf16[256,384]{1,0:T(8,128)(2,1)S(1)} %collective-permute-done.16.refs_1_) | copy-start | bytes 589828
  154.2 1.0 copy-start.16
  (9 other events, 6.6 us)

commit v7 on v6

--- a/solution.py
+++ b/solution.py
@@ -59,10 +59,9 @@
     return pl.BlockSpec(shape, lambda i: (0,) * len(shape))
 
 
-def keys_kernel(t_ref, wk_ref, wv_ref, wr_ref, kv_ref, rates_ref):
+def keys_kernel(t_ref, w_ref, wr_ref, kv_ref, rates_ref):
     t = t_ref[...]
-    kv_ref[:, :DH] = mm(t, wk_ref[...]).astype(BF)
-    kv_ref[:, DH:] = mm(t, wv_ref[...]).astype(BF)
+    kv_ref[...] = mm(t, w_ref[...]).astype(BF)
     raw = lax.dot_general(t, wr_ref[...], NT, preferred_element_type=F32)
     rates_ref[...] = (0.25 / math.sqrt(TOKENS)) * (
         jnp.maximum(raw, 0.0) + jnp.log1p(jnp.exp(-jnp.abs(raw)))
@@ -77,8 +76,7 @@
         grid=(rows // block,),
         in_specs=[
             pl.BlockSpec((block, wide), lambda i: (i, 0)),
-            pl.BlockSpec((wide, DH), lambda i: (0, 1)),
-            pl.BlockSpec((wide, DH), lambda i: (0, 2)),
+            pl.BlockSpec((pl.Element(wide), pl.Element(2 * DH)), lambda i: (0, DH)),
             full((3, wide)),
         ],
         out_specs=[
@@ -88,7 +86,7 @@
         out_shape=[sds((rows, 2 * DH), BF), sds((rows, 3), F32)],
         compiler_params=params(),
         name="keys",
-    )(tokens, qkv_weight, qkv_weight, rate_weight.T)
+    )(tokens, qkv_weight, rate_weight.T)
 
 
 def update_kernel(pos_ref, kv_ref, r_ref, w1_ref, w3_ref, w2_ref, send_ref, keep_ref, second):
@@ -211,22 +209,20 @@
     )(old, got, *deps)
 
 
-def owned_kernel(got_ref, *rest):
-    out = rest[-1]
-    for o in range(OWNERS):
-        out[o * ROWS : (o + 1) * ROWS, :] = got_ref[o]
-
-
-def owned(got, deps):
-    return pl.pallas_call(
-        owned_kernel,
-        grid=(1,),
-        in_specs=[full((ZS, ROWS, WIDE))] + [DEP] * len(deps),
-        out_specs=full((XROWS, WIDE)),
-        out_shape=sds((XROWS, WIDE), BF),
-        compiler_params=params(),
-        name="owned",
-    )(got, *deps)
+def hold_kernel(value_ref, dep_ref, out_ref):
+    pass
+
+
+def hold(value, dep):
+    return pl.pallas_call(
+        hold_kernel,
+        in_specs=[DEP, DEP],
+        out_specs=DEP,
+        out_shape=sds(value.shape, value.dtype),
+        input_output_aliases={0: 0},
+        compiler_params=params(),
+        name="hold",
+    )(value, dep)
 
 
 def ag_x_kernel(pos_ref, *rest):
@@ -469,17 +465,18 @@
     def exchange(blocks):
         return lax.all_to_all(blocks, "tok", 0, 0, axis_index_groups=ALONG_Z)
 
-    own, *gives = rs_x(pos, keep, got, [before, after])
+    query = project(tokens, qkv_weight, [give])
+    own, *gives = rs_x(pos, keep, got, [before, after, query])
     got = [send(g, shift_x(d + 1)) for d, g in enumerate(gives)]
-    query = project(tokens, qkv_weight, [own, ends, old])
     att = functools.partial(attend, pos=pos, ends=ends, query=query, before=before, mine=kv, after=after)
-    total = rs_z(own, got, [query])
+    att0 = att(0, dep=own)
+    total = rs_z(own, got, [att0, old])
     got = exchange(total)
     att1 = att(1, dep=total)
     fresh = renorm(old, got, [att1, weights[1], weights[3]])
     got = exchange(fresh)
     att2 = att(2, dep=fresh)
-    block = owned(got, [att2])
+    block = hold(got, att2)[:OWNERS].reshape(XROWS, WIDE)
     att3 = att(3, dep=block)
     half = ag_x(pos, [block] + [send(block, shift_x(d)) for d in range(1, XS)], [att3, weights[2]])
     other = send(half, SWAP_C)
@@ -488,7 +485,6 @@
         apply, pos=pos, query=query, own=half, other=other, gain=fast_gain[None, :]
     )
     away = mix((1, 2, 3), attended=[att1, att2, att3], deps=[])
-    att0 = att(0, dep=away[0])
     [home] = mix((0,), attended=[att0], deps=[away[0]])
     parts = spread([home, *away])
     ahead = output(pos, parts, weights)

time: 159 us -> 159 us (level)
  local copies, waits for them, and re-layouts: 8.37 us -> 10.7 us
    ppermute x10, waiting for transfers between devices: 10.3 us -> 4.8 us  [body(): send = lambda value, pairs: lax.ppermute(value, 'tok', pairs)]
    ppermute x9, waiting for transfers between devices: 9.1 us -> 14 us  [spread(): lax.ppermute(p, 'head', shift_h(d))]
    all_to_all x2, starting transfers between devices: 15.1 us -> 10.9 us  [exchange(): return lax.all_to_all(blocks, 'tok', 0, 0, axis_index_groups=ALONG_Z)]
    pallas_call x1, Pallas kernels: 1.68 us -> 0.01 us  [hold(): pl.pallas_call(hold_kernel, in_specs=[DEP, DEP], out_specs=DEP, out_shape...]
    ppermute x10, starting transfers between devices: 21.9 us -> 23.5 us  [body(): send = lambda value, pairs: lax.ppermute(value, 'tok', pairs)]
    all_to_all x2, waiting for transfers between devices: 4.69 us -> 6.3 us  [exchange(): return lax.all_to_all(blocks, 'tok', 0, 0, axis_index_groups=ALONG_Z)]
    unnamed x40 -> x42, local copies, waits for them, and re-layouts: 7.05 us -> 8.44 us
  transfers between devices with their start and end apart: 21 -> 21, of which waited for: 11 -> 10; matrix products, arithmetic and copies ran while one was open for 3% -> 3% of each run, Pallas kernels for 33% -> 32%
where the time goes in v7:
time: 159 us
  Pallas kernels  73.6 us (46%)
  starting transfers between devices  46.8 us (29%)
  waiting for transfers between devices  25.1 us (16%)
  local copies, waits for them, and re-layouts  10.7 us (7%)
  other arithmetic  2.64 us (2%)
    pallas_call x4, Pallas kernels, attend(): pl.pallas_call(functools.partial(attend_kernel, ahead), grid=(1,), in_spe...  26.4 us
    ppermute x10, starting transfers between devices, body(): send = lambda value, pairs: lax.ppermute(value, 'tok', pairs)  23.5 us
    ppermute x9, waiting for transfers between devices, spread(): lax.ppermute(p, 'head', shift_h(d))  14 us
    ppermute x9, starting transfers between devices, spread(): lax.ppermute(p, 'head', shift_h(d))  12.3 us
    all_to_all x2, starting transfers between devices, exchange(): return lax.all_to_all(blocks, 'tok', 0, 0, axis_index_groups=ALONG_Z)  10.9 us
    pallas_call x1, Pallas kernels, update(): pl.pallas_call(update_kernel, grid=(1,), in_specs=[SMEM, full(kv.shape),...  9.67 us
    pallas_call x2, Pallas kernels, apply(): pl.pallas_call(functools.partial(apply_kernel, aheads), grid=(1,), in_spe...  8.86 us
    unnamed x42, local copies, waits for them, and re-layouts  8.44 us
  transfers between devices with their start and end apart: 21, of which 10 were waited for; matrix products, arithmetic and copies ran while one was open for 3% of the time, Pallas kernels for 32%

profile of v7, /device:TPU:1, one launch (start us, length us, event | category | flops | bytes accessed | tf_op | source)
XLA Modules:
  0.0 159.0 jit_solution(3814287909707314240)
XLA Ops:
  0.0 6.7 %keys.1 = (bf16[1024,768]{1,0:T(8,128)(2,1)}, f32[1024,3]{1,0:T(8,128)}) custom-call(bf16[1024,1536]{1,0:T(8,128)(2,1)} %t_ref.3, bf16[1536,1152]{1,0:T(8,128)(2,1)} %w_ref.3, bf16[3,1536]{1,0:T(4,128)(2,1)} %bitcast.16), custom_call_target="tpu_custom_call" | custom-call | tf_op jit(solution)/shard_map/keys/pallas_call | solution.py:74
  6.7 4.9 %collective-permute-start.1 = (bf16[1024,768]{1,0:T(8,128)(2,1)}, bf16[1024,768]{1,0:T(8,128)(2,1)S(1)}, u32[]{:S(2)}, u32[]{:S(2)}) collective-permute-start(bf16[1024,768]{1,0:T(8,128)(2,1)} %get-tuple-element.20.kv_ref.mine), channel_id=1, source_target_pairs={{0,4},{4,8},{8,12},{12,16},{16,20},{20,24},{24,28},{28,32},{32,36}... | collective-permute-start | bytes 4718600 | tf_op jit(solution)/shard_map/ppermute | solution.py:433
  11.7 1.9 %collective-permute-start.2 = (bf16[1024,768]{1,0:T(8,128)(2,1)}, bf16[1024,768]{1,0:T(8,128)(2,1)S(1)}, u32[]{:S(2)}, u32[]{:S(2)}) collective-permute-start(bf16[1024,768]{1,0:T(8,128)(2,1)} %get-tuple-element.20.kv_ref.mine), channel_id=1, source_target_pairs={{4,0},{8,4},{12,8},{16,12},{20,16},{24,20},{28,24},{32,28},{36,32}... | collective-permute-start | bytes 4718600 | tf_op jit(solution)/shard_map/ppermute | solution.py:433
  14.2 9.7 %update.1 = (bf16[384,1152]{1,0:T(8,128)(2,1)}, f32[384,1152]{1,0:T(8,128)}) custom-call(s32[4]{0:T(128)} %pad_add_fusion.pos_ref, bf16[1024,768]{1,0:T(8,128)(2,1)} %get-tuple-element.20.kv_ref.mine, f32[1024,3]{1,0:T(8,128)} %get-tuple-element.21.r_ref, bf16[1,384,768]{2,1,0:T(8,128)(2,1)} %w1_ref.1, bf16[1,384,768]{2,1,0:T(8,128)(2,1)} %w3_ref.1, ...), custom_call_target="tpu_custom_call" | custom-call | tf_op jit(solution)/shard_map/update/pallas_call | solution.py:121
  26.8 5.2 %project.1.rest_2_.q_ref = bf16[1024,384]{1,0:T(8,128)(2,1)} custom-call(bf16[1024,1536]{1,0:T(8,128)(2,1)} %t_ref.3, bf16[1536,1152]{1,0:T(8,128)(2,1)} %w_ref.3, bf16[384,1152]{1,0:T(8,128)(2,1)} %get-tuple-element.22.rest_0_), custom_call_target="tpu_custom_call" | custom-call | tf_op jit(solution)/shard_map/project/pallas_call | solution.py:256
  35.8 2.8 %rs_x.1 = (f32[96,1152]{1,0:T(8,128)}, bf16[96,1152]{1,0:T(8,128)(2,1)}, bf16[96,1152]{1,0:T(8,128)(2,1)}, bf16[96,1152]{1,0:T(8,128)(2,1)}) custom-call(s32[4]{0:T(128)} %pad_add_fusion.pos_ref, f32[384,1152]{1,0:T(8,128)} %get-tuple-element.23.keep_ref, bf16[384,1152]{1,0:T(8,128)(2,1)} %collective-permute-done.got_ref, bf16[1024,768]{1,0:T(8,128)(2,1)} %copy-done, ...), custom_call_target="tpu_custom_call" | custom-call | tf_op jit(solution)/shard_map/rs_x/pallas_call | solution.py:149
  38.7 4.8 %collective-permute-start.3 = (bf16[96,1152]{1,0:T(8,128)(2,1)}, bf16[96,1152]{1,0:T(8,128)(2,1)S(1)}, u32[]{:S(2)}, u32[]{:S(2)}) collective-permute-start(bf16[96,1152]{1,0:T(8,128)(2,1)} %get-tuple-element.25), channel_id=1, source_target_pairs={{0,64},{4,68},{8,72},{12,76},{16,80},{20,84},{24,88},{28,92},{32,9... | collective-permute-start | bytes 663560 | tf_op jit(solution)/shard_map/ppermute | solution.py:433
  43.5 2.7 %collective-permute-start.4 = (bf16[96,1152]{1,0:T(8,128)(2,1)}, bf16[96,1152]{1,0:T(8,128)(2,1)S(1)}, u32[]{:S(2)}, u32[]{:S(2)}) collective-permute-start(bf16[96,1152]{1,0:T(8,128)(2,1)} %get-tuple-element.26), channel_id=1, source_target_pairs={{0,128},{4,132},{8,136},{12,140},{16,144},{20,148},{24,152},{28,15... | collective-permute-start | bytes 663560 | tf_op jit(solution)/shard_map/ppermute | solution.py:433
  47.7 6.6 %attend_0.1.rest_0_ = f32[256,384]{1,0:T(8,128)} custom-call(s32[4]{0:T(128)} %pad_add_fusion.pos_ref, s32[1,128]{1,0:T(1,128)} %bitcast.17, bf16[1024,384]{1,0:T(8,128)(2,1)} %project.1.rest_2_.q_ref, bf16[1024,768]{1,0:T(8,128)(2,1)} %copy-done, bf16[1024,768]{1,0:T(8,128)(2,1)} %get-tuple-element.20.kv_ref.mine, bf16[1024,768]{1,0:T(8,128)(2,1)} %copy-done.1, ...), custom_call_target="tpu_custom_call" | custom-call | tf_op jit(solution)/shard_map/attend_0/pallas_call | solution.py:328
  54.3 1.8 %collective-permute-done.4.g2 = bf16[96,1152]{1,0:T(8,128)(2,1)S(1)} collective-permute-done((bf16[96,1152]{1,0:T(8,128)(2,1)}, bf16[96,1152]{1,0:T(8,128)(2,1)S(1)}, u32[]{:S(2)}, u32[]{:S(2)}) %collective-permute-start.4) | collective-permute-done | bytes 221216 | tf_op jit(solution)/shard_map/ppermute | solution.py:433
  57.5 2.1 %rs_z.1.dep_ref = bf16[8,16,1152]{2,1,0:T(8,128)(2,1)} custom-call(f32[96,1152]{1,0:T(8,128)} %get-tuple-element.24.dep_ref.own_ref, bf16[96,1152]{1,0:T(8,128)(2,1)} %copy-done.10, bf16[96,1152]{1,0:T(8,128)(2,1)} %copy-done.11, bf16[96,1152]{1,0:T(8,128)(2,1)} %copy-done.12, f32[256,384]{1,0:T(8,128)} %attend_0.1.rest_0_, ...), custom_call_target="tpu_custom_call" | custom-call | tf_op jit(solution)/shard_map/rs_z/pallas_call | solution.py:172
  59.6 5.6 %all-to-all-start = ((bf16[8,16,1152]{2,1,0:T(8,128)(2,1)}), bf16[8,16,1152]{2,1,0:T(8,128)(2,1)S(1)}, u32[]{:S(2)}, u32[]{:S(2)}) async-start(bf16[8,16,1152]{2,1,0:T(8,128)(2,1)} %rs_z.1.dep_ref), calls=%async_computation | async-start | bytes 589824 | tf_op jit(solution)/shard_map/all_to_all | solution.py:466
  65.1 1.6 %collective-permute-start.11 = (bf16[384,1536]{1,0:T(8,128)(2,1)}, bf16[384,1536]{1,0:T(8,128)(2,1)S(1)}, u32[]{:S(2)}, u32[]{:S(2)}) collective-permute-start(bf16[384,1536]{1,0:T(8,128)(2,1)} %refs_4_.1), channel_id=1, source_target_pairs={{0,2},{1,3},{2,0},{3,1},{4,6},{5,7},{6,4},{7,5},{8,10},{9,11},{10,... | collective-permute-start | bytes 3538952 | tf_op jit(solution)/shard_map/ppermute | solution.py:451
  66.7 6.6 %attend_1.1.rest_0_ = f32[256,384]{1,0:T(8,128)} custom-call(s32[4]{0:T(128)} %pad_add_fusion.pos_ref, s32[1,128]{1,0:T(1,128)} %bitcast.18, bf16[1024,384]{1,0:T(8,128)(2,1)} %project.1.rest_2_.q_ref, bf16[1024,768]{1,0:T(8,128)(2,1)} %copy-done, bf16[1024,768]{1,0:T(8,128)(2,1)} %get-tuple-element.20.kv_ref.mine, bf16[1024,768]{1,0:T(8,128)(2,1)} %copy-done.1, ...), custom_call_target="tpu_custom_call" | custom-call | tf_op jit(solution)/shard_map/attend_1/pallas_call | solution.py:328
  73.3 2.4 %all-to-all-done.got_ref = bf16[8,16,1152]{2,1,0:T(8,128)(2,1)S(1)} async-done(((bf16[8,16,1152]{2,1,0:T(8,128)(2,1)}), bf16[8,16,1152]{2,1,0:T(8,128)(2,1)S(1)}, u32[]{:S(2)}, u32[]{:S(2)}) %all-to-all-start) | async-done | bytes 294944 | tf_op jit(solution)/shard_map/all_to_all | solution.py:466
  76.4 1.9 %renorm.1.dep_ref = bf16[8,16,1152]{2,1,0:T(8,128)(2,1)} custom-call(f32[16,1152]{1,0:T(8,128)} %maximum_convert_fusion.rest_1_.old_ref, bf16[8,16,1152]{2,1,0:T(8,128)(2,1)} %copy-done.6, f32[256,384]{1,0:T(8,128)} %attend_1.1.rest_0_, bf16[384,1536]{1,0:T(8,128)(2,1)} %collective-permute-done.6.rest_1_.refs_5_, ...), custom_call_target="tpu_custom_call" | custom-call | tf_op jit(solution)/shard_map/renorm/pallas_call | solution.py:201
  78.3 5.4 %all-to-all-start.1 = ((bf16[8,16,1152]{2,1,0:T(8,128)(2,1)}), bf16[8,16,1152]{2,1,0:T(8,128)(2,1)S(1)}, u32[]{:S(2)}, u32[]{:S(2)}) async-start(bf16[8,16,1152]{2,1,0:T(8,128)(2,1)} %renorm.1.dep_ref), calls=%async_computation.1 | async-start | bytes 589824 | tf_op jit(solution)/shard_map/all_to_all | solution.py:466
  83.7 6.6 %attend_2.1.dep_ref.rest_1_ = f32[256,384]{1,0:T(8,128)} custom-call(s32[4]{0:T(128)} %pad_add_fusion.pos_ref, s32[1,128]{1,0:T(1,128)} %bitcast.19, bf16[1024,384]{1,0:T(8,128)(2,1)} %project.1.rest_2_.q_ref, bf16[1024,768]{1,0:T(8,128)(2,1)} %copy-done, bf16[1024,768]{1,0:T(8,128)(2,1)} %get-tuple-element.20.kv_ref.mine, bf16[1024,768]{1,0:T(8,128)(2,1)} %copy-done.1, ...), custom_call_target="tpu_custom_call" | custom-call | tf_op jit(solution)/shard_map/attend_2/pallas_call | solution.py:328
  90.3 3.9 %all-to-all-done.1.value_ref = bf16[8,16,1152]{2,1,0:T(8,128)(2,1)S(1)} async-done(((bf16[8,16,1152]{2,1,0:T(8,128)(2,1)}), bf16[8,16,1152]{2,1,0:T(8,128)(2,1)S(1)}, u32[]{:S(2)}, u32[]{:S(2)}) %all-to-all-start.1) | async-done | bytes 294944 | tf_op jit(solution)/shard_map/all_to_all | solution.py:466
  95.9 2.4 %collective-permute-start.10 = (bf16[96,1152]{1,0:T(8,128)(2,1)S(1)}, bf16[96,1152]{1,0:T(8,128)(2,1)S(1)}, u32[]{:S(2)}, u32[]{:S(2)}) collective-permute-start(bf16[96,1152]{1,0:T(8,128)(2,1)S(1)} %bitcast.11), channel_id=1, source_target_pairs={{0,192},{4,196},{8,200},{12,204},{16,208},{20,212},{24,216},{28,22... | collective-permute-start | bytes 663560 | tf_op jit(solution)/shard_map/ppermute | solution.py:433
  99.6 6.6 %attend_3.1.rest_4_.rest_2_ = f32[256,384]{1,0:T(8,128)} custom-call(s32[4]{0:T(128)} %pad_add_fusion.pos_ref, s32[1,128]{1,0:T(1,128)} %bitcast.20, bf16[1024,384]{1,0:T(8,128)(2,1)} %project.1.rest_2_.q_ref, bf16[1024,768]{1,0:T(8,128)(2,1)} %copy-done, bf16[1024,768]{1,0:T(8,128)(2,1)} %get-tuple-element.20.kv_ref.mine, bf16[1024,768]{1,0:T(8,128)(2,1)} %copy-done.1, ...), custom_call_target="tpu_custom_call" | custom-call | tf_op jit(solution)/shard_map/attend_3/pallas_call | solution.py:328
  108.9 2.3 %ag_x.1.own_ref = bf16[384,1152]{1,0:T(8,128)(2,1)} custom-call(s32[4]{0:T(128)} %pad_add_fusion.pos_ref, bf16[96,1152]{1,0:T(8,128)(2,1)} %bitcast.15, bf16[96,1152]{1,0:T(8,128)(2,1)} %copy-done.8, bf16[96,1152]{1,0:T(8,128)(2,1)} %copy-done.9, bf16[96,1152]{1,0:T(8,128)(2,1)} %copy-done.7, f32[256,384]{1,0:T(8,128)} %attend_3.1.rest_4_.rest_2_, ...), custom_call_target="tpu_custom_call" | custom-call | tf_op jit(solution)/shard_map/ag_x/pallas_call | solution.py:237
  111.2 4.6 %collective-permute-start.12 = (bf16[384,1152]{1,0:T(8,128)(2,1)}, bf16[384,1152]{1,0:T(8,128)(2,1)S(1)}, u32[]{:S(2)}, u32[]{:S(2)}) collective-permute-start(bf16[384,1152]{1,0:T(8,128)(2,1)} %ag_x.1.own_ref), channel_id=1, source_target_pairs={{0,4},{4,0},{8,12},{12,8},{16,20},{20,16},{24,28},{28,24},{32,36},... | collective-permute-start | bytes 2654216 | tf_op jit(solution)/shard_map/ppermute | solution.py:433
  116.4 1.7 %collective-permute-done.12.other_ref = bf16[384,1152]{1,0:T(8,128)(2,1)S(1)} collective-permute-done((bf16[384,1152]{1,0:T(8,128)(2,1)}, bf16[384,1152]{1,0:T(8,128)(2,1)S(1)}, u32[]{:S(2)}, u32[]{:S(2)}) %collective-permute-start.12) | collective-permute-done | bytes 884768 | tf_op jit(solution)/shard_map/ppermute | solution.py:433
  119.0 5.3 %apply_3.1 = (bf16[256,384]{1,0:T(8,128)(2,1)}, bf16[256,384]{1,0:T(8,128)(2,1)}, bf16[256,384]{1,0:T(8,128)(2,1)}) custom-call(s32[4]{0:T(128)} %pad_add_fusion.pos_ref, bf16[1024,384]{1,0:T(8,128)(2,1)} %project.1.rest_2_.q_ref, bf16[384,1152]{1,0:T(8,128)(2,1)} %ag_x.1.own_ref, bf16[384,1152]{1,0:T(8,128)(2,1)} %copy-done.3, ...), custom_call_target="tpu_custom_call" | custom-call | tf_op jit(solution)/shard_map/apply_3/pallas_call | solution.py:363
  127.8 3.5 %apply_1.1.refs_0_ = bf16[256,384]{1,0:T(8,128)(2,1)} custom-call(s32[4]{0:T(128)} %pad_add_fusion.pos_ref, bf16[1024,384]{1,0:T(8,128)(2,1)} %project.1.rest_2_.q_ref, bf16[384,1152]{1,0:T(8,128)(2,1)} %ag_x.1.own_ref, bf16[384,1152]{1,0:T(8,128)(2,1)} %copy-done.3, f32[1,384]{1,0:T(1,128)} %broadcast_in_dim.24.gain_ref, f32[256,384]{1,0:T(8,128)} %attend_0.1.rest_0_, ...), custom_call_target="tpu_custom_call" | custom-call | tf_op jit(solution)/shard_map/apply_1/pallas_call | solution.py:363
  131.9 4.1 %collective-permute-done.14.refs_2_ = bf16[256,384]{1,0:T(8,128)(2,1)S(1)} collective-permute-done((bf16[256,384]{1,0:T(8,128)(2,1)}, bf16[256,384]{1,0:T(8,128)(2,1)S(1)}, u32[]{:S(2)}, u32[]{:S(2)}) %collective-permute-start.14) | collective-permute-done | bytes 196640 | tf_op jit(solution)/shard_map/ppermute | solution.py:451
  137.4 5.5 %output.1 = (bf16[256,384]{1,0:T(8,128)(2,1)}, bf16[256,384]{1,0:T(8,128)(2,1)}, bf16[256,384]{1,0:T(8,128)(2,1)}, bf16[256,384]{1,0:T(8,128)(2,1)}) custom-call(s32[4]{0:T(128)} %pad_add_fusion.pos_ref, bf16[256,384]{1,0:T(8,128)(2,1)} %apply_1.1.refs_0_, bf16[256,384]{1,0:T(8,128)(2,1)} %copy-done.13, bf16[256,384]{1,0:T(8,128)(2,1)} %copy-done.14, ...), custom_call_target="tpu_custom_call" | custom-call | tf_op jit(solution)/shard_map/output/pallas_call | solution.py:388
  144.4 2.7 %collective-permute-start.17 = (bf16[256,384]{1,0:T(8,128)(2,1)}, bf16[256,384]{1,0:T(8,128)(2,1)S(1)}, u32[]{:S(2)}, u32[]{:S(2)}) collective-permute-start(bf16[256,384]{1,0:T(8,128)(2,1)} %get-tuple-element.33), channel_id=1, source_target_pairs={{0,2},{1,3},{2,0},{3,1},{4,6},{5,7},{6,4},{7,5},{8,10},{9,11},{10,... | collective-permute-start | bytes 589832 | tf_op jit(solution)/shard_map/ppermute | solution.py:451
  147.1 3.1 %collective-permute-done.16.refs_1_ = bf16[256,384]{1,0:T(8,128)(2,1)S(1)} collective-permute-done((bf16[256,384]{1,0:T(8,128)(2,1)}, bf16[256,384]{1,0:T(8,128)(2,1)S(1)}, u32[]{:S(2)}, u32[]{:S(2)}) %collective-permute-start.16) | collective-permute-done | bytes 196640 | tf_op jit(solution)/shard_map/ppermute | solution.py:451
  150.2 5.8 %collective-permute-done.17.refs_2_ = bf16[256,384]{1,0:T(8,128)(2,1)S(1)} collective-permute-done((bf16[256,384]{1,0:T(8,128)(2,1)}, bf16[256,384]{1,0:T(8,128)(2,1)S(1)}, u32[]{:S(2)}, u32[]{:S(2)}) %collective-permute-start.17) | collective-permute-done | bytes 196640 | tf_op jit(solution)/shard_map/ppermute | solution.py:451
  156.8 2.2 %arrange.1 = bf16[1024,384]{1,0:T(8,128)(2,1)} custom-call(s32[4]{0:T(128)} %pad_add_fusion.pos_ref, bf16[256,384]{1,0:T(8,128)(2,1)} %get-tuple-element.31.refs_0_, bf16[256,384]{1,0:T(8,128)(2,1)} %copy-done.16, bf16[256,384]{1,0:T(8,128)(2,1)} %copy-done.17, bf16[256,384]{1,0:T(8,128)(2,1)} %copy-done.18), custom_call_target="tpu_custom_call" | custom-call | tf_op jit(solution)/shard_map/arrange/pallas_call | solution.py:408
  (75 shorter events, 25.7 us)
Async XLA Ops:
  6.7 27.4 %collective-permute-start.1 = (bf16[1024,768]{1,0:T(8,128)(2,1)}, bf16[1024,768]{1,0:T(8,128)(2,1)S(1)}, u32[]{:S(2)}, u32[]{:S(2)}) collective-permute-start(bf16[1024,768]{1,0:T(8,128)(2,1)} %get-tuple-element.20.kv_ref.mine), channel_id=1, source_target_pairs={{0,4},{4,8},{8,12},{12,16},{16,20},{20,24},{24,28},{28,32},{32,36}... | collective-permute-start | bytes 4718600 | tf_op jit(solution)/shard_map/ppermute | solution.py:433
  11.7 22.5 %collective-permute-start.2 = (bf16[1024,768]{1,0:T(8,128)(2,1)}, bf16[1024,768]{1,0:T(8,128)(2,1)S(1)}, u32[]{:S(2)}, u32[]{:S(2)}) collective-permute-start(bf16[1024,768]{1,0:T(8,128)(2,1)} %get-tuple-element.20.kv_ref.mine), channel_id=1, source_target_pairs={{4,0},{8,4},{12,8},{16,12},{20,16},{24,20},{28,24},{32,28},{36,32}... | collective-permute-start | bytes 4718600 | tf_op jit(solution)/shard_map/ppermute | solution.py:433
  23.9 9.7 %copy-start.20 = (s32[128]{0:T(128)S(1)}, s32[128]{0:T(128)}, u32[]{:S(2)}) copy-start(s32[128]{0:T(128)} %param.17) | copy-start | bytes 1540
  23.9 10.3 %collective-permute-start = (bf16[384,1152]{1,0:T(8,128)(2,1)}, bf16[384,1152]{1,0:T(8,128)(2,1)}, u32[]{:S(2)}, u32[]{:S(2)}) collective-permute-start(bf16[384,1152]{1,0:T(8,128)(2,1)} %get-tuple-element.22.rest_0_), channel_id=1, source_target_pairs={{0,4},{4,0},{8,12},{12,8},{16,20},{20,16},{24,28},{28,24},{32,36},... | collective-permute-start | bytes 2654216 | tf_op jit(solution)/shard_map/ppermute | solution.py:433
  23.9 49.4 %collective-permute-start.6 = (bf16[384,1536]{1,0:T(8,128)(2,1)}, bf16[384,1536]{1,0:T(8,128)(2,1)}, u32[]{:S(2)}, u32[]{:S(2)}) collective-permute-start(bf16[384,1536]{1,0:T(8,128)(2,1)} %refs_4_.1), channel_id=1, source_target_pairs={{0,1},{1,2},{2,3},{3,0},{4,5},{5,6},{6,7},{7,4},{8,9},{9,10},{10,1... | collective-permute-start | bytes 3538952 | tf_op jit(solution)/shard_map/ppermute | solution.py:451
  25.2 48.1 %collective-permute-start.7 = (bf16[384,1536]{1,0:T(8,128)(2,1)}, bf16[384,1536]{1,0:T(8,128)(2,1)}, u32[]{:S(2)}, u32[]{:S(2)}) collective-permute-start(bf16[384,1536]{1,0:T(8,128)(2,1)} %refs_4_.1), channel_id=1, source_target_pairs={{0,3},{1,0},{2,1},{3,2},{4,7},{5,4},{6,5},{7,6},{8,11},{9,8},{10,9... | collective-permute-start | bytes 3538952 | tf_op jit(solution)/shard_map/ppermute | solution.py:451
  34.2 1.2 copy-start
  34.2 1.7 %copy-start.1 = (bf16[1024,768]{1,0:T(8,128)(2,1)}, bf16[1024,768]{1,0:T(8,128)(2,1)S(1)}, u32[]{:S(2)}) copy-start(bf16[1024,768]{1,0:T(8,128)(2,1)S(1)} %collective-permute-done.2.rest_1_.after) | copy-start | bytes 4718596
  38.7 15.6 %collective-permute-start.3 = (bf16[96,1152]{1,0:T(8,128)(2,1)}, bf16[96,1152]{1,0:T(8,128)(2,1)S(1)}, u32[]{:S(2)}, u32[]{:S(2)}) collective-permute-start(bf16[96,1152]{1,0:T(8,128)(2,1)} %get-tuple-element.25), channel_id=1, source_target_pairs={{0,64},{4,68},{8,72},{12,76},{16,80},{20,84},{24,88},{28,92},{32,9... | collective-permute-start | bytes 663560 | tf_op jit(solution)/shard_map/ppermute | solution.py:433
  43.5 12.6 %collective-permute-start.4 = (bf16[96,1152]{1,0:T(8,128)(2,1)}, bf16[96,1152]{1,0:T(8,128)(2,1)S(1)}, u32[]{:S(2)}, u32[]{:S(2)}) collective-permute-start(bf16[96,1152]{1,0:T(8,128)(2,1)} %get-tuple-element.26), channel_id=1, source_target_pairs={{0,128},{4,132},{8,136},{12,140},{16,144},{20,148},{24,152},{28,15... | collective-permute-start | bytes 663560 | tf_op jit(solution)/shard_map/ppermute | solution.py:433
  46.2 9.9 %collective-permute-start.5 = (bf16[96,1152]{1,0:T(8,128)(2,1)}, bf16[96,1152]{1,0:T(8,128)(2,1)S(1)}, u32[]{:S(2)}, u32[]{:S(2)}) collective-permute-start(bf16[96,1152]{1,0:T(8,128)(2,1)} %get-tuple-element.27), channel_id=1, source_target_pairs={{0,192},{4,196},{8,200},{12,204},{16,208},{20,212},{24,216},{28,22... | collective-permute-start | bytes 663560 | tf_op jit(solution)/shard_map/ppermute | solution.py:433
  54.3 1.8 %copy-start.10 = (bf16[96,1152]{1,0:T(8,128)(2,1)}, bf16[96,1152]{1,0:T(8,128)(2,1)S(1)}, u32[]{:S(2)}) copy-start(bf16[96,1152]{1,0:T(8,128)(2,1)S(1)} %collective-permute-done.3.g1) | copy-start | bytes 663556
  59.6 16.1 %all-to-all-start = ((bf16[8,16,1152]{2,1,0:T(8,128)(2,1)}), bf16[8,16,1152]{2,1,0:T(8,128)(2,1)S(1)}, u32[]{:S(2)}, u32[]{:S(2)}) async-start(bf16[8,16,1152]{2,1,0:T(8,128)(2,1)} %rs_z.1.dep_ref), calls=%async_computation | async-start | bytes 589824 | tf_op jit(solution)/shard_map/all_to_all | solution.py:466
  65.1 41.1 %collective-permute-start.11 = (bf16[384,1536]{1,0:T(8,128)(2,1)}, bf16[384,1536]{1,0:T(8,128)(2,1)S(1)}, u32[]{:S(2)}, u32[]{:S(2)}) collective-permute-start(bf16[384,1536]{1,0:T(8,128)(2,1)} %refs_4_.1), channel_id=1, source_target_pairs={{0,2},{1,3},{2,0},{3,1},{4,6},{5,7},{6,4},{7,5},{8,10},{9,11},{10,... | collective-permute-start | bytes 3538952 | tf_op jit(solution)/shard_map/ppermute | solution.py:451
  78.3 15.9 %all-to-all-start.1 = ((bf16[8,16,1152]{2,1,0:T(8,128)(2,1)}), bf16[8,16,1152]{2,1,0:T(8,128)(2,1)S(1)}, u32[]{:S(2)}, u32[]{:S(2)}) async-start(bf16[8,16,1152]{2,1,0:T(8,128)(2,1)} %renorm.1.dep_ref), calls=%async_computation.1 | async-start | bytes 589824 | tf_op jit(solution)/shard_map/all_to_all | solution.py:466
  95.9 3.7 %copy-start.5 = (bf16[6,16,1152]{2,1,0:T(8,128)(2,1)}, bf16[6,16,1152]{2,1,0:T(8,128)(2,1)S(1)}, u32[]{:S(2)}) copy-start(bf16[6,16,1152]{2,1,0:T(8,128)(2,1)S(1)} %slice.4) | copy-start | bytes 663556
  95.9 10.3 %collective-permute-start.10 = (bf16[96,1152]{1,0:T(8,128)(2,1)S(1)}, bf16[96,1152]{1,0:T(8,128)(2,1)S(1)}, u32[]{:S(2)}, u32[]{:S(2)}) collective-permute-start(bf16[96,1152]{1,0:T(8,128)(2,1)S(1)} %bitcast.11), channel_id=1, source_target_pairs={{0,192},{4,196},{8,200},{12,204},{16,208},{20,212},{24,216},{28,22... | collective-permute-start | bytes 663560 | tf_op jit(solution)/shard_map/ppermute | solution.py:433
  98.3 9.2 %collective-permute-start.8 = (bf16[96,1152]{1,0:T(8,128)(2,1)S(1)}, bf16[96,1152]{1,0:T(8,128)(2,1)S(1)}, u32[]{:S(2)}, u32[]{:S(2)}) collective-permute-start(bf16[96,1152]{1,0:T(8,128)(2,1)S(1)} %bitcast.12), channel_id=1, source_target_pairs={{0,64},{4,68},{8,72},{12,76},{16,80},{20,84},{24,88},{28,92},{32,9... | collective-permute-start | bytes 663560 | tf_op jit(solution)/shard_map/ppermute | solution.py:433
  98.3 9.2 %collective-permute-start.9 = (bf16[96,1152]{1,0:T(8,128)(2,1)S(1)}, bf16[96,1152]{1,0:T(8,128)(2,1)S(1)}, u32[]{:S(2)}, u32[]{:S(2)}) collective-permute-start(bf16[96,1152]{1,0:T(8,128)(2,1)S(1)} %bitcast.13), channel_id=1, source_target_pairs={{0,128},{4,132},{8,136},{12,140},{16,144},{20,148},{24,152},{28,15... | collective-permute-start | bytes 663560 | tf_op jit(solution)/shard_map/ppermute | solution.py:433
  106.2 9.6 %copy-start.19 = (f32[384]{0:T(512)S(1)}, f32[384]{0:T(512)}, u32[]{:S(2)}) copy-start(f32[384]{0:T(512)} %param.15) | copy-start | bytes 4612
  106.2 1.3 copy-start.2
  106.2 1.3 copy-start.7
  111.2 6.9 %collective-permute-start.12 = (bf16[384,1152]{1,0:T(8,128)(2,1)}, bf16[384,1152]{1,0:T(8,128)(2,1)S(1)}, u32[]{:S(2)}, u32[]{:S(2)}) collective-permute-start(bf16[384,1152]{1,0:T(8,128)(2,1)} %ag_x.1.own_ref), channel_id=1, source_target_pairs={{0,4},{4,0},{8,12},{12,8},{16,20},{20,16},{24,28},{28,24},{32,36},... | collective-permute-start | bytes 2654216 | tf_op jit(solution)/shard_map/ppermute | solution.py:433
  118.1 0.9 copy-start.3
  124.3 7.6 %collective-permute-start.13 = (bf16[256,384]{1,0:T(8,128)(2,1)}, bf16[256,384]{1,0:T(8,128)(2,1)S(1)}, u32[]{:S(2)}, u32[]{:S(2)}) collective-permute-start(bf16[256,384]{1,0:T(8,128)(2,1)} %get-tuple-element.28.rest_1_), channel_id=1, source_target_pairs={{0,1},{1,2},{2,3},{3,0},{4,5},{5,6},{6,7},{7,4},{8,9},{9,10},{10,1... | collective-permute-start | bytes 589832 | tf_op jit(solution)/shard_map/ppermute | solution.py:451
  125.5 10.6 %collective-permute-start.14 = (bf16[256,384]{1,0:T(8,128)(2,1)}, bf16[256,384]{1,0:T(8,128)(2,1)S(1)}, u32[]{:S(2)}, u32[]{:S(2)}) collective-permute-start(bf16[256,384]{1,0:T(8,128)(2,1)} %get-tuple-element.29), channel_id=1, source_target_pairs={{0,2},{1,3},{2,0},{3,1},{4,6},{5,7},{6,4},{7,5},{8,10},{9,11},{10,... | collective-permute-start | bytes 589832 | tf_op jit(solution)/shard_map/ppermute | solution.py:451
  126.9 9.5 %collective-permute-start.15 = (bf16[256,384]{1,0:T(8,128)(2,1)}, bf16[256,384]{1,0:T(8,128)(2,1)S(1)}, u32[]{:S(2)}, u32[]{:S(2)}) collective-permute-start(bf16[256,384]{1,0:T(8,128)(2,1)} %get-tuple-element.30), channel_id=1, source_target_pairs={{0,3},{1,0},{2,1},{3,2},{4,7},{5,4},{6,5},{7,6},{8,11},{9,8},{10,9... | collective-permute-start | bytes 589832 | tf_op jit(solution)/shard_map/ppermute | solution.py:451
  131.9 4.5 %copy-start.13 = (bf16[256,384]{1,0:T(8,128)(2,1)}, bf16[256,384]{1,0:T(8,128)(2,1)S(1)}, u32[]{:S(2)}) copy-start(bf16[256,384]{1,0:T(8,128)(2,1)S(1)} %collective-permute-done.13.refs_1_) | copy-start | bytes 589828
  142.8 7.4 %collective-permute-start.16 = (bf16[256,384]{1,0:T(8,128)(2,1)}, bf16[256,384]{1,0:T(8,128)(2,1)S(1)}, u32[]{:S(2)}, u32[]{:S(2)}) collective-permute-start(bf16[256,384]{1,0:T(8,128)(2,1)} %get-tuple-element.32), channel_id=1, source_target_pairs={{0,1},{1,2},{2,3},{3,0},{4,5},{5,6},{6,7},{7,4},{8,9},{9,10},{10,1... | collective-permute-start | bytes 589832 | tf_op jit(solution)/shard_map/ppermute | solution.py:451
  144.4 11.7 %collective-permute-start.17 = (bf16[256,384]{1,0:T(8,128)(2,1)}, bf16[256,384]{1,0:T(8,128)(2,1)S(1)}, u32[]{:S(2)}, u32[]{:S(2)}) collective-permute-start(bf16[256,384]{1,0:T(8,128)(2,1)} %get-tuple-element.33), channel_id=1, source_target_pairs={{0,2},{1,3},{2,0},{3,1},{4,6},{5,7},{6,4},{7,5},{8,10},{9,11},{10,... | collective-permute-start | bytes 589832 | tf_op jit(solution)/shard_map/ppermute | solution.py:451
  147.1 8.9 %collective-permute-start.18 = (bf16[256,384]{1,0:T(8,128)(2,1)}, bf16[256,384]{1,0:T(8,128)(2,1)S(1)}, u32[]{:S(2)}, u32[]{:S(2)}) collective-permute-start(bf16[256,384]{1,0:T(8,128)(2,1)} %get-tuple-element.34), channel_id=1, source_target_pairs={{0,3},{1,0},{2,1},{3,2},{4,7},{5,4},{6,5},{7,6},{8,11},{9,8},{10,9... | collective-permute-start | bytes 589832 | tf_op jit(solution)/shard_map/ppermute | solution.py:451
  150.2 5.8 %copy-start.16 = (bf16[256,384]{1,0:T(8,128)(2,1)}, bf16[256,384]{1,0:T(8,128)(2,1)S(1)}, u32[]{:S(2)}) copy-start(bf16[256,384]{1,0:T(8,128)(2,1)S(1)} %collective-permute-done.16.refs_1_) | copy-start | bytes 589828
  (10 other events, 7.0 us)

commit v8 on v7

--- a/solution.py
+++ b/solution.py
@@ -209,40 +209,43 @@
     )(old, got, *deps)
 
 
-def hold_kernel(value_ref, dep_ref, out_ref):
+def hold_kernel(value_ref, *rest):
     pass
 
 
-def hold(value, dep):
+def hold(value, deps):
     return pl.pallas_call(
         hold_kernel,
-        in_specs=[DEP, DEP],
+        in_specs=[DEP] * (1 + len(deps)),
         out_specs=DEP,
         out_shape=sds(value.shape, value.dtype),
         input_output_aliases={0: 0},
         compiler_params=params(),
         name="hold",
-    )(value, dep)
-
-
-def ag_x_kernel(pos_ref, *rest):
-    blocks, out = rest[:XS], rest[-1]
-    x = pos_ref[1]
-    for d, block in enumerate(blocks):
-        owner = lax.rem(x - d + XS, XS)
-        out[pl.ds(pl.multiple_of(owner * XROWS, XROWS), XROWS), :] = block[...]
-
-
-def ag_x(pos, blocks, deps):
-    return pl.pallas_call(
-        ag_x_kernel,
-        grid=(1,),
-        in_specs=[SMEM] + [full((XROWS, WIDE))] * XS + [DEP] * len(deps),
-        out_specs=full((DH, WIDE)),
-        out_shape=sds((DH, WIDE), BF),
-        compiler_params=params(),
-        name="ag_x",
-    )(pos, *blocks, *deps)
+    )(value, *deps)
+
+
+def old_rows_kernel(pos_ref, w1_ref, w3_ref, w2_ref, dep_ref, out_ref):
+    core, x, mine = pos_ref[0], pos_ref[1], pos_ref[3]
+    z = lax.rem(lax.div(mine, CS), ZS)
+    row = pl.multiple_of(jnp.minimum(x * XROWS + z * ROWS, DH - ROWS), ROWS)
+    rows = pl.ds(row, ROWS)
+    w1, w3 = w1_ref[0, rows, :].astype(F32), w3_ref[0, rows, :].astype(F32)
+    out_ref[:, :HID] = jnp.where(core == 0, w1, w3)
+    rows = pl.ds(pl.multiple_of(core * DH + row, ROWS), ROWS)
+    out_ref[:, HID:] = w2_ref[0, rows, :].astype(F32)
+
+
+def old_rows(pos, first_fast, gate_fast, second_fast, dep):
+    return pl.pallas_call(
+        old_rows_kernel,
+        grid=(1,),
+        in_specs=[SMEM, full((1, DH, HID)), full((1, DH, HID)), full((1, HID, DH)), DEP],
+        out_specs=full((ROWS, WIDE)),
+        out_shape=sds((ROWS, WIDE), F32),
+        compiler_params=params(),
+        name="old_rows",
+    )(pos, first_fast, gate_fast, second_fast, dep)
 
 
 def project_kernel(t_ref, w_ref, *rest):
@@ -268,12 +271,18 @@
     )(tokens, qkv_weight, *deps)
 
 
-def attend_kernel(ahead, pos_ref, ends_ref, q_ref, before, mine, after, dep_ref, out_ref, s_ref):
+def attend_kernel(ahead, pos_ref, lengths_ref, q_ref, before, mine, after, dep_ref, out_ref, s_ref):
     shard = pos_ref[3]
     piece = lax.rem(pos_ref[2] + ahead, HS)
     row = lax.broadcasted_iota(I32, (QB, 1), 0)
     place = row + (shard * TOK + piece * QB)
-    ends = ends_ref[...]
+    lengths = lengths_ref[...].astype(F32)
+    count = lengths.shape[1]
+    down = jnp.broadcast_to(lengths, (count, count)).T
+    upper = lax.broadcasted_iota(I32, (count, count), 0) <= lax.broadcasted_iota(
+        I32, (count, count), 1
+    )
+    ends = jnp.sum(jnp.where(upper, down, 0.0), axis=0, keepdims=True).astype(I32)
     shift = (shard - 1) * TOK
     begin = jnp.max(jnp.where(ends <= place, ends, 0), axis=1, keepdims=True) - shift
     end = jnp.min(jnp.where(ends <= place, TOKENS, ends), axis=1, keepdims=True) - shift
@@ -323,23 +332,29 @@
     segments(gather, 0)
 
 
-def attend(ahead, pos, ends, query, before, mine, after, dep):
+def attend(ahead, pos, lengths, query, before, mine, after, dep):
     whole = full((TOK, 2 * DH))
     return pl.pallas_call(
         functools.partial(attend_kernel, ahead),
         grid=(1,),
-        in_specs=[SMEM, full(ends.shape), full((TOK, DH)), whole, whole, whole, DEP],
+        in_specs=[SMEM, full(lengths.shape), full((TOK, DH)), whole, whole, whole, DEP],
         out_specs=full((QB, DH)),
         out_shape=sds((QB, DH), F32),
         scratch_shapes=[pltpu.VMEM((3 * TOK // KB, QB, KB), F32)],
         compiler_params=params(),
         name=f"attend_{ahead}",
-    )(pos, ends, query, before, mine, after, dep)
-
-
-def apply_kernel(aheads, pos_ref, q_ref, own_ref, other_ref, gain_ref, *rest):
+    )(pos, lengths, query, before, mine, after, dep)
+
+
+def apply_kernel(aheads, pos_ref, q_ref, gain_ref, *rest):
     count = len(aheads)
-    attended, outs = rest[:count], rest[-count:]
+    own_ref, other_ref = rest[-2:]
+    attended, outs = rest[2 * XS : 2 * XS + count], rest[-count - 2 : -2]
+    for d in range(XS):
+        at = lax.rem(pos_ref[1] - d + XS, XS) * XROWS
+        rows = pl.ds(pl.multiple_of(at, XROWS), XROWS)
+        own_ref[rows, :] = rest[d][...]
+        other_ref[rows, :] = rest[XS + d][...]
     even = pos_ref[0] == 0
     for ahead, att_ref, out in zip(aheads, attended, outs):
         piece = lax.rem(pos_ref[2] + ahead, HS)
@@ -358,19 +373,21 @@
         out[...] = (att_ref[...] + normed).astype(BF)
 
 
-def apply(aheads, pos, query, own, other, gain, attended, deps):
+def apply(aheads, pos, query, gain, own, other, attended, deps):
     count = len(aheads)
     return pl.pallas_call(
         functools.partial(apply_kernel, aheads),
         grid=(1,),
-        in_specs=[SMEM, full((TOK, DH)), full((DH, WIDE)), full((DH, WIDE)), full((1, DH))]
+        in_specs=[SMEM, full((TOK, DH)), full((1, DH))]
+        + [full((XROWS, WIDE))] * (2 * XS)
         + [full((QB, DH))] * count
         + [DEP] * len(deps),
         out_specs=[full((QB, DH))] * count,
         out_shape=[sds((QB, DH), BF)] * count,
+        scratch_shapes=[pltpu.VMEM((DH, WIDE), BF)] * 2,
         compiler_params=params(),
         name=f"apply_{count}",
-    )(pos, query, own, other, gain, *attended, *deps)
+    )(pos, query, gain, *own, *other, *attended, *deps)
 
 
 def output_kernel(pos_ref, *refs):
@@ -429,7 +446,7 @@
 ):
     mine = lax.axis_index("tok")
     head = lax.axis_index("head")
-    x, z, core = mine // (ZS * CS), mine // CS % ZS, mine % CS
+    x, core = mine // (ZS * CS), mine % CS
     send = lambda value, pairs: lax.ppermute(value, "tok", pairs)
 
     kv, rates = keys(tokens, qkv_weight, rate_weight)
@@ -440,27 +457,10 @@
     give, keep = update(pos, kv, rates, first_fast, gate_fast, second_fast)
     got = send(give, SWAP_C)
 
-    order = jnp.arange(frame_lengths.shape[0], dtype=I32)
-    ends = jnp.sum(
-        jnp.where(order[:, None] <= order[None, :], frame_lengths[:, None], 0),
-        axis=0,
-        keepdims=True,
-    )
-
     def spread(parts):
         return [lax.ppermute(p, "head", shift_h(d)) if d else p for d, p in enumerate(parts)]
 
     weights = spread([out_weight] * HS)
-
-    row = jnp.minimum(x * XROWS + z * ROWS, DH - ROWS)
-    pick = lambda w, at: lax.dynamic_slice_in_dim(w[0], at, ROWS, 0)
-    old = jnp.concatenate(
-        [
-            jnp.where(core == 0, pick(first_fast, row), pick(gate_fast, row)),
-            pick(second_fast, core * DH + row),
-        ],
-        axis=1,
-    ).astype(F32)
 
     def exchange(blocks):
         return lax.all_to_all(blocks, "tok", 0, 0, axis_index_groups=ALONG_Z)
@@ -468,21 +468,23 @@
     query = project(tokens, qkv_weight, [give])
     own, *gives = rs_x(pos, keep, got, [before, after, query])
     got = [send(g, shift_x(d + 1)) for d, g in enumerate(gives)]
-    att = functools.partial(attend, pos=pos, ends=ends, query=query, before=before, mine=kv, after=after)
+    att = functools.partial(attend, pos=pos, lengths=frame_lengths[None, :], query=query, before=before, mine=kv, after=after)
     att0 = att(0, dep=own)
+    old = old_rows(pos, first_fast, gate_fast, second_fast, own)
     total = rs_z(own, got, [att0, old])
     got = exchange(total)
     att1 = att(1, dep=total)
-    fresh = renorm(old, got, [att1, weights[1], weights[3]])
+    fresh = renorm(old, got, [att1])
     got = exchange(fresh)
     att2 = att(2, dep=fresh)
-    block = hold(got, att2)[:OWNERS].reshape(XROWS, WIDE)
+    block = hold(got, [att2, weights[1], weights[3]])[:OWNERS].reshape(XROWS, WIDE)
     att3 = att(3, dep=block)
-    half = ag_x(pos, [block] + [send(block, shift_x(d)) for d in range(1, XS)], [att3, weights[2]])
-    other = send(half, SWAP_C)
+    near, *far = [send(block, shift_x(d)) for d in range(1, XS)]
+    blocks = [block, hold(near, [att3]), *far]
+    others = [send(b, SWAP_C) for b in blocks]
 
     mix = functools.partial(
-        apply, pos=pos, query=query, own=half, other=other, gain=fast_gain[None, :]
+        apply, pos=pos, query=query, gain=fast_gain[None, :], own=blocks, other=others
     )
     away = mix((1, 2, 3), attended=[att1, att2, att3], deps=[])
     [home] = mix((0,), attended=[att0], deps=[away[0]])

time: 159 us -> 159 us (level)
  other arithmetic: 2.64 us -> 0.62 us
  local copies, waits for them, and re-layouts: 10.7 us -> 8.89 us
  waiting for transfers between devices: 25.1 us -> 26.9 us
    ppermute x10 -> x13, starting transfers between devices: 23.5 us -> 17.6 us  [body(): send = lambda value, pairs: lax.ppermute(value, 'tok', pairs)]
    all_to_all x2, starting transfers between devices: 10.9 us -> 15.1 us  [exchange(): return lax.all_to_all(blocks, 'tok', 0, 0, axis_index_groups=ALONG_Z)]
    ppermute x9, starting transfers between devices: 12.3 us -> 14.6 us  [spread(): lax.ppermute(p, 'head', shift_h(d))]
    ppermute x10 -> x13, waiting for transfers between devices: 4.8 us -> 6.85 us  [body(): send = lambda value, pairs: lax.ppermute(value, 'tok', pairs)]
    unnamed x42 -> x50, local copies, waits for them, and re-layouts: 8.44 us -> 7.35 us
  transfers between devices with their start and end apart: 21 -> 24, of which waited for: 10 -> 13; matrix products, arithmetic and copies ran while one was open for 3% -> 1% of each run, Pallas kernels for 32% -> 36%
where the time goes in v8:
time: 159 us
  Pallas kernels  74.7 us (47%)
  starting transfers between devices  47.4 us (30%)
  waiting for transfers between devices  26.9 us (17%)
  local copies, waits for them, and re-layouts  8.89 us (6%)
    pallas_call x4, Pallas kernels, attend(): pl.pallas_call(functools.partial(attend_kernel, ahead), grid=(1,), in_spe...  27.1 us
    ppermute x13, starting transfers between devices, body(): send = lambda value, pairs: lax.ppermute(value, 'tok', pairs)  17.6 us
    all_to_all x2, starting transfers between devices, exchange(): return lax.all_to_all(blocks, 'tok', 0, 0, axis_index_groups=ALONG_Z)  15.1 us
    ppermute x9, starting transfers between devices, spread(): lax.ppermute(p, 'head', shift_h(d))  14.6 us
    ppermute x9, waiting for transfers between devices, spread(): lax.ppermute(p, 'head', shift_h(d))  13.1 us
    pallas_call x1, Pallas kernels, update(): pl.pallas_call(update_kernel, grid=(1,), in_specs=[SMEM, full(kv.shape),...  9.66 us
    pallas_call x2, Pallas kernels, apply(): pl.pallas_call(functools.partial(apply_kernel, aheads), grid=(1,), in_spe...  9.42 us
    unnamed x50, local copies, waits for them, and re-layouts  7.35 us
  transfers between devices with their start and end apart: 24, of which 13 were waited for; matrix products, arithmetic and copies ran while one was open for 1% of the time, Pallas kernels for 36%

profile of v8, /device:TPU:1, one launch (start us, length us, event | category | flops | bytes accessed | tf_op | source)
XLA Modules:
  0.0 158.7 jit_solution(10975858209763525994)
XLA Ops:
  0.0 6.7 %keys.1 = (bf16[1024,768]{1,0:T(8,128)(2,1)}, f32[1024,3]{1,0:T(8,128)}) custom-call(bf16[1024,1536]{1,0:T(8,128)(2,1)} %t_ref.3, bf16[1536,1152]{1,0:T(8,128)(2,1)} %w_ref.3, bf16[3,1536]{1,0:T(4,128)(2,1)} %bitcast.14), custom_call_target="tpu_custom_call" | custom-call | tf_op jit(solution)/shard_map/keys/pallas_call | solution.py:74
  6.7 4.9 %collective-permute-start.1 = (bf16[1024,768]{1,0:T(8,128)(2,1)}, bf16[1024,768]{1,0:T(8,128)(2,1)S(1)}, u32[]{:S(2)}, u32[]{:S(2)}) collective-permute-start(bf16[1024,768]{1,0:T(8,128)(2,1)} %get-tuple-element.20.kv_ref.mine), channel_id=1, source_target_pairs={{0,4},{4,8},{8,12},{12,16},{16,20},{20,24},{24,28},{28,32},{32,36}... | collective-permute-start | bytes 4718600 | tf_op jit(solution)/shard_map/ppermute | solution.py:450
  11.7 1.9 %collective-permute-start.2 = (bf16[1024,768]{1,0:T(8,128)(2,1)}, bf16[1024,768]{1,0:T(8,128)(2,1)S(1)}, u32[]{:S(2)}, u32[]{:S(2)}) collective-permute-start(bf16[1024,768]{1,0:T(8,128)(2,1)} %get-tuple-element.20.kv_ref.mine), channel_id=1, source_target_pairs={{4,0},{8,4},{12,8},{16,12},{20,16},{24,20},{28,24},{32,28},{36,32}... | collective-permute-start | bytes 4718600 | tf_op jit(solution)/shard_map/ppermute | solution.py:450
  14.2 9.7 %update.1 = (bf16[384,1152]{1,0:T(8,128)(2,1)}, f32[384,1152]{1,0:T(8,128)}) custom-call(s32[4]{0:T(128)} %pad_add_fusion.pos_ref, bf16[1024,768]{1,0:T(8,128)(2,1)} %get-tuple-element.20.kv_ref.mine, f32[1024,3]{1,0:T(8,128)} %get-tuple-element.21.r_ref, bf16[1,384,768]{2,1,0:T(8,128)(2,1)} %w1_ref.3, bf16[1,384,768]{2,1,0:T(8,128)(2,1)} %w3_ref.3, ...), custom_call_target="tpu_custom_call" | custom-call | tf_op jit(solution)/shard_map/update/pallas_call | solution.py:121
  23.9 5.2 %project.1.rest_2_.q_ref = bf16[1024,384]{1,0:T(8,128)(2,1)} custom-call(bf16[1024,1536]{1,0:T(8,128)(2,1)} %t_ref.3, bf16[1536,1152]{1,0:T(8,128)(2,1)} %w_ref.3, bf16[384,1152]{1,0:T(8,128)(2,1)} %get-tuple-element.22.rest_0_), custom_call_target="tpu_custom_call" | custom-call | tf_op jit(solution)/shard_map/project/pallas_call | solution.py:259
  29.3 4.3 %collective-permute-done.2.rest_1_.after = bf16[1024,768]{1,0:T(8,128)(2,1)S(1)} collective-permute-done((bf16[1024,768]{1,0:T(8,128)(2,1)}, bf16[1024,768]{1,0:T(8,128)(2,1)S(1)}, u32[]{:S(2)}, u32[]{:S(2)}) %collective-permute-start.2) | collective-permute-done | bytes 1572896 | tf_op jit(solution)/shard_map/ppermute | solution.py:450
  34.9 2.9 %rs_x.1 = (f32[96,1152]{1,0:T(8,128)}, bf16[96,1152]{1,0:T(8,128)(2,1)}, bf16[96,1152]{1,0:T(8,128)(2,1)}, bf16[96,1152]{1,0:T(8,128)(2,1)}) custom-call(s32[4]{0:T(128)} %pad_add_fusion.pos_ref, f32[384,1152]{1,0:T(8,128)} %get-tuple-element.23.keep_ref, bf16[384,1152]{1,0:T(8,128)(2,1)} %copy-done.14, bf16[1024,768]{1,0:T(8,128)(2,1)} %copy-done, ...), custom_call_target="tpu_custom_call" | custom-call | tf_op jit(solution)/shard_map/rs_x/pallas_call | solution.py:149
  39.0 2.7 %collective-permute-start.4 = (bf16[96,1152]{1,0:T(8,128)(2,1)}, bf16[96,1152]{1,0:T(8,128)(2,1)S(1)}, u32[]{:S(2)}, u32[]{:S(2)}) collective-permute-start(bf16[96,1152]{1,0:T(8,128)(2,1)} %get-tuple-element.26), channel_id=1, source_target_pairs={{0,128},{4,132},{8,136},{12,140},{16,144},{20,148},{24,152},{28,15... | collective-permute-start | bytes 663560 | tf_op jit(solution)/shard_map/ppermute | solution.py:450
  45.3 2.1 %old_rows.1.rest_1_.old_ref = f32[16,1152]{1,0:T(8,128)} custom-call(s32[4]{0:T(128)} %pad_add_fusion.pos_ref, bf16[1,384,768]{2,1,0:T(8,128)(2,1)} %w1_ref.3, bf16[1,384,768]{2,1,0:T(8,128)(2,1)} %w3_ref.3, bf16[1,768,384]{2,1,0:T(8,128)(2,1)} %w2_ref.3, f32[96,1152]{1,0:T(8,128)} %get-tuple-element.24.dep_ref.own_ref), custom_call_target="tpu_custom_call" | custom-call | tf_op jit(solution)/shard_map/old_rows/pallas_call | solution.py:240
  47.4 6.9 %attend_0.1.rest_0_.rest_8_ = f32[256,384]{1,0:T(8,128)} custom-call(s32[4]{0:T(128)} %pad_add_fusion.pos_ref, s32[1,128]{1,0:T(1,128)} %bitcast.15, bf16[1024,384]{1,0:T(8,128)(2,1)} %project.1.rest_2_.q_ref, bf16[1024,768]{1,0:T(8,128)(2,1)} %copy-done, bf16[1024,768]{1,0:T(8,128)(2,1)} %get-tuple-element.20.kv_ref.mine, bf16[1024,768]{1,0:T(8,128)(2,1)} %copy-done.1, ...), custom_call_target="tpu_custom_call" | custom-call | tf_op jit(solution)/shard_map/attend_0/pallas_call | solution.py:337
  55.8 2.1 %rs_z.1.dep_ref = bf16[8,16,1152]{2,1,0:T(8,128)(2,1)} custom-call(f32[96,1152]{1,0:T(8,128)} %get-tuple-element.24.dep_ref.own_ref, bf16[96,1152]{1,0:T(8,128)(2,1)} %copy-done.15, bf16[96,1152]{1,0:T(8,128)(2,1)} %copy-done.16, bf16[96,1152]{1,0:T(8,128)(2,1)} %copy-done.17, f32[256,384]{1,0:T(8,128)} %attend_0.1.rest_0_.rest_8_, ...), custom_call_target="tpu_custom_call" | custom-call | tf_op jit(solution)/shard_map/rs_z/pallas_call | solution.py:172
  57.8 8.0 %all-to-all-start = ((bf16[8,16,1152]{2,1,0:T(8,128)(2,1)}), bf16[8,16,1152]{2,1,0:T(8,128)(2,1)S(1)}, u32[]{:S(2)}, u32[]{:S(2)}) async-start(bf16[8,16,1152]{2,1,0:T(8,128)(2,1)} %rs_z.1.dep_ref), calls=%async_computation | async-start | bytes 589824 | tf_op jit(solution)/shard_map/all_to_all | solution.py:466
  65.9 3.3 %collective-permute-start.18 = (bf16[384,1536]{1,0:T(8,128)(2,1)}, bf16[384,1536]{1,0:T(8,128)(2,1)}, u32[]{:S(2)}, u32[]{:S(2)}) collective-permute-start(bf16[384,1536]{1,0:T(8,128)(2,1)} %refs_4_.1), channel_id=1, source_target_pairs={{0,2},{1,3},{2,0},{3,1},{4,6},{5,7},{6,4},{7,5},{8,10},{9,11},{10,... | collective-permute-start | bytes 3538952 | tf_op jit(solution)/shard_map/ppermute | solution.py:461
  69.2 6.7 %attend_1.1.rest_0_.rest_8_ = f32[256,384]{1,0:T(8,128)} custom-call(s32[4]{0:T(128)} %pad_add_fusion.pos_ref, s32[1,128]{1,0:T(1,128)} %bitcast.16, bf16[1024,384]{1,0:T(8,128)(2,1)} %project.1.rest_2_.q_ref, bf16[1024,768]{1,0:T(8,128)(2,1)} %copy-done, bf16[1024,768]{1,0:T(8,128)(2,1)} %get-tuple-element.20.kv_ref.mine, bf16[1024,768]{1,0:T(8,128)(2,1)} %copy-done.1, ...), custom_call_target="tpu_custom_call" | custom-call | tf_op jit(solution)/shard_map/attend_1/pallas_call | solution.py:337
  77.2 1.9 %renorm.1.dep_ref = bf16[8,16,1152]{2,1,0:T(8,128)(2,1)} custom-call(f32[16,1152]{1,0:T(8,128)} %old_rows.1.rest_1_.old_ref, bf16[8,16,1152]{2,1,0:T(8,128)(2,1)} %copy-done.7, f32[256,384]{1,0:T(8,128)} %attend_1.1.rest_0_.rest_8_), custom_call_target="tpu_custom_call" | custom-call | tf_op jit(solution)/shard_map/renorm/pallas_call | solution.py:201
  79.1 7.1 %all-to-all-start.1 = ((bf16[8,16,1152]{2,1,0:T(8,128)(2,1)}), bf16[8,16,1152]{2,1,0:T(8,128)(2,1)S(1)}, u32[]{:S(2)}, u32[]{:S(2)}) async-start(bf16[8,16,1152]{2,1,0:T(8,128)(2,1)} %renorm.1.dep_ref), calls=%async_computation.1 | async-start | bytes 589824 | tf_op jit(solution)/shard_map/all_to_all | solution.py:466
  86.2 6.7 %attend_2.1.rest_0_.rest_9_ = f32[256,384]{1,0:T(8,128)} custom-call(s32[4]{0:T(128)} %pad_add_fusion.pos_ref, s32[1,128]{1,0:T(1,128)} %bitcast.17, bf16[1024,384]{1,0:T(8,128)(2,1)} %project.1.rest_2_.q_ref, bf16[1024,768]{1,0:T(8,128)(2,1)} %copy-done, bf16[1024,768]{1,0:T(8,128)(2,1)} %get-tuple-element.20.kv_ref.mine, bf16[1024,768]{1,0:T(8,128)(2,1)} %copy-done.1, ...), custom_call_target="tpu_custom_call" | custom-call | tf_op jit(solution)/shard_map/attend_2/pallas_call | solution.py:337
  93.0 6.3 %all-to-all-done.1.value_ref = bf16[8,16,1152]{2,1,0:T(8,128)(2,1)S(1)} async-done(((bf16[8,16,1152]{2,1,0:T(8,128)(2,1)}), bf16[8,16,1152]{2,1,0:T(8,128)(2,1)S(1)}, u32[]{:S(2)}, u32[]{:S(2)}) %all-to-all-start.1) | async-done | bytes 294944 | tf_op jit(solution)/shard_map/all_to_all | solution.py:466
  102.1 2.1 %collective-permute-start.10 = (bf16[96,1152]{1,0:T(8,128)(2,1)S(1)}, bf16[96,1152]{1,0:T(8,128)(2,1)S(1)}, u32[]{:S(2)}, u32[]{:S(2)}) collective-permute-start(bf16[96,1152]{1,0:T(8,128)(2,1)S(1)} %bitcast.9), channel_id=1, source_target_pairs={{0,192},{4,196},{8,200},{12,204},{16,208},{20,212},{24,216},{28,22... | collective-permute-start | bytes 663560 | tf_op jit(solution)/shard_map/ppermute | solution.py:450
  105.2 6.7 %attend_3.1.rest_0_.rest_10_ = f32[256,384]{1,0:T(8,128)} custom-call(s32[4]{0:T(128)} %pad_add_fusion.pos_ref, s32[1,128]{1,0:T(1,128)} %bitcast.18, bf16[1024,384]{1,0:T(8,128)(2,1)} %project.1.rest_2_.q_ref, bf16[1024,768]{1,0:T(8,128)(2,1)} %copy-done, bf16[1024,768]{1,0:T(8,128)(2,1)} %get-tuple-element.20.kv_ref.mine, bf16[1024,768]{1,0:T(8,128)(2,1)} %copy-done.1, ...), custom_call_target="tpu_custom_call" | custom-call | tf_op jit(solution)/shard_map/attend_3/pallas_call | solution.py:337
  112.0 1.6 %collective-permute-done.8.value_ref = bf16[96,1152]{1,0:T(8,128)(2,1)S(1)} collective-permute-done((bf16[96,1152]{1,0:T(8,128)(2,1)S(1)}, bf16[96,1152]{1,0:T(8,128)(2,1)S(1)}, u32[]{:S(2)}, u32[]{:S(2)}) %collective-permute-start.8) | collective-permute-done | bytes 221216 | tf_op jit(solution)/shard_map/ppermute | solution.py:450
  118.5 5.6 %apply_3.1 = (bf16[256,384]{1,0:T(8,128)(2,1)}, bf16[256,384]{1,0:T(8,128)(2,1)}, bf16[256,384]{1,0:T(8,128)(2,1)}) custom-call(s32[4]{0:T(128)} %pad_add_fusion.pos_ref, bf16[1024,384]{1,0:T(8,128)(2,1)} %project.1.rest_2_.q_ref, f32[1,384]{1,0:T(1,128)} %broadcast_in_dim.6.gain_ref, bf16[96,1152]{1,0:T(8,128)(2,1)} %bitcast.12, ...), custom_call_target="tpu_custom_call" | custom-call | tf_op jit(solution)/shard_map/apply_3/pallas_call | solution.py:378
  124.1 2.0 %collective-permute-start.16 = (bf16[256,384]{1,0:T(8,128)(2,1)}, bf16[256,384]{1,0:T(8,128)(2,1)S(1)}, u32[]{:S(2)}, u32[]{:S(2)}) collective-permute-start(bf16[256,384]{1,0:T(8,128)(2,1)} %get-tuple-element.29), channel_id=1, source_target_pairs={{0,2},{1,3},{2,0},{3,1},{4,6},{5,7},{6,4},{7,5},{8,10},{9,11},{10,... | collective-permute-start | bytes 589832 | tf_op jit(solution)/shard_map/ppermute | solution.py:461
  126.0 2.0 %collective-permute-start.17 = (bf16[256,384]{1,0:T(8,128)(2,1)}, bf16[256,384]{1,0:T(8,128)(2,1)S(1)}, u32[]{:S(2)}, u32[]{:S(2)}) collective-permute-start(bf16[256,384]{1,0:T(8,128)(2,1)} %get-tuple-element.30), channel_id=1, source_target_pairs={{0,3},{1,0},{2,1},{3,2},{4,7},{5,4},{6,5},{7,6},{8,11},{9,8},{10,9... | collective-permute-start | bytes 589832 | tf_op jit(solution)/shard_map/ppermute | solution.py:461
  128.0 3.8 %apply_1.1.refs_0_ = bf16[256,384]{1,0:T(8,128)(2,1)} custom-call(s32[4]{0:T(128)} %pad_add_fusion.pos_ref, bf16[1024,384]{1,0:T(8,128)(2,1)} %project.1.rest_2_.q_ref, f32[1,384]{1,0:T(1,128)} %broadcast_in_dim.6.gain_ref, bf16[96,1152]{1,0:T(8,128)(2,1)} %bitcast.13, bf16[96,1152]{1,0:T(8,128)(2,1)} %hold.3.rest_1_, bf16[96,1152]{1,0:T(8,128)(2,1)} %copy-done.8, ...), custom_call_target="tpu_custom_call" | custom-call | tf_op jit(solution)/shard_map/apply_1/pallas_call | solution.py:378
  132.1 3.4 %collective-permute-done.16.refs_2_ = bf16[256,384]{1,0:T(8,128)(2,1)S(1)} collective-permute-done((bf16[256,384]{1,0:T(8,128)(2,1)}, bf16[256,384]{1,0:T(8,128)(2,1)S(1)}, u32[]{:S(2)}, u32[]{:S(2)}) %collective-permute-start.16) | collective-permute-done | bytes 196640 | tf_op jit(solution)/shard_map/ppermute | solution.py:461
  136.9 5.5 %output.1 = (bf16[256,384]{1,0:T(8,128)(2,1)}, bf16[256,384]{1,0:T(8,128)(2,1)}, bf16[256,384]{1,0:T(8,128)(2,1)}, bf16[256,384]{1,0:T(8,128)(2,1)}) custom-call(s32[4]{0:T(128)} %pad_add_fusion.pos_ref, bf16[256,384]{1,0:T(8,128)(2,1)} %apply_1.1.refs_0_, bf16[256,384]{1,0:T(8,128)(2,1)} %copy-done.18, bf16[256,384]{1,0:T(8,128)(2,1)} %copy-done.19, ...), custom_call_target="tpu_custom_call" | custom-call | tf_op jit(solution)/shard_map/output/pallas_call | solution.py:405
  142.4 2.2 %collective-permute-start.19 = (bf16[256,384]{1,0:T(8,128)(2,1)}, bf16[256,384]{1,0:T(8,128)(2,1)S(1)}, u32[]{:S(2)}, u32[]{:S(2)}) collective-permute-start(bf16[256,384]{1,0:T(8,128)(2,1)} %get-tuple-element.32), channel_id=1, source_target_pairs={{0,1},{1,2},{2,3},{3,0},{4,5},{5,6},{6,7},{7,4},{8,9},{9,10},{10,1... | collective-permute-start | bytes 589832 | tf_op jit(solution)/shard_map/ppermute | solution.py:461
  144.5 2.3 %collective-permute-start.20 = (bf16[256,384]{1,0:T(8,128)(2,1)}, bf16[256,384]{1,0:T(8,128)(2,1)S(1)}, u32[]{:S(2)}, u32[]{:S(2)}) collective-permute-start(bf16[256,384]{1,0:T(8,128)(2,1)} %get-tuple-element.33), channel_id=1, source_target_pairs={{0,2},{1,3},{2,0},{3,1},{4,6},{5,7},{6,4},{7,5},{8,10},{9,11},{10,... | collective-permute-start | bytes 589832 | tf_op jit(solution)/shard_map/ppermute | solution.py:461
  147.0 2.9 %collective-permute-done.19.refs_1_ = bf16[256,384]{1,0:T(8,128)(2,1)S(1)} collective-permute-done((bf16[256,384]{1,0:T(8,128)(2,1)}, bf16[256,384]{1,0:T(8,128)(2,1)S(1)}, u32[]{:S(2)}, u32[]{:S(2)}) %collective-permute-start.19) | collective-permute-done | bytes 196640 | tf_op jit(solution)/shard_map/ppermute | solution.py:461
  149.9 5.9 %collective-permute-done.20.refs_2_ = bf16[256,384]{1,0:T(8,128)(2,1)S(1)} collective-permute-done((bf16[256,384]{1,0:T(8,128)(2,1)}, bf16[256,384]{1,0:T(8,128)(2,1)S(1)}, u32[]{:S(2)}, u32[]{:S(2)}) %collective-permute-start.20) | collective-permute-done | bytes 196640 | tf_op jit(solution)/shard_map/ppermute | solution.py:461
  156.5 2.2 %arrange.1 = bf16[1024,384]{1,0:T(8,128)(2,1)} custom-call(s32[4]{0:T(128)} %pad_add_fusion.pos_ref, bf16[256,384]{1,0:T(8,128)(2,1)} %get-tuple-element.31.refs_0_, bf16[256,384]{1,0:T(8,128)(2,1)} %copy-done.21, bf16[256,384]{1,0:T(8,128)(2,1)} %copy-done.22, bf16[256,384]{1,0:T(8,128)(2,1)} %copy-done.23), custom_call_target="tpu_custom_call" | custom-call | tf_op jit(solution)/shard_map/arrange/pallas_call | solution.py:425
  (86 shorter events, 20.9 us)
Async XLA Ops:
  6.7 22.6 %collective-permute-start.1 = (bf16[1024,768]{1,0:T(8,128)(2,1)}, bf16[1024,768]{1,0:T(8,128)(2,1)S(1)}, u32[]{:S(2)}, u32[]{:S(2)}) collective-permute-start(bf16[1024,768]{1,0:T(8,128)(2,1)} %get-tuple-element.20.kv_ref.mine), channel_id=1, source_target_pairs={{0,4},{4,8},{8,12},{12,16},{16,20},{20,24},{24,28},{28,32},{32,36}... | collective-permute-start | bytes 4718600 | tf_op jit(solution)/shard_map/ppermute | solution.py:450
  11.7 21.9 %collective-permute-start.2 = (bf16[1024,768]{1,0:T(8,128)(2,1)}, bf16[1024,768]{1,0:T(8,128)(2,1)S(1)}, u32[]{:S(2)}, u32[]{:S(2)}) collective-permute-start(bf16[1024,768]{1,0:T(8,128)(2,1)} %get-tuple-element.20.kv_ref.mine), channel_id=1, source_target_pairs={{4,0},{8,4},{12,8},{16,12},{20,16},{24,20},{28,24},{32,28},{36,32}... | collective-permute-start | bytes 4718600 | tf_op jit(solution)/shard_map/ppermute | solution.py:450
  23.9 5.2 %collective-permute-start = (bf16[384,1152]{1,0:T(8,128)(2,1)}, bf16[384,1152]{1,0:T(8,128)(2,1)S(1)}, u32[]{:S(2)}, u32[]{:S(2)}) collective-permute-start(bf16[384,1152]{1,0:T(8,128)(2,1)} %get-tuple-element.22.rest_0_), channel_id=1, source_target_pairs={{0,4},{4,0},{8,12},{12,8},{16,20},{20,16},{24,28},{28,24},{32,36},... | collective-permute-start | bytes 2654216 | tf_op jit(solution)/shard_map/ppermute | solution.py:450
  29.1 4.5 %copy-start.14 = (bf16[384,1152]{1,0:T(8,128)(2,1)}, bf16[384,1152]{1,0:T(8,128)(2,1)S(1)}, u32[]{:S(2)}) copy-start(bf16[384,1152]{1,0:T(8,128)(2,1)S(1)} %collective-permute-done.got_ref) | copy-start | bytes 2654212
  29.3 4.3 %copy-start = (bf16[1024,768]{1,0:T(8,128)(2,1)}, bf16[1024,768]{1,0:T(8,128)(2,1)S(1)}, u32[]{:S(2)}) copy-start(bf16[1024,768]{1,0:T(8,128)(2,1)S(1)} %collective-permute-done.1.rest_0_.before) | copy-start | bytes 4718596
  37.8 16.5 %collective-permute-start.3 = (bf16[96,1152]{1,0:T(8,128)(2,1)}, bf16[96,1152]{1,0:T(8,128)(2,1)S(1)}, u32[]{:S(2)}, u32[]{:S(2)}) collective-permute-start(bf16[96,1152]{1,0:T(8,128)(2,1)} %get-tuple-element.25), channel_id=1, source_target_pairs={{0,64},{4,68},{8,72},{12,76},{16,80},{20,84},{24,88},{28,92},{32,9... | collective-permute-start | bytes 663560 | tf_op jit(solution)/shard_map/ppermute | solution.py:450
  39.0 15.3 %collective-permute-start.4 = (bf16[96,1152]{1,0:T(8,128)(2,1)}, bf16[96,1152]{1,0:T(8,128)(2,1)S(1)}, u32[]{:S(2)}, u32[]{:S(2)}) collective-permute-start(bf16[96,1152]{1,0:T(8,128)(2,1)} %get-tuple-element.26), channel_id=1, source_target_pairs={{0,128},{4,132},{8,136},{12,140},{16,144},{20,148},{24,152},{28,15... | collective-permute-start | bytes 663560 | tf_op jit(solution)/shard_map/ppermute | solution.py:450
  41.7 12.6 %collective-permute-start.5 = (bf16[96,1152]{1,0:T(8,128)(2,1)}, bf16[96,1152]{1,0:T(8,128)(2,1)S(1)}, u32[]{:S(2)}, u32[]{:S(2)}) collective-permute-start(bf16[96,1152]{1,0:T(8,128)(2,1)} %get-tuple-element.27), channel_id=1, source_target_pairs={{0,192},{4,196},{8,200},{12,204},{16,208},{20,212},{24,216},{28,22... | collective-permute-start | bytes 663560 | tf_op jit(solution)/shard_map/ppermute | solution.py:450
  42.6 50.4 %collective-permute-start.6 = (bf16[384,1536]{1,0:T(8,128)(2,1)}, bf16[384,1536]{1,0:T(8,128)(2,1)S(1)}, u32[]{:S(2)}, u32[]{:S(2)}) collective-permute-start(bf16[384,1536]{1,0:T(8,128)(2,1)} %refs_4_.1), channel_id=1, source_target_pairs={{0,1},{1,2},{2,3},{3,0},{4,5},{5,6},{6,7},{7,4},{8,9},{9,10},{10,1... | collective-permute-start | bytes 3538952 | tf_op jit(solution)/shard_map/ppermute | solution.py:461
  43.9 49.1 %collective-permute-start.7 = (bf16[384,1536]{1,0:T(8,128)(2,1)}, bf16[384,1536]{1,0:T(8,128)(2,1)S(1)}, u32[]{:S(2)}, u32[]{:S(2)}) collective-permute-start(bf16[384,1536]{1,0:T(8,128)(2,1)} %refs_4_.1), channel_id=1, source_target_pairs={{0,3},{1,0},{2,1},{3,2},{4,7},{5,4},{6,5},{7,6},{8,11},{9,8},{10,9... | collective-permute-start | bytes 3538952 | tf_op jit(solution)/shard_map/ppermute | solution.py:461
  57.8 18.6 %all-to-all-start = ((bf16[8,16,1152]{2,1,0:T(8,128)(2,1)}), bf16[8,16,1152]{2,1,0:T(8,128)(2,1)S(1)}, u32[]{:S(2)}, u32[]{:S(2)}) async-start(bf16[8,16,1152]{2,1,0:T(8,128)(2,1)} %rs_z.1.dep_ref), calls=%async_computation | async-start | bytes 589824 | tf_op jit(solution)/shard_map/all_to_all | solution.py:466
  65.9 66.0 %collective-permute-start.18 = (bf16[384,1536]{1,0:T(8,128)(2,1)}, bf16[384,1536]{1,0:T(8,128)(2,1)}, u32[]{:S(2)}, u32[]{:S(2)}) collective-permute-start(bf16[384,1536]{1,0:T(8,128)(2,1)} %refs_4_.1), channel_id=1, source_target_pairs={{0,2},{1,3},{2,0},{3,1},{4,6},{5,7},{6,4},{7,5},{8,10},{9,11},{10,... | collective-permute-start | bytes 3538952 | tf_op jit(solution)/shard_map/ppermute | solution.py:461
  79.1 20.2 %all-to-all-start.1 = ((bf16[8,16,1152]{2,1,0:T(8,128)(2,1)}), bf16[8,16,1152]{2,1,0:T(8,128)(2,1)S(1)}, u32[]{:S(2)}, u32[]{:S(2)}) async-start(bf16[8,16,1152]{2,1,0:T(8,128)(2,1)} %renorm.1.dep_ref), calls=%async_computation.1 | async-start | bytes 589824 | tf_op jit(solution)/shard_map/all_to_all | solution.py:466
  93.0 6.4 %copy-start.2 = (bf16[384,1536]{1,0:T(8,128)(2,1)}, bf16[384,1536]{1,0:T(8,128)(2,1)S(1)}, u32[]{:S(2)}) copy-start(bf16[384,1536]{1,0:T(8,128)(2,1)S(1)} %collective-permute-done.6.rest_1_.refs_5_) | copy-start | bytes 3538948
  93.0 6.4 %copy-start.3 = (bf16[384,1536]{1,0:T(8,128)(2,1)}, bf16[384,1536]{1,0:T(8,128)(2,1)S(1)}, u32[]{:S(2)}) copy-start(bf16[384,1536]{1,0:T(8,128)(2,1)S(1)} %collective-permute-done.7.rest_2_.refs_7_) | copy-start | bytes 3538948
  101.0 4.2 %copy-start.4 = (bf16[6,16,1152]{2,1,0:T(8,128)(2,1)}, bf16[6,16,1152]{2,1,0:T(8,128)(2,1)S(1)}, u32[]{:S(2)}) copy-start(bf16[6,16,1152]{2,1,0:T(8,128)(2,1)S(1)} %slice.4) | copy-start | bytes 663556
  101.0 15.1 %copy-start.24 = (f32[384]{0:T(512)S(1)}, f32[384]{0:T(512)}, u32[]{:S(2)}) copy-start(f32[384]{0:T(512)} %param.15) | copy-start | bytes 4612
  101.0 12.6 %collective-permute-start.8 = (bf16[96,1152]{1,0:T(8,128)(2,1)S(1)}, bf16[96,1152]{1,0:T(8,128)(2,1)S(1)}, u32[]{:S(2)}, u32[]{:S(2)}) collective-permute-start(bf16[96,1152]{1,0:T(8,128)(2,1)S(1)} %bitcast.7), channel_id=1, source_target_pairs={{0,64},{4,68},{8,72},{12,76},{16,80},{20,84},{24,88},{28,92},{32,9... | collective-permute-start | bytes 663560 | tf_op jit(solution)/shard_map/ppermute | solution.py:450
  101.7 13.9 %collective-permute-start.9 = (bf16[96,1152]{1,0:T(8,128)(2,1)S(1)}, bf16[96,1152]{1,0:T(8,128)(2,1)S(1)}, u32[]{:S(2)}, u32[]{:S(2)}) collective-permute-start(bf16[96,1152]{1,0:T(8,128)(2,1)S(1)} %bitcast.8), channel_id=1, source_target_pairs={{0,128},{4,132},{8,136},{12,140},{16,144},{20,148},{24,152},{28,15... | collective-permute-start | bytes 663560 | tf_op jit(solution)/shard_map/ppermute | solution.py:450
  102.1 13.6 %collective-permute-start.10 = (bf16[96,1152]{1,0:T(8,128)(2,1)S(1)}, bf16[96,1152]{1,0:T(8,128)(2,1)S(1)}, u32[]{:S(2)}, u32[]{:S(2)}) collective-permute-start(bf16[96,1152]{1,0:T(8,128)(2,1)S(1)} %bitcast.9), channel_id=1, source_target_pairs={{0,192},{4,196},{8,200},{12,204},{16,208},{20,212},{24,216},{28,22... | collective-permute-start | bytes 663560 | tf_op jit(solution)/shard_map/ppermute | solution.py:450
  104.2 12.5 %collective-permute-start.11 = (bf16[96,1152]{1,0:T(8,128)(2,1)S(1)}, bf16[96,1152]{1,0:T(8,128)(2,1)S(1)}, u32[]{:S(2)}, u32[]{:S(2)}) collective-permute-start(bf16[96,1152]{1,0:T(8,128)(2,1)S(1)} %bitcast.10), channel_id=1, source_target_pairs={{0,4},{4,0},{8,12},{12,8},{16,20},{20,16},{24,28},{28,24},{32,36},... | collective-permute-start | bytes 663560 | tf_op jit(solution)/shard_map/ppermute | solution.py:450
  114.3 2.6 %collective-permute-start.12 = (bf16[96,1152]{1,0:T(8,128)(2,1)}, bf16[96,1152]{1,0:T(8,128)(2,1)S(1)}, u32[]{:S(2)}, u32[]{:S(2)}) collective-permute-start(bf16[96,1152]{1,0:T(8,128)(2,1)} %hold.3.rest_1_), channel_id=1, source_target_pairs={{0,4},{4,0},{8,12},{12,8},{16,20},{20,16},{24,28},{28,24},{32,36},... | collective-permute-start | bytes 663560 | tf_op jit(solution)/shard_map/ppermute | solution.py:450
  115.6 1.5 collective-permute-start.13
  115.7 1.7 %collective-permute-start.14 = (bf16[96,1152]{1,0:T(8,128)(2,1)S(1)}, bf16[96,1152]{1,0:T(8,128)(2,1)S(1)}, u32[]{:S(2)}, u32[]{:S(2)}) collective-permute-start(bf16[96,1152]{1,0:T(8,128)(2,1)S(1)} %collective-permute-done.10.rest_3_), channel_id=1, source_target_pairs={{0,4},{4,0},{8,12},{12,8},{16,20},{20,16},{24,28},{28,24},{32,36},... | collective-permute-start | bytes 663560 | tf_op jit(solution)/shard_map/ppermute | solution.py:450
  124.1 8.0 %collective-permute-start.15 = (bf16[256,384]{1,0:T(8,128)(2,1)}, bf16[256,384]{1,0:T(8,128)(2,1)S(1)}, u32[]{:S(2)}, u32[]{:S(2)}) collective-permute-start(bf16[256,384]{1,0:T(8,128)(2,1)} %get-tuple-element.28.rest_9_), channel_id=1, source_target_pairs={{0,1},{1,2},{2,3},{3,0},{4,5},{5,6},{6,7},{7,4},{8,9},{9,10},{10,1... | collective-permute-start | bytes 589832 | tf_op jit(solution)/shard_map/ppermute | solution.py:461
  124.1 11.4 %collective-permute-start.16 = (bf16[256,384]{1,0:T(8,128)(2,1)}, bf16[256,384]{1,0:T(8,128)(2,1)S(1)}, u32[]{:S(2)}, u32[]{:S(2)}) collective-permute-start(bf16[256,384]{1,0:T(8,128)(2,1)} %get-tuple-element.29), channel_id=1, source_target_pairs={{0,2},{1,3},{2,0},{3,1},{4,6},{5,7},{6,4},{7,5},{8,10},{9,11},{10,... | collective-permute-start | bytes 589832 | tf_op jit(solution)/shard_map/ppermute | solution.py:461
  126.0 10.1 %collective-permute-start.17 = (bf16[256,384]{1,0:T(8,128)(2,1)}, bf16[256,384]{1,0:T(8,128)(2,1)S(1)}, u32[]{:S(2)}, u32[]{:S(2)}) collective-permute-start(bf16[256,384]{1,0:T(8,128)(2,1)} %get-tuple-element.30), channel_id=1, source_target_pairs={{0,3},{1,0},{2,1},{3,2},{4,7},{5,4},{6,5},{7,6},{8,11},{9,8},{10,9... | collective-permute-start | bytes 589832 | tf_op jit(solution)/shard_map/ppermute | solution.py:461
  132.1 4.1 %copy-start.18 = (bf16[256,384]{1,0:T(8,128)(2,1)}, bf16[256,384]{1,0:T(8,128)(2,1)S(1)}, u32[]{:S(2)}) copy-start(bf16[256,384]{1,0:T(8,128)(2,1)S(1)} %collective-permute-done.15.refs_1_) | copy-start | bytes 589828
  142.4 7.5 %collective-permute-start.19 = (bf16[256,384]{1,0:T(8,128)(2,1)}, bf16[256,384]{1,0:T(8,128)(2,1)S(1)}, u32[]{:S(2)}, u32[]{:S(2)}) collective-permute-start(bf16[256,384]{1,0:T(8,128)(2,1)} %get-tuple-element.32), channel_id=1, source_target_pairs={{0,1},{1,2},{2,3},{3,0},{4,5},{5,6},{6,7},{7,4},{8,9},{9,10},{10,1... | collective-permute-start | bytes 589832 | tf_op jit(solution)/shard_map/ppermute | solution.py:461
  144.5 11.2 %collective-permute-start.20 = (bf16[256,384]{1,0:T(8,128)(2,1)}, bf16[256,384]{1,0:T(8,128)(2,1)S(1)}, u32[]{:S(2)}, u32[]{:S(2)}) collective-permute-start(bf16[256,384]{1,0:T(8,128)(2,1)} %get-tuple-element.33), channel_id=1, source_target_pairs={{0,2},{1,3},{2,0},{3,1},{4,6},{5,7},{6,4},{7,5},{8,10},{9,11},{10,... | collective-permute-start | bytes 589832 | tf_op jit(solution)/shard_map/ppermute | solution.py:461
  146.8 8.9 %collective-permute-start.21 = (bf16[256,384]{1,0:T(8,128)(2,1)}, bf16[256,384]{1,0:T(8,128)(2,1)S(1)}, u32[]{:S(2)}, u32[]{:S(2)}) collective-permute-start(bf16[256,384]{1,0:T(8,128)(2,1)} %get-tuple-element.34), channel_id=1, source_target_pairs={{0,3},{1,0},{2,1},{3,2},{4,7},{5,4},{6,5},{7,6},{8,11},{9,8},{10,9... | collective-permute-start | bytes 589832 | tf_op jit(solution)/shard_map/ppermute | solution.py:461
  149.9 5.9 %copy-start.21 = (bf16[256,384]{1,0:T(8,128)(2,1)}, bf16[256,384]{1,0:T(8,128)(2,1)S(1)}, u32[]{:S(2)}) copy-start(bf16[256,384]{1,0:T(8,128)(2,1)S(1)} %collective-permute-done.19.refs_1_) | copy-start | bytes 589828
  (17 other events, 14.7 us)

commit v9 on v8

--- a/solution.py
+++ b/solution.py
@@ -18,7 +18,7 @@
 ROWS = 16
 OWNERS = XROWS // ROWS
 WIDE = HID + DH
-KB = 256
+KB = 512
 QB = 256
 BF, F32, I32 = jnp.bfloat16, jnp.float32, jnp.int32
 NT = (((1,), (1,)), ((), ()))
@@ -225,29 +225,6 @@
     )(value, *deps)
 
 
-def old_rows_kernel(pos_ref, w1_ref, w3_ref, w2_ref, dep_ref, out_ref):
-    core, x, mine = pos_ref[0], pos_ref[1], pos_ref[3]
-    z = lax.rem(lax.div(mine, CS), ZS)
-    row = pl.multiple_of(jnp.minimum(x * XROWS + z * ROWS, DH - ROWS), ROWS)
-    rows = pl.ds(row, ROWS)
-    w1, w3 = w1_ref[0, rows, :].astype(F32), w3_ref[0, rows, :].astype(F32)
-    out_ref[:, :HID] = jnp.where(core == 0, w1, w3)
-    rows = pl.ds(pl.multiple_of(core * DH + row, ROWS), ROWS)
-    out_ref[:, HID:] = w2_ref[0, rows, :].astype(F32)
-
-
-def old_rows(pos, first_fast, gate_fast, second_fast, dep):
-    return pl.pallas_call(
-        old_rows_kernel,
-        grid=(1,),
-        in_specs=[SMEM, full((1, DH, HID)), full((1, DH, HID)), full((1, HID, DH)), DEP],
-        out_specs=full((ROWS, WIDE)),
-        out_shape=sds((ROWS, WIDE), F32),
-        compiler_params=params(),
-        name="old_rows",
-    )(pos, first_fast, gate_fast, second_fast, dep)
-
-
 def project_kernel(t_ref, w_ref, *rest):
     q_ref = rest[-1]
     q_ref[...] = mm(t_ref[...], w_ref[...]).astype(BF)
@@ -271,9 +248,15 @@
     )(tokens, qkv_weight, *deps)
 
 
-def attend_kernel(ahead, pos_ref, lengths_ref, q_ref, before, mine, after, dep_ref, out_ref, s_ref):
+def attend_kernel(
+    ahead, pos_ref, lengths_ref, q_all, before, mine, after, dep_ref,
+    out_ref, s_ref, kv_ref, q_ref, sems, q_sem,
+):
     shard = pos_ref[3]
     piece = lax.rem(pos_ref[2] + ahead, HS)
+    q_rows = pl.ds(pl.multiple_of(piece * QB, QB), QB)
+    q_copy = pltpu.make_async_copy(q_all.at[q_rows, :], q_ref, q_sem)
+    q_copy.start()
     row = lax.broadcasted_iota(I32, (QB, 1), 0)
     place = row + (shard * TOK + piece * QB)
     lengths = lengths_ref[...].astype(F32)
@@ -288,19 +271,28 @@
     end = jnp.min(jnp.where(ends <= place, TOKENS, ends), axis=1, keepdims=True) - shift
     first = lax.div(jnp.min(begin), KB)
     last = lax.div(jnp.max(end) + KB - 1, KB)
-    q = q_ref[pl.ds(pl.multiple_of(piece * QB, QB), QB), :]
     per = TOK // KB
     scale = 1.0 / math.sqrt(DH)
 
-    def segments(step, carry):
-        for s, ref in enumerate((before, mine, after)):
-            lo = jnp.clip(first, s * per, (s + 1) * per)
-            hi = jnp.clip(last, s * per, (s + 1) * per)
-            carry = lax.fori_loop(lo, hi, functools.partial(step, s, ref), carry)
-        return carry
-
-    def scores(s, ref, kb, top):
-        k = ref[pl.ds(pl.multiple_of((kb - s * per) * KB, KB), KB), :DH]
+    def fetch(ref, at, kb):
+        rows = pl.ds(pl.multiple_of(at * KB, KB), KB)
+        return pltpu.make_async_copy(ref.at[rows, :], kv_ref.at[kb], sems.at[kb])
+
+    for s, ref in enumerate((before, mine, after)):
+
+        def start(kb, carry, s=s, ref=ref):
+            fetch(ref, kb - s * per, kb).start()
+            return carry
+
+        lo = jnp.clip(first, s * per, (s + 1) * per)
+        hi = jnp.clip(last, s * per, (s + 1) * per)
+        lax.fori_loop(lo, hi, start, 0)
+    q_copy.wait()
+    q = q_ref[...]
+
+    def scores(kb, top):
+        fetch(mine, 0, kb).wait()
+        k = kv_ref[kb, :, :DH]
         sc = lax.dot_general(q, k, NT, preferred_element_type=F32) * scale
         col = lax.broadcasted_iota(I32, (QB, KB), 1) + kb * KB
         sc = jnp.where((col >= begin) & (col < end), sc, -1e30)
@@ -309,7 +301,7 @@
             top = jnp.maximum(top, sc[:, lane : lane + 128])
         return top
 
-    top = segments(scores, jnp.full((QB, 128), -1e30, F32))
+    top = lax.fori_loop(first, last, scores, jnp.full((QB, 128), -1e30, F32))
     top = jnp.max(top, axis=1, keepdims=True)
 
     def weigh(kb, total):
@@ -323,27 +315,70 @@
     inverse = 1.0 / jnp.sum(total, axis=1, keepdims=True)
     out_ref[...] = jnp.zeros_like(out_ref)
 
-    def gather(s, ref, kb, carry):
-        v = ref[pl.ds(pl.multiple_of((kb - s * per) * KB, KB), KB), DH:]
+    def gather(kb, carry):
         probs = (s_ref[kb] * inverse).astype(BF)
-        out_ref[...] += mm(probs, v)
+        out_ref[...] += mm(probs, kv_ref[kb, :, DH:])
         return carry
 
-    segments(gather, 0)
-
-
-def attend(ahead, pos, lengths, query, before, mine, after, dep):
-    whole = full((TOK, 2 * DH))
-    return pl.pallas_call(
-        functools.partial(attend_kernel, ahead),
-        grid=(1,),
-        in_specs=[SMEM, full(lengths.shape), full((TOK, DH)), whole, whole, whole, DEP],
-        out_specs=full((QB, DH)),
-        out_shape=sds((QB, DH), F32),
-        scratch_shapes=[pltpu.VMEM((3 * TOK // KB, QB, KB), F32)],
+    lax.fori_loop(first, last, gather, 0)
+
+
+def first_kernel(pos_ref, w1_ref, w3_ref, w2_ref, *rest):
+    ins, outs, (wide, narrow, row_sems), scratch = rest[:7], rest[7:9], rest[9:12], rest[12:]
+    core, x, mine = pos_ref[0], pos_ref[1], pos_ref[3]
+    z = lax.rem(lax.div(mine, CS), ZS)
+    row = pl.multiple_of(jnp.minimum(x * XROWS + z * ROWS, DH - ROWS), ROWS)
+    rows = pl.ds(row, ROWS)
+    rows2 = pl.ds(pl.multiple_of(core * DH + row, ROWS), ROWS)
+    copies = [
+        pltpu.make_async_copy(w1_ref.at[0, rows, :], wide.at[0], row_sems.at[0]),
+        pltpu.make_async_copy(w3_ref.at[0, rows, :], wide.at[1], row_sems.at[1]),
+        pltpu.make_async_copy(w2_ref.at[0, rows2, :], narrow, row_sems.at[2]),
+    ]
+    for copy in copies:
+        copy.start()
+    attend_kernel(0, pos_ref, *ins[1:], outs[0], *scratch)
+    for copy in copies:
+        copy.wait()
+    out_ref = outs[1]
+    out_ref[:, :HID] = jnp.where(core == 0, wide[0].astype(F32), wide[1].astype(F32))
+    out_ref[:, HID:] = narrow[...].astype(F32)
+
+
+def attend(ahead, pos, lengths, query, before, mine, after, dep, old=()):
+    blocks = 3 * TOK // KB
+    kernel = functools.partial(attend_kernel, ahead)
+    outs, shapes, scratch, lead = [full((QB, DH))], [sds((QB, DH), F32)], [], ()
+    if old:
+        kernel = first_kernel
+        outs = outs + [full((ROWS, WIDE))]
+        shapes = shapes + [sds((ROWS, WIDE), F32)]
+        scratch = [
+            pltpu.VMEM((2, ROWS, HID), BF),
+            pltpu.VMEM((ROWS, DH), BF),
+            pltpu.SemaphoreType.DMA((3,)),
+        ]
+        lead = (pos, *old)
+    result = pl.pallas_call(
+        kernel,
+        grid=(1,),
+        in_specs=([SMEM] + [DEP] * 3 if old else [])
+        + [SMEM, full(lengths.shape)]
+        + [DEP] * 5,
+        out_specs=outs,
+        out_shape=shapes,
+        scratch_shapes=scratch
+        + [
+            pltpu.VMEM((blocks, QB, KB), F32),
+            pltpu.VMEM((blocks, KB, 2 * DH), BF),
+            pltpu.VMEM((QB, DH), BF),
+            pltpu.SemaphoreType.DMA((blocks,)),
+            pltpu.SemaphoreType.DMA,
+        ],
         compiler_params=params(),
         name=f"attend_{ahead}",
-    )(pos, lengths, query, before, mine, after, dep)
+    )(*lead, pos, lengths, query, before, mine, after, dep)
+    return result if old else result[0]
 
 
 def apply_kernel(aheads, pos_ref, q_ref, gain_ref, *rest):
@@ -469,8 +504,7 @@
     own, *gives = rs_x(pos, keep, got, [before, after, query])
     got = [send(g, shift_x(d + 1)) for d, g in enumerate(gives)]
     att = functools.partial(attend, pos=pos, lengths=frame_lengths[None, :], query=query, before=before, mine=kv, after=after)
-    att0 = att(0, dep=own)
-    old = old_rows(pos, first_fast, gate_fast, second_fast, own)
+    att0, old = att(0, dep=own, old=(first_fast, gate_fast, second_fast))
     total = rs_z(own, got, [att0, old])
     got = exchange(total)
     att1 = att(1, dep=total)

time: 159 us -> 159 us (level)
  the two profiles are of different devices: /device:TPU:1 before, /device:TPU:32 now
where the time goes in v9:
time: 159 us; the launch traced here: 158 us
  Pallas kernels  67.2 us (42%)
  starting transfers between devices  56.3 us (35%)
  waiting for transfers between devices  24.5 us (15%)
  local copies, waits for them, and re-layouts  8.85 us (6%)
    ppermute x9, starting transfers between devices, spread(): lax.ppermute(p, 'head', shift_h(d))  23.2 us
    pallas_call x4, Pallas kernels, attend(): pl.pallas_call(kernel, grid=(1,), in_specs=([SMEM] + [DEP] * 3 if old els...  21.7 us
    ppermute x13, starting transfers between devices, body(): send = lambda value, pairs: lax.ppermute(value, 'tok', pairs)  18.8 us
    ppermute x9, waiting for transfers between devices, spread(): lax.ppermute(p, 'head', shift_h(d))  14.8 us
    all_to_all x2, starting transfers between devices, exchange(): return lax.all_to_all(blocks, 'tok', 0, 0, axis_index_groups=ALONG_Z)  14.3 us
    pallas_call x1, Pallas kernels, update(): pl.pallas_call(update_kernel, grid=(1,), in_specs=[SMEM, full(kv.shape),...  9.65 us
    pallas_call x2, Pallas kernels, apply(): pl.pallas_call(functools.partial(apply_kernel, aheads), grid=(1,), in_spe...  9.4 us
    unnamed x50, local copies, waits for them, and re-layouts  7.31 us
  transfers between devices with their start and end apart: 24, of which 12 were waited for; matrix products, arithmetic and copies ran while one was open for 1% of the time, Pallas kernels for 32%

profile of v9, /device:TPU:32, one launch (start us, length us, event | category | flops | bytes accessed | tf_op | source)
XLA Modules:
  0.0 157.8 jit_solution(17533527464101991218)
XLA Ops:
  0.0 6.7 %keys.1 = (bf16[1024,768]{1,0:T(8,128)(2,1)}, f32[1024,3]{1,0:T(8,128)}) custom-call(bf16[1024,1536]{1,0:T(8,128)(2,1)} %t_ref.3, bf16[1536,1152]{1,0:T(8,128)(2,1)} %w_ref.3, bf16[3,1536]{1,0:T(4,128)(2,1)} %bitcast.14), custom_call_target="tpu_custom_call" | custom-call | tf_op jit(solution)/shard_map/keys/pallas_call | solution.py:74
  6.7 1.9 %collective-permute-start = (bf16[1024,768]{1,0:T(8,128)(2,1)}, bf16[1024,768]{1,0:T(8,128)(2,1)S(1)}, u32[]{:S(2)}, u32[]{:S(2)}) collective-permute-start(bf16[1024,768]{1,0:T(8,128)(2,1)} %get-tuple-element.22.kv_ref.rest_4_.mine), channel_id=1, source_target_pairs={{0,4},{4,8},{8,12},{12,16},{16,20},{20,24},{24,28},{28,32},{32,36}... | collective-permute-start | bytes 4718600 | tf_op jit(solution)/shard_map/ppermute | solution.py:485
  8.7 3.6 %collective-permute-start.1 = (bf16[1024,768]{1,0:T(8,128)(2,1)}, bf16[1024,768]{1,0:T(8,128)(2,1)S(1)}, u32[]{:S(2)}, u32[]{:S(2)}) collective-permute-start(bf16[1024,768]{1,0:T(8,128)(2,1)} %get-tuple-element.22.kv_ref.rest_4_.mine), channel_id=1, source_target_pairs={{4,0},{8,4},{12,8},{16,12},{20,16},{24,20},{28,24},{32,28},{36,32}... | collective-permute-start | bytes 4718600 | tf_op jit(solution)/shard_map/ppermute | solution.py:485
  13.0 9.7 %update.1 = (bf16[384,1152]{1,0:T(8,128)(2,1)}, f32[384,1152]{1,0:T(8,128)}) custom-call(s32[4]{0:T(128)} %pad_add_fusion.pos_ref.rest_0_, bf16[1024,768]{1,0:T(8,128)(2,1)} %get-tuple-element.22.kv_ref.rest_4_.mine, f32[1024,3]{1,0:T(8,128)} %get-tuple-element.23.r_ref, bf16[1,384,768]{2,1,0:T(8,128)(2,1)} %w1_ref.3, bf16[1,384,768]{2,1,0:T(8,128)(2,1)} %w3_ref.3, ...), custom_call_target="tpu_custom_call" | custom-call | tf_op jit(solution)/shard_map/update/pallas_call | solution.py:121
  22.9 5.2 %project.1.rest_2_.q_all.q_ref = bf16[1024,384]{1,0:T(8,128)(2,1)} custom-call(bf16[1024,1536]{1,0:T(8,128)(2,1)} %t_ref.3, bf16[1536,1152]{1,0:T(8,128)(2,1)} %w_ref.3, bf16[384,1152]{1,0:T(8,128)(2,1)} %get-tuple-element.24.rest_0_), custom_call_target="tpu_custom_call" | custom-call | tf_op jit(solution)/shard_map/project/pallas_call | solution.py:236
  28.7 1.9 %collective-permute-done.1.rest_1_.rest_5_.after = bf16[1024,768]{1,0:T(8,128)(2,1)S(1)} collective-permute-done((bf16[1024,768]{1,0:T(8,128)(2,1)}, bf16[1024,768]{1,0:T(8,128)(2,1)S(1)}, u32[]{:S(2)}, u32[]{:S(2)}) %collective-permute-start.1) | collective-permute-done | bytes 1572896 | tf_op jit(solution)/shard_map/ppermute | solution.py:485
  31.8 2.9 %rs_x.1 = (f32[96,1152]{1,0:T(8,128)}, bf16[96,1152]{1,0:T(8,128)(2,1)}, bf16[96,1152]{1,0:T(8,128)(2,1)}, bf16[96,1152]{1,0:T(8,128)(2,1)}) custom-call(s32[4]{0:T(128)} %pad_add_fusion.pos_ref.rest_0_, f32[384,1152]{1,0:T(8,128)} %get-tuple-element.25.keep_ref, bf16[384,1152]{1,0:T(8,128)(2,1)} %copy-done.14, bf16[1024,768]{1,0:T(8,128)(2,1)} %copy-done, ...), custom_call_target="tpu_custom_call" | custom-call | tf_op jit(solution)/shard_map/rs_x/pallas_call | solution.py:149
  34.7 1.5 collective-permute-start.3
  36.2 2.7 %collective-permute-start.4 = (bf16[96,1152]{1,0:T(8,128)(2,1)}, bf16[96,1152]{1,0:T(8,128)(2,1)S(1)}, u32[]{:S(2)}, u32[]{:S(2)}) collective-permute-start(bf16[96,1152]{1,0:T(8,128)(2,1)} %get-tuple-element.29), channel_id=1, source_target_pairs={{0,128},{4,132},{8,136},{12,140},{16,144},{20,148},{24,152},{28,15... | collective-permute-start | bytes 663560 | tf_op jit(solution)/shard_map/ppermute | solution.py:485
  40.3 1.6 collective-permute-start.6
  41.9 1.7 %collective-permute-start.7 = (bf16[384,1536]{1,0:T(8,128)(2,1)}, bf16[384,1536]{1,0:T(8,128)(2,1)S(1)}, u32[]{:S(2)}, u32[]{:S(2)}) collective-permute-start(bf16[384,1536]{1,0:T(8,128)(2,1)} %refs_4_.1), channel_id=1, source_target_pairs={{0,3},{1,0},{2,1},{3,2},{4,7},{5,4},{6,5},{7,6},{8,11},{9,8},{10,9... | collective-permute-start | bytes 3538952 | tf_op jit(solution)/shard_map/ppermute | solution.py:496
  43.6 5.7 %attend_0.1 = (f32[256,384]{1,0:T(8,128)}, f32[16,1152]{1,0:T(8,128)}) custom-call(s32[4]{0:T(128)} %pad_add_fusion.pos_ref.rest_0_, bf16[1,384,768]{2,1,0:T(8,128)(2,1)} %w1_ref.3, bf16[1,384,768]{2,1,0:T(8,128)(2,1)} %w3_ref.3, bf16[1,768,384]{2,1,0:T(8,128)(2,1)} %w2_ref.3, s32[4]{0:T(128)} %pad_add_fusion.pos_ref.rest_0_, s32[1,128]{1,0:T(1,128)} %bitcast.15, ...), custom_call_target="tpu_custom_call" | custom-call | tf_op jit(solution)/shard_map/attend_0/pallas_call | solution.py:362
  50.2 2.1 %rs_z.1.dep_ref = bf16[8,16,1152]{2,1,0:T(8,128)(2,1)} custom-call(f32[96,1152]{1,0:T(8,128)} %get-tuple-element.26.rest_6_.own_ref, bf16[96,1152]{1,0:T(8,128)(2,1)} %copy-done.15, bf16[96,1152]{1,0:T(8,128)(2,1)} %copy-done.16, bf16[96,1152]{1,0:T(8,128)(2,1)} %copy-done.17, f32[256,384]{1,0:T(8,128)} %get-tuple-element.31.rest_0_.rest_8_, ...), custom_call_target="tpu_custom_call" | custom-call | tf_op jit(solution)/shard_map/rs_z/pallas_call | solution.py:172
  52.2 9.6 %all-to-all-start = ((bf16[8,16,1152]{2,1,0:T(8,128)(2,1)}), bf16[8,16,1152]{2,1,0:T(8,128)(2,1)S(1)}, u32[]{:S(2)}, u32[]{:S(2)}) async-start(bf16[8,16,1152]{2,1,0:T(8,128)(2,1)} %rs_z.1.dep_ref), calls=%async_computation | async-start | bytes 589824 | tf_op jit(solution)/shard_map/all_to_all | solution.py:501
  61.8 3.2 %collective-permute-start.18 = (bf16[384,1536]{1,0:T(8,128)(2,1)}, bf16[384,1536]{1,0:T(8,128)(2,1)}, u32[]{:S(2)}, u32[]{:S(2)}) collective-permute-start(bf16[384,1536]{1,0:T(8,128)(2,1)} %refs_4_.1), channel_id=1, source_target_pairs={{0,2},{1,3},{2,0},{3,1},{4,6},{5,7},{6,4},{7,5},{8,10},{9,11},{10,... | collective-permute-start | bytes 3538952 | tf_op jit(solution)/shard_map/ppermute | solution.py:496
  65.0 5.6 %attend_1.1.rest_0_.rest_8_ = f32[256,384]{1,0:T(8,128)} custom-call(s32[4]{0:T(128)} %pad_add_fusion.pos_ref.rest_0_, s32[1,128]{1,0:T(1,128)} %bitcast.16, bf16[1024,384]{1,0:T(8,128)(2,1)} %project.1.rest_2_.q_all.q_ref, bf16[1024,768]{1,0:T(8,128)(2,1)} %copy-done, bf16[1024,768]{1,0:T(8,128)(2,1)} %get-tuple-element.22.kv_ref.rest_4_.mine, ...), custom_call_target="tpu_custom_call" | custom-call | tf_op jit(solution)/shard_map/attend_1/pallas_call | solution.py:362
  70.6 2.4 %all-to-all-done.got_ref = bf16[8,16,1152]{2,1,0:T(8,128)(2,1)S(1)} async-done(((bf16[8,16,1152]{2,1,0:T(8,128)(2,1)}), bf16[8,16,1152]{2,1,0:T(8,128)(2,1)S(1)}, u32[]{:S(2)}, u32[]{:S(2)}) %all-to-all-start) | async-done | bytes 294944 | tf_op jit(solution)/shard_map/all_to_all | solution.py:501
  73.7 1.9 %renorm.1.dep_ref = bf16[8,16,1152]{2,1,0:T(8,128)(2,1)} custom-call(f32[16,1152]{1,0:T(8,128)} %get-tuple-element.27.rest_1_.old_ref, bf16[8,16,1152]{2,1,0:T(8,128)(2,1)} %copy-done.7, f32[256,384]{1,0:T(8,128)} %attend_1.1.rest_0_.rest_8_), custom_call_target="tpu_custom_call" | custom-call | tf_op jit(solution)/shard_map/renorm/pallas_call | solution.py:201
  75.6 4.8 %all-to-all-start.1 = ((bf16[8,16,1152]{2,1,0:T(8,128)(2,1)}), bf16[8,16,1152]{2,1,0:T(8,128)(2,1)S(1)}, u32[]{:S(2)}, u32[]{:S(2)}) async-start(bf16[8,16,1152]{2,1,0:T(8,128)(2,1)} %renorm.1.dep_ref), calls=%async_computation.1 | async-start | bytes 589824 | tf_op jit(solution)/shard_map/all_to_all | solution.py:501
  80.4 5.6 %attend_2.1.rest_0_.rest_9_ = f32[256,384]{1,0:T(8,128)} custom-call(s32[4]{0:T(128)} %pad_add_fusion.pos_ref.rest_0_, s32[1,128]{1,0:T(1,128)} %bitcast.17, bf16[1024,384]{1,0:T(8,128)(2,1)} %project.1.rest_2_.q_all.q_ref, bf16[1024,768]{1,0:T(8,128)(2,1)} %copy-done, bf16[1024,768]{1,0:T(8,128)(2,1)} %get-tuple-element.22.kv_ref.rest_4_.mine, ...), custom_call_target="tpu_custom_call" | custom-call | tf_op jit(solution)/shard_map/attend_2/pallas_call | solution.py:362
  86.0 4.2 %all-to-all-done.1.value_ref = bf16[8,16,1152]{2,1,0:T(8,128)(2,1)S(1)} async-done(((bf16[8,16,1152]{2,1,0:T(8,128)(2,1)}), bf16[8,16,1152]{2,1,0:T(8,128)(2,1)S(1)}, u32[]{:S(2)}, u32[]{:S(2)}) %all-to-all-start.1) | async-done | bytes 294944 | tf_op jit(solution)/shard_map/all_to_all | solution.py:501
  93.2 3.1 %collective-permute-start.9 = (bf16[96,1152]{1,0:T(8,128)(2,1)S(1)}, bf16[96,1152]{1,0:T(8,128)(2,1)S(1)}, u32[]{:S(2)}, u32[]{:S(2)}) collective-permute-start(bf16[96,1152]{1,0:T(8,128)(2,1)S(1)} %bitcast.8), channel_id=1, source_target_pairs={{0,128},{4,132},{8,136},{12,140},{16,144},{20,148},{24,152},{28,15... | collective-permute-start | bytes 663560 | tf_op jit(solution)/shard_map/ppermute | solution.py:485
  97.4 4.8 %attend_3.1.rest_0_.rest_10_ = f32[256,384]{1,0:T(8,128)} custom-call(s32[4]{0:T(128)} %pad_add_fusion.pos_ref.rest_0_, s32[1,128]{1,0:T(1,128)} %bitcast.18, bf16[1024,384]{1,0:T(8,128)(2,1)} %project.1.rest_2_.q_all.q_ref, bf16[1024,768]{1,0:T(8,128)(2,1)} %copy-done, bf16[1024,768]{1,0:T(8,128)(2,1)} %get-tuple-element.22.kv_ref.rest_4_.mine, ...), custom_call_target="tpu_custom_call" | custom-call | tf_op jit(solution)/shard_map/attend_3/pallas_call | solution.py:362
  107.1 5.6 %apply_3.1 = (bf16[256,384]{1,0:T(8,128)(2,1)}, bf16[256,384]{1,0:T(8,128)(2,1)}, bf16[256,384]{1,0:T(8,128)(2,1)}) custom-call(s32[4]{0:T(128)} %pad_add_fusion.pos_ref.rest_0_, bf16[1024,384]{1,0:T(8,128)(2,1)} %project.1.rest_2_.q_all.q_ref, f32[1,384]{1,0:T(1,128)} %broadcast_in_dim.6.gain_ref, bf16[96,1152]{1,0:T(8,128)(2,1)} %bitcast.12, ...), custom_call_target="tpu_custom_call" | custom-call | tf_op jit(solution)/shard_map/apply_3/pallas_call | solution.py:413
  113.1 13.0 %collective-permute-start.16 = (bf16[256,384]{1,0:T(8,128)(2,1)}, bf16[256,384]{1,0:T(8,128)(2,1)S(1)}, u32[]{:S(2)}, u32[]{:S(2)}) collective-permute-start(bf16[256,384]{1,0:T(8,128)(2,1)} %get-tuple-element.33), channel_id=1, source_target_pairs={{0,2},{1,3},{2,0},{3,1},{4,6},{5,7},{6,4},{7,5},{8,10},{9,11},{10,... | collective-permute-start | bytes 589832 | tf_op jit(solution)/shard_map/ppermute | solution.py:496
  126.2 3.8 %apply_1.1.refs_0_ = bf16[256,384]{1,0:T(8,128)(2,1)} custom-call(s32[4]{0:T(128)} %pad_add_fusion.pos_ref.rest_0_, bf16[1024,384]{1,0:T(8,128)(2,1)} %project.1.rest_2_.q_all.q_ref, f32[1,384]{1,0:T(1,128)} %broadcast_in_dim.6.gain_ref, bf16[96,1152]{1,0:T(8,128)(2,1)} %bitcast.13, bf16[96,1152]{1,0:T(8,128)(2,1)} %hold.3.rest_1_, ...), custom_call_target="tpu_custom_call" | custom-call | tf_op jit(solution)/shard_map/apply_1/pallas_call | solution.py:413
  130.2 5.4 %collective-permute-done.16.refs_2_ = bf16[256,384]{1,0:T(8,128)(2,1)S(1)} collective-permute-done((bf16[256,384]{1,0:T(8,128)(2,1)}, bf16[256,384]{1,0:T(8,128)(2,1)S(1)}, u32[]{:S(2)}, u32[]{:S(2)}) %collective-permute-start.16) | collective-permute-done | bytes 196640 | tf_op jit(solution)/shard_map/ppermute | solution.py:496
  137.0 5.5 %output.1 = (bf16[256,384]{1,0:T(8,128)(2,1)}, bf16[256,384]{1,0:T(8,128)(2,1)}, bf16[256,384]{1,0:T(8,128)(2,1)}, bf16[256,384]{1,0:T(8,128)(2,1)}) custom-call(s32[4]{0:T(128)} %pad_add_fusion.pos_ref.rest_0_, bf16[256,384]{1,0:T(8,128)(2,1)} %apply_1.1.refs_0_, bf16[256,384]{1,0:T(8,128)(2,1)} %copy-done.18, bf16[256,384]{1,0:T(8,128)(2,1)} %copy-done.19, ...), custom_call_target="tpu_custom_call" | custom-call | tf_op jit(solution)/shard_map/output/pallas_call | solution.py:440
  142.4 2.9 %collective-permute-start.20 = (bf16[256,384]{1,0:T(8,128)(2,1)}, bf16[256,384]{1,0:T(8,128)(2,1)S(1)}, u32[]{:S(2)}, u32[]{:S(2)}) collective-permute-start(bf16[256,384]{1,0:T(8,128)(2,1)} %get-tuple-element.37), channel_id=1, source_target_pairs={{0,2},{1,3},{2,0},{3,1},{4,6},{5,7},{6,4},{7,5},{8,10},{9,11},{10,... | collective-permute-start | bytes 589832 | tf_op jit(solution)/shard_map/ppermute | solution.py:496
  145.7 5.0 %collective-permute-done.19.refs_1_ = bf16[256,384]{1,0:T(8,128)(2,1)S(1)} collective-permute-done((bf16[256,384]{1,0:T(8,128)(2,1)}, bf16[256,384]{1,0:T(8,128)(2,1)S(1)}, u32[]{:S(2)}, u32[]{:S(2)}) %collective-permute-start.19) | collective-permute-done | bytes 196640 | tf_op jit(solution)/shard_map/ppermute | solution.py:496
  150.7 3.9 %collective-permute-done.20.refs_2_ = bf16[256,384]{1,0:T(8,128)(2,1)S(1)} collective-permute-done((bf16[256,384]{1,0:T(8,128)(2,1)}, bf16[256,384]{1,0:T(8,128)(2,1)S(1)}, u32[]{:S(2)}, u32[]{:S(2)}) %collective-permute-start.20) | collective-permute-done | bytes 196640 | tf_op jit(solution)/shard_map/ppermute | solution.py:496
  155.6 2.2 %arrange.1 = bf16[1024,384]{1,0:T(8,128)(2,1)} custom-call(s32[4]{0:T(128)} %pad_add_fusion.pos_ref.rest_0_, bf16[256,384]{1,0:T(8,128)(2,1)} %get-tuple-element.35.refs_0_, bf16[256,384]{1,0:T(8,128)(2,1)} %copy-done.21, bf16[256,384]{1,0:T(8,128)(2,1)} %copy-done.22, bf16[256,384]{1,0:T(8,128)(2,1)} %copy-done.23), custom_call_target="tpu_custom_call" | custom-call | tf_op jit(solution)/shard_map/arrange/pallas_call | solution.py:460
  (85 shorter events, 18.0 us)
Async XLA Ops:
  6.7 21.9 %collective-permute-start = (bf16[1024,768]{1,0:T(8,128)(2,1)}, bf16[1024,768]{1,0:T(8,128)(2,1)S(1)}, u32[]{:S(2)}, u32[]{:S(2)}) collective-permute-start(bf16[1024,768]{1,0:T(8,128)(2,1)} %get-tuple-element.22.kv_ref.rest_4_.mine), channel_id=1, source_target_pairs={{0,4},{4,8},{8,12},{12,16},{16,20},{20,24},{24,28},{28,32},{32,36}... | collective-permute-start | bytes 4718600 | tf_op jit(solution)/shard_map/ppermute | solution.py:485
  8.7 21.9 %collective-permute-start.1 = (bf16[1024,768]{1,0:T(8,128)(2,1)}, bf16[1024,768]{1,0:T(8,128)(2,1)S(1)}, u32[]{:S(2)}, u32[]{:S(2)}) collective-permute-start(bf16[1024,768]{1,0:T(8,128)(2,1)} %get-tuple-element.22.kv_ref.rest_4_.mine), channel_id=1, source_target_pairs={{4,0},{8,4},{12,8},{16,12},{20,16},{24,20},{28,24},{32,28},{36,32}... | collective-permute-start | bytes 4718600 | tf_op jit(solution)/shard_map/ppermute | solution.py:485
  22.6 5.5 %collective-permute-start.2 = (bf16[384,1152]{1,0:T(8,128)(2,1)}, bf16[384,1152]{1,0:T(8,128)(2,1)S(1)}, u32[]{:S(2)}, u32[]{:S(2)}) collective-permute-start(bf16[384,1152]{1,0:T(8,128)(2,1)} %get-tuple-element.24.rest_0_), channel_id=1, source_target_pairs={{0,4},{4,0},{8,12},{12,8},{16,20},{20,16},{24,28},{28,24},{32,36},... | collective-permute-start | bytes 2654216 | tf_op jit(solution)/shard_map/ppermute | solution.py:485
  28.1 2.4 %copy-start.14 = (bf16[384,1152]{1,0:T(8,128)(2,1)}, bf16[384,1152]{1,0:T(8,128)(2,1)S(1)}, u32[]{:S(2)}) copy-start(bf16[384,1152]{1,0:T(8,128)(2,1)S(1)} %collective-permute-done.2.got_ref) | copy-start | bytes 2654212
  28.7 1.9 %copy-start = (bf16[1024,768]{1,0:T(8,128)(2,1)}, bf16[1024,768]{1,0:T(8,128)(2,1)S(1)}, u32[]{:S(2)}) copy-start(bf16[1024,768]{1,0:T(8,128)(2,1)S(1)} %collective-permute-done.rest_0_.rest_3_.before) | copy-start | bytes 4718596
  34.7 14.6 %collective-permute-start.3 = (bf16[96,1152]{1,0:T(8,128)(2,1)}, bf16[96,1152]{1,0:T(8,128)(2,1)S(1)}, u32[]{:S(2)}, u32[]{:S(2)}) collective-permute-start(bf16[96,1152]{1,0:T(8,128)(2,1)} %get-tuple-element.28), channel_id=1, source_target_pairs={{0,64},{4,68},{8,72},{12,76},{16,80},{20,84},{24,88},{28,92},{32,9... | collective-permute-start | bytes 663560 | tf_op jit(solution)/shard_map/ppermute | solution.py:485
  36.2 13.1 %collective-permute-start.4 = (bf16[96,1152]{1,0:T(8,128)(2,1)}, bf16[96,1152]{1,0:T(8,128)(2,1)S(1)}, u32[]{:S(2)}, u32[]{:S(2)}) collective-permute-start(bf16[96,1152]{1,0:T(8,128)(2,1)} %get-tuple-element.29), channel_id=1, source_target_pairs={{0,128},{4,132},{8,136},{12,140},{16,144},{20,148},{24,152},{28,15... | collective-permute-start | bytes 663560 | tf_op jit(solution)/shard_map/ppermute | solution.py:485
  38.9 10.4 %collective-permute-start.5 = (bf16[96,1152]{1,0:T(8,128)(2,1)}, bf16[96,1152]{1,0:T(8,128)(2,1)S(1)}, u32[]{:S(2)}, u32[]{:S(2)}) collective-permute-start(bf16[96,1152]{1,0:T(8,128)(2,1)} %get-tuple-element.30), channel_id=1, source_target_pairs={{0,192},{4,196},{8,200},{12,204},{16,208},{20,212},{24,216},{28,22... | collective-permute-start | bytes 663560 | tf_op jit(solution)/shard_map/ppermute | solution.py:485
  40.3 45.6 %collective-permute-start.6 = (bf16[384,1536]{1,0:T(8,128)(2,1)}, bf16[384,1536]{1,0:T(8,128)(2,1)S(1)}, u32[]{:S(2)}, u32[]{:S(2)}) collective-permute-start(bf16[384,1536]{1,0:T(8,128)(2,1)} %refs_4_.1), channel_id=1, source_target_pairs={{0,1},{1,2},{2,3},{3,0},{4,5},{5,6},{6,7},{7,4},{8,9},{9,10},{10,1... | collective-permute-start | bytes 3538952 | tf_op jit(solution)/shard_map/ppermute | solution.py:496
  41.9 44.1 %collective-permute-start.7 = (bf16[384,1536]{1,0:T(8,128)(2,1)}, bf16[384,1536]{1,0:T(8,128)(2,1)S(1)}, u32[]{:S(2)}, u32[]{:S(2)}) collective-permute-start(bf16[384,1536]{1,0:T(8,128)(2,1)} %refs_4_.1), channel_id=1, source_target_pairs={{0,3},{1,0},{2,1},{3,2},{4,7},{5,4},{6,5},{7,6},{8,11},{9,8},{10,9... | collective-permute-start | bytes 3538952 | tf_op jit(solution)/shard_map/ppermute | solution.py:496
  52.2 20.7 %all-to-all-start = ((bf16[8,16,1152]{2,1,0:T(8,128)(2,1)}), bf16[8,16,1152]{2,1,0:T(8,128)(2,1)S(1)}, u32[]{:S(2)}, u32[]{:S(2)}) async-start(bf16[8,16,1152]{2,1,0:T(8,128)(2,1)} %rs_z.1.dep_ref), calls=%async_computation | async-start | bytes 589824 | tf_op jit(solution)/shard_map/all_to_all | solution.py:501
  61.8 68.2 %collective-permute-start.18 = (bf16[384,1536]{1,0:T(8,128)(2,1)}, bf16[384,1536]{1,0:T(8,128)(2,1)}, u32[]{:S(2)}, u32[]{:S(2)}) collective-permute-start(bf16[384,1536]{1,0:T(8,128)(2,1)} %refs_4_.1), channel_id=1, source_target_pairs={{0,2},{1,3},{2,0},{3,1},{4,6},{5,7},{6,4},{7,5},{8,10},{9,11},{10,... | collective-permute-start | bytes 3538952 | tf_op jit(solution)/shard_map/ppermute | solution.py:496
  75.6 14.6 %all-to-all-start.1 = ((bf16[8,16,1152]{2,1,0:T(8,128)(2,1)}), bf16[8,16,1152]{2,1,0:T(8,128)(2,1)S(1)}, u32[]{:S(2)}, u32[]{:S(2)}) async-start(bf16[8,16,1152]{2,1,0:T(8,128)(2,1)} %renorm.1.dep_ref), calls=%async_computation.1 | async-start | bytes 589824 | tf_op jit(solution)/shard_map/all_to_all | solution.py:501
  86.0 4.3 %copy-start.2 = (bf16[384,1536]{1,0:T(8,128)(2,1)}, bf16[384,1536]{1,0:T(8,128)(2,1)S(1)}, u32[]{:S(2)}) copy-start(bf16[384,1536]{1,0:T(8,128)(2,1)S(1)} %collective-permute-done.6.rest_1_.refs_5_) | copy-start | bytes 3538948
  86.0 4.2 %copy-start.3 = (bf16[384,1536]{1,0:T(8,128)(2,1)}, bf16[384,1536]{1,0:T(8,128)(2,1)S(1)}, u32[]{:S(2)}) copy-start(bf16[384,1536]{1,0:T(8,128)(2,1)S(1)} %collective-permute-done.7.rest_2_.refs_7_) | copy-start | bytes 3538948
  91.9 5.5 %copy-start.4 = (bf16[6,16,1152]{2,1,0:T(8,128)(2,1)}, bf16[6,16,1152]{2,1,0:T(8,128)(2,1)S(1)}, u32[]{:S(2)}) copy-start(bf16[6,16,1152]{2,1,0:T(8,128)(2,1)S(1)} %slice.4) | copy-start | bytes 663556
  91.9 12.9 %copy-start.24 = (f32[384]{0:T(512)S(1)}, f32[384]{0:T(512)}, u32[]{:S(2)}) copy-start(f32[384]{0:T(512)} %param.15) | copy-start | bytes 4612
  91.9 10.4 %collective-permute-start.8 = (bf16[96,1152]{1,0:T(8,128)(2,1)S(1)}, bf16[96,1152]{1,0:T(8,128)(2,1)S(1)}, u32[]{:S(2)}, u32[]{:S(2)}) collective-permute-start(bf16[96,1152]{1,0:T(8,128)(2,1)S(1)} %bitcast.7), channel_id=1, source_target_pairs={{0,64},{4,68},{8,72},{12,76},{16,80},{20,84},{24,88},{28,92},{32,9... | collective-permute-start | bytes 663560 | tf_op jit(solution)/shard_map/ppermute | solution.py:485
  93.2 11.1 %collective-permute-start.9 = (bf16[96,1152]{1,0:T(8,128)(2,1)S(1)}, bf16[96,1152]{1,0:T(8,128)(2,1)S(1)}, u32[]{:S(2)}, u32[]{:S(2)}) collective-permute-start(bf16[96,1152]{1,0:T(8,128)(2,1)S(1)} %bitcast.8), channel_id=1, source_target_pairs={{0,128},{4,132},{8,136},{12,140},{16,144},{20,148},{24,152},{28,15... | collective-permute-start | bytes 663560 | tf_op jit(solution)/shard_map/ppermute | solution.py:485
  96.3 8.1 %collective-permute-start.10 = (bf16[96,1152]{1,0:T(8,128)(2,1)S(1)}, bf16[96,1152]{1,0:T(8,128)(2,1)S(1)}, u32[]{:S(2)}, u32[]{:S(2)}) collective-permute-start(bf16[96,1152]{1,0:T(8,128)(2,1)S(1)} %bitcast.9), channel_id=1, source_target_pairs={{0,192},{4,196},{8,200},{12,204},{16,208},{20,212},{24,216},{28,22... | collective-permute-start | bytes 663560 | tf_op jit(solution)/shard_map/ppermute | solution.py:485
  97.4 7.9 %collective-permute-start.11 = (bf16[96,1152]{1,0:T(8,128)(2,1)S(1)}, bf16[96,1152]{1,0:T(8,128)(2,1)S(1)}, u32[]{:S(2)}, u32[]{:S(2)}) collective-permute-start(bf16[96,1152]{1,0:T(8,128)(2,1)S(1)} %bitcast.10), channel_id=1, source_target_pairs={{0,4},{4,0},{8,12},{12,8},{16,20},{20,16},{24,28},{28,24},{32,36},... | collective-permute-start | bytes 663560 | tf_op jit(solution)/shard_map/ppermute | solution.py:485
  103.0 2.6 %collective-permute-start.12 = (bf16[96,1152]{1,0:T(8,128)(2,1)}, bf16[96,1152]{1,0:T(8,128)(2,1)S(1)}, u32[]{:S(2)}, u32[]{:S(2)}) collective-permute-start(bf16[96,1152]{1,0:T(8,128)(2,1)} %hold.3.rest_1_), channel_id=1, source_target_pairs={{0,4},{4,0},{8,12},{12,8},{16,20},{20,16},{24,28},{28,24},{32,36},... | collective-permute-start | bytes 663560 | tf_op jit(solution)/shard_map/ppermute | solution.py:485
  104.2 1.5 collective-permute-start.13
  104.3 1.7 %collective-permute-start.14 = (bf16[96,1152]{1,0:T(8,128)(2,1)S(1)}, bf16[96,1152]{1,0:T(8,128)(2,1)S(1)}, u32[]{:S(2)}, u32[]{:S(2)}) collective-permute-start(bf16[96,1152]{1,0:T(8,128)(2,1)S(1)} %collective-permute-done.10.rest_3_), channel_id=1, source_target_pairs={{0,4},{4,0},{8,12},{12,8},{16,20},{20,16},{24,28},{28,24},{32,36},... | collective-permute-start | bytes 663560 | tf_op jit(solution)/shard_map/ppermute | solution.py:485
  112.7 17.5 %collective-permute-start.15 = (bf16[256,384]{1,0:T(8,128)(2,1)}, bf16[256,384]{1,0:T(8,128)(2,1)S(1)}, u32[]{:S(2)}, u32[]{:S(2)}) collective-permute-start(bf16[256,384]{1,0:T(8,128)(2,1)} %get-tuple-element.32.rest_9_), channel_id=1, source_target_pairs={{0,1},{1,2},{2,3},{3,0},{4,5},{5,6},{6,7},{7,4},{8,9},{9,10},{10,1... | collective-permute-start | bytes 589832 | tf_op jit(solution)/shard_map/ppermute | solution.py:496
  113.1 22.5 %collective-permute-start.16 = (bf16[256,384]{1,0:T(8,128)(2,1)}, bf16[256,384]{1,0:T(8,128)(2,1)S(1)}, u32[]{:S(2)}, u32[]{:S(2)}) collective-permute-start(bf16[256,384]{1,0:T(8,128)(2,1)} %get-tuple-element.33), channel_id=1, source_target_pairs={{0,2},{1,3},{2,0},{3,1},{4,6},{5,7},{6,4},{7,5},{8,10},{9,11},{10,... | collective-permute-start | bytes 589832 | tf_op jit(solution)/shard_map/ppermute | solution.py:496
  126.2 9.4 %collective-permute-start.17 = (bf16[256,384]{1,0:T(8,128)(2,1)}, bf16[256,384]{1,0:T(8,128)(2,1)S(1)}, u32[]{:S(2)}, u32[]{:S(2)}) collective-permute-start(bf16[256,384]{1,0:T(8,128)(2,1)} %get-tuple-element.34), channel_id=1, source_target_pairs={{0,3},{1,0},{2,1},{3,2},{4,7},{5,4},{6,5},{7,6},{8,11},{9,8},{10,9... | collective-permute-start | bytes 589832 | tf_op jit(solution)/shard_map/ppermute | solution.py:496
  130.2 5.4 %copy-start.18 = (bf16[256,384]{1,0:T(8,128)(2,1)}, bf16[256,384]{1,0:T(8,128)(2,1)S(1)}, u32[]{:S(2)}) copy-start(bf16[256,384]{1,0:T(8,128)(2,1)S(1)} %collective-permute-done.15.refs_1_) | copy-start | bytes 589828
  142.4 8.2 %collective-permute-start.19 = (bf16[256,384]{1,0:T(8,128)(2,1)}, bf16[256,384]{1,0:T(8,128)(2,1)S(1)}, u32[]{:S(2)}, u32[]{:S(2)}) collective-permute-start(bf16[256,384]{1,0:T(8,128)(2,1)} %get-tuple-element.36), channel_id=1, source_target_pairs={{0,1},{1,2},{2,3},{3,0},{4,5},{5,6},{6,7},{7,4},{8,9},{9,10},{10,1... | collective-permute-start | bytes 589832 | tf_op jit(solution)/shard_map/ppermute | solution.py:496
  142.4 12.2 %collective-permute-start.20 = (bf16[256,384]{1,0:T(8,128)(2,1)}, bf16[256,384]{1,0:T(8,128)(2,1)S(1)}, u32[]{:S(2)}, u32[]{:S(2)}) collective-permute-start(bf16[256,384]{1,0:T(8,128)(2,1)} %get-tuple-element.37), channel_id=1, source_target_pairs={{0,2},{1,3},{2,0},{3,1},{4,6},{5,7},{6,4},{7,5},{8,10},{9,11},{10,... | collective-permute-start | bytes 589832 | tf_op jit(solution)/shard_map/ppermute | solution.py:496
  145.4 9.5 %collective-permute-start.21 = (bf16[256,384]{1,0:T(8,128)(2,1)}, bf16[256,384]{1,0:T(8,128)(2,1)S(1)}, u32[]{:S(2)}, u32[]{:S(2)}) collective-permute-start(bf16[256,384]{1,0:T(8,128)(2,1)} %get-tuple-element.38), channel_id=1, source_target_pairs={{0,3},{1,0},{2,1},{3,2},{4,7},{5,4},{6,5},{7,6},{8,11},{9,8},{10,9... | collective-permute-start | bytes 589832 | tf_op jit(solution)/shard_map/ppermute | solution.py:496
  150.7 4.2 %copy-start.21 = (bf16[256,384]{1,0:T(8,128)(2,1)}, bf16[256,384]{1,0:T(8,128)(2,1)S(1)}, u32[]{:S(2)}) copy-start(bf16[256,384]{1,0:T(8,128)(2,1)S(1)} %collective-permute-done.19.refs_1_) | copy-start | bytes 589828
  (17 other events, 14.6 us)

commit v10 on v9

--- a/solution.py
+++ b/solution.py
@@ -508,13 +508,13 @@
     total = rs_z(own, got, [att0, old])
     got = exchange(total)
     att1 = att(1, dep=total)
-    fresh = renorm(old, got, [att1])
+    fresh = renorm(old, got, [att1, weights[1], weights[3]])
     got = exchange(fresh)
     att2 = att(2, dep=fresh)
-    block = hold(got, [att2, weights[1], weights[3]])[:OWNERS].reshape(XROWS, WIDE)
+    block = hold(got, [att2])[:OWNERS].reshape(XROWS, WIDE)
     att3 = att(3, dep=block)
     near, *far = [send(block, shift_x(d)) for d in range(1, XS)]
-    blocks = [block, hold(near, [att3]), *far]
+    blocks = [block, hold(near, [att3, weights[2]]), *far]
     others = [send(b, SWAP_C) for b in blocks]
 
     mix = functools.partial(

time: 159 us -> 153 us (0.962)
  the two profiles are of different devices: /device:TPU:32 before, /device:TPU:1 now
where the time goes in v10:
time: 153 us; the launch traced here: 152 us
  Pallas kernels  69.5 us (45%)
  starting transfers between devices  48 us (31%)
  waiting for transfers between devices  23.6 us (15%)
  local copies, waits for them, and re-layouts  9.83 us (6%)
    ppermute x13, starting transfers between devices, body(): send = lambda value, pairs: lax.ppermute(value, 'tok', pairs)  24.1 us
    pallas_call x4, Pallas kernels, attend(): pl.pallas_call(kernel, grid=(1,), in_specs=([SMEM] + [DEP] * 3 if old els...  24 us
    ppermute x9, starting transfers between devices, spread(): lax.ppermute(p, 'head', shift_h(d))  14.4 us
    ppermute x9, waiting for transfers between devices, spread(): lax.ppermute(p, 'head', shift_h(d))  11.7 us
    pallas_call x1, Pallas kernels, update(): pl.pallas_call(update_kernel, grid=(1,), in_specs=[SMEM, full(kv.shape),...  9.69 us
    all_to_all x2, starting transfers between devices, exchange(): return lax.all_to_all(blocks, 'tok', 0, 0, axis_index_groups=ALONG_Z)  9.43 us
    pallas_call x2, Pallas kernels, apply(): pl.pallas_call(functools.partial(apply_kernel, aheads), grid=(1,), in_spe...  9.38 us
    unnamed x48, local copies, waits for them, and re-layouts  8.3 us
  transfers between devices with their start and end apart: 24, of which 10 were waited for; matrix products, arithmetic and copies ran while one was open for 1% of the time, Pallas kernels for 33%

profile of v10, /device:TPU:1, one launch (start us, length us, event | category | flops | bytes accessed | tf_op | source)
XLA Modules:
  0.0 151.8 jit_solution(14322715470794146239)
XLA Ops:
  0.0 6.7 %keys.1 = (bf16[1024,768]{1,0:T(8,128)(2,1)}, f32[1024,3]{1,0:T(8,128)}) custom-call(bf16[1024,1536]{1,0:T(8,128)(2,1)} %t_ref.3, bf16[1536,1152]{1,0:T(8,128)(2,1)} %w_ref.3, bf16[3,1536]{1,0:T(4,128)(2,1)} %bitcast.14), custom_call_target="tpu_custom_call" | custom-call | tf_op jit(solution)/shard_map/keys/pallas_call | solution.py:74
  6.7 4.9 %collective-permute-start = (bf16[1024,768]{1,0:T(8,128)(2,1)}, bf16[1024,768]{1,0:T(8,128)(2,1)S(1)}, u32[]{:S(2)}, u32[]{:S(2)}) collective-permute-start(bf16[1024,768]{1,0:T(8,128)(2,1)} %get-tuple-element.22.kv_ref.rest_4_.mine), channel_id=1, source_target_pairs={{0,4},{4,8},{8,12},{12,16},{16,20},{20,24},{24,28},{28,32},{32,36}... | collective-permute-start | bytes 4718600 | tf_op jit(solution)/shard_map/ppermute | solution.py:485
  11.7 1.9 %collective-permute-start.1 = (bf16[1024,768]{1,0:T(8,128)(2,1)}, bf16[1024,768]{1,0:T(8,128)(2,1)S(1)}, u32[]{:S(2)}, u32[]{:S(2)}) collective-permute-start(bf16[1024,768]{1,0:T(8,128)(2,1)} %get-tuple-element.22.kv_ref.rest_4_.mine), channel_id=1, source_target_pairs={{4,0},{8,4},{12,8},{16,12},{20,16},{24,20},{28,24},{32,28},{36,32}... | collective-permute-start | bytes 4718600 | tf_op jit(solution)/shard_map/ppermute | solution.py:485
  14.3 9.7 %update.1 = (bf16[384,1152]{1,0:T(8,128)(2,1)}, f32[384,1152]{1,0:T(8,128)}) custom-call(s32[4]{0:T(128)} %pad_add_fusion.pos_ref.rest_0_, bf16[1024,768]{1,0:T(8,128)(2,1)} %get-tuple-element.22.kv_ref.rest_4_.mine, f32[1024,3]{1,0:T(8,128)} %get-tuple-element.23.r_ref, bf16[1,384,768]{2,1,0:T(8,128)(2,1)} %w1_ref.3, bf16[1,384,768]{2,1,0:T(8,128)(2,1)} %w3_ref.3, ...), custom_call_target="tpu_custom_call" | custom-call | tf_op jit(solution)/shard_map/update/pallas_call | solution.py:121
  26.8 5.2 %project.1.rest_2_.q_all.q_ref = bf16[1024,384]{1,0:T(8,128)(2,1)} custom-call(bf16[1024,1536]{1,0:T(8,128)(2,1)} %t_ref.3, bf16[1536,1152]{1,0:T(8,128)(2,1)} %w_ref.3, bf16[384,1152]{1,0:T(8,128)(2,1)} %get-tuple-element.24.rest_0_), custom_call_target="tpu_custom_call" | custom-call | tf_op jit(solution)/shard_map/project/pallas_call | solution.py:236
  32.0 2.0 %collective-permute-done.1.rest_1_.rest_5_.after = bf16[1024,768]{1,0:T(8,128)(2,1)S(1)} collective-permute-done((bf16[1024,768]{1,0:T(8,128)(2,1)}, bf16[1024,768]{1,0:T(8,128)(2,1)S(1)}, u32[]{:S(2)}, u32[]{:S(2)}) %collective-permute-start.1) | collective-permute-done | bytes 1572896 | tf_op jit(solution)/shard_map/ppermute | solution.py:485
  35.2 2.9 %rs_x.1 = (f32[96,1152]{1,0:T(8,128)}, bf16[96,1152]{1,0:T(8,128)(2,1)}, bf16[96,1152]{1,0:T(8,128)(2,1)}, bf16[96,1152]{1,0:T(8,128)(2,1)}) custom-call(s32[4]{0:T(128)} %pad_add_fusion.pos_ref.rest_0_, f32[384,1152]{1,0:T(8,128)} %get-tuple-element.25.keep_ref, bf16[384,1152]{1,0:T(8,128)(2,1)} %copy-done.13, bf16[1024,768]{1,0:T(8,128)(2,1)} %copy-done, ...), custom_call_target="tpu_custom_call" | custom-call | tf_op jit(solution)/shard_map/rs_x/pallas_call | solution.py:149
  38.1 3.6 %collective-permute-start.3 = (bf16[96,1152]{1,0:T(8,128)(2,1)}, bf16[96,1152]{1,0:T(8,128)(2,1)S(1)}, u32[]{:S(2)}, u32[]{:S(2)}) collective-permute-start(bf16[96,1152]{1,0:T(8,128)(2,1)} %get-tuple-element.28), channel_id=1, source_target_pairs={{0,64},{4,68},{8,72},{12,76},{16,80},{20,84},{24,88},{28,92},{32,9... | collective-permute-start | bytes 663560 | tf_op jit(solution)/shard_map/ppermute | solution.py:485
  41.7 2.7 %collective-permute-start.4 = (bf16[96,1152]{1,0:T(8,128)(2,1)}, bf16[96,1152]{1,0:T(8,128)(2,1)S(1)}, u32[]{:S(2)}, u32[]{:S(2)}) collective-permute-start(bf16[96,1152]{1,0:T(8,128)(2,1)} %get-tuple-element.29), channel_id=1, source_target_pairs={{0,128},{4,132},{8,136},{12,140},{16,144},{20,148},{24,152},{28,15... | collective-permute-start | bytes 663560 | tf_op jit(solution)/shard_map/ppermute | solution.py:485
  45.3 5.7 %attend_0.1 = (f32[256,384]{1,0:T(8,128)}, f32[16,1152]{1,0:T(8,128)}) custom-call(s32[4]{0:T(128)} %pad_add_fusion.pos_ref.rest_0_, bf16[1,384,768]{2,1,0:T(8,128)(2,1)} %w1_ref.3, bf16[1,384,768]{2,1,0:T(8,128)(2,1)} %w3_ref.3, bf16[1,768,384]{2,1,0:T(8,128)(2,1)} %w2_ref.3, s32[4]{0:T(128)} %pad_add_fusion.pos_ref.rest_0_, s32[1,128]{1,0:T(1,128)} %bitcast.15, ...), custom_call_target="tpu_custom_call" | custom-call | tf_op jit(solution)/shard_map/attend_0/pallas_call | solution.py:362
  51.0 3.4 %collective-permute-done.4.g2 = bf16[96,1152]{1,0:T(8,128)(2,1)S(1)} collective-permute-done((bf16[96,1152]{1,0:T(8,128)(2,1)}, bf16[96,1152]{1,0:T(8,128)(2,1)S(1)}, u32[]{:S(2)}, u32[]{:S(2)}) %collective-permute-start.4) | collective-permute-done | bytes 221216 | tf_op jit(solution)/shard_map/ppermute | solution.py:485
  55.2 2.1 %rs_z.1.dep_ref = bf16[8,16,1152]{2,1,0:T(8,128)(2,1)} custom-call(f32[96,1152]{1,0:T(8,128)} %get-tuple-element.26.rest_6_.own_ref, bf16[96,1152]{1,0:T(8,128)(2,1)} %copy-done.14, bf16[96,1152]{1,0:T(8,128)(2,1)} %copy-done.15, bf16[96,1152]{1,0:T(8,128)(2,1)} %copy-done.16, f32[256,384]{1,0:T(8,128)} %get-tuple-element.31.rest_0_.rest_8_, ...), custom_call_target="tpu_custom_call" | custom-call | tf_op jit(solution)/shard_map/rs_z/pallas_call | solution.py:172
  57.3 5.6 %all-to-all-start = ((bf16[8,16,1152]{2,1,0:T(8,128)(2,1)}), bf16[8,16,1152]{2,1,0:T(8,128)(2,1)S(1)}, u32[]{:S(2)}, u32[]{:S(2)}) async-start(bf16[8,16,1152]{2,1,0:T(8,128)(2,1)} %rs_z.1.dep_ref), calls=%async_computation | async-start | bytes 589824 | tf_op jit(solution)/shard_map/all_to_all | solution.py:501
  62.8 2.2 %collective-permute-start.9 = (bf16[384,1536]{1,0:T(8,128)(2,1)}, bf16[384,1536]{1,0:T(8,128)(2,1)S(1)}, u32[]{:S(2)}, u32[]{:S(2)}) collective-permute-start(bf16[384,1536]{1,0:T(8,128)(2,1)} %refs_4_.1), channel_id=1, source_target_pairs={{0,2},{1,3},{2,0},{3,1},{4,6},{5,7},{6,4},{7,5},{8,10},{9,11},{10,... | collective-permute-start | bytes 3538952 | tf_op jit(solution)/shard_map/ppermute | solution.py:496
  65.0 7.1 %attend_1.1.rest_0_.rest_8_ = f32[256,384]{1,0:T(8,128)} custom-call(s32[4]{0:T(128)} %pad_add_fusion.pos_ref.rest_0_, s32[1,128]{1,0:T(1,128)} %bitcast.16, bf16[1024,384]{1,0:T(8,128)(2,1)} %project.1.rest_2_.q_all.q_ref, bf16[1024,768]{1,0:T(8,128)(2,1)} %copy-done, bf16[1024,768]{1,0:T(8,128)(2,1)} %get-tuple-element.22.kv_ref.rest_4_.mine, ...), custom_call_target="tpu_custom_call" | custom-call | tf_op jit(solution)/shard_map/attend_1/pallas_call | solution.py:362
  76.0 3.9 %all-to-all-start.1 = ((bf16[8,16,1152]{2,1,0:T(8,128)(2,1)}), bf16[8,16,1152]{2,1,0:T(8,128)(2,1)S(1)}, u32[]{:S(2)}, u32[]{:S(2)}) async-start(bf16[8,16,1152]{2,1,0:T(8,128)(2,1)} %renorm.1.dep_ref), calls=%async_computation.1 | async-start | bytes 589824 | tf_op jit(solution)/shard_map/all_to_all | solution.py:501
  79.9 5.6 %attend_2.1.rest_0_.rest_9_ = f32[256,384]{1,0:T(8,128)} custom-call(s32[4]{0:T(128)} %pad_add_fusion.pos_ref.rest_0_, s32[1,128]{1,0:T(1,128)} %bitcast.17, bf16[1024,384]{1,0:T(8,128)(2,1)} %project.1.rest_2_.q_all.q_ref, bf16[1024,768]{1,0:T(8,128)(2,1)} %copy-done, bf16[1024,768]{1,0:T(8,128)(2,1)} %get-tuple-element.22.kv_ref.rest_4_.mine, ...), custom_call_target="tpu_custom_call" | custom-call | tf_op jit(solution)/shard_map/attend_2/pallas_call | solution.py:362
  85.5 4.4 %all-to-all-done.1.value_ref = bf16[8,16,1152]{2,1,0:T(8,128)(2,1)S(1)} async-done(((bf16[8,16,1152]{2,1,0:T(8,128)(2,1)}), bf16[8,16,1152]{2,1,0:T(8,128)(2,1)S(1)}, u32[]{:S(2)}, u32[]{:S(2)}) %all-to-all-start.1) | async-done | bytes 294944 | tf_op jit(solution)/shard_map/all_to_all | solution.py:501
  91.6 2.3 %collective-permute-start.8 = (bf16[96,1152]{1,0:T(8,128)(2,1)S(1)}, bf16[96,1152]{1,0:T(8,128)(2,1)S(1)}, u32[]{:S(2)}, u32[]{:S(2)}) collective-permute-start(bf16[96,1152]{1,0:T(8,128)(2,1)S(1)} %bitcast.7), channel_id=1, source_target_pairs={{0,64},{4,68},{8,72},{12,76},{16,80},{20,84},{24,88},{28,92},{32,9... | collective-permute-start | bytes 663560 | tf_op jit(solution)/shard_map/ppermute | solution.py:485
  93.8 3.9 %collective-permute-start.10 = (bf16[96,1152]{1,0:T(8,128)(2,1)S(1)}, bf16[96,1152]{1,0:T(8,128)(2,1)S(1)}, u32[]{:S(2)}, u32[]{:S(2)}) collective-permute-start(bf16[96,1152]{1,0:T(8,128)(2,1)S(1)} %bitcast.8), channel_id=1, source_target_pairs={{0,128},{4,132},{8,136},{12,140},{16,144},{20,148},{24,152},{28,15... | collective-permute-start | bytes 663560 | tf_op jit(solution)/shard_map/ppermute | solution.py:485
  97.7 3.3 %collective-permute-start.12 = (bf16[96,1152]{1,0:T(8,128)(2,1)S(1)}, bf16[96,1152]{1,0:T(8,128)(2,1)S(1)}, u32[]{:S(2)}, u32[]{:S(2)}) collective-permute-start(bf16[96,1152]{1,0:T(8,128)(2,1)S(1)} %bitcast.10), channel_id=1, source_target_pairs={{0,4},{4,0},{8,12},{12,8},{16,20},{20,16},{24,28},{28,24},{32,36},... | collective-permute-start | bytes 663560 | tf_op jit(solution)/shard_map/ppermute | solution.py:485
  101.0 5.6 %attend_3.1.rest_0_.rest_10_ = f32[256,384]{1,0:T(8,128)} custom-call(s32[4]{0:T(128)} %pad_add_fusion.pos_ref.rest_0_, s32[1,128]{1,0:T(1,128)} %bitcast.18, bf16[1024,384]{1,0:T(8,128)(2,1)} %project.1.rest_2_.q_all.q_ref, bf16[1024,768]{1,0:T(8,128)(2,1)} %copy-done, bf16[1024,768]{1,0:T(8,128)(2,1)} %get-tuple-element.22.kv_ref.rest_4_.mine, ...), custom_call_target="tpu_custom_call" | custom-call | tf_op jit(solution)/shard_map/attend_3/pallas_call | solution.py:362
  111.6 5.6 %apply_3.1 = (bf16[256,384]{1,0:T(8,128)(2,1)}, bf16[256,384]{1,0:T(8,128)(2,1)}, bf16[256,384]{1,0:T(8,128)(2,1)}) custom-call(s32[4]{0:T(128)} %pad_add_fusion.pos_ref.rest_0_, bf16[1024,384]{1,0:T(8,128)(2,1)} %project.1.rest_2_.q_all.q_ref, f32[1,384]{1,0:T(1,128)} %broadcast_in_dim.6.gain_ref, bf16[96,1152]{1,0:T(8,128)(2,1)} %bitcast.12, ...), custom_call_target="tpu_custom_call" | custom-call | tf_op jit(solution)/shard_map/apply_3/pallas_call | solution.py:413
  117.2 3.0 %collective-permute-start.17 = (bf16[256,384]{1,0:T(8,128)(2,1)}, bf16[256,384]{1,0:T(8,128)(2,1)S(1)}, u32[]{:S(2)}, u32[]{:S(2)}) collective-permute-start(bf16[256,384]{1,0:T(8,128)(2,1)} %get-tuple-element.33), channel_id=1, source_target_pairs={{0,2},{1,3},{2,0},{3,1},{4,6},{5,7},{6,4},{7,5},{8,10},{9,11},{10,... | collective-permute-start | bytes 589832 | tf_op jit(solution)/shard_map/ppermute | solution.py:496
  120.2 2.0 %collective-permute-start.18 = (bf16[256,384]{1,0:T(8,128)(2,1)}, bf16[256,384]{1,0:T(8,128)(2,1)S(1)}, u32[]{:S(2)}, u32[]{:S(2)}) collective-permute-start(bf16[256,384]{1,0:T(8,128)(2,1)} %get-tuple-element.34), channel_id=1, source_target_pairs={{0,3},{1,0},{2,1},{3,2},{4,7},{5,4},{6,5},{7,6},{8,11},{9,8},{10,9... | collective-permute-start | bytes 589832 | tf_op jit(solution)/shard_map/ppermute | solution.py:496
  122.2 3.8 %apply_1.1.refs_0_ = bf16[256,384]{1,0:T(8,128)(2,1)} custom-call(s32[4]{0:T(128)} %pad_add_fusion.pos_ref.rest_0_, bf16[1024,384]{1,0:T(8,128)(2,1)} %project.1.rest_2_.q_all.q_ref, f32[1,384]{1,0:T(1,128)} %broadcast_in_dim.6.gain_ref, bf16[96,1152]{1,0:T(8,128)(2,1)} %bitcast.13, bf16[96,1152]{1,0:T(8,128)(2,1)} %hold.3.rest_1_, ...), custom_call_target="tpu_custom_call" | custom-call | tf_op jit(solution)/shard_map/apply_1/pallas_call | solution.py:413
  126.0 3.4 %collective-permute-done.17.refs_2_ = bf16[256,384]{1,0:T(8,128)(2,1)S(1)} collective-permute-done((bf16[256,384]{1,0:T(8,128)(2,1)}, bf16[256,384]{1,0:T(8,128)(2,1)S(1)}, u32[]{:S(2)}, u32[]{:S(2)}) %collective-permute-start.17) | collective-permute-done | bytes 196640 | tf_op jit(solution)/shard_map/ppermute | solution.py:496
  130.8 5.5 %output.1 = (bf16[256,384]{1,0:T(8,128)(2,1)}, bf16[256,384]{1,0:T(8,128)(2,1)}, bf16[256,384]{1,0:T(8,128)(2,1)}, bf16[256,384]{1,0:T(8,128)(2,1)}) custom-call(s32[4]{0:T(128)} %pad_add_fusion.pos_ref.rest_0_, bf16[256,384]{1,0:T(8,128)(2,1)} %apply_1.1.refs_0_, bf16[256,384]{1,0:T(8,128)(2,1)} %copy-done.17, bf16[256,384]{1,0:T(8,128)(2,1)} %copy-done.18, ...), custom_call_target="tpu_custom_call" | custom-call | tf_op jit(solution)/shard_map/output/pallas_call | solution.py:440
  136.9 3.0 %collective-permute-start.20 = (bf16[256,384]{1,0:T(8,128)(2,1)}, bf16[256,384]{1,0:T(8,128)(2,1)S(1)}, u32[]{:S(2)}, u32[]{:S(2)}) collective-permute-start(bf16[256,384]{1,0:T(8,128)(2,1)} %get-tuple-element.37), channel_id=1, source_target_pairs={{0,2},{1,3},{2,0},{3,1},{4,6},{5,7},{6,4},{7,5},{8,10},{9,11},{10,... | collective-permute-start | bytes 589832 | tf_op jit(solution)/shard_map/ppermute | solution.py:496
  140.6 2.5 %collective-permute-done.19.refs_1_ = bf16[256,384]{1,0:T(8,128)(2,1)S(1)} collective-permute-done((bf16[256,384]{1,0:T(8,128)(2,1)}, bf16[256,384]{1,0:T(8,128)(2,1)S(1)}, u32[]{:S(2)}, u32[]{:S(2)}) %collective-permute-start.19) | collective-permute-done | bytes 196640 | tf_op jit(solution)/shard_map/ppermute | solution.py:496
  143.1 5.8 %collective-permute-done.20.refs_2_ = bf16[256,384]{1,0:T(8,128)(2,1)S(1)} collective-permute-done((bf16[256,384]{1,0:T(8,128)(2,1)}, bf16[256,384]{1,0:T(8,128)(2,1)S(1)}, u32[]{:S(2)}, u32[]{:S(2)}) %collective-permute-start.20) | collective-permute-done | bytes 196640 | tf_op jit(solution)/shard_map/ppermute | solution.py:496
  149.6 2.2 %arrange.1 = bf16[1024,384]{1,0:T(8,128)(2,1)} custom-call(s32[4]{0:T(128)} %pad_add_fusion.pos_ref.rest_0_, bf16[256,384]{1,0:T(8,128)(2,1)} %get-tuple-element.35.refs_0_, bf16[256,384]{1,0:T(8,128)(2,1)} %copy-done.20, bf16[256,384]{1,0:T(8,128)(2,1)} %copy-done.21, bf16[256,384]{1,0:T(8,128)(2,1)} %copy-done.22), custom_call_target="tpu_custom_call" | custom-call | tf_op jit(solution)/shard_map/arrange/pallas_call | solution.py:460
  (83 shorter events, 20.2 us)
Async XLA Ops:
  6.7 25.3 %collective-permute-start = (bf16[1024,768]{1,0:T(8,128)(2,1)}, bf16[1024,768]{1,0:T(8,128)(2,1)S(1)}, u32[]{:S(2)}, u32[]{:S(2)}) collective-permute-start(bf16[1024,768]{1,0:T(8,128)(2,1)} %get-tuple-element.22.kv_ref.rest_4_.mine), channel_id=1, source_target_pairs={{0,4},{4,8},{8,12},{12,16},{16,20},{20,24},{24,28},{28,32},{32,36}... | collective-permute-start | bytes 4718600 | tf_op jit(solution)/shard_map/ppermute | solution.py:485
  11.7 22.3 %collective-permute-start.1 = (bf16[1024,768]{1,0:T(8,128)(2,1)}, bf16[1024,768]{1,0:T(8,128)(2,1)S(1)}, u32[]{:S(2)}, u32[]{:S(2)}) collective-permute-start(bf16[1024,768]{1,0:T(8,128)(2,1)} %get-tuple-element.22.kv_ref.rest_4_.mine), channel_id=1, source_target_pairs={{4,0},{8,4},{12,8},{16,12},{20,16},{24,20},{28,24},{32,28},{36,32}... | collective-permute-start | bytes 4718600 | tf_op jit(solution)/shard_map/ppermute | solution.py:485
  24.0 8.0 %collective-permute-start.2 = (bf16[384,1152]{1,0:T(8,128)(2,1)}, bf16[384,1152]{1,0:T(8,128)(2,1)S(1)}, u32[]{:S(2)}, u32[]{:S(2)}) collective-permute-start(bf16[384,1152]{1,0:T(8,128)(2,1)} %get-tuple-element.24.rest_0_), channel_id=1, source_target_pairs={{0,4},{4,0},{8,12},{12,8},{16,20},{20,16},{24,28},{28,24},{32,36},... | collective-permute-start | bytes 2654216 | tf_op jit(solution)/shard_map/ppermute | solution.py:485
  24.0 48.2 %collective-permute-start.6 = (bf16[384,1536]{1,0:T(8,128)(2,1)}, bf16[384,1536]{1,0:T(8,128)(2,1)}, u32[]{:S(2)}, u32[]{:S(2)}) collective-permute-start(bf16[384,1536]{1,0:T(8,128)(2,1)} %refs_4_.1), channel_id=1, source_target_pairs={{0,1},{1,2},{2,3},{3,0},{4,5},{5,6},{6,7},{7,4},{8,9},{9,10},{10,1... | collective-permute-start | bytes 3538952 | tf_op jit(solution)/shard_map/ppermute | solution.py:496
  25.3 46.9 %collective-permute-start.7 = (bf16[384,1536]{1,0:T(8,128)(2,1)}, bf16[384,1536]{1,0:T(8,128)(2,1)}, u32[]{:S(2)}, u32[]{:S(2)}) collective-permute-start(bf16[384,1536]{1,0:T(8,128)(2,1)} %refs_4_.1), channel_id=1, source_target_pairs={{0,3},{1,0},{2,1},{3,2},{4,7},{5,4},{6,5},{7,6},{8,11},{9,8},{10,9... | collective-permute-start | bytes 3538952 | tf_op jit(solution)/shard_map/ppermute | solution.py:496
  32.0 2.0 %copy-start.13 = (bf16[384,1152]{1,0:T(8,128)(2,1)}, bf16[384,1152]{1,0:T(8,128)(2,1)S(1)}, u32[]{:S(2)}) copy-start(bf16[384,1152]{1,0:T(8,128)(2,1)S(1)} %collective-permute-done.2.got_ref) | copy-start | bytes 2654212
  32.0 2.0 %copy-start = (bf16[1024,768]{1,0:T(8,128)(2,1)}, bf16[1024,768]{1,0:T(8,128)(2,1)S(1)}, u32[]{:S(2)}) copy-start(bf16[1024,768]{1,0:T(8,128)(2,1)S(1)} %collective-permute-done.rest_0_.rest_3_.before) | copy-start | bytes 4718596
  38.1 12.9 %collective-permute-start.3 = (bf16[96,1152]{1,0:T(8,128)(2,1)}, bf16[96,1152]{1,0:T(8,128)(2,1)S(1)}, u32[]{:S(2)}, u32[]{:S(2)}) collective-permute-start(bf16[96,1152]{1,0:T(8,128)(2,1)} %get-tuple-element.28), channel_id=1, source_target_pairs={{0,64},{4,68},{8,72},{12,76},{16,80},{20,84},{24,88},{28,92},{32,9... | collective-permute-start | bytes 663560 | tf_op jit(solution)/shard_map/ppermute | solution.py:485
  41.7 12.7 %collective-permute-start.4 = (bf16[96,1152]{1,0:T(8,128)(2,1)}, bf16[96,1152]{1,0:T(8,128)(2,1)S(1)}, u32[]{:S(2)}, u32[]{:S(2)}) collective-permute-start(bf16[96,1152]{1,0:T(8,128)(2,1)} %get-tuple-element.29), channel_id=1, source_target_pairs={{0,128},{4,132},{8,136},{12,140},{16,144},{20,148},{24,152},{28,15... | collective-permute-start | bytes 663560 | tf_op jit(solution)/shard_map/ppermute | solution.py:485
  44.4 10.0 %collective-permute-start.5 = (bf16[96,1152]{1,0:T(8,128)(2,1)}, bf16[96,1152]{1,0:T(8,128)(2,1)S(1)}, u32[]{:S(2)}, u32[]{:S(2)}) collective-permute-start(bf16[96,1152]{1,0:T(8,128)(2,1)} %get-tuple-element.30), channel_id=1, source_target_pairs={{0,192},{4,196},{8,200},{12,204},{16,208},{20,212},{24,216},{28,22... | collective-permute-start | bytes 663560 | tf_op jit(solution)/shard_map/ppermute | solution.py:485
  51.0 3.4 %copy-start.14 = (bf16[96,1152]{1,0:T(8,128)(2,1)}, bf16[96,1152]{1,0:T(8,128)(2,1)S(1)}, u32[]{:S(2)}) copy-start(bf16[96,1152]{1,0:T(8,128)(2,1)S(1)} %collective-permute-done.3.g1) | copy-start | bytes 663556
  57.3 16.2 %all-to-all-start = ((bf16[8,16,1152]{2,1,0:T(8,128)(2,1)}), bf16[8,16,1152]{2,1,0:T(8,128)(2,1)S(1)}, u32[]{:S(2)}, u32[]{:S(2)}) async-start(bf16[8,16,1152]{2,1,0:T(8,128)(2,1)} %rs_z.1.dep_ref), calls=%async_computation | async-start | bytes 589824 | tf_op jit(solution)/shard_map/all_to_all | solution.py:501
  62.8 43.8 %collective-permute-start.9 = (bf16[384,1536]{1,0:T(8,128)(2,1)}, bf16[384,1536]{1,0:T(8,128)(2,1)S(1)}, u32[]{:S(2)}, u32[]{:S(2)}) collective-permute-start(bf16[384,1536]{1,0:T(8,128)(2,1)} %refs_4_.1), channel_id=1, source_target_pairs={{0,2},{1,3},{2,0},{3,1},{4,6},{5,7},{6,4},{7,5},{8,10},{9,11},{10,... | collective-permute-start | bytes 3538952 | tf_op jit(solution)/shard_map/ppermute | solution.py:496
  76.0 13.8 %all-to-all-start.1 = ((bf16[8,16,1152]{2,1,0:T(8,128)(2,1)}), bf16[8,16,1152]{2,1,0:T(8,128)(2,1)S(1)}, u32[]{:S(2)}, u32[]{:S(2)}) async-start(bf16[8,16,1152]{2,1,0:T(8,128)(2,1)} %renorm.1.dep_ref), calls=%async_computation.1 | async-start | bytes 589824 | tf_op jit(solution)/shard_map/all_to_all | solution.py:501
  91.5 9.5 %copy-start.3 = (bf16[6,16,1152]{2,1,0:T(8,128)(2,1)}, bf16[6,16,1152]{2,1,0:T(8,128)(2,1)S(1)}, u32[]{:S(2)}) copy-start(bf16[6,16,1152]{2,1,0:T(8,128)(2,1)S(1)} %slice.4) | copy-start | bytes 663556
  91.6 15.1 %collective-permute-start.8 = (bf16[96,1152]{1,0:T(8,128)(2,1)S(1)}, bf16[96,1152]{1,0:T(8,128)(2,1)S(1)}, u32[]{:S(2)}, u32[]{:S(2)}) collective-permute-start(bf16[96,1152]{1,0:T(8,128)(2,1)S(1)} %bitcast.7), channel_id=1, source_target_pairs={{0,64},{4,68},{8,72},{12,76},{16,80},{20,84},{24,88},{28,92},{32,9... | collective-permute-start | bytes 663560 | tf_op jit(solution)/shard_map/ppermute | solution.py:485
  93.8 14.6 %collective-permute-start.10 = (bf16[96,1152]{1,0:T(8,128)(2,1)S(1)}, bf16[96,1152]{1,0:T(8,128)(2,1)S(1)}, u32[]{:S(2)}, u32[]{:S(2)}) collective-permute-start(bf16[96,1152]{1,0:T(8,128)(2,1)S(1)} %bitcast.8), channel_id=1, source_target_pairs={{0,128},{4,132},{8,136},{12,140},{16,144},{20,148},{24,152},{28,15... | collective-permute-start | bytes 663560 | tf_op jit(solution)/shard_map/ppermute | solution.py:485
  97.7 11.2 %collective-permute-start.11 = (bf16[96,1152]{1,0:T(8,128)(2,1)S(1)}, bf16[96,1152]{1,0:T(8,128)(2,1)S(1)}, u32[]{:S(2)}, u32[]{:S(2)}) collective-permute-start(bf16[96,1152]{1,0:T(8,128)(2,1)S(1)} %bitcast.9), channel_id=1, source_target_pairs={{0,192},{4,196},{8,200},{12,204},{16,208},{20,212},{24,216},{28,22... | collective-permute-start | bytes 663560 | tf_op jit(solution)/shard_map/ppermute | solution.py:485
  97.7 11.9 %collective-permute-start.12 = (bf16[96,1152]{1,0:T(8,128)(2,1)S(1)}, bf16[96,1152]{1,0:T(8,128)(2,1)S(1)}, u32[]{:S(2)}, u32[]{:S(2)}) collective-permute-start(bf16[96,1152]{1,0:T(8,128)(2,1)S(1)} %bitcast.10), channel_id=1, source_target_pairs={{0,4},{4,0},{8,12},{12,8},{16,20},{20,16},{24,28},{28,24},{32,36},... | collective-permute-start | bytes 663560 | tf_op jit(solution)/shard_map/ppermute | solution.py:485
  106.6 2.4 %copy-start.23 = (f32[384]{0:T(512)S(1)}, f32[384]{0:T(512)}, u32[]{:S(2)}) copy-start(f32[384]{0:T(512)} %param.15) | copy-start | bytes 4612
  108.4 1.7 %collective-permute-start.13 = (bf16[96,1152]{1,0:T(8,128)(2,1)}, bf16[96,1152]{1,0:T(8,128)(2,1)S(1)}, u32[]{:S(2)}, u32[]{:S(2)}) collective-permute-start(bf16[96,1152]{1,0:T(8,128)(2,1)} %hold.3.rest_1_), channel_id=1, source_target_pairs={{0,4},{4,0},{8,12},{12,8},{16,20},{20,16},{24,28},{28,24},{32,36},... | collective-permute-start | bytes 663560 | tf_op jit(solution)/shard_map/ppermute | solution.py:485
  108.4 2.1 %copy-start.7 = (bf16[96,1152]{1,0:T(8,128)(2,1)}, bf16[96,1152]{1,0:T(8,128)(2,1)S(1)}, u32[]{:S(2)}) copy-start(bf16[96,1152]{1,0:T(8,128)(2,1)S(1)} %collective-permute-done.10.rest_2_) | copy-start | bytes 663556
  108.4 1.8 %collective-permute-start.14 = (bf16[96,1152]{1,0:T(8,128)(2,1)S(1)}, bf16[96,1152]{1,0:T(8,128)(2,1)S(1)}, u32[]{:S(2)}, u32[]{:S(2)}) collective-permute-start(bf16[96,1152]{1,0:T(8,128)(2,1)S(1)} %collective-permute-done.10.rest_2_), channel_id=1, source_target_pairs={{0,4},{4,0},{8,12},{12,8},{16,20},{20,16},{24,28},{28,24},{32,36},... | collective-permute-start | bytes 663560 | tf_op jit(solution)/shard_map/ppermute | solution.py:485
  108.9 1.6 %collective-permute-start.15 = (bf16[96,1152]{1,0:T(8,128)(2,1)S(1)}, bf16[96,1152]{1,0:T(8,128)(2,1)S(1)}, u32[]{:S(2)}, u32[]{:S(2)}) collective-permute-start(bf16[96,1152]{1,0:T(8,128)(2,1)S(1)} %collective-permute-done.11.rest_3_), channel_id=1, source_target_pairs={{0,4},{4,0},{8,12},{12,8},{16,20},{20,16},{24,28},{28,24},{32,36},... | collective-permute-start | bytes 663560 | tf_op jit(solution)/shard_map/ppermute | solution.py:485
  117.2 8.8 %collective-permute-start.16 = (bf16[256,384]{1,0:T(8,128)(2,1)}, bf16[256,384]{1,0:T(8,128)(2,1)S(1)}, u32[]{:S(2)}, u32[]{:S(2)}) collective-permute-start(bf16[256,384]{1,0:T(8,128)(2,1)} %get-tuple-element.32.rest_9_), channel_id=1, source_target_pairs={{0,1},{1,2},{2,3},{3,0},{4,5},{5,6},{6,7},{7,4},{8,9},{9,10},{10,1... | collective-permute-start | bytes 589832 | tf_op jit(solution)/shard_map/ppermute | solution.py:496
  117.2 12.2 %collective-permute-start.17 = (bf16[256,384]{1,0:T(8,128)(2,1)}, bf16[256,384]{1,0:T(8,128)(2,1)S(1)}, u32[]{:S(2)}, u32[]{:S(2)}) collective-permute-start(bf16[256,384]{1,0:T(8,128)(2,1)} %get-tuple-element.33), channel_id=1, source_target_pairs={{0,2},{1,3},{2,0},{3,1},{4,6},{5,7},{6,4},{7,5},{8,10},{9,11},{10,... | collective-permute-start | bytes 589832 | tf_op jit(solution)/shard_map/ppermute | solution.py:496
  120.2 9.2 %collective-permute-start.18 = (bf16[256,384]{1,0:T(8,128)(2,1)}, bf16[256,384]{1,0:T(8,128)(2,1)S(1)}, u32[]{:S(2)}, u32[]{:S(2)}) collective-permute-start(bf16[256,384]{1,0:T(8,128)(2,1)} %get-tuple-element.34), channel_id=1, source_target_pairs={{0,3},{1,0},{2,1},{3,2},{4,7},{5,4},{6,5},{7,6},{8,11},{9,8},{10,9... | collective-permute-start | bytes 589832 | tf_op jit(solution)/shard_map/ppermute | solution.py:496
  126.0 3.4 %copy-start.17 = (bf16[256,384]{1,0:T(8,128)(2,1)}, bf16[256,384]{1,0:T(8,128)(2,1)S(1)}, u32[]{:S(2)}) copy-start(bf16[256,384]{1,0:T(8,128)(2,1)S(1)} %collective-permute-done.16.refs_1_) | copy-start | bytes 589828
  136.3 6.8 %collective-permute-start.19 = (bf16[256,384]{1,0:T(8,128)(2,1)}, bf16[256,384]{1,0:T(8,128)(2,1)S(1)}, u32[]{:S(2)}, u32[]{:S(2)}) collective-permute-start(bf16[256,384]{1,0:T(8,128)(2,1)} %get-tuple-element.36), channel_id=1, source_target_pairs={{0,1},{1,2},{2,3},{3,0},{4,5},{5,6},{6,7},{7,4},{8,9},{9,10},{10,1... | collective-permute-start | bytes 589832 | tf_op jit(solution)/shard_map/ppermute | solution.py:496
  136.9 12.0 %collective-permute-start.20 = (bf16[256,384]{1,0:T(8,128)(2,1)}, bf16[256,384]{1,0:T(8,128)(2,1)S(1)}, u32[]{:S(2)}, u32[]{:S(2)}) collective-permute-start(bf16[256,384]{1,0:T(8,128)(2,1)} %get-tuple-element.37), channel_id=1, source_target_pairs={{0,2},{1,3},{2,0},{3,1},{4,6},{5,7},{6,4},{7,5},{8,10},{9,11},{10,... | collective-permute-start | bytes 589832 | tf_op jit(solution)/shard_map/ppermute | solution.py:496
  140.0 8.9 %collective-permute-start.21 = (bf16[256,384]{1,0:T(8,128)(2,1)}, bf16[256,384]{1,0:T(8,128)(2,1)S(1)}, u32[]{:S(2)}, u32[]{:S(2)}) collective-permute-start(bf16[256,384]{1,0:T(8,128)(2,1)} %get-tuple-element.38), channel_id=1, source_target_pairs={{0,3},{1,0},{2,1},{3,2},{4,7},{5,4},{6,5},{7,6},{8,11},{9,8},{10,9... | collective-permute-start | bytes 589832 | tf_op jit(solution)/shard_map/ppermute | solution.py:496
  143.1 5.8 %copy-start.20 = (bf16[256,384]{1,0:T(8,128)(2,1)}, bf16[256,384]{1,0:T(8,128)(2,1)S(1)}, u32[]{:S(2)}) copy-start(bf16[256,384]{1,0:T(8,128)(2,1)S(1)} %collective-permute-done.19.refs_1_) | copy-start | bytes 589828
  (16 other events, 13.2 us)

commit v11 on v10

--- a/solution.py
+++ b/solution.py
@@ -500,9 +500,9 @@
     def exchange(blocks):
         return lax.all_to_all(blocks, "tok", 0, 0, axis_index_groups=ALONG_Z)
 
-    query = project(tokens, qkv_weight, [give])
-    own, *gives = rs_x(pos, keep, got, [before, after, query])
+    own, *gives = rs_x(pos, keep, got, [before, after])
     got = [send(g, shift_x(d + 1)) for d, g in enumerate(gives)]
+    query = project(tokens, qkv_weight, [own])
     att = functools.partial(attend, pos=pos, lengths=frame_lengths[None, :], query=query, before=before, mine=kv, after=after)
     att0, old = att(0, dep=own, old=(first_fast, gate_fast, second_fast))
     total = rs_z(own, got, [att0, old])

time: 153 us -> 157 us (1.026)
  starting transfers between devices: 48 us -> 51.9 us
    ppermute x9, starting transfers between devices: 14.4 us -> 18.4 us  [spread(): lax.ppermute(p, 'head', shift_h(d))]
    ppermute x13, starting transfers between devices: 24.1 us -> 21.4 us  [body(): send = lambda value, pairs: lax.ppermute(value, 'tok', pairs)]
    all_to_all x2, starting transfers between devices: 9.43 us -> 12.2 us  [exchange(): return lax.all_to_all(blocks, 'tok', 0, 0, axis_index_groups=ALONG_Z)]
    ppermute x13, waiting for transfers between devices: 6.32 us -> 8.11 us  [body(): send = lambda value, pairs: lax.ppermute(value, 'tok', pairs)]
  transfers between devices with their start and end apart: 24 -> 24, of which waited for: 10 -> 11; matrix products, arithmetic and copies ran while one was open for 1% -> 1% of each run, Pallas kernels for 33% -> 32%
where the time goes in v11:
time: 157 us; the launch traced here: 156 us
  Pallas kernels  69.5 us (44%)
  starting transfers between devices  51.9 us (33%)
  waiting for transfers between devices  23.6 us (15%)
  local copies, waits for them, and re-layouts  9.79 us (6%)
    pallas_call x4, Pallas kernels, attend(): pl.pallas_call(kernel, grid=(1,), in_specs=([SMEM] + [DEP] * 3 if old els...  24 us
    ppermute x13, starting transfers between devices, body(): send = lambda value, pairs: lax.ppermute(value, 'tok', pairs)  21.4 us
    ppermute x9, starting transfers between devices, spread(): lax.ppermute(p, 'head', shift_h(d))  18.4 us
    all_to_all x2, starting transfers between devices, exchange(): return lax.all_to_all(blocks, 'tok', 0, 0, axis_index_groups=ALONG_Z)  12.2 us
    ppermute x9, waiting for transfers between devices, spread(): lax.ppermute(p, 'head', shift_h(d))  11.2 us
    pallas_call x1, Pallas kernels, update(): pl.pallas_call(update_kernel, grid=(1,), in_specs=[SMEM, full(kv.shape),...  9.69 us
    pallas_call x2, Pallas kernels, apply(): pl.pallas_call(functools.partial(apply_kernel, aheads), grid=(1,), in_spe...  9.38 us
    unnamed x48, local copies, waits for them, and re-layouts  8.26 us
  transfers between devices with their start and end apart: 24, of which 11 were waited for; matrix products, arithmetic and copies ran while one was open for 1% of the time, Pallas kernels for 32%

profile of v11, /device:TPU:1, one launch (start us, length us, event | category | flops | bytes accessed | tf_op | source)
XLA Modules:
  0.0 155.6 jit_solution(4766316952941549003)
XLA Ops:
  0.0 6.7 %keys.1 = (bf16[1024,768]{1,0:T(8,128)(2,1)}, f32[1024,3]{1,0:T(8,128)}) custom-call(bf16[1024,1536]{1,0:T(8,128)(2,1)} %t_ref.3, bf16[1536,1152]{1,0:T(8,128)(2,1)} %w_ref.3, bf16[3,1536]{1,0:T(4,128)(2,1)} %bitcast.14), custom_call_target="tpu_custom_call" | custom-call | tf_op jit(solution)/shard_map/keys/pallas_call | solution.py:74
  6.7 4.9 %collective-permute-start.1 = (bf16[1024,768]{1,0:T(8,128)(2,1)}, bf16[1024,768]{1,0:T(8,128)(2,1)S(1)}, u32[]{:S(2)}, u32[]{:S(2)}) collective-permute-start(bf16[1024,768]{1,0:T(8,128)(2,1)} %get-tuple-element.22.kv_ref.rest_4_.mine), channel_id=1, source_target_pairs={{0,4},{4,8},{8,12},{12,16},{16,20},{20,24},{24,28},{28,32},{32,36}... | collective-permute-start | bytes 4718600 | tf_op jit(solution)/shard_map/ppermute | solution.py:485
  11.7 1.9 %collective-permute-start.2 = (bf16[1024,768]{1,0:T(8,128)(2,1)}, bf16[1024,768]{1,0:T(8,128)(2,1)S(1)}, u32[]{:S(2)}, u32[]{:S(2)}) collective-permute-start(bf16[1024,768]{1,0:T(8,128)(2,1)} %get-tuple-element.22.kv_ref.rest_4_.mine), channel_id=1, source_target_pairs={{4,0},{8,4},{12,8},{16,12},{20,16},{24,20},{28,24},{32,28},{36,32}... | collective-permute-start | bytes 4718600 | tf_op jit(solution)/shard_map/ppermute | solution.py:485
  14.3 9.7 %update.1 = (bf16[384,1152]{1,0:T(8,128)(2,1)}, f32[384,1152]{1,0:T(8,128)}) custom-call(s32[4]{0:T(128)} %pad_add_fusion.pos_ref.rest_0_, bf16[1024,768]{1,0:T(8,128)(2,1)} %get-tuple-element.22.kv_ref.rest_4_.mine, f32[1024,3]{1,0:T(8,128)} %get-tuple-element.23.r_ref, bf16[1,384,768]{2,1,0:T(8,128)(2,1)} %w1_ref.3, bf16[1,384,768]{2,1,0:T(8,128)(2,1)} %w3_ref.3, ...), custom_call_target="tpu_custom_call" | custom-call | tf_op jit(solution)/shard_map/update/pallas_call | solution.py:121
  25.3 1.5 collective-permute-start.7
  26.8 2.5 %collective-permute-done.1.rest_0_.rest_3_.before = bf16[1024,768]{1,0:T(8,128)(2,1)S(1)} collective-permute-done((bf16[1024,768]{1,0:T(8,128)(2,1)}, bf16[1024,768]{1,0:T(8,128)(2,1)S(1)}, u32[]{:S(2)}, u32[]{:S(2)}) %collective-permute-start.1) | collective-permute-done | bytes 1572896 | tf_op jit(solution)/shard_map/ppermute | solution.py:485
  29.3 4.7 %collective-permute-done.2.rest_1_.rest_5_.after = bf16[1024,768]{1,0:T(8,128)(2,1)S(1)} collective-permute-done((bf16[1024,768]{1,0:T(8,128)(2,1)}, bf16[1024,768]{1,0:T(8,128)(2,1)S(1)}, u32[]{:S(2)}, u32[]{:S(2)}) %collective-permute-start.2) | collective-permute-done | bytes 1572896 | tf_op jit(solution)/shard_map/ppermute | solution.py:485
  35.2 2.9 %rs_x.1 = (f32[96,1152]{1,0:T(8,128)}, bf16[96,1152]{1,0:T(8,128)(2,1)}, bf16[96,1152]{1,0:T(8,128)(2,1)}, bf16[96,1152]{1,0:T(8,128)(2,1)}) custom-call(s32[4]{0:T(128)} %pad_add_fusion.pos_ref.rest_0_, f32[384,1152]{1,0:T(8,128)} %get-tuple-element.24.keep_ref, bf16[384,1152]{1,0:T(8,128)(2,1)} %copy-done.13, bf16[1024,768]{1,0:T(8,128)(2,1)} %copy-done, ...), custom_call_target="tpu_custom_call" | custom-call | tf_op jit(solution)/shard_map/rs_x/pallas_call | solution.py:149
  39.3 2.4 %collective-permute-start.4 = (bf16[96,1152]{1,0:T(8,128)(2,1)}, bf16[96,1152]{1,0:T(8,128)(2,1)S(1)}, u32[]{:S(2)}, u32[]{:S(2)}) collective-permute-start(bf16[96,1152]{1,0:T(8,128)(2,1)} %get-tuple-element.29), channel_id=1, source_target_pairs={{0,128},{4,132},{8,136},{12,140},{16,144},{20,148},{24,152},{28,15... | collective-permute-start | bytes 663560 | tf_op jit(solution)/shard_map/ppermute | solution.py:485
  42.9 5.2 %project.1.rest_2_.q_all.q_ref = bf16[1024,384]{1,0:T(8,128)(2,1)} custom-call(bf16[1024,1536]{1,0:T(8,128)(2,1)} %t_ref.3, bf16[1536,1152]{1,0:T(8,128)(2,1)} %w_ref.3, f32[96,1152]{1,0:T(8,128)} %get-tuple-element.26.rest_0_.rest_6_.own_ref), custom_call_target="tpu_custom_call" | custom-call | tf_op jit(solution)/shard_map/project/pallas_call | solution.py:236
  48.1 5.7 %attend_0.1 = (f32[256,384]{1,0:T(8,128)}, f32[16,1152]{1,0:T(8,128)}) custom-call(s32[4]{0:T(128)} %pad_add_fusion.pos_ref.rest_0_, bf16[1,384,768]{2,1,0:T(8,128)(2,1)} %w1_ref.3, bf16[1,384,768]{2,1,0:T(8,128)(2,1)} %w3_ref.3, bf16[1,768,384]{2,1,0:T(8,128)(2,1)} %w2_ref.3, s32[4]{0:T(128)} %pad_add_fusion.pos_ref.rest_0_, s32[1,128]{1,0:T(1,128)} %bitcast.15, ...), custom_call_target="tpu_custom_call" | custom-call | tf_op jit(solution)/shard_map/attend_0/pallas_call | solution.py:362
  54.6 2.1 %rs_z.1.dep_ref = bf16[8,16,1152]{2,1,0:T(8,128)(2,1)} custom-call(f32[96,1152]{1,0:T(8,128)} %get-tuple-element.26.rest_0_.rest_6_.own_ref, bf16[96,1152]{1,0:T(8,128)(2,1)} %copy-done.14, bf16[96,1152]{1,0:T(8,128)(2,1)} %copy-done.15, bf16[96,1152]{1,0:T(8,128)(2,1)} %copy-done.16, f32[256,384]{1,0:T(8,128)} %get-tuple-element.31.rest_0_.rest_8_, ...), custom_call_target="tpu_custom_call" | custom-call | tf_op jit(solution)/shard_map/rs_z/pallas_call | solution.py:172
  56.7 8.1 %all-to-all-start = ((bf16[8,16,1152]{2,1,0:T(8,128)(2,1)}), bf16[8,16,1152]{2,1,0:T(8,128)(2,1)S(1)}, u32[]{:S(2)}, u32[]{:S(2)}) async-start(bf16[8,16,1152]{2,1,0:T(8,128)(2,1)} %rs_z.1.dep_ref), calls=%async_computation | async-start | bytes 589824 | tf_op jit(solution)/shard_map/all_to_all | solution.py:501
  64.8 3.3 %collective-permute-start.9 = (bf16[384,1536]{1,0:T(8,128)(2,1)}, bf16[384,1536]{1,0:T(8,128)(2,1)S(1)}, u32[]{:S(2)}, u32[]{:S(2)}) collective-permute-start(bf16[384,1536]{1,0:T(8,128)(2,1)} %refs_4_.1), channel_id=1, source_target_pairs={{0,2},{1,3},{2,0},{3,1},{4,6},{5,7},{6,4},{7,5},{8,10},{9,11},{10,... | collective-permute-start | bytes 3538952 | tf_op jit(solution)/shard_map/ppermute | solution.py:496
  68.0 7.1 %attend_1.1.rest_0_.rest_8_ = f32[256,384]{1,0:T(8,128)} custom-call(s32[4]{0:T(128)} %pad_add_fusion.pos_ref.rest_0_, s32[1,128]{1,0:T(1,128)} %bitcast.16, bf16[1024,384]{1,0:T(8,128)(2,1)} %project.1.rest_2_.q_all.q_ref, bf16[1024,768]{1,0:T(8,128)(2,1)} %copy-done, bf16[1024,768]{1,0:T(8,128)(2,1)} %get-tuple-element.22.kv_ref.rest_4_.mine, ...), custom_call_target="tpu_custom_call" | custom-call | tf_op jit(solution)/shard_map/attend_1/pallas_call | solution.py:362
  76.2 1.9 %renorm.1.dep_ref = bf16[8,16,1152]{2,1,0:T(8,128)(2,1)} custom-call(f32[16,1152]{1,0:T(8,128)} %get-tuple-element.27.rest_1_.old_ref, bf16[8,16,1152]{2,1,0:T(8,128)(2,1)} %copy-done.6, f32[256,384]{1,0:T(8,128)} %attend_1.1.rest_0_.rest_8_, bf16[384,1536]{1,0:T(8,128)(2,1)} %collective-permute-done.6.rest_1_.refs_5_, ...), custom_call_target="tpu_custom_call" | custom-call | tf_op jit(solution)/shard_map/renorm/pallas_call | solution.py:201
  78.0 4.1 %all-to-all-start.1 = ((bf16[8,16,1152]{2,1,0:T(8,128)(2,1)}), bf16[8,16,1152]{2,1,0:T(8,128)(2,1)S(1)}, u32[]{:S(2)}, u32[]{:S(2)}) async-start(bf16[8,16,1152]{2,1,0:T(8,128)(2,1)} %renorm.1.dep_ref), calls=%async_computation.1 | async-start | bytes 589824 | tf_op jit(solution)/shard_map/all_to_all | solution.py:501
  82.1 5.6 %attend_2.1.rest_0_.rest_9_ = f32[256,384]{1,0:T(8,128)} custom-call(s32[4]{0:T(128)} %pad_add_fusion.pos_ref.rest_0_, s32[1,128]{1,0:T(1,128)} %bitcast.17, bf16[1024,384]{1,0:T(8,128)(2,1)} %project.1.rest_2_.q_all.q_ref, bf16[1024,768]{1,0:T(8,128)(2,1)} %copy-done, bf16[1024,768]{1,0:T(8,128)(2,1)} %get-tuple-element.22.kv_ref.rest_4_.mine, ...), custom_call_target="tpu_custom_call" | custom-call | tf_op jit(solution)/shard_map/attend_2/pallas_call | solution.py:362
  87.7 4.0 %all-to-all-done.1.value_ref = bf16[8,16,1152]{2,1,0:T(8,128)(2,1)S(1)} async-done(((bf16[8,16,1152]{2,1,0:T(8,128)(2,1)}), bf16[8,16,1152]{2,1,0:T(8,128)(2,1)S(1)}, u32[]{:S(2)}, u32[]{:S(2)}) %all-to-all-start.1) | async-done | bytes 294944 | tf_op jit(solution)/shard_map/all_to_all | solution.py:501
  93.4 5.2 %collective-permute-start.8 = (bf16[96,1152]{1,0:T(8,128)(2,1)S(1)}, bf16[96,1152]{1,0:T(8,128)(2,1)S(1)}, u32[]{:S(2)}, u32[]{:S(2)}) collective-permute-start(bf16[96,1152]{1,0:T(8,128)(2,1)S(1)} %bitcast.7), channel_id=1, source_target_pairs={{0,64},{4,68},{8,72},{12,76},{16,80},{20,84},{24,88},{28,92},{32,9... | collective-permute-start | bytes 663560 | tf_op jit(solution)/shard_map/ppermute | solution.py:485
  99.2 2.0 %collective-permute-start.11 = (bf16[96,1152]{1,0:T(8,128)(2,1)S(1)}, bf16[96,1152]{1,0:T(8,128)(2,1)S(1)}, u32[]{:S(2)}, u32[]{:S(2)}) collective-permute-start(bf16[96,1152]{1,0:T(8,128)(2,1)S(1)} %bitcast.9), channel_id=1, source_target_pairs={{0,192},{4,196},{8,200},{12,204},{16,208},{20,212},{24,216},{28,22... | collective-permute-start | bytes 663560 | tf_op jit(solution)/shard_map/ppermute | solution.py:485
  102.5 5.6 %attend_3.1.rest_0_.rest_10_ = f32[256,384]{1,0:T(8,128)} custom-call(s32[4]{0:T(128)} %pad_add_fusion.pos_ref.rest_0_, s32[1,128]{1,0:T(1,128)} %bitcast.18, bf16[1024,384]{1,0:T(8,128)(2,1)} %project.1.rest_2_.q_all.q_ref, bf16[1024,768]{1,0:T(8,128)(2,1)} %copy-done, bf16[1024,768]{1,0:T(8,128)(2,1)} %get-tuple-element.22.kv_ref.rest_4_.mine, ...), custom_call_target="tpu_custom_call" | custom-call | tf_op jit(solution)/shard_map/attend_3/pallas_call | solution.py:362
  113.1 5.6 %apply_3.1 = (bf16[256,384]{1,0:T(8,128)(2,1)}, bf16[256,384]{1,0:T(8,128)(2,1)}, bf16[256,384]{1,0:T(8,128)(2,1)}) custom-call(s32[4]{0:T(128)} %pad_add_fusion.pos_ref.rest_0_, bf16[1024,384]{1,0:T(8,128)(2,1)} %project.1.rest_2_.q_all.q_ref, f32[1,384]{1,0:T(1,128)} %broadcast_in_dim.6.gain_ref, bf16[96,1152]{1,0:T(8,128)(2,1)} %bitcast.12, ...), custom_call_target="tpu_custom_call" | custom-call | tf_op jit(solution)/shard_map/apply_3/pallas_call | solution.py:413
  119.5 5.4 %collective-permute-start.17 = (bf16[256,384]{1,0:T(8,128)(2,1)}, bf16[256,384]{1,0:T(8,128)(2,1)S(1)}, u32[]{:S(2)}, u32[]{:S(2)}) collective-permute-start(bf16[256,384]{1,0:T(8,128)(2,1)} %get-tuple-element.33), channel_id=1, source_target_pairs={{0,2},{1,3},{2,0},{3,1},{4,6},{5,7},{6,4},{7,5},{8,10},{9,11},{10,... | collective-permute-start | bytes 589832 | tf_op jit(solution)/shard_map/ppermute | solution.py:496
  124.9 2.0 %collective-permute-start.18 = (bf16[256,384]{1,0:T(8,128)(2,1)}, bf16[256,384]{1,0:T(8,128)(2,1)S(1)}, u32[]{:S(2)}, u32[]{:S(2)}) collective-permute-start(bf16[256,384]{1,0:T(8,128)(2,1)} %get-tuple-element.34), channel_id=1, source_target_pairs={{0,3},{1,0},{2,1},{3,2},{4,7},{5,4},{6,5},{7,6},{8,11},{9,8},{10,9... | collective-permute-start | bytes 589832 | tf_op jit(solution)/shard_map/ppermute | solution.py:496
  126.8 3.8 %apply_1.1.refs_0_ = bf16[256,384]{1,0:T(8,128)(2,1)} custom-call(s32[4]{0:T(128)} %pad_add_fusion.pos_ref.rest_0_, bf16[1024,384]{1,0:T(8,128)(2,1)} %project.1.rest_2_.q_all.q_ref, f32[1,384]{1,0:T(1,128)} %broadcast_in_dim.6.gain_ref, bf16[96,1152]{1,0:T(8,128)(2,1)} %bitcast.13, bf16[96,1152]{1,0:T(8,128)(2,1)} %hold.3.rest_1_, ...), custom_call_target="tpu_custom_call" | custom-call | tf_op jit(solution)/shard_map/apply_1/pallas_call | solution.py:413
  130.7 3.6 %collective-permute-done.17.refs_2_ = bf16[256,384]{1,0:T(8,128)(2,1)S(1)} collective-permute-done((bf16[256,384]{1,0:T(8,128)(2,1)}, bf16[256,384]{1,0:T(8,128)(2,1)S(1)}, u32[]{:S(2)}, u32[]{:S(2)}) %collective-permute-start.17) | collective-permute-done | bytes 196640 | tf_op jit(solution)/shard_map/ppermute | solution.py:496
  135.6 5.5 %output.1 = (bf16[256,384]{1,0:T(8,128)(2,1)}, bf16[256,384]{1,0:T(8,128)(2,1)}, bf16[256,384]{1,0:T(8,128)(2,1)}, bf16[256,384]{1,0:T(8,128)(2,1)}) custom-call(s32[4]{0:T(128)} %pad_add_fusion.pos_ref.rest_0_, bf16[256,384]{1,0:T(8,128)(2,1)} %apply_1.1.refs_0_, bf16[256,384]{1,0:T(8,128)(2,1)} %copy-done.17, bf16[256,384]{1,0:T(8,128)(2,1)} %copy-done.18, ...), custom_call_target="tpu_custom_call" | custom-call | tf_op jit(solution)/shard_map/output/pallas_call | solution.py:440
  141.1 2.7 %collective-permute-start.20 = (bf16[256,384]{1,0:T(8,128)(2,1)}, bf16[256,384]{1,0:T(8,128)(2,1)S(1)}, u32[]{:S(2)}, u32[]{:S(2)}) collective-permute-start(bf16[256,384]{1,0:T(8,128)(2,1)} %get-tuple-element.37), channel_id=1, source_target_pairs={{0,2},{1,3},{2,0},{3,1},{4,6},{5,7},{6,4},{7,5},{8,10},{9,11},{10,... | collective-permute-start | bytes 589832 | tf_op jit(solution)/shard_map/ppermute | solution.py:496
  145.2 2.9 %collective-permute-done.19.refs_1_ = bf16[256,384]{1,0:T(8,128)(2,1)S(1)} collective-permute-done((bf16[256,384]{1,0:T(8,128)(2,1)}, bf16[256,384]{1,0:T(8,128)(2,1)S(1)}, u32[]{:S(2)}, u32[]{:S(2)}) %collective-permute-start.19) | collective-permute-done | bytes 196640 | tf_op jit(solution)/shard_map/ppermute | solution.py:496
  148.1 4.4 %collective-permute-done.20.refs_2_ = bf16[256,384]{1,0:T(8,128)(2,1)S(1)} collective-permute-done((bf16[256,384]{1,0:T(8,128)(2,1)}, bf16[256,384]{1,0:T(8,128)(2,1)S(1)}, u32[]{:S(2)}, u32[]{:S(2)}) %collective-permute-start.20) | collective-permute-done | bytes 196640 | tf_op jit(solution)/shard_map/ppermute | solution.py:496
  153.4 2.2 %arrange.1 = bf16[1024,384]{1,0:T(8,128)(2,1)} custom-call(s32[4]{0:T(128)} %pad_add_fusion.pos_ref.rest_0_, bf16[256,384]{1,0:T(8,128)(2,1)} %get-tuple-element.35.refs_0_, bf16[256,384]{1,0:T(8,128)(2,1)} %copy-done.20, bf16[256,384]{1,0:T(8,128)(2,1)} %copy-done.21, bf16[256,384]{1,0:T(8,128)(2,1)} %copy-done.22), custom_call_target="tpu_custom_call" | custom-call | tf_op jit(solution)/shard_map/arrange/pallas_call | solution.py:460
  (83 shorter events, 20.1 us)
Async XLA Ops:
  6.7 22.6 %collective-permute-start.1 = (bf16[1024,768]{1,0:T(8,128)(2,1)}, bf16[1024,768]{1,0:T(8,128)(2,1)S(1)}, u32[]{:S(2)}, u32[]{:S(2)}) collective-permute-start(bf16[1024,768]{1,0:T(8,128)(2,1)} %get-tuple-element.22.kv_ref.rest_4_.mine), channel_id=1, source_target_pairs={{0,4},{4,8},{8,12},{12,16},{16,20},{20,24},{24,28},{28,32},{32,36}... | collective-permute-start | bytes 4718600 | tf_op jit(solution)/shard_map/ppermute | solution.py:485
  11.7 22.3 %collective-permute-start.2 = (bf16[1024,768]{1,0:T(8,128)(2,1)}, bf16[1024,768]{1,0:T(8,128)(2,1)S(1)}, u32[]{:S(2)}, u32[]{:S(2)}) collective-permute-start(bf16[1024,768]{1,0:T(8,128)(2,1)} %get-tuple-element.22.kv_ref.rest_4_.mine), channel_id=1, source_target_pairs={{4,0},{8,4},{12,8},{16,12},{20,16},{24,20},{28,24},{32,28},{36,32}... | collective-permute-start | bytes 4718600 | tf_op jit(solution)/shard_map/ppermute | solution.py:485
  24.0 2.8 %collective-permute-start = (bf16[384,1152]{1,0:T(8,128)(2,1)}, bf16[384,1152]{1,0:T(8,128)(2,1)S(1)}, u32[]{:S(2)}, u32[]{:S(2)}) collective-permute-start(bf16[384,1152]{1,0:T(8,128)(2,1)} %get-tuple-element.25), channel_id=1, source_target_pairs={{0,4},{4,0},{8,12},{12,8},{16,20},{20,16},{24,28},{28,24},{32,36},... | collective-permute-start | bytes 2654216 | tf_op jit(solution)/shard_map/ppermute | solution.py:485
  24.0 51.2 %collective-permute-start.6 = (bf16[384,1536]{1,0:T(8,128)(2,1)}, bf16[384,1536]{1,0:T(8,128)(2,1)}, u32[]{:S(2)}, u32[]{:S(2)}) collective-permute-start(bf16[384,1536]{1,0:T(8,128)(2,1)} %refs_4_.1), channel_id=1, source_target_pairs={{0,1},{1,2},{2,3},{3,0},{4,5},{5,6},{6,7},{7,4},{8,9},{9,10},{10,1... | collective-permute-start | bytes 3538952 | tf_op jit(solution)/shard_map/ppermute | solution.py:496
  25.3 49.9 %collective-permute-start.7 = (bf16[384,1536]{1,0:T(8,128)(2,1)}, bf16[384,1536]{1,0:T(8,128)(2,1)}, u32[]{:S(2)}, u32[]{:S(2)}) collective-permute-start(bf16[384,1536]{1,0:T(8,128)(2,1)} %refs_4_.1), channel_id=1, source_target_pairs={{0,3},{1,0},{2,1},{3,2},{4,7},{5,4},{6,5},{7,6},{8,11},{9,8},{10,9... | collective-permute-start | bytes 3538952 | tf_op jit(solution)/shard_map/ppermute | solution.py:496
  26.8 7.2 %copy-start.13 = (bf16[384,1152]{1,0:T(8,128)(2,1)}, bf16[384,1152]{1,0:T(8,128)(2,1)S(1)}, u32[]{:S(2)}) copy-start(bf16[384,1152]{1,0:T(8,128)(2,1)S(1)} %collective-permute-done.got_ref) | copy-start | bytes 2654212
  29.3 4.7 %copy-start = (bf16[1024,768]{1,0:T(8,128)(2,1)}, bf16[1024,768]{1,0:T(8,128)(2,1)S(1)}, u32[]{:S(2)}) copy-start(bf16[1024,768]{1,0:T(8,128)(2,1)S(1)} %collective-permute-done.1.rest_0_.rest_3_.before) | copy-start | bytes 4718596
  38.1 15.7 %collective-permute-start.3 = (bf16[96,1152]{1,0:T(8,128)(2,1)}, bf16[96,1152]{1,0:T(8,128)(2,1)S(1)}, u32[]{:S(2)}, u32[]{:S(2)}) collective-permute-start(bf16[96,1152]{1,0:T(8,128)(2,1)} %get-tuple-element.28), channel_id=1, source_target_pairs={{0,64},{4,68},{8,72},{12,76},{16,80},{20,84},{24,88},{28,92},{32,9... | collective-permute-start | bytes 663560 | tf_op jit(solution)/shard_map/ppermute | solution.py:485
  39.3 14.5 %collective-permute-start.4 = (bf16[96,1152]{1,0:T(8,128)(2,1)}, bf16[96,1152]{1,0:T(8,128)(2,1)S(1)}, u32[]{:S(2)}, u32[]{:S(2)}) collective-permute-start(bf16[96,1152]{1,0:T(8,128)(2,1)} %get-tuple-element.29), channel_id=1, source_target_pairs={{0,128},{4,132},{8,136},{12,140},{16,144},{20,148},{24,152},{28,15... | collective-permute-start | bytes 663560 | tf_op jit(solution)/shard_map/ppermute | solution.py:485
  41.7 12.1 %collective-permute-start.5 = (bf16[96,1152]{1,0:T(8,128)(2,1)}, bf16[96,1152]{1,0:T(8,128)(2,1)S(1)}, u32[]{:S(2)}, u32[]{:S(2)}) collective-permute-start(bf16[96,1152]{1,0:T(8,128)(2,1)} %get-tuple-element.30), channel_id=1, source_target_pairs={{0,192},{4,196},{8,200},{12,204},{16,208},{20,212},{24,216},{28,22... | collective-permute-start | bytes 663560 | tf_op jit(solution)/shard_map/ppermute | solution.py:485
  56.7 18.7 %all-to-all-start = ((bf16[8,16,1152]{2,1,0:T(8,128)(2,1)}), bf16[8,16,1152]{2,1,0:T(8,128)(2,1)S(1)}, u32[]{:S(2)}, u32[]{:S(2)}) async-start(bf16[8,16,1152]{2,1,0:T(8,128)(2,1)} %rs_z.1.dep_ref), calls=%async_computation | async-start | bytes 589824 | tf_op jit(solution)/shard_map/all_to_all | solution.py:501
  64.8 43.4 %collective-permute-start.9 = (bf16[384,1536]{1,0:T(8,128)(2,1)}, bf16[384,1536]{1,0:T(8,128)(2,1)S(1)}, u32[]{:S(2)}, u32[]{:S(2)}) collective-permute-start(bf16[384,1536]{1,0:T(8,128)(2,1)} %refs_4_.1), channel_id=1, source_target_pairs={{0,2},{1,3},{2,0},{3,1},{4,6},{5,7},{6,4},{7,5},{8,10},{9,11},{10,... | collective-permute-start | bytes 3538952 | tf_op jit(solution)/shard_map/ppermute | solution.py:496
  78.0 13.7 %all-to-all-start.1 = ((bf16[8,16,1152]{2,1,0:T(8,128)(2,1)}), bf16[8,16,1152]{2,1,0:T(8,128)(2,1)S(1)}, u32[]{:S(2)}, u32[]{:S(2)}) async-start(bf16[8,16,1152]{2,1,0:T(8,128)(2,1)} %renorm.1.dep_ref), calls=%async_computation.1 | async-start | bytes 589824 | tf_op jit(solution)/shard_map/all_to_all | solution.py:501
  93.4 9.1 %copy-start.3 = (bf16[6,16,1152]{2,1,0:T(8,128)(2,1)}, bf16[6,16,1152]{2,1,0:T(8,128)(2,1)S(1)}, u32[]{:S(2)}) copy-start(bf16[6,16,1152]{2,1,0:T(8,128)(2,1)S(1)} %slice.4) | copy-start | bytes 663556
  93.4 14.7 %collective-permute-start.8 = (bf16[96,1152]{1,0:T(8,128)(2,1)S(1)}, bf16[96,1152]{1,0:T(8,128)(2,1)S(1)}, u32[]{:S(2)}, u32[]{:S(2)}) collective-permute-start(bf16[96,1152]{1,0:T(8,128)(2,1)S(1)} %bitcast.7), channel_id=1, source_target_pairs={{0,64},{4,68},{8,72},{12,76},{16,80},{20,84},{24,88},{28,92},{32,9... | collective-permute-start | bytes 663560 | tf_op jit(solution)/shard_map/ppermute | solution.py:485
  98.7 11.2 %collective-permute-start.10 = (bf16[96,1152]{1,0:T(8,128)(2,1)S(1)}, bf16[96,1152]{1,0:T(8,128)(2,1)S(1)}, u32[]{:S(2)}, u32[]{:S(2)}) collective-permute-start(bf16[96,1152]{1,0:T(8,128)(2,1)S(1)} %bitcast.8), channel_id=1, source_target_pairs={{0,128},{4,132},{8,136},{12,140},{16,144},{20,148},{24,152},{28,15... | collective-permute-start | bytes 663560 | tf_op jit(solution)/shard_map/ppermute | solution.py:485
  99.2 11.2 %collective-permute-start.11 = (bf16[96,1152]{1,0:T(8,128)(2,1)S(1)}, bf16[96,1152]{1,0:T(8,128)(2,1)S(1)}, u32[]{:S(2)}, u32[]{:S(2)}) collective-permute-start(bf16[96,1152]{1,0:T(8,128)(2,1)S(1)} %bitcast.9), channel_id=1, source_target_pairs={{0,192},{4,196},{8,200},{12,204},{16,208},{20,212},{24,216},{28,22... | collective-permute-start | bytes 663560 | tf_op jit(solution)/shard_map/ppermute | solution.py:485
  101.2 9.9 %collective-permute-start.12 = (bf16[96,1152]{1,0:T(8,128)(2,1)S(1)}, bf16[96,1152]{1,0:T(8,128)(2,1)S(1)}, u32[]{:S(2)}, u32[]{:S(2)}) collective-permute-start(bf16[96,1152]{1,0:T(8,128)(2,1)S(1)} %bitcast.10), channel_id=1, source_target_pairs={{0,4},{4,0},{8,12},{12,8},{16,20},{20,16},{24,28},{28,24},{32,36},... | collective-permute-start | bytes 663560 | tf_op jit(solution)/shard_map/ppermute | solution.py:485
  108.1 2.4 %copy-start.23 = (f32[384]{0:T(512)S(1)}, f32[384]{0:T(512)}, u32[]{:S(2)}) copy-start(f32[384]{0:T(512)} %param.15) | copy-start | bytes 4612
  109.9 1.7 %collective-permute-start.13 = (bf16[96,1152]{1,0:T(8,128)(2,1)}, bf16[96,1152]{1,0:T(8,128)(2,1)S(1)}, u32[]{:S(2)}, u32[]{:S(2)}) collective-permute-start(bf16[96,1152]{1,0:T(8,128)(2,1)} %hold.3.rest_1_), channel_id=1, source_target_pairs={{0,4},{4,0},{8,12},{12,8},{16,20},{20,16},{24,28},{28,24},{32,36},... | collective-permute-start | bytes 663560 | tf_op jit(solution)/shard_map/ppermute | solution.py:485
  109.9 2.1 %copy-start.7 = (bf16[96,1152]{1,0:T(8,128)(2,1)}, bf16[96,1152]{1,0:T(8,128)(2,1)S(1)}, u32[]{:S(2)}) copy-start(bf16[96,1152]{1,0:T(8,128)(2,1)S(1)} %collective-permute-done.10.rest_2_) | copy-start | bytes 663556
  109.9 1.8 %collective-permute-start.14 = (bf16[96,1152]{1,0:T(8,128)(2,1)S(1)}, bf16[96,1152]{1,0:T(8,128)(2,1)S(1)}, u32[]{:S(2)}, u32[]{:S(2)}) collective-permute-start(bf16[96,1152]{1,0:T(8,128)(2,1)S(1)} %collective-permute-done.10.rest_2_), channel_id=1, source_target_pairs={{0,4},{4,0},{8,12},{12,8},{16,20},{20,16},{24,28},{28,24},{32,36},... | collective-permute-start | bytes 663560 | tf_op jit(solution)/shard_map/ppermute | solution.py:485
  110.4 1.6 %copy-start.8 = (bf16[96,1152]{1,0:T(8,128)(2,1)}, bf16[96,1152]{1,0:T(8,128)(2,1)S(1)}, u32[]{:S(2)}) copy-start(bf16[96,1152]{1,0:T(8,128)(2,1)S(1)} %collective-permute-done.11.rest_3_) | copy-start | bytes 663556
  110.4 1.6 %collective-permute-start.15 = (bf16[96,1152]{1,0:T(8,128)(2,1)S(1)}, bf16[96,1152]{1,0:T(8,128)(2,1)S(1)}, u32[]{:S(2)}, u32[]{:S(2)}) collective-permute-start(bf16[96,1152]{1,0:T(8,128)(2,1)S(1)} %collective-permute-done.11.rest_3_), channel_id=1, source_target_pairs={{0,4},{4,0},{8,12},{12,8},{16,20},{20,16},{24,28},{28,24},{32,36},... | collective-permute-start | bytes 663560 | tf_op jit(solution)/shard_map/ppermute | solution.py:485
  118.7 12.0 %collective-permute-start.16 = (bf16[256,384]{1,0:T(8,128)(2,1)}, bf16[256,384]{1,0:T(8,128)(2,1)S(1)}, u32[]{:S(2)}, u32[]{:S(2)}) collective-permute-start(bf16[256,384]{1,0:T(8,128)(2,1)} %get-tuple-element.32.rest_9_), channel_id=1, source_target_pairs={{0,1},{1,2},{2,3},{3,0},{4,5},{5,6},{6,7},{7,4},{8,9},{9,10},{10,1... | collective-permute-start | bytes 589832 | tf_op jit(solution)/shard_map/ppermute | solution.py:496
  119.5 14.8 %collective-permute-start.17 = (bf16[256,384]{1,0:T(8,128)(2,1)}, bf16[256,384]{1,0:T(8,128)(2,1)S(1)}, u32[]{:S(2)}, u32[]{:S(2)}) collective-permute-start(bf16[256,384]{1,0:T(8,128)(2,1)} %get-tuple-element.33), channel_id=1, source_target_pairs={{0,2},{1,3},{2,0},{3,1},{4,6},{5,7},{6,4},{7,5},{8,10},{9,11},{10,... | collective-permute-start | bytes 589832 | tf_op jit(solution)/shard_map/ppermute | solution.py:496
  124.9 9.4 %collective-permute-start.18 = (bf16[256,384]{1,0:T(8,128)(2,1)}, bf16[256,384]{1,0:T(8,128)(2,1)S(1)}, u32[]{:S(2)}, u32[]{:S(2)}) collective-permute-start(bf16[256,384]{1,0:T(8,128)(2,1)} %get-tuple-element.34), channel_id=1, source_target_pairs={{0,3},{1,0},{2,1},{3,2},{4,7},{5,4},{6,5},{7,6},{8,11},{9,8},{10,9... | collective-permute-start | bytes 589832 | tf_op jit(solution)/shard_map/ppermute | solution.py:496
  130.7 3.6 %copy-start.17 = (bf16[256,384]{1,0:T(8,128)(2,1)}, bf16[256,384]{1,0:T(8,128)(2,1)S(1)}, u32[]{:S(2)}) copy-start(bf16[256,384]{1,0:T(8,128)(2,1)S(1)} %collective-permute-done.16.refs_1_) | copy-start | bytes 589828
  141.1 7.0 %collective-permute-start.19 = (bf16[256,384]{1,0:T(8,128)(2,1)}, bf16[256,384]{1,0:T(8,128)(2,1)S(1)}, u32[]{:S(2)}, u32[]{:S(2)}) collective-permute-start(bf16[256,384]{1,0:T(8,128)(2,1)} %get-tuple-element.36), channel_id=1, source_target_pairs={{0,1},{1,2},{2,3},{3,0},{4,5},{5,6},{6,7},{7,4},{8,9},{9,10},{10,1... | collective-permute-start | bytes 589832 | tf_op jit(solution)/shard_map/ppermute | solution.py:496
  141.1 11.5 %collective-permute-start.20 = (bf16[256,384]{1,0:T(8,128)(2,1)}, bf16[256,384]{1,0:T(8,128)(2,1)S(1)}, u32[]{:S(2)}, u32[]{:S(2)}) collective-permute-start(bf16[256,384]{1,0:T(8,128)(2,1)} %get-tuple-element.37), channel_id=1, source_target_pairs={{0,2},{1,3},{2,0},{3,1},{4,6},{5,7},{6,4},{7,5},{8,10},{9,11},{10,... | collective-permute-start | bytes 589832 | tf_op jit(solution)/shard_map/ppermute | solution.py:496
  143.8 8.9 %collective-permute-start.21 = (bf16[256,384]{1,0:T(8,128)(2,1)}, bf16[256,384]{1,0:T(8,128)(2,1)S(1)}, u32[]{:S(2)}, u32[]{:S(2)}) collective-permute-start(bf16[256,384]{1,0:T(8,128)(2,1)} %get-tuple-element.38), channel_id=1, source_target_pairs={{0,3},{1,0},{2,1},{3,2},{4,7},{5,4},{6,5},{7,6},{8,11},{9,8},{10,9... | collective-permute-start | bytes 589832 | tf_op jit(solution)/shard_map/ppermute | solution.py:496
  148.1 4.7 %copy-start.20 = (bf16[256,384]{1,0:T(8,128)(2,1)}, bf16[256,384]{1,0:T(8,128)(2,1)S(1)}, u32[]{:S(2)}) copy-start(bf16[256,384]{1,0:T(8,128)(2,1)S(1)} %collective-permute-done.19.refs_1_) | copy-start | bytes 589828
  (16 other events, 12.3 us)
